TPU v7x, 128 devices: a whole 4x4x4 slice. The times are simulated.
128 devices in a mesh: dp: 4 (over x), fsdp: 4 (over z_hi, core), seq: 8 (over z_lo, y).
Axes of the slice: x: 4, y: 4, z: 4 (z_hi: 2, z_lo: 2; z = z_hi * 2 + z_lo), core: 2. Of those that a mesh axis runs over, the one named last changes fastest.
Arguments:
- frames: bfloat16 [16, 2048, 1536], P(('dp', 'fsdp'), 'seq'), may hold values from -6 to 6
- projection: bfloat16 [1536, 3072], P('fsdp'), may hold values from -1 to 1
- lengths: int32 [16], P(('dp', 'fsdp')), may hold values from 512 to 2048
- cotangent: bfloat16 [16, 2048, 1024], P(('dp', 'fsdp'), 'seq'), may hold values from -24 to 24
Outputs:
- context: bfloat16 [16, 2048, 1024], P(('dp', 'fsdp'), 'seq')
- input_gradient: float32 [16, 2048, 1536], P(('dp', 'fsdp'), 'seq')
- projection_gradient: float32 [1536, 3072], P(('dp', 'fsdp', 'seq'))
All inputs are finite; a program needn't handle non-finite values.
Results may differ from a plain program's by a relative error of at most 0.007.
The roundings to bfloat16 on the way count: a program that leaves them out, or rounds other values in their place, can miss the bound.
Values may be sent and summed in bfloat16 or wider, within the bound.
No kernel may reach another device: no remote copies, remote signals or barrier semaphores. Data moves between devices by JAX's collectives and lax.ppermute only.
A program may use at most 128 MiB of HBM per device.

v0:
```python
import math

import jax
import jax.numpy as jnp
from jax import lax
from jax.sharding import PartitionSpec as P

HEADS = 16
HD = 64


EPS = 1e-05


def block_probabilities(query_block, key_rows, valid):
    factor = 1.0 / math.sqrt(query_block.shape[-1])
    scores = (
        jnp.einsum("qhd,khd->hqk", query_block, key_rows, preferred_element_type=jnp.float32)
        * factor
    )
    scores = jnp.where(valid[None, None, :], scores, -jnp.inf)
    row_peak = jnp.max(scores, axis=2, keepdims=True)
    exponentials = jnp.exp(scores - row_peak)
    return exponentials / jnp.sum(exponentials, axis=2, keepdims=True)


def forward_heads(query_rows, key_rows, value_rows, valid, block_rows):
    total_rows = query_rows.shape[0]

    def forward_one_block(block_index):
        first_row = block_index * block_rows
        query_block = lax.dynamic_slice_in_dim(query_rows, first_row, block_rows, 0)
        probabilities = block_probabilities(query_block, key_rows, valid)
        mixture = jnp.einsum(
            "hqk,khd->qhd",
            probabilities.astype(jnp.bfloat16),
            value_rows,
            preferred_element_type=jnp.float32,
        )
        keep_rows = lax.dynamic_slice_in_dim(valid, first_row, block_rows, 0)
        return jnp.where(keep_rows[:, None, None], mixture, jnp.zeros_like(mixture)).astype(
            jnp.bfloat16
        )

    blocks = lax.map(forward_one_block, jnp.arange(total_rows // block_rows, dtype=jnp.int32))
    return blocks.reshape(query_rows.shape)


def backward_heads(query_rows, key_rows, value_rows, upstream, valid, block_rows):
    total_rows = query_rows.shape[0]
    factor = 1.0 / math.sqrt(query_rows.shape[-1])

    def backward_one_block(running, block_index):
        key_sum, value_sum = running
        first_row = block_index * block_rows
        query_block = lax.dynamic_slice_in_dim(query_rows, first_row, block_rows, 0)
        upstream_block = lax.dynamic_slice_in_dim(upstream, first_row, block_rows, 0)
        keep_rows = lax.dynamic_slice_in_dim(valid, first_row, block_rows, 0)
        upstream_block = jnp.where(
            keep_rows[:, None, None], upstream_block, jnp.zeros_like(upstream_block)
        )
        probabilities = block_probabilities(query_block, key_rows, valid)
        value_sum = value_sum + jnp.einsum(
            "hqk,qhd->khd",
            probabilities.astype(jnp.bfloat16),
            upstream_block,
            preferred_element_type=jnp.float32,
        )
        prob_gradient = jnp.einsum(
            "qhd,khd->hqk", upstream_block, value_rows, preferred_element_type=jnp.float32
        )
        row_inner = jnp.sum(probabilities * prob_gradient, axis=2, keepdims=True)
        score_gradient = (probabilities * (prob_gradient - row_inner) * factor).astype(jnp.bfloat16)
        query_gradient = jnp.einsum(
            "hqk,khd->qhd", score_gradient, key_rows, preferred_element_type=jnp.float32
        ).astype(jnp.bfloat16)
        key_sum = key_sum + jnp.einsum(
            "hqk,qhd->khd", score_gradient, query_block, preferred_element_type=jnp.float32
        )
        return ((key_sum, value_sum), query_gradient)

    empty_sum = jnp.zeros(key_rows.shape, jnp.float32)
    sums, query_blocks = lax.scan(
        backward_one_block,
        (empty_sum, empty_sum),
        jnp.arange(total_rows // block_rows, dtype=jnp.int32),
    )
    return (
        query_blocks.reshape(query_rows.shape),
        sums[0].astype(jnp.bfloat16),
        sums[1].astype(jnp.bfloat16),
    )


def body(frames, projection, lengths, cotangent):
    inputs = frames[0]
    upstream = cotangent[0]
    length = lengths[0]
    seq_count = lax.axis_size("seq")
    local_rows, feature_count = inputs.shape
    total_rows = local_rows * seq_count
    head_count = HEADS // seq_count
    group_width = head_count * HD
    block_rows = 512
    as_float = inputs.astype(jnp.float32)
    centered = as_float - jnp.mean(as_float, axis=1, keepdims=True)
    inv_std = lax.rsqrt(jnp.mean(centered * centered, axis=1, keepdims=True) + EPS)
    standard = centered * inv_std
    normed = standard.astype(jnp.bfloat16)
    valid = jnp.arange(total_rows, dtype=jnp.int32) < length
    weight_full = lax.all_gather(projection, "fsdp", axis=0, tiled=True)
    packed = jnp.dot(normed, weight_full, preferred_element_type=jnp.float32).astype(jnp.bfloat16)
    packed = packed.reshape(local_rows, 3, seq_count, group_width)
    upstream_four = upstream.reshape(local_rows, 1, seq_count, group_width)
    head_inputs, head_upstream = (
        lax.all_to_all(packed, "seq", split_axis=2, concat_axis=0, tiled=True),
        lax.all_to_all(upstream_four, "seq", split_axis=2, concat_axis=0, tiled=True),
    )
    head_inputs = head_inputs.reshape(total_rows, 3, head_count, HD)
    head_grads = head_upstream.reshape(total_rows, head_count, HD)
    query_rows = head_inputs[:, 0]
    key_rows = head_inputs[:, 1]
    value_rows = head_inputs[:, 2]
    mixture = forward_heads(query_rows, key_rows, value_rows, valid, block_rows)
    returned_context = lax.all_to_all(
        mixture.reshape(total_rows, 1, group_width), "seq", split_axis=0, concat_axis=1, tiled=True
    )
    context = returned_context.reshape(local_rows, seq_count * group_width)
    query_gradient, key_gradient, value_gradient = backward_heads(
        query_rows, key_rows, value_rows, head_grads, valid, block_rows
    )
    stacked = jnp.stack([query_gradient, key_gradient, value_gradient], axis=1).reshape(
        total_rows, 3, 1, group_width
    )
    returned = lax.all_to_all(stacked, "seq", split_axis=0, concat_axis=2, tiled=True)
    packed_gradient = returned.reshape(local_rows, 3 * seq_count * group_width)
    normed_gradient = lax.dot_general(
        packed_gradient, weight_full, (((1,), (1,)), ((), ())), preferred_element_type=jnp.float32
    )
    projection_gradient = lax.psum_scatter(
        lax.dot_general(
            normed, packed_gradient, (((0,), (0,)), ((), ())), preferred_element_type=jnp.float32
        ),
        ("dp", "fsdp", "seq"),
        scatter_dimension=0,
        tiled=True,
    )
    row_mean = jnp.mean(normed_gradient, axis=1, keepdims=True)
    projected = jnp.mean(normed_gradient * standard, axis=1, keepdims=True)
    input_gradient = inv_std * (normed_gradient - row_mean - standard * projected)
    return (context[None], input_gradient[None], projection_gradient)


def solution(mesh):
    placed = (
        P(("dp", "fsdp"), "seq", None),
        P("fsdp", None),
        P(("dp", "fsdp")),
        P(("dp", "fsdp"), "seq", None),
    )
    return jax.shard_map(
        body,
        mesh=mesh,
        in_specs=placed,
        out_specs=(
            P(("dp", "fsdp"), "seq", None),
            P(("dp", "fsdp"), "seq", None),
            P(("dp", "fsdp", "seq"), None),
        ),
        check_vma=False,
    )
```

profile of v0, /device:TPU:0, one launch (start us, length us, event | category | flops | bytes accessed | tf_op | source)
XLA Modules:
  0.0 1031.1 jit_solution(2263338651254375848)
XLA Ops:
  9.9 5.9 all-to-all-start.2
  18.7 61.9 %all-gather.2.cloned.1.call-done = bf16[1536,3072]{1,0:T(8,128)(2,1)} async-done(((bf16[384,3072]{1,0:T(8,128)(2,1)}), bf16[1536,3072]{1,0:T(8,128)(2,1)}) %all-gather.2.cloned.1.call-update) | async-done | bytes 9437200 | tf_op jit(solution)/shard_map/all_gather | solution.py:111
  80.6 6.7 fusion.105
  94.7 20.5 %all-to-all-done = bf16[256,3,8,128]{3,0,1,2:T(8,128)(2,1)S(1)} async-done(((bf16[256,3,8,128]{3,0,1,2:T(8,128)(2,1)}), bf16[256,3,8,128]{3,0,1,2:T(8,128)(2,1)S(1)}, u32[]{:S(2)}, u32[]{:S(2)}) %all-to-all-start) | async-done | bytes 1572896 | tf_op jit(solution)/shard_map/all_to_all | solution.py:116
  120.6 197.0 %while.26 = (s32[]{:T(128)}, f32[2048,2,64]{0,2,1:T(8,128)}, f32[2048,2,64]{0,2,1:T(8,128)}, bf16[4,512,2,64]{1,3,2,0:T(8,128)(2,1)S(1)}, s32[4]{0:T(128)S(1)}, ...) while((s32[]{:T(128)}, f32[2048,2,64]{0,2,1:T(8,128)}, ...), condition=%wide.region_10.11_spmd.clone, body=%wide.region_6.10_spmd.clone.sunk | while | flops 1385373696 | bytes 107115288 | solution.py:83
  126.5 6.6 fusion.168
  133.0 14.4 %fusion.171 = bf16[4,512,2,64]{1,3,2,0:T(8,128)(2,1)S(1)} fusion(bf16[4,512,2,64]{1,3,2,0:T(8,128)(2,1)S(1)} %get-tuple-element.351, s32[]{:T(128)} %get-tuple-element.348, bf16[2048,2,64]{0,2,1:T(8,128)(2,1)S(1)} %get-tuple-element.369, f32[2,512,2048]{2,1,0:T(8,128)} %fusion.167, f32[2,512,2048]{2,1,0:T(8,128)} %get-tuple-element.299, ...), kind=kOutput, calls=%fused_computation.43.clone.1 | convolution fusion | flops 283184128 | bytes 34218496 | tf_op jit(solution)/shard_map/while/body/eval_jaxpr/hqk,khd->qhd/dot_general | solution.py:74
  152.9 15.8 %fusion.169 = f32[2048,2,64]{0,2,1:T(8,128)S(1)} fusion(f32[2,512,2048]{2,1,0:T(8,128)} %fusion.167, f32[2048,2,64]{0,2,1:T(8,128)S(1)} %copy-done.1, pred[]{:T(512)S(6)} %compare.3, bf16[2048,2,64]{0,2,1:T(8,128)(2,1)} %get-tuple-element.367, s32[]{:T(128)S(6)} %select_n.71, f32[2,512,2048]{2,1,0:T(8,128)} %get-tuple-element.299, ...), kind=kOutput, calls=%fused_computation.40.clone.1 | convolution fusion | flops 283642880 | bytes 35790852 | tf_op jit(solution)/shard_map/while/body/eval_jaxpr/hqk,qhd->khd/dot_general | solution.py:77
  175.6 6.6 fusion.168
  182.1 14.4 %fusion.171 = bf16[4,512,2,64]{1,3,2,0:T(8,128)(2,1)S(1)} fusion(bf16[4,512,2,64]{1,3,2,0:T(8,128)(2,1)S(1)} %get-tuple-element.351, s32[]{:T(128)} %get-tuple-element.348, bf16[2048,2,64]{0,2,1:T(8,128)(2,1)S(1)} %get-tuple-element.369, f32[2,512,2048]{2,1,0:T(8,128)} %fusion.167, f32[2,512,2048]{2,1,0:T(8,128)} %get-tuple-element.299, ...), kind=kOutput, calls=%fused_computation.43.clone.1 | convolution fusion | flops 283184128 | bytes 34218496 | tf_op jit(solution)/shard_map/while/body/eval_jaxpr/hqk,khd->qhd/dot_general | solution.py:74
  196.5 5.6 fusion.170
  202.2 15.8 %fusion.169 = f32[2048,2,64]{0,2,1:T(8,128)S(1)} fusion(f32[2,512,2048]{2,1,0:T(8,128)} %fusion.167, f32[2048,2,64]{0,2,1:T(8,128)S(1)} %copy-done.1, pred[]{:T(512)S(6)} %compare.3, bf16[2048,2,64]{0,2,1:T(8,128)(2,1)} %get-tuple-element.367, s32[]{:T(128)S(6)} %select_n.71, f32[2,512,2048]{2,1,0:T(8,128)} %get-tuple-element.299, ...), kind=kOutput, calls=%fused_computation.40.clone.1 | convolution fusion | flops 283642880 | bytes 35790852 | tf_op jit(solution)/shard_map/while/body/eval_jaxpr/hqk,qhd->khd/dot_general | solution.py:77
  224.9 6.6 fusion.168
  231.4 14.4 %fusion.171 = bf16[4,512,2,64]{1,3,2,0:T(8,128)(2,1)S(1)} fusion(bf16[4,512,2,64]{1,3,2,0:T(8,128)(2,1)S(1)} %get-tuple-element.351, s32[]{:T(128)} %get-tuple-element.348, bf16[2048,2,64]{0,2,1:T(8,128)(2,1)S(1)} %get-tuple-element.369, f32[2,512,2048]{2,1,0:T(8,128)} %fusion.167, f32[2,512,2048]{2,1,0:T(8,128)} %get-tuple-element.299, ...), kind=kOutput, calls=%fused_computation.43.clone.1 | convolution fusion | flops 283184128 | bytes 34218496 | tf_op jit(solution)/shard_map/while/body/eval_jaxpr/hqk,khd->qhd/dot_general | solution.py:74
  251.5 15.8 %fusion.169 = f32[2048,2,64]{0,2,1:T(8,128)S(1)} fusion(f32[2,512,2048]{2,1,0:T(8,128)} %fusion.167, f32[2048,2,64]{0,2,1:T(8,128)S(1)} %copy-done.1, pred[]{:T(512)S(6)} %compare.3, bf16[2048,2,64]{0,2,1:T(8,128)(2,1)} %get-tuple-element.367, s32[]{:T(128)S(6)} %select_n.71, f32[2,512,2048]{2,1,0:T(8,128)} %get-tuple-element.299, ...), kind=kOutput, calls=%fused_computation.40.clone.1 | convolution fusion | flops 283642880 | bytes 35790852 | tf_op jit(solution)/shard_map/while/body/eval_jaxpr/hqk,qhd->khd/dot_general | solution.py:77
  274.2 6.6 fusion.168
  280.8 14.4 %fusion.171 = bf16[4,512,2,64]{1,3,2,0:T(8,128)(2,1)S(1)} fusion(bf16[4,512,2,64]{1,3,2,0:T(8,128)(2,1)S(1)} %get-tuple-element.351, s32[]{:T(128)} %get-tuple-element.348, bf16[2048,2,64]{0,2,1:T(8,128)(2,1)S(1)} %get-tuple-element.369, f32[2,512,2048]{2,1,0:T(8,128)} %fusion.167, f32[2,512,2048]{2,1,0:T(8,128)} %get-tuple-element.299, ...), kind=kOutput, calls=%fused_computation.43.clone.1 | convolution fusion | flops 283184128 | bytes 34218496 | tf_op jit(solution)/shard_map/while/body/eval_jaxpr/hqk,khd->qhd/dot_general | solution.py:74
  300.8 15.8 %fusion.169 = f32[2048,2,64]{0,2,1:T(8,128)S(1)} fusion(f32[2,512,2048]{2,1,0:T(8,128)} %fusion.167, f32[2048,2,64]{0,2,1:T(8,128)S(1)} %copy-done.1, pred[]{:T(512)S(6)} %compare.3, bf16[2048,2,64]{0,2,1:T(8,128)(2,1)} %get-tuple-element.367, s32[]{:T(128)S(6)} %select_n.71, f32[2,512,2048]{2,1,0:T(8,128)} %get-tuple-element.299, ...), kind=kOutput, calls=%fused_computation.40.clone.1 | convolution fusion | flops 283642880 | bytes 35790852 | tf_op jit(solution)/shard_map/while/body/eval_jaxpr/hqk,qhd->khd/dot_general | solution.py:77
  325.4 30.3 %all_to_all.60 = bf16[2048,3,1,128]{3,1,2,0:T(4,128)(2,1)S(1)} all-to-all(bf16[2048,3,1,128]{3,1,2,0:T(4,128)(2,1)S(1)} %copy.54), channel_id=1, replica_groups=mesh['dp'=4,'fsdp'=4,'seq'=8] {'seq'}, dimensions={0} | all-to-all | bytes 3145728 | tf_op jit(solution)/shard_map/all_to_all | solution.py:135
  358.8 8.0 fusion.107
  366.8 370.0 %fusion = f32[16,3072]{1,0:T(8,128)} fusion(f32[1536,3072]{1,0:T(8,128)} %fusion.107), kind=kCustom, calls=%all-reduce-scatter | all-reduce-scatter fusion | flops 6291457 | bytes 19070976
  750.4 51.9 %while.25 = (s32[]{:T(128)}, bf16[4,512,2,64]{1,3,2,0:T(8,128)(2,1)S(1)}, s32[4]{0:T(128)S(1)}, pred[2048]{0:T(1024)(128)(4,1)S(1)}, bf16[2048,2,64]{0,2,1:T(8,1...) while((s32[]{:T(128)}, ...), condition=%wide.region_5.6_spmd, body=%wide.region_2.5_spmd.sunk | while | flops 549586944 | bytes 18099892 | solution.py:45
  751.6 6.9 fusion.157
  764.6 6.9 fusion.157
  777.5 6.9 fusion.157
  790.5 6.9 fusion.157
  809.8 12.6 %reduce.1 = bf16[2048,128]{1,0:T(8,128)(2,1)S(1)} reduce(bf16[2048,1,128]{2,1,0:T(2,128)(2,1)} %reshape.82, bf16[]{:T(256)} %broadcast.123), dimensions={1}, to_apply=%reshape.82.reduce_sub_computation | reduce | bytes 1048578 | tf_op jit(solution)/shard_map/reshape;reshape | solution.py:126
  823.3 6.7 all-to-all-start.1
  836.5 10.2 collective-permute-start.16
  861.9 13.2 %collective-permute-start.21 = (f32[16,3072]{1,0:T(8,128)}, f32[16,3072]{1,0:T(8,128)}, u32[]{:S(2)}, u32[]{:S(2)}) collective-permute-start(f32[16,3072]{1,0:T(8,128)} %fusion), channel_id=1, source_target_pairs={{0,22},{1,23},{2,24},{3,25},{4,26},{5,27},{6,28},{7,29},{8,30},{9,... | collective-permute-start | bytes 589832
  929.0 5.8 collective-permute-start.9
  938.7 84.0 %concatenate.1 = f32[524,3072]{1,0:T(8,128)} concatenate(f32[12,3072]{1,0:T(8,128)S(1)} %copy-done.7, f32[16,3072]{1,0:T(8,128)S(1)} %collective-permute-done.30, f32[16,3072]{1,0:T(8,128)S(1)} %collective-permute-done.29, f32[16,3072]{1,0:T(8,128)S(1)} %collective-permute-done.28, f32[16,3072]{1,0:T(8,128)} %copy-done.9, f32[16,3072]{1,0:T(8,128)} %copy-done.8, ...), dimensions={0} | concatenate | bytes 12877824
  (173 shorter events, 195.0 us)
Async XLA Ops:
  7.2 73.4 %all-gather.2.cloned.1.call-start = ((), (), s32[]{:S(2)}) async-start(), calls=%async_computation.4 | async-start | bytes 11796480 | tf_op jit(solution)/shard_map/all_gather | solution.py:111
  9.9 79.2 %all-to-all-start.2 = ((bf16[256,1,8,128]{0,3,1,2:T(8,128)(2,1)}), bf16[256,1,8,128]{0,3,1,2:T(8,128)(2,1)S(1)}, u32[]{:S(2)}, u32[]{:S(2)}) async-start(bf16[256,1,8,128]{0,3,1,2:T(8,128)(2,1)} %bitcast.12), calls=%async_computation.2 | async-start | bytes 1048576 | tf_op jit(solution)/shard_map/all_to_all | solution.py:117
  89.1 26.1 %all-to-all-start = ((bf16[256,3,8,128]{3,0,1,2:T(8,128)(2,1)}), bf16[256,3,8,128]{3,0,1,2:T(8,128)(2,1)S(1)}, u32[]{:S(2)}, u32[]{:S(2)}) async-start(bf16[256,3,8,128]{3,0,1,2:T(8,128)(2,1)} %copy.46), calls=%async_computation | async-start | bytes 3145728 | tf_op jit(solution)/shard_map/all_to_all | solution.py:116
  740.4 89.7 %collective-permute-start.1 = (f32[16,3072]{1,0:T(8,128)}, f32[16,3072]{1,0:T(8,128)}, u32[]{:S(2)}, u32[]{:S(2)}) collective-permute-start(f32[16,3072]{1,0:T(8,128)} %fusion), channel_id=1, source_target_pairs={{0,2},{1,3},{2,4},{3,5},{4,6},{5,7},{6,8},{7,9},{8,10},{9,11},{10,... | collective-permute-start | bytes 589832
  742.5 92.0 %collective-permute-start.10 = (f32[16,3072]{1,0:T(8,128)}, f32[16,3072]{1,0:T(8,128)}, u32[]{:S(2)}, u32[]{:S(2)}) collective-permute-start(f32[16,3072]{1,0:T(8,128)} %fusion), channel_id=1, source_target_pairs={{0,11},{1,12},{2,13},{3,14},{4,15},{5,16},{6,17},{7,18},{8,19},{9,... | collective-permute-start | bytes 589832
  744.5 92.0 %collective-permute-start.11 = (f32[16,3072]{1,0:T(8,128)}, f32[16,3072]{1,0:T(8,128)}, u32[]{:S(2)}, u32[]{:S(2)}) collective-permute-start(f32[16,3072]{1,0:T(8,128)} %fusion), channel_id=1, source_target_pairs={{0,12},{1,13},{2,14},{3,15},{4,16},{5,17},{6,18},{7,19},{8,20},{9,... | collective-permute-start | bytes 589832
  746.4 100.2 %collective-permute-start.12 = (f32[16,3072]{1,0:T(8,128)}, f32[16,3072]{1,0:T(8,128)}, u32[]{:S(2)}, u32[]{:S(2)}) collective-permute-start(f32[16,3072]{1,0:T(8,128)} %fusion), channel_id=1, source_target_pairs={{0,13},{1,14},{2,15},{3,16},{4,17},{5,18},{6,19},{7,20},{8,21},{9,... | collective-permute-start | bytes 589832
  748.4 103.1 %collective-permute-start.13 = (f32[16,3072]{1,0:T(8,128)}, f32[16,3072]{1,0:T(8,128)}, u32[]{:S(2)}, u32[]{:S(2)}) collective-permute-start(f32[16,3072]{1,0:T(8,128)} %fusion), channel_id=1, source_target_pairs={{0,14},{1,15},{2,16},{3,17},{4,18},{5,19},{6,20},{7,21},{8,22},{9,... | collective-permute-start | bytes 589832
  823.3 56.3 %all-to-all-start.1 = ((bf16[8,2,16384]{2,1,0:T(2,128)(2,1)}), bf16[8,2,16384]{2,1,0:T(2,128)(2,1)S(1)}, u32[]{:S(2)}, u32[]{:S(2)}) async-start(bf16[8,2,16384]{2,1,0:T(2,128)(2,1)} %reshape.83), calls=%async_computation.1 | async-start | bytes 1048576 | tf_op jit(solution)/shard_map/all_to_all | solution.py:125
  830.0 26.0 %collective-permute-start.14 = (f32[16,3072]{1,0:T(8,128)}, f32[16,3072]{1,0:T(8,128)}, u32[]{:S(2)}, u32[]{:S(2)}) collective-permute-start(f32[16,3072]{1,0:T(8,128)} %fusion), channel_id=1, source_target_pairs={{0,15},{1,16},{2,17},{3,18},{4,19},{5,20},{6,21},{7,22},{8,23},{9,... | collective-permute-start | bytes 589832
  834.5 23.5 %collective-permute-start.15 = (f32[16,3072]{1,0:T(8,128)}, f32[16,3072]{1,0:T(8,128)}, u32[]{:S(2)}, u32[]{:S(2)}) collective-permute-start(f32[16,3072]{1,0:T(8,128)} %fusion), channel_id=1, source_target_pairs={{0,16},{1,17},{2,18},{3,19},{4,20},{5,21},{6,22},{7,23},{8,24},{9,... | collective-permute-start | bytes 589832
  836.5 23.5 %collective-permute-start.16 = (f32[16,3072]{1,0:T(8,128)}, f32[16,3072]{1,0:T(8,128)}, u32[]{:S(2)}, u32[]{:S(2)}) collective-permute-start(f32[16,3072]{1,0:T(8,128)} %fusion), channel_id=1, source_target_pairs={{0,17},{1,18},{2,19},{3,20},{4,21},{5,22},{6,23},{7,24},{8,25},{9,... | collective-permute-start | bytes 589832
  846.6 15.3 %collective-permute-start.17 = (f32[16,3072]{1,0:T(8,128)}, f32[16,3072]{1,0:T(8,128)}, u32[]{:S(2)}, u32[]{:S(2)}) collective-permute-start(f32[16,3072]{1,0:T(8,128)} %fusion), channel_id=1, source_target_pairs={{0,18},{1,19},{2,20},{3,21},{4,22},{5,23},{6,24},{7,25},{8,26},{9,... | collective-permute-start | bytes 589832
  851.5 23.6 %collective-permute-start.18 = (f32[16,3072]{1,0:T(8,128)}, f32[16,3072]{1,0:T(8,128)}, u32[]{:S(2)}, u32[]{:S(2)}) collective-permute-start(f32[16,3072]{1,0:T(8,128)} %fusion), channel_id=1, source_target_pairs={{0,19},{1,20},{2,21},{3,22},{4,23},{5,24},{6,25},{7,26},{8,27},{9,... | collective-permute-start | bytes 589832
  856.0 27.9 %collective-permute-start.19 = (f32[16,3072]{1,0:T(8,128)}, f32[16,3072]{1,0:T(8,128)}, u32[]{:S(2)}, u32[]{:S(2)}) collective-permute-start(f32[16,3072]{1,0:T(8,128)} %fusion), channel_id=1, source_target_pairs={{0,20},{1,21},{2,22},{3,23},{4,24},{5,25},{6,26},{7,27},{8,28},{9,... | collective-permute-start | bytes 589832
  858.0 28.8 %collective-permute-start.2 = (f32[16,3072]{1,0:T(8,128)}, f32[16,3072]{1,0:T(8,128)}, u32[]{:S(2)}, u32[]{:S(2)}) collective-permute-start(f32[16,3072]{1,0:T(8,128)} %fusion), channel_id=1, source_target_pairs={{0,3},{1,4},{2,5},{3,6},{4,7},{5,8},{6,9},{7,10},{8,11},{9,12},{10... | collective-permute-start | bytes 589832
  860.0 30.9 %collective-permute-start.20 = (f32[16,3072]{1,0:T(8,128)}, f32[16,3072]{1,0:T(8,128)}, u32[]{:S(2)}, u32[]{:S(2)}) collective-permute-start(f32[16,3072]{1,0:T(8,128)} %fusion), channel_id=1, source_target_pairs={{0,21},{1,22},{2,23},{3,24},{4,25},{5,26},{6,27},{7,28},{8,29},{9,... | collective-permute-start | bytes 589832
  861.9 31.6 %collective-permute-start.21 = (f32[16,3072]{1,0:T(8,128)}, f32[16,3072]{1,0:T(8,128)}, u32[]{:S(2)}, u32[]{:S(2)}) collective-permute-start(f32[16,3072]{1,0:T(8,128)} %fusion), channel_id=1, source_target_pairs={{0,22},{1,23},{2,24},{3,25},{4,26},{5,27},{6,28},{7,29},{8,30},{9,... | collective-permute-start | bytes 589832
  875.1 19.7 %collective-permute-start.22 = (f32[16,3072]{1,0:T(8,128)}, f32[16,3072]{1,0:T(8,128)}, u32[]{:S(2)}, u32[]{:S(2)}) collective-permute-start(f32[16,3072]{1,0:T(8,128)} %fusion), channel_id=1, source_target_pairs={{0,23},{1,24},{2,25},{3,26},{4,27},{5,28},{6,29},{7,30},{8,31},{9,... | collective-permute-start | bytes 589832
  883.9 18.3 %collective-permute-start.23 = (f32[16,3072]{1,0:T(8,128)}, f32[16,3072]{1,0:T(8,128)S(1)}, u32[]{:S(2)}, u32[]{:S(2)}) collective-permute-start(f32[16,3072]{1,0:T(8,128)} %fusion), channel_id=1, source_target_pairs={{0,24},{1,25},{2,26},{3,27},{4,28},{5,29},{6,30},{7,31},{8,32},{9,... | collective-permute-start | bytes 589832
  886.8 16.8 %collective-permute-start.24 = (f32[16,3072]{1,0:T(8,128)}, f32[16,3072]{1,0:T(8,128)S(1)}, u32[]{:S(2)}, u32[]{:S(2)}) collective-permute-start(f32[16,3072]{1,0:T(8,128)} %fusion), channel_id=1, source_target_pairs={{0,25},{1,26},{2,27},{3,28},{4,29},{5,30},{6,31},{7,32},{8,33},{9,... | collective-permute-start | bytes 589832
  890.9 15.1 %collective-permute-start.25 = (f32[16,3072]{1,0:T(8,128)}, f32[16,3072]{1,0:T(8,128)S(1)}, u32[]{:S(2)}, u32[]{:S(2)}) collective-permute-start(f32[16,3072]{1,0:T(8,128)} %fusion), channel_id=1, source_target_pairs={{0,26},{1,27},{2,28},{3,29},{4,30},{5,31},{6,32},{7,33},{8,34},{9,... | collective-permute-start | bytes 589832
  893.5 16.8 %collective-permute-start.26 = (f32[16,3072]{1,0:T(8,128)}, f32[16,3072]{1,0:T(8,128)S(1)}, u32[]{:S(2)}, u32[]{:S(2)}) collective-permute-start(f32[16,3072]{1,0:T(8,128)} %fusion), channel_id=1, source_target_pairs={{0,27},{1,28},{2,29},{3,30},{4,31},{5,32},{6,33},{7,34},{8,35},{9,... | collective-permute-start | bytes 589832
  894.8 18.3 %collective-permute-start.27 = (f32[16,3072]{1,0:T(8,128)}, f32[16,3072]{1,0:T(8,128)S(1)}, u32[]{:S(2)}, u32[]{:S(2)}) collective-permute-start(f32[16,3072]{1,0:T(8,128)} %fusion), channel_id=1, source_target_pairs={{0,28},{1,29},{2,30},{3,31},{4,32},{5,33},{6,34},{7,35},{8,36},{9,... | collective-permute-start | bytes 589832
  902.3 12.2 %collective-permute-start.28 = (f32[16,3072]{1,0:T(8,128)}, f32[16,3072]{1,0:T(8,128)S(1)}, u32[]{:S(2)}, u32[]{:S(2)}) collective-permute-start(f32[16,3072]{1,0:T(8,128)} %fusion), channel_id=1, source_target_pairs={{0,29},{1,30},{2,31},{3,32},{4,33},{5,34},{6,35},{7,36},{8,37},{9,... | collective-permute-start | bytes 589832
  903.6 16.3 %collective-permute-start.29 = (f32[16,3072]{1,0:T(8,128)}, f32[16,3072]{1,0:T(8,128)S(1)}, u32[]{:S(2)}, u32[]{:S(2)}) collective-permute-start(f32[16,3072]{1,0:T(8,128)} %fusion), channel_id=1, source_target_pairs={{0,30},{1,31},{2,32},{3,33},{4,34},{5,35},{6,36},{7,37},{8,38},{9,... | collective-permute-start | bytes 589832
  906.0 17.9 %collective-permute-start.3 = (f32[16,3072]{1,0:T(8,128)}, f32[16,3072]{1,0:T(8,128)S(1)}, u32[]{:S(2)}, u32[]{:S(2)}) collective-permute-start(f32[16,3072]{1,0:T(8,128)} %fusion), channel_id=1, source_target_pairs={{0,4},{1,5},{2,6},{3,7},{4,8},{5,9},{6,10},{7,11},{8,12},{9,13},{1... | collective-permute-start | bytes 589832
  910.3 15.0 %collective-permute-start.30 = (f32[16,3072]{1,0:T(8,128)}, f32[16,3072]{1,0:T(8,128)S(1)}, u32[]{:S(2)}, u32[]{:S(2)}) collective-permute-start(f32[16,3072]{1,0:T(8,128)} %fusion), channel_id=1, source_target_pairs={{0,31},{1,32},{2,33},{3,34},{4,35},{5,36},{6,37},{7,38},{8,39},{9,... | collective-permute-start | bytes 589832
  913.2 15.8 %collective-permute-start.4 = (f32[16,3072]{1,0:T(8,128)}, f32[16,3072]{1,0:T(8,128)S(1)}, u32[]{:S(2)}, u32[]{:S(2)}) collective-permute-start(f32[16,3072]{1,0:T(8,128)} %fusion), channel_id=1, source_target_pairs={{0,5},{1,6},{2,7},{3,8},{4,9},{5,10},{6,11},{7,12},{8,13},{9,14},{... | collective-permute-start | bytes 589832
  914.5 21.9 %collective-permute-start.5 = (f32[16,3072]{1,0:T(8,128)}, f32[16,3072]{1,0:T(8,128)S(1)}, u32[]{:S(2)}, u32[]{:S(2)}) collective-permute-start(f32[16,3072]{1,0:T(8,128)} %fusion), channel_id=1, source_target_pairs={{0,6},{1,7},{2,8},{3,9},{4,10},{5,11},{6,12},{7,13},{8,14},{9,15},... | collective-permute-start | bytes 589832
  919.9 16.6 %collective-permute-start.6 = (f32[16,3072]{1,0:T(8,128)}, f32[16,3072]{1,0:T(8,128)S(1)}, u32[]{:S(2)}, u32[]{:S(2)}) collective-permute-start(f32[16,3072]{1,0:T(8,128)} %fusion), channel_id=1, source_target_pairs={{0,7},{1,8},{2,9},{3,10},{4,11},{5,12},{6,13},{7,14},{8,15},{9,16}... | collective-permute-start | bytes 589832
  924.0 12.5 %collective-permute-start.7 = (f32[16,3072]{1,0:T(8,128)}, f32[16,3072]{1,0:T(8,128)S(1)}, u32[]{:S(2)}, u32[]{:S(2)}) collective-permute-start(f32[16,3072]{1,0:T(8,128)} %fusion), channel_id=1, source_target_pairs={{0,8},{1,9},{2,10},{3,11},{4,12},{5,13},{6,14},{7,15},{8,16},{9,17... | collective-permute-start | bytes 589832
  (24 other events, 486.5 us)
Sparse Core Ops, SparseCore 0:
  9.7 70.8 all-gather.1
where the time goes:
time: 1040 us; the launch traced here: 1030 us
  blocking collectives  400 us (38%)
  matrix products  254 us (24%)
  local copies, waits for them, and re-layouts  125 us (12%)
  starting transfers between devices  124 us (12%)
  waiting for transfers between devices  85.4 us (8%)
  other arithmetic  20.9 us (2%)
  between operations  15.2 us (1%)
    unnamed x1, blocking collectives  370 us
    unnamed x32, starting transfers between devices  107 us
    unnamed x33, local copies, waits for them, and re-layouts  93.9 us
    dot_general x4, matrix products, backward_one_block(): jnp.einsum('hqk,qhd->khd', score_gradient, query_block, preferred_element...  63.1 us
    all_gather x1, waiting for transfers between devices, body(): weight_full = lax.all_gather(projection, 'fsdp', axis=0, tiled=True)  61.9 us
    dot_general x4, matrix products, backward_one_block(): jnp.einsum('hqk,khd->qhd', score_gradient, key_rows, preferred_element_ty...  57.5 us
    sub x8, matrix products, block_probabilities(): exponentials = jnp.exp(scores - row_peak)  53.7 us
    all_to_all x1, blocking collectives, body(): lax.all_to_all(stacked, 'seq', split_axis=0, concat_axis=2, tiled=True)  30.3 us
  transfers between devices with their start and end apart: 36, of which 3 were waited for; matrix products, arithmetic and copies ran while one was open for 9% of the time, Pallas kernels for 0%

commit v1 on v0

v1 whole, which is shorter than its diff:
```python
import jax
import jax.numpy as jnp
from jax import lax
from jax.experimental import pallas as pl
from jax.experimental.pallas import tpu as pltpu
from jax.sharding import PartitionSpec as P

BF = jnp.bfloat16
F32 = jnp.float32
D = 1536
HD = 64
T = 2048
ROWS = 256
SEQ = 8
GW = 128
EPS = 1e-05
BQ = 256
CH = 512
NC = T // CH
VM = pl.BlockSpec(memory_space=pltpu.VMEM)
SM = pl.BlockSpec(memory_space=pltpu.SMEM)
PARAMS = pltpu.CompilerParams(vmem_limit_bytes=56 * 2**20)


def dot(a, b, dims=((1,), (0,))):
    return lax.dot_general(a, b, (dims, ((), ())), preferred_element_type=F32)


def standardize(x):
    centered = x - jnp.mean(x, axis=1, keepdims=True)
    inv_std = lax.rsqrt(jnp.mean(centered * centered, axis=1, keepdims=True) + EPS)
    return centered * inv_std, inv_std


def norm_kernel(x_ref, out_ref):
    out_ref[...] = standardize(x_ref[...].astype(F32))[0].astype(BF)


def project_kernel(pos_ref, w_ref, *refs):
    blocks, out_ref = refs[:SEQ], refs[SEQ]
    for b in range(SEQ):
        first = pl.multiple_of(pos_ref[b] * ROWS, ROWS)
        out_ref[pl.ds(first, ROWS), :] = dot(blocks[b][...], w_ref[...]).astype(BF)


def attention_kernel(
    len_ref, qkv_ref, up_ref, out_ref, ka, vt, kt, qt, ut, s_ref, e_ref, dk_acc, dv_acc
):
    length = len_ref[0]
    lane = lax.broadcasted_iota(jnp.int32, (CH, 128), 1)
    for c in range(NC):
        r = slice(c * CH, (c + 1) * CH)
        k = qkv_ref[r, 128:256].astype(F32)
        row = lax.broadcasted_iota(jnp.int32, (CH, 128), 0) + c * CH
        bias = jnp.where(row < length, 0.0, -1e30)
        for h in range(2):
            other = jnp.where(lane == (1 - h) * HD, bias, 0.0)
            ka[h, r, :] = jnp.where(lane // HD == h, k, other).astype(BF)
        kt[:, r] = k.T.astype(BF)
        v = qkv_ref[r, 256:384].astype(F32).T
        for h in range(2):
            vt[h, 0:HD, r] = v[h * HD : (h + 1) * HD].astype(BF)
            vt[h, HD : HD + 16, r] = jnp.ones((16, CH), BF)
        qt[:, r] = (qkv_ref[r, 0:128].astype(F32) * 0.125).T.astype(BF)
        u = jnp.where(row < length, up_ref[r, :].astype(F32), 0.0)
        ut[:, r] = u.T.astype(BF)
    dk_acc[...] = jnp.zeros_like(dk_acc)
    dv_acc[...] = jnp.zeros_like(dv_acc)
    zeros = jnp.zeros((HD, BQ), BF)
    ones_row = jnp.where(lax.broadcasted_iota(jnp.int32, (HD, BQ), 0) == 0, 1.0, 0.0).astype(BF)

    def place(x, other, h):
        return jnp.concatenate([x, other] if h == 0 else [other, x], axis=0)

    def step(i, carry):
        q0 = pl.multiple_of(i * BQ, BQ)
        cols = pl.ds(q0, BQ)
        contexts, ups, queries, inners = [], [], [], []
        for h in range(2):
            hrows = slice(h * HD, (h + 1) * HD)
            qh = qt[hrows, cols]
            qa = place(qh, ones_row, h)
            peak = None
            for c in range(NC):
                r = slice(c * CH, (c + 1) * CH)
                s = dot(ka[h, r, :], qa)
                s_ref[h, r, :] = s
                t = jnp.max(s.reshape(CH // 8, 8, BQ), axis=0)
                peak = t if peak is None else jnp.maximum(peak, t)
            peak = jnp.max(peak, axis=0, keepdims=True)
            total = None
            for c in range(NC):
                r = slice(c * CH, (c + 1) * CH)
                e = jnp.exp(s_ref[h, r, :] - peak).astype(BF)
                e_ref[h, r, :] = e
                t = dot(vt[h, :, r], e)
                total = t if total is None else total + t
            inverse = 1.0 / total[HD : HD + 1]
            context = total[0:HD] * inverse
            up = (ut[hrows, cols].astype(F32) * inverse).astype(BF)
            inner = jnp.sum(up.astype(F32) * context, axis=0, keepdims=True)
            contexts.append(context)
            ups.append(place(up, zeros, h))
            queries.append(place(qh, zeros, h))
            inners.append(inner)
        dq = [None, None]
        for c in range(NC):
            r = slice(c * CH, (c + 1) * CH)
            dss, es = [], []
            for h in range(2):
                dp = dot(qkv_ref[r, 256:384], ups[h])
                e = e_ref[h, r, :]
                ds = (e.astype(F32) * (dp - inners[h])).astype(BF)
                t = dot(kt[h * HD : (h + 1) * HD, r], ds)
                dq[h] = t if dq[h] is None else dq[h] + t
                dss.append(ds)
                es.append(e)
            nt = ((1,), (1,))
            dv_acc[r, :] += dot(es[0], ups[0], nt) + dot(es[1], ups[1], nt)
            dk_acc[r, :] += dot(dss[0], queries[0], nt) + dot(dss[1], queries[1], nt)
        context = jnp.concatenate(contexts, axis=0)
        col = lax.broadcasted_iota(jnp.int32, (128, BQ), 1) + q0
        context = jnp.where(col < length, context, 0.0)
        out_ref[cols, 384:512] = context.T.astype(BF)
        out_ref[cols, 0:128] = (jnp.concatenate(dq, axis=0) * 0.125).T.astype(BF)
        return carry

    lax.fori_loop(0, T // BQ, step, 0)
    for c in range(NC):
        r = slice(c * CH, (c + 1) * CH)
        out_ref[r, 128:256] = dk_acc[r, :].astype(BF)
        out_ref[r, 256:384] = dv_acc[r, :].astype(BF)


def weight_gradient_kernel(pos_ref, grad_ref, *refs):
    blocks, out_ref, acc = refs[:SEQ], refs[SEQ], refs[SEQ + 1]
    for b in range(SEQ):
        first = pl.multiple_of(pos_ref[b] * ROWS, ROWS)
        gt = grad_ref[pl.ds(first, ROWS), 0:384].astype(F32).T.astype(BF)
        for c in range(3):
            cs = slice(c * 512, (c + 1) * 512)
            t = dot(gt, blocks[b][:, cs])
            if b == 0:
                acc[:, cs] = t
            else:
                acc[:, cs] += t
    for c in range(12):
        cs = slice(c * 128, (c + 1) * 128)
        out_ref[cs, :] = acc[:, cs].T.astype(BF)


def input_gradient_kernel(grads_ref, w_ref, x_ref, ctx_ref, out_ref, packed):
    for s in range(SEQ):
        ctx_ref[:, s * GW : (s + 1) * GW] = grads_ref[s, :, 384:512]
        for kind in range(3):
            to = kind * 1024 + s * GW
            packed[:, to : to + GW] = grads_ref[s, :, kind * GW : (kind + 1) * GW]
    g = packed[...]
    for c in range(4):
        cs = slice(c * 384, (c + 1) * 384)
        out_ref[:, cs] = dot(g, w_ref[cs, :], ((1,), (1,)))
    standard, inv_std = standardize(x_ref[...].astype(F32))
    ng = out_ref[...]
    row_mean = jnp.mean(ng, axis=1, keepdims=True)
    projected = jnp.mean(ng * standard, axis=1, keepdims=True)
    out_ref[...] = inv_std * (ng - row_mean - standard * projected)


def shape(dims, dtype=BF):
    return jax.ShapeDtypeStruct(dims, dtype)


def gather_rows(x):
    up = [(i, (i // 4) * 4 + (i % 4 + 1) % 4) for i in range(8)]
    down = [(i, (i // 4) * 4 + (i % 4 + 3) % 4) for i in range(8)]
    across = [(i, i ^ 4) for i in range(8)]

    def send(v, way):
        return lax.ppermute(v, "seq", way)

    half = ROWS // 2
    below = send(x, up)
    above = send(x, down)
    other = send(x, across)
    far = jnp.concatenate([send(below[:half], up), send(above[half:], down)], axis=0)
    other_below = send(other, up)
    other_above = send(other, down)
    other_far = send(far, across)
    offsets = [(0, 0), (0, 3), (0, 1), (1, 0), (0, 2), (1, 3), (1, 1), (1, 2)]
    return offsets, [x, below, above, other, far, other_below, other_above, other_far]


def body(frames, projection, lengths, cotangent):
    x = frames[0]
    me = lax.axis_index("seq")
    normed = pl.pallas_call(norm_kernel, out_shape=shape((ROWS, D)), in_specs=[VM], out_specs=VM)(x)
    offsets, blocks = gather_rows(normed)
    place = jnp.stack([(me // 4 ^ dz) * 4 + (me % 4 + dy) % 4 for dz, dy in offsets]).astype(jnp.int32)

    columns = lax.dynamic_slice_in_dim(projection.reshape(384, 3, SEQ, GW), me, 1, 2).reshape(384, 384)
    columns = lax.all_gather(columns, "fsdp", axis=0, tiled=True)
    upstream = lax.all_to_all(
        cotangent[0].reshape(ROWS, SEQ, GW).transpose(1, 0, 2), "seq", 0, 0, tiled=True
    ).reshape(T, GW)
    weight_full = lax.all_gather(projection, "fsdp", axis=0, tiled=True)

    qkv = pl.pallas_call(
        project_kernel,
        out_shape=shape((T, 384)),
        in_specs=[SM, VM] + [VM] * SEQ,
        out_specs=VM,
        compiler_params=PARAMS,
    )(place, columns, *blocks)
    grads = pl.pallas_call(
        attention_kernel,
        out_shape=shape((T, 512)),
        in_specs=[SM, VM, VM],
        out_specs=VM,
        scratch_shapes=[
            pltpu.VMEM((2, T, 128), BF),
            pltpu.VMEM((2, HD + 16, T), BF),
            pltpu.VMEM((128, T), BF),
            pltpu.VMEM((128, T), BF),
            pltpu.VMEM((128, T), BF),
            pltpu.VMEM((2, T, BQ), F32),
            pltpu.VMEM((2, T, BQ), BF),
            pltpu.VMEM((T, 128), F32),
            pltpu.VMEM((T, 128), F32),
        ],
        compiler_params=PARAMS,
        cost_estimate=pl.CostEstimate(
            flops=40 * 2 * T * T * HD, bytes_accessed=4 * 2**20, transcendentals=2 * T * T
        ),
    )(lengths, qkv, upstream)
    returned = lax.all_to_all(grads.reshape(SEQ, ROWS, 512), "seq", 0, 0, tiled=True)
    partial = pl.pallas_call(
        weight_gradient_kernel,
        out_shape=shape((D, 384)),
        in_specs=[SM, VM] + [VM] * SEQ,
        out_specs=VM,
        scratch_shapes=[pltpu.VMEM((384, D), F32)],
        compiler_params=PARAMS,
        cost_estimate=pl.CostEstimate(
            flops=2 * T * D * 384, bytes_accessed=10 * 2**20, transcendentals=0
        ),
    )(place, grads, *blocks)
    partial = lax.all_to_all(partial.reshape(16, 96, 384), ("dp", "fsdp"), 0, 0, tiled=True)
    summed = jnp.sum(partial.astype(F32), axis=0)
    spread = lax.all_to_all(summed.reshape(SEQ, 12, 384), "seq", 0, 0, tiled=True)
    projection_gradient = (
        spread.reshape(SEQ, 12, 3, GW).transpose(1, 2, 0, 3).reshape(12, 3072)
    )
    context, input_gradient = pl.pallas_call(
        input_gradient_kernel,
        out_shape=(shape((ROWS, 1024)), shape((ROWS, D), F32)),
        in_specs=[VM, VM, VM],
        out_specs=(VM, VM),
        scratch_shapes=[pltpu.VMEM((ROWS, 3072), BF)],
        compiler_params=PARAMS,
        cost_estimate=pl.CostEstimate(
            flops=2 * ROWS * D * 3072, bytes_accessed=14 * 2**20, transcendentals=0
        ),
    )(returned, weight_full, x)
    return (context[None], input_gradient[None], projection_gradient)


def solution(mesh):
    placed = (
        P(("dp", "fsdp"), "seq", None),
        P("fsdp", None),
        P(("dp", "fsdp")),
        P(("dp", "fsdp"), "seq", None),
    )
    return jax.shard_map(
        body,
        mesh=mesh,
        in_specs=placed,
        out_specs=(
            P(("dp", "fsdp"), "seq", None),
            P(("dp", "fsdp"), "seq", None),
            P(("dp", "fsdp", "seq"), None),
        ),
        check_vma=False,
    )
```

time: 1040 us -> 227 us (0.22)
  blocking collectives: 400 us -> 39.7 us
  matrix products: 254 us -> 0 us
  local copies, waits for them, and re-layouts: 125 us -> 8.6 us
  starting transfers between devices: 124 us -> 22.3 us
  Pallas kernels: 0 us -> 68.3 us
  other arithmetic: 20.9 us -> 0.16 us
  waiting for transfers between devices: 85.4 us -> 72.1 us
    unnamed x1 -> x0, blocking collectives: 370 us -> none
    dot_general x23 -> x0, matrix products: 201 us -> none  [the longest x4 63.1 us: backward_one_block(): jnp.einsum('hqk,qhd->khd', score_gradient, query_block, preferred_element...]
    unnamed x32 -> x0, starting transfers between devices: 107 us -> none
    unnamed x33 -> x19, local copies, waits for them, and re-layouts: 93.9 us -> 5.97 us
    pallas_call x0 -> x5, Pallas kernels: none -> 68.3 us  [the longest x1 41.1 us: body(): pl.pallas_call(attention_kernel, out_shape=shape((T, 512)), in_specs=[SM,...]
    all_gather x1, waiting for transfers between devices: 61.9 us -> 0.01 us  [body(): weight_full = lax.all_gather(projection, 'fsdp', axis=0, tiled=True)]
    sub x8 -> x0, matrix products: 53.7 us -> none  [block_probabilities(): exponentials = jnp.exp(scores - row_peak)]
    ppermute x0 -> x8, waiting for transfers between devices: none -> 46.4 us  [send(): return lax.ppermute(v, 'seq', way)]
  transfers between devices with their start and end apart: 36 -> 12, of which waited for: 3 -> 6; matrix products, arithmetic and copies ran while one was open for 9% -> 1% of each run, Pallas kernels for 0% -> 26%
where the time goes in v1:
time: 227 us; the launch traced here: 226 us
  waiting for transfers between devices  72.1 us (32%)
  Pallas kernels  68.3 us (30%)
  blocking collectives  39.7 us (17%)
  starting transfers between devices  22.3 us (10%)
  between operations  14.8 us (7%)
  local copies, waits for them, and re-layouts  8.6 us (4%)
    ppermute x8, waiting for transfers between devices, send(): return lax.ppermute(v, 'seq', way)  46.4 us
    pallas_call x1, Pallas kernels, body(): pl.pallas_call(attention_kernel, out_shape=shape((T, 512)), in_specs=[SM,...  41.1 us
    all_to_all x1, blocking collectives, body(): lax.all_to_all(partial.reshape(16, 96, 384), ('dp', 'fsdp'), 0, 0, tiled=...  27.2 us
    all_to_all x1, waiting for transfers between devices, body(): lax.all_to_all(grads.reshape(SEQ, ROWS, 512), 'seq', 0, 0, tiled=True)  25.1 us
    ppermute x8, starting transfers between devices, send(): return lax.ppermute(v, 'seq', way)  14 us
    all_to_all x1, blocking collectives, body(): lax.all_to_all(summed.reshape(SEQ, 12, 384), 'seq', 0, 0, tiled=True)  12.5 us
    pallas_call x1, Pallas kernels, body(): pl.pallas_call(input_gradient_kernel, out_shape=(shape((ROWS, 1024)), sha...  9.74 us
    pallas_call x1, Pallas kernels, body(): pl.pallas_call(project_kernel, out_shape=shape((T, 384)), in_specs=[SM, V...  7.72 us
  transfers between devices with their start and end apart: 12, of which 6 were waited for; matrix products, arithmetic and copies ran while one was open for 1% of the time, Pallas kernels for 26%

profile of v1, /device:TPU:0, one launch (start us, length us, event | category | flops | bytes accessed | tf_op | source)
XLA Modules:
  0.0 226.0 jit_solution(3169390781266733560)
XLA Ops:
  7.2 3.0 %copy.12 = bf16[384,3072]{0,1:T(8,128)(2,1)S(1)} copy(bf16[384,3072]{1,0:T(8,128)(2,1)} %param.5) | data formatting | bytes 4718592 | tf_op args[1]
  10.3 0.9 copy.13
  11.2 0.7 all-gather.5.cloned.1.call-update
  11.9 2.5 %shard_map.67.refs_0_ = bf16[256,1536]{1,0:T(8,128)(2,1)} custom-call(bf16[256,1536]{1,0:T(8,128)(2,1)} %bitcast.32), custom_call_target="tpu_custom_call" | custom-call | tf_op jit(solution)/shard_map/pallas_call | solution.py:196
  14.4 1.7 collective-permute-start
  16.1 1.6 collective-permute-start.1
  17.7 2.0 collective-permute-start.2
  19.7 15.6 %collective-permute-done.refs_1_ = bf16[256,1536]{1,0:T(8,128)(2,1)S(1)} collective-permute-done((bf16[256,1536]{1,0:T(8,128)(2,1)}, bf16[256,1536]{1,0:T(8,128)(2,1)S(1)}, u32[]{:S(2)}, u32[]{:S(2)}) %collective-permute-start) | collective-permute-done | bytes 786464 | tf_op jit(solution)/shard_map/ppermute | solution.py:179
  35.3 0.4 collective-permute-start.3
  35.7 3.0 %collective-permute-start.4 = (bf16[128,1536]{1,0:T(8,128)(2,1)S(1)}, bf16[128,1536]{1,0:T(8,128)(2,1)S(1)}, u32[]{:S(2)}, u32[]{:S(2)}) collective-permute-start(bf16[128,1536]{1,0:T(8,128)(2,1)S(1)} %slice.9), channel_id=1, source_target_pairs={{0,3},{1,0},{2,1},{3,2},{4,7},{5,4},{6,5},{7,6},{8,11},{9,8},{10,9... | collective-permute-start | bytes 1179656 | tf_op jit(solution)/shard_map/ppermute | solution.py:179
  38.7 4.5 %collective-permute-done.2.refs_3_ = bf16[256,1536]{1,0:T(8,128)(2,1)S(1)} collective-permute-done((bf16[256,1536]{1,0:T(8,128)(2,1)}, bf16[256,1536]{1,0:T(8,128)(2,1)S(1)}, u32[]{:S(2)}, u32[]{:S(2)}) %collective-permute-start.2) | collective-permute-done | bytes 786464 | tf_op jit(solution)/shard_map/ppermute | solution.py:179
  43.3 0.3 collective-permute-start.5
  43.6 2.9 %collective-permute-start.6 = (bf16[256,1536]{1,0:T(8,128)(2,1)S(1)}, bf16[256,1536]{1,0:T(8,128)(2,1)}, u32[]{:S(2)}, u32[]{:S(2)}) collective-permute-start(bf16[256,1536]{1,0:T(8,128)(2,1)S(1)} %collective-permute-done.2.refs_3_), channel_id=1, source_target_pairs={{0,3},{1,0},{2,1},{3,2},{4,7},{5,4},{6,5},{7,6},{8,11},{9,8},{10,9... | collective-permute-start | bytes 2359304 | tf_op jit(solution)/shard_map/ppermute | solution.py:179
  46.5 1.3 collective-permute-done.3
  47.9 2.1 collective-permute-start.7
  50.2 0.9 copy.20
  51.0 4.4 %all-to-all-start = ((bf16[8,256,128]{2,1,0:T(8,128)(2,1)}), bf16[8,256,128]{2,1,0:T(8,128)(2,1)S(1)}, u32[]{:S(2)}, u32[]{:S(2)}) async-start(bf16[8,256,128]{2,1,0:T(8,128)(2,1)} %bitcast.29), calls=%async_computation | async-start | bytes 1048576 | tf_op jit(solution)/shard_map/all_to_all | solution.py:202
  56.1 0.7 stack.35.pos_ref
  56.8 11.1 %collective-permute-done.5.refs_5_ = bf16[256,1536]{1,0:T(8,128)(2,1)} collective-permute-done((bf16[256,1536]{1,0:T(8,128)(2,1)S(1)}, bf16[256,1536]{1,0:T(8,128)(2,1)}, u32[]{:S(2)}, u32[]{:S(2)}) %collective-permute-start.5) | collective-permute-done | bytes 786464 | tf_op jit(solution)/shard_map/ppermute | solution.py:179
  67.9 13.8 %collective-permute-done.7.refs_7_ = bf16[256,1536]{1,0:T(8,128)(2,1)} collective-permute-done((bf16[256,1536]{1,0:T(8,128)(2,1)S(1)}, bf16[256,1536]{1,0:T(8,128)(2,1)}, u32[]{:S(2)}, u32[]{:S(2)}) %collective-permute-start.7) | collective-permute-done | bytes 786464 | tf_op jit(solution)/shard_map/ppermute | solution.py:179
  81.7 7.7 %shard_map.68.qkv_ref = bf16[2048,384]{1,0:T(8,128)(2,1)} custom-call(s32[8]{0:T(128)} %stack.35.pos_ref, bf16[1536,384]{1,0:T(8,128)(2,1)} %all-gather.3.cloned.1.call-done.w_ref, bf16[256,1536]{1,0:T(8,128)(2,1)} %shard_map.67.refs_0_, bf16[256,1536]{1,0:T(8,128)(2,1)} %copy-done.1, bf16[256,1536]{1,0:T(8,128)(2,1)} %copy-done.2, ...), custom_call_target="tpu_custom_call" | custom-call | tf_op jit(solution)/shard_map/pallas_call | solution.py:207
  89.4 0.8 copy-done.6
  90.2 41.1 %shard_map.69.grad_ref = bf16[2048,512]{1,0:T(8,128)(2,1)} custom-call(s32[1]{0:T(128)S(6)} %copy.23.len_ref, bf16[2048,384]{1,0:T(8,128)(2,1)} %shard_map.68.qkv_ref, bf16[2048,128]{1,0:T(8,128)(2,1)} %bitcast.40), custom_call_target="tpu_custom_call" | custom-call | flops 21474836480 | bytes 4194304 | tf_op jit(solution)/shard_map/pallas_call | solution.py:214
  131.3 7.2 %shard_map.71 = bf16[1536,384]{1,0:T(8,128)(2,1)} custom-call(s32[8]{0:T(128)} %stack.35.pos_ref, bf16[2048,512]{1,0:T(8,128)(2,1)} %shard_map.69.grad_ref, bf16[256,1536]{1,0:T(8,128)(2,1)} %shard_map.67.refs_0_, bf16[256,1536]{1,0:T(8,128)(2,1)} %copy-done.1, bf16[256,1536]{1,0:T(8,128)(2,1)} %copy-done.2, bf16[256,1536]{1,0:T(8,128)(2,1)} %copy-done.4, ...), custom_call_target="tpu_custom_call" | custom-call | flops 2415919104 | bytes 10485760 | tf_op jit(solution)/shard_map/pallas_call | solution.py:236
  138.5 27.2 %all_to_all.20 = bf16[16,96,384]{2,1,0:T(8,128)(2,1)S(1)} all-to-all(bf16[16,96,384]{2,1,0:T(8,128)(2,1)} %bitcast.31), channel_id=1, replica_groups=mesh['dp'=4,'fsdp'=4,'seq'=8] {'dp','fsdp'}, dimensions={0} | all-to-all | bytes 2359296 | tf_op jit(solution)/shard_map/all_to_all | solution.py:247
  165.7 0.2 convert_reduce_fusion
  165.9 12.5 %all_to_all.21 = f32[8,12,384]{2,1,0:T(8,128)S(1)} all-to-all(f32[8,12,384]{2,1,0:T(8,128)S(1)} %reshape.35), channel_id=1, replica_groups=mesh['dp'=4,'fsdp'=4,'seq'=8] {'seq'}, dimensions={0} | all-to-all | bytes 294912 | tf_op jit(solution)/shard_map/all_to_all | solution.py:249
  178.4 3.8 %all-to-all-start.1 = ((bf16[8,256,512]{2,1,0:T(8,128)(2,1)}), bf16[8,256,512]{2,1,0:T(8,128)(2,1)S(1)}, u32[]{:S(2)}, u32[]{:S(2)}) async-start(bf16[8,256,512]{2,1,0:T(8,128)(2,1)} %bitcast.13), calls=%async_computation.1 | async-start | bytes 4194304 | tf_op jit(solution)/shard_map/all_to_all | solution.py:235
  182.3 0.7 copy.17
  183.0 25.1 %all-to-all-done.1.grads_ref = bf16[8,256,512]{2,1,0:T(8,128)(2,1)S(1)} async-done(((bf16[8,256,512]{2,1,0:T(8,128)(2,1)}), bf16[8,256,512]{2,1,0:T(8,128)(2,1)S(1)}, u32[]{:S(2)}, u32[]{:S(2)}) %all-to-all-start.1) | async-done | bytes 2097184 | tf_op jit(solution)/shard_map/all_to_all | solution.py:235
  208.1 1.3 copy-done
  209.4 9.7 %shard_map.70 = (bf16[256,1024]{1,0:T(8,128)(2,1)}, f32[256,1536]{1,0:T(8,128)}) custom-call(bf16[8,256,512]{2,1,0:T(8,128)(2,1)} %copy-done, bf16[1536,3072]{1,0:T(8,128)(2,1)} %all-gather.5.cloned.1.call-done.w_ref, bf16[256,1536]{1,0:T(8,128)(2,1)} %bitcast.33), custom_call_target="tpu_custom_call" | custom-call | flops 2415919104 | bytes 14680064 | tf_op jit(solution)/shard_map/pallas_call | solution.py:253
  (30 shorter events, 0.5 us)
Async XLA Ops:
  7.2 60.7 %all-gather.3.cloned.1.call-start = ((), (), s32[]{:S(2)}) async-start(), calls=%async_computation.4 | async-start | bytes 1474560 | tf_op jit(solution)/shard_map/all_gather | solution.py:201
  11.2 196.9 %all-gather.5.cloned.1.call-start = ((), (), s32[]{:S(2)}) async-start(), calls=%async_computation.5 | async-start | bytes 11796480 | tf_op jit(solution)/shard_map/all_gather | solution.py:205
  14.4 35.6 %copy-start.5 = (bf16[1,256,1024]{2,1,0:T(8,128)(2,1)S(1)}, bf16[1,256,1024]{2,1,0:T(8,128)(2,1)}, u32[]{:S(2)}) copy-start(bf16[1,256,1024]{2,1,0:T(8,128)(2,1)} %param.7) | copy-start | bytes 1572868
  14.4 20.8 %collective-permute-start = (bf16[256,1536]{1,0:T(8,128)(2,1)}, bf16[256,1536]{1,0:T(8,128)(2,1)S(1)}, u32[]{:S(2)}, u32[]{:S(2)}) collective-permute-start(bf16[256,1536]{1,0:T(8,128)(2,1)} %shard_map.67.refs_0_), channel_id=1, source_target_pairs={{0,1},{1,2},{2,3},{3,0},{4,5},{5,6},{6,7},{7,4},{8,9},{9,10},{10,1... | collective-permute-start | bytes 2359304 | tf_op jit(solution)/shard_map/ppermute | solution.py:179
  16.1 19.6 %collective-permute-start.1 = (bf16[256,1536]{1,0:T(8,128)(2,1)}, bf16[256,1536]{1,0:T(8,128)(2,1)S(1)}, u32[]{:S(2)}, u32[]{:S(2)}) collective-permute-start(bf16[256,1536]{1,0:T(8,128)(2,1)} %shard_map.67.refs_0_), channel_id=1, source_target_pairs={{0,3},{1,0},{2,1},{3,2},{4,7},{5,4},{6,5},{7,6},{8,11},{9,8},{10,9... | collective-permute-start | bytes 2359304 | tf_op jit(solution)/shard_map/ppermute | solution.py:179
  17.7 25.6 %collective-permute-start.2 = (bf16[256,1536]{1,0:T(8,128)(2,1)}, bf16[256,1536]{1,0:T(8,128)(2,1)S(1)}, u32[]{:S(2)}, u32[]{:S(2)}) collective-permute-start(bf16[256,1536]{1,0:T(8,128)(2,1)} %shard_map.67.refs_0_), channel_id=1, source_target_pairs={{0,4},{1,5},{2,6},{3,7},{4,0},{5,1},{6,2},{7,3},{8,12},{9,13},{10,... | collective-permute-start | bytes 2359304 | tf_op jit(solution)/shard_map/ppermute | solution.py:179
  35.3 14.9 %copy-start.1 = (bf16[256,1536]{1,0:T(8,128)(2,1)}, bf16[256,1536]{1,0:T(8,128)(2,1)S(1)}, u32[]{:S(2)}) copy-start(bf16[256,1536]{1,0:T(8,128)(2,1)S(1)} %collective-permute-done.refs_1_) | copy-start | bytes 2359300
  35.3 12.5 %collective-permute-start.3 = (bf16[128,1536]{1,0:T(8,128)(2,1)S(1)}, bf16[128,1536]{1,0:T(8,128)(2,1)S(1)}, u32[]{:S(2)}, u32[]{:S(2)}) collective-permute-start(bf16[128,1536]{1,0:T(8,128)(2,1)S(1)} %slice.8), channel_id=1, source_target_pairs={{0,1},{1,2},{2,3},{3,0},{4,5},{5,6},{6,7},{7,4},{8,9},{9,10},{10,1... | collective-permute-start | bytes 1179656 | tf_op jit(solution)/shard_map/ppermute | solution.py:179
  35.7 15.3 %copy-start.2 = (bf16[256,1536]{1,0:T(8,128)(2,1)}, bf16[256,1536]{1,0:T(8,128)(2,1)S(1)}, u32[]{:S(2)}) copy-start(bf16[256,1536]{1,0:T(8,128)(2,1)S(1)} %collective-permute-done.1.refs_2_) | copy-start | bytes 2359300
  35.7 12.1 %collective-permute-start.4 = (bf16[128,1536]{1,0:T(8,128)(2,1)S(1)}, bf16[128,1536]{1,0:T(8,128)(2,1)S(1)}, u32[]{:S(2)}, u32[]{:S(2)}) collective-permute-start(bf16[128,1536]{1,0:T(8,128)(2,1)S(1)} %slice.9), channel_id=1, source_target_pairs={{0,3},{1,0},{2,1},{3,2},{4,7},{5,4},{6,5},{7,6},{8,11},{9,8},{10,9... | collective-permute-start | bytes 1179656 | tf_op jit(solution)/shard_map/ppermute | solution.py:179
  43.3 7.8 %copy-start.4 = (bf16[256,1536]{1,0:T(8,128)(2,1)}, bf16[256,1536]{1,0:T(8,128)(2,1)S(1)}, u32[]{:S(2)}) copy-start(bf16[256,1536]{1,0:T(8,128)(2,1)S(1)} %collective-permute-done.2.refs_3_) | copy-start | bytes 2359300
  43.3 24.6 %collective-permute-start.5 = (bf16[256,1536]{1,0:T(8,128)(2,1)S(1)}, bf16[256,1536]{1,0:T(8,128)(2,1)}, u32[]{:S(2)}, u32[]{:S(2)}) collective-permute-start(bf16[256,1536]{1,0:T(8,128)(2,1)S(1)} %collective-permute-done.2.refs_3_), channel_id=1, source_target_pairs={{0,1},{1,2},{2,3},{3,0},{4,5},{5,6},{6,7},{7,4},{8,9},{9,10},{10,1... | collective-permute-start | bytes 2359304 | tf_op jit(solution)/shard_map/ppermute | solution.py:179
  43.6 24.3 %collective-permute-start.6 = (bf16[256,1536]{1,0:T(8,128)(2,1)S(1)}, bf16[256,1536]{1,0:T(8,128)(2,1)}, u32[]{:S(2)}, u32[]{:S(2)}) collective-permute-start(bf16[256,1536]{1,0:T(8,128)(2,1)S(1)} %collective-permute-done.2.refs_3_), channel_id=1, source_target_pairs={{0,3},{1,0},{2,1},{3,2},{4,7},{5,4},{6,5},{7,6},{8,11},{9,8},{10,9... | collective-permute-start | bytes 2359304 | tf_op jit(solution)/shard_map/ppermute | solution.py:179
  47.9 33.7 %copy-start.3 = (bf16[256,1536]{1,0:T(8,128)(2,1)}, bf16[256,1536]{1,0:T(8,128)(2,1)S(1)}, u32[]{:S(2)}) copy-start(bf16[256,1536]{1,0:T(8,128)(2,1)S(1)} %constant_dynamic-update-slice_fusion.refs_4_) | copy-start | bytes 2359300
  47.9 33.7 %collective-permute-start.7 = (bf16[256,1536]{1,0:T(8,128)(2,1)S(1)}, bf16[256,1536]{1,0:T(8,128)(2,1)}, u32[]{:S(2)}, u32[]{:S(2)}) collective-permute-start(bf16[256,1536]{1,0:T(8,128)(2,1)S(1)} %constant_dynamic-update-slice_fusion.refs_4_), channel_id=1, source_target_pairs={{0,4},{1,5},{2,6},{3,7},{4,0},{5,1},{6,2},{7,3},{8,12},{9,13},{10,... | collective-permute-start | bytes 2359304 | tf_op jit(solution)/shard_map/ppermute | solution.py:179
  51.0 38.3 %all-to-all-start = ((bf16[8,256,128]{2,1,0:T(8,128)(2,1)}), bf16[8,256,128]{2,1,0:T(8,128)(2,1)S(1)}, u32[]{:S(2)}, u32[]{:S(2)}) async-start(bf16[8,256,128]{2,1,0:T(8,128)(2,1)} %bitcast.29), calls=%async_computation | async-start | bytes 1048576 | tf_op jit(solution)/shard_map/all_to_all | solution.py:202
  89.4 0.8 copy-start.6
  178.4 29.7 %all-to-all-start.1 = ((bf16[8,256,512]{2,1,0:T(8,128)(2,1)}), bf16[8,256,512]{2,1,0:T(8,128)(2,1)S(1)}, u32[]{:S(2)}, u32[]{:S(2)}) async-start(bf16[8,256,512]{2,1,0:T(8,128)(2,1)} %bitcast.13), calls=%async_computation.1 | async-start | bytes 4194304 | tf_op jit(solution)/shard_map/all_to_all | solution.py:235
  208.1 1.3 copy-start
Sparse Core Ops, SparseCore 0:
  11.3 30.5 all-gather.2
  43.6 82.4 all-gather.4

commit v2 on v1

v2 whole, which is shorter than its diff:
```python
import functools

import jax
import jax.numpy as jnp
from jax import lax
from jax.experimental import pallas as pl
from jax.experimental.pallas import tpu as pltpu
from jax.sharding import PartitionSpec as P

BF = jnp.bfloat16
F32 = jnp.float32
D = 1536
HD = 64
T = 2048
ROWS = 256
SEQ = 8
GW = 128
EPS = 1e-05
BQ = 256
CH = 512
NC = T // CH
VM = pl.BlockSpec(memory_space=pltpu.VMEM)
SM = pl.BlockSpec(memory_space=pltpu.SMEM)


def dot(a, b, dims=((1,), (0,))):
    return lax.dot_general(a, b, (dims, ((), ())), preferred_element_type=F32)


def standardize(x):
    centered = x - jnp.mean(x, axis=1, keepdims=True)
    inv_std = lax.rsqrt(jnp.mean(centered * centered, axis=1, keepdims=True) + EPS)
    return centered * inv_std, inv_std


def norm_kernel(x_ref, out_ref):
    out_ref[...] = standardize(x_ref[...].astype(F32))[0].astype(BF)


def columns_kernel(me_ref, w_ref, out_ref):
    s = me_ref[0] * GW
    q, k, v = (
        w_ref[:, pl.ds(pl.multiple_of(kind * 1024 + s, GW), GW)].astype(F32) for kind in range(3)
    )
    low = lax.broadcasted_iota(jnp.int32, k.shape, 1) < HD
    out_ref[:, 0:128] = jnp.where(low, k, pltpu.roll(v, HD, 1)).astype(BF)
    out_ref[:, 128:256] = jnp.where(low, pltpu.roll(k, HD, 1), v).astype(BF)
    out_ref[:, 256:384] = q.astype(BF)


def project_kernel(n, owner_ref, *refs):
    weights, blocks, out_ref = refs[:4], refs[4 : 4 + n], refs[4 + n]
    first = 0
    for block in blocks:
        count = block.shape[0]
        total = None
        for f in range(4):
            rows = pl.ds(pl.multiple_of(owner_ref[f] * 384, 384), 384)
            t = dot(block[:, rows], weights[f][...])
            total = t if total is None else total + t
        out_ref[first : first + count, :] = total.astype(BF)
        first += count


def attention_kernel(
    head, pos_ref, len_ref, near_ref, far_ref, up_ref, out_ref, kv, ka, vt, kt, qt, ut, s_ref, e_ref, acc
):
    length = len_ref[0]
    hrows = slice(head * HD, (head + 1) * HD)
    lane = lax.broadcasted_iota(jnp.int32, (BQ, 128), 1)
    for b in range(SEQ):
        r = slice(b * BQ, (b + 1) * BQ)
        source = near_ref if b < 4 else far_ref
        own = slice(b % 4 * BQ, (b % 4 + 1) * BQ)
        first = pl.multiple_of(pos_ref[b] * BQ, BQ)
        mine = source[own, head * 128 : (head + 1) * 128]
        kv[r, :] = mine
        keys = mine.astype(F32)
        row = lax.broadcasted_iota(jnp.int32, (BQ, 128), 0) + first
        bias = jnp.where(lane == HD, jnp.where(row < length, 0.0, -1e30), 0.0)
        ka[r, :] = jnp.where(lane < HD, keys, bias).astype(BF)
        flipped = keys.T.astype(BF)
        kt[:, r] = flipped[0:HD]
        vt[0:HD, r] = flipped[HD:128]
        vt[HD : HD + 16, r] = jnp.ones((16, BQ), BF)
        qt[:, r] = (source[own, 256:384].astype(F32) * 0.125).T[hrows].astype(BF)
        u = jnp.where(row < length, up_ref[pl.ds(first, BQ), :].astype(F32), 0.0)
        ut[:, r] = u.T[hrows].astype(BF)
    acc[...] = jnp.zeros_like(acc)
    zeros = jnp.zeros((HD, BQ), BF)
    ones_row = jnp.where(lax.broadcasted_iota(jnp.int32, (HD, BQ), 0) == 0, 1.0, 0.0).astype(BF)
    nt = ((1,), (1,))

    def step(i, carry):
        contexts, ups, queries, inners = [], [], [], []
        starts = [pl.multiple_of((2 * i + j) * BQ, BQ) for j in range(2)]
        for j in range(2):
            cols = pl.ds(starts[j], BQ)
            qh = qt[:, cols]
            qa = jnp.concatenate([qh, ones_row], axis=0)
            peak = None
            for c in range(NC):
                r = slice(c * CH, (c + 1) * CH)
                s = dot(ka[r, :], qa)
                s_ref[j, r, :] = s
                t = jnp.max(s.reshape(CH // 8, 8, BQ), axis=0)
                peak = t if peak is None else jnp.maximum(peak, t)
            peak = jnp.max(peak, axis=0, keepdims=True)
            total = None
            for c in range(NC):
                r = slice(c * CH, (c + 1) * CH)
                e = jnp.exp(s_ref[j, r, :] - peak).astype(BF)
                e_ref[j, r, :] = e
                t = dot(vt[:, r], e)
                total = t if total is None else total + t
            inverse = 1.0 / total[HD : HD + 1]
            context = total[0:HD] * inverse
            up = (ut[:, cols].astype(F32) * inverse).astype(BF)
            inner = jnp.sum(up.astype(F32) * context, axis=0, keepdims=True)
            contexts.append(context)
            ups.append(jnp.concatenate([zeros, up], axis=0))
            queries.append(jnp.concatenate([qh, zeros], axis=0))
            inners.append(inner)
        dq = [None, None]
        for c in range(NC):
            r = slice(c * CH, (c + 1) * CH)
            total = acc[r, :]
            for j in range(2):
                dp = dot(kv[r, :], ups[j])
                e = e_ref[j, r, :]
                ds = (e.astype(F32) * (dp - inners[j])).astype(BF)
                t = dot(kt[:, r], ds)
                dq[j] = t if dq[j] is None else dq[j] + t
                total = total + (dot(ds, queries[j], nt) + dot(e, ups[j], nt))
            acc[r, :] = total
        for j in range(2):
            first = pl.multiple_of(pos_ref[2 * i + j] * BQ, BQ)
            col = lax.broadcasted_iota(jnp.int32, (HD, BQ), 1) + first
            context = jnp.where(col < length, contexts[j], 0.0)
            both = jnp.concatenate([dq[j] * 0.125, context], axis=0)
            out_ref[pl.ds(first, BQ), 0:128] = both.T.astype(BF)
        return carry

    lax.fori_loop(0, T // BQ // 2, step, 0)
    for b in range(SEQ):
        rows = pl.ds(pl.multiple_of(pos_ref[b] * BQ, BQ), BQ)
        out_ref[rows, 128:256] = acc[b * BQ : (b + 1) * BQ, :].astype(BF)


def weight_gradient_kernel(pos_ref, first_ref, second_ref, *refs):
    blocks, (keep_ref, send_ref, acc) = refs[:-3], refs[-3:]
    at = [0] * SEQ
    which = 0
    for i, block in enumerate(blocks):
        count = block.shape[0]
        rows = pl.ds(pl.multiple_of(pos_ref[which] * ROWS + at[which], 128), count)
        both = [g[rows, :].astype(F32).T.astype(BF) for g in (first_ref, second_ref)]
        parts = [g[128:256] for g in both] + [g[0:HD] for g in both]
        flipped = jnp.concatenate(parts, axis=0)
        for c in range(3):
            cs = slice(c * 512, (c + 1) * 512)
            t = dot(flipped, block[:, cs])
            if i == 0:
                acc[:, cs] = t
            else:
                acc[:, cs] += t
        at[which] += count
        which += at[which] == ROWS
    core = pos_ref[SEQ]
    for c in range(4):
        flipped = acc[:, c * 384 : (c + 1) * 384].T
        halves = [[flipped[i * 96 : (i + 1) * 96] for i in (k, k + 2)] for k in range(2)]
        for k in range(2):
            for i in range(2):
                r = slice((c * 2 + i) * 96, (c * 2 + i + 1) * 96)

                @pl.when(core == k)
                def _():
                    keep_ref[r, :] = halves[k][i]

                @pl.when(core != k)
                def _():
                    send_ref[r, :] = halves[k][i].astype(BF)


def add_kernel(keep_ref, got_ref, out_ref):
    out_ref[...] = (keep_ref[...] + got_ref[...].astype(F32)).astype(BF)


def join(first, second, part):
    low = lax.broadcasted_iota(jnp.int32, first.shape, first.ndim - 1) < HD
    if part == 0:
        return jnp.where(low, first, pltpu.roll(second, HD, first.ndim - 1))
    return jnp.where(low, pltpu.roll(first, HD, first.ndim - 1), second)


def combine_kernel(parts_ref, out_ref):
    for s in range(SEQ):
        total = None
        for r in range(8):
            t = parts_ref[r * SEQ + s].astype(F32)
            total = t if total is None else total + t
        at = s * GW
        low, high = total[:, 0:128], total[:, 128:256]
        out_ref[:, at : at + GW] = total[:, 256:384]
        out_ref[:, 1024 + at : 1024 + at + GW] = join(low, high, 0)
        out_ref[:, 2048 + at : 2048 + at + GW] = join(low, high, 1)


def input_gradient_kernel(
    pos_ref, first_ref, second_ref, w0_ref, w1_ref, w2_ref, w3_ref, x_ref, ctx_ref, out_ref, packed
):
    for s in range(SEQ):
        at = s * GW
        a = [first_ref[s, :, i * 128 : (i + 1) * 128].astype(F32) for i in range(2)]
        b = [second_ref[s, :, i * 128 : (i + 1) * 128].astype(F32) for i in range(2)]
        ctx_ref[:, at : at + GW] = join(a[0], b[0], 1).astype(BF)
        packed[:, at : at + GW] = join(a[0], b[0], 0).astype(BF)
        packed[:, 1024 + at : 1024 + at + GW] = join(a[1], b[1], 0).astype(BF)
        packed[:, 2048 + at : 2048 + at + GW] = join(a[1], b[1], 1).astype(BF)
    for f, w_ref in enumerate((w0_ref, w1_ref, w2_ref, w3_ref)):
        to = pl.ds(pl.multiple_of(pos_ref[f] * 384, 384), 384)
        out_ref[:, to] = dot(packed[...], w_ref[...], ((1,), (1,)))
    standard, inv_std = standardize(x_ref[...].astype(F32))
    ng = out_ref[...]
    row_mean = jnp.mean(ng, axis=1, keepdims=True)
    projected = jnp.mean(ng * standard, axis=1, keepdims=True)
    out_ref[...] = inv_std * (ng - row_mean - standard * projected)


def shape(dims, dtype=BF):
    return jax.ShapeDtypeStruct(dims, dtype)


def gather_rows(x, extra):
    up = [(i, (i // 4) * 4 + (i % 4 + 1) % 4) for i in range(8)]
    down = [(i, (i // 4) * 4 + (i % 4 + 3) % 4) for i in range(8)]
    across = [(i, i ^ 4) for i in range(8)]

    def send(v, way):
        return lax.ppermute(v, "seq", way)

    half = ROWS // 2
    below, above, other = send(x, up), send(x, down), send(x, across)
    below, above, other, extra = lax.optimization_barrier((below, above, other, extra))
    far = [send(below[:half], up), send(above[half:], down)]
    other_below, other_above = send(other, up), send(other, down)
    other_far = [send(v, across) for v in far]
    offsets = [(0, 0), (0, 3), (0, 1), (1, 0), (0, 2), (1, 3), (1, 1), (1, 2)]
    return offsets, [x, below, above, other], [*far, other_below, other_above, *other_far], extra


def sibling(v):
    return lax.ppermute(v, "core", [(0, 1), (1, 0)])


def gather_columns(mine):
    over = lax.ppermute(mine, "zh", [(0, 1), (1, 0)])
    return [mine, sibling(mine), over, sibling(over)]


def gather_weight(w):
    swap = [(f * 8 + s, (f ^ 1) * 8 + (s ^ 4)) for f in range(2) for s in range(8)]
    over = lax.ppermute(w, ("zh", "seq"), swap)
    return [w, sibling(w), over, sibling(over)]


def call(kernel, out, in_specs, flops=0, scratch=(), transcendentals=0, vmem=32):
    return pl.pallas_call(
        kernel,
        out_shape=out,
        in_specs=in_specs,
        out_specs=jax.tree.map(lambda _: VM, out),
        scratch_shapes=list(scratch),
        compiler_params=pltpu.CompilerParams(vmem_limit_bytes=vmem * 2**20),
        cost_estimate=pl.CostEstimate(
            flops=flops, bytes_accessed=2**20, transcendentals=transcendentals
        ),
    )


def body(frames, projection, lengths, cotangent):
    x = frames[0]
    me = lax.axis_index("seq")
    core = lax.axis_index("core")
    fsdp = lax.axis_index("zh") * 2 + core
    normed = call(norm_kernel, shape((ROWS, D)), [VM])(x)
    mine = call(columns_kernel, shape((384, 384)), [SM, VM])(me[None].astype(jnp.int32), projection)
    upstream = cotangent[0].reshape(ROWS, SEQ, GW).transpose(1, 0, 2)
    offsets, near, far, (mine, upstream) = gather_rows(normed, (mine, upstream))
    blocks = near + far
    index = [(me // 4 ^ dz) * 4 + (me % 4 + dy) % 4 for dz, dy in offsets]
    place = jnp.stack(index + [core]).astype(jnp.int32)
    owners = jnp.stack([fsdp ^ i for i in range(4)]).astype(jnp.int32)

    columns = gather_columns(mine)
    upstream = lax.all_to_all(upstream, "seq", 0, 0, tiled=True).reshape(T, GW)
    weights = gather_weight(projection)

    def project(rows):
        return call(
            functools.partial(project_kernel, len(rows)),
            shape((T // 2, 384)),
            [SM] + [VM] * (4 + len(rows)),
            T * D * 384,
        )(owners, *columns, *rows)

    near_packed, far_packed = project(near), project(far)

    def attend(head):
        return call(
            functools.partial(attention_kernel, head),
            shape((T, 256)),
            [SM, SM, VM, VM, VM],
            20 * 2 * T * T * HD,
            [
                pltpu.VMEM((T, 128), BF),
                pltpu.VMEM((T, 128), BF),
                pltpu.VMEM((HD + 16, T), BF),
                pltpu.VMEM((HD, T), BF),
                pltpu.VMEM((HD, T), BF),
                pltpu.VMEM((HD, T), BF),
                pltpu.VMEM((2, T, BQ), F32),
                pltpu.VMEM((2, T, BQ), BF),
                pltpu.VMEM((T, 128), F32),
            ],
            T * T,
        )(place, lengths, near_packed, far_packed, upstream)

    def send_back(grads):
        return lax.all_to_all(grads.reshape(SEQ, ROWS, 256), "seq", 0, 0, tiled=True)

    first = attend(0)
    back0 = send_back(first)
    second = attend(1)
    second, back0 = lax.optimization_barrier((second, back0))
    back1 = send_back(second)
    keep, send = call(
        weight_gradient_kernel,
        (shape((768, 384), F32), shape((768, 384))),
        [SM] + [VM] * (2 + len(blocks)),
        2 * T * D * 384,
        [pltpu.VMEM((384, D), F32)],
    )(place, first, second, *blocks)
    got = sibling(send)
    got, back1 = lax.optimization_barrier((got, back1))
    partial = call(add_kernel, shape((768, 384)), [VM, VM])(keep, got)
    partial = lax.all_to_all(
        partial.reshape(64, 12, 384), ("dp", "zh", "seq"), 0, 0, tiled=True
    )
    projection_gradient = call(combine_kernel, shape((12, 3072), F32), [VM])(partial)
    context, input_gradient = call(
        input_gradient_kernel,
        (shape((ROWS, 1024)), shape((ROWS, D), F32)),
        [SM] + [VM] * 7,
        2 * ROWS * D * 3072,
        [pltpu.VMEM((ROWS, 3072), BF)],
    )(owners, back0, back1, *weights, x)
    return (context[None], input_gradient[None], projection_gradient)


def solution(mesh):
    split = jax.sharding.Mesh(mesh.devices.reshape(4, 2, 2, 8), ("dp", "zh", "core", "seq"))
    record = ("dp", "zh", "core")
    placed = (P(record, "seq", None), P(("zh", "core"), None), P(record), P(record, "seq", None))
    return jax.shard_map(
        body,
        mesh=split,
        in_specs=placed,
        out_specs=(P(record, "seq", None), P(record, "seq", None), P((*record, "seq"), None)),
        check_vma=False,
    )
```

time: 227 us -> 181 us (0.80)
  waiting for transfers between devices: 72.1 us -> 31.6 us
  local copies, waits for them, and re-layouts: 8.6 us -> 32.5 us
  blocking collectives: 39.7 us -> 24.9 us
  between operations: 14.8 us -> 1.62 us
  Pallas kernels: 68.3 us -> 58.3 us
  starting transfers between devices: 22.3 us -> 31 us
    all_to_all x2 -> x3, waiting for transfers between devices: 25.1 us -> 0.59 us  [the longest x2 0.59 us: send_back(): lax.all_to_all(grads.reshape(SEQ, ROWS, 256), 'seq', 0, 0, tiled=True)]
    unnamed x19 -> x69, local copies, waits for them, and re-layouts: 5.97 us -> 29.5 us
    ppermute x8 -> x9, waiting for transfers between devices: 46.4 us -> 25.4 us  [send(): return lax.ppermute(v, 'seq', way)]
    all_to_all x2 -> x1, blocking collectives: 39.7 us -> 24.9 us  [body(): lax.all_to_all(partial.reshape(64, 12, 384), ('dp', 'zh', 'seq'), 0, 0, t...]
    pallas_call x5 -> x10, Pallas kernels: 68.3 us -> 58.3 us  [the longest x2 34.2 us: attend(): call(functools.partial(attention_kernel, head), shape((T, 256)), [SM, SM,...]
    ppermute x0 -> x7, starting transfers between devices: none -> 6.45 us  [the longest x1 3.58 us: gather_columns(): over = lax.ppermute(mine, 'zh', [(0, 1), (1, 0)])]
    ppermute x0 -> x7, waiting for transfers between devices: none -> 5.57 us  [the longest x1 3.8 us: gather_columns(): over = lax.ppermute(mine, 'zh', [(0, 1), (1, 0)])]
    all_to_all x2 -> x3, starting transfers between devices: 8.22 us -> 13.2 us  [the longest x2 9.1 us: send_back(): lax.all_to_all(grads.reshape(SEQ, ROWS, 256), 'seq', 0, 0, tiled=True)]
  transfers between devices with their start and end apart: 12 -> 19, of which waited for: 6 -> 8; matrix products, arithmetic and copies ran while one was open for 1% -> 2% of each run, Pallas kernels for 26% -> 27%
where the time goes in v2:
time: 181 us; the launch traced here: 180 us
  Pallas kernels  58.3 us (32%)
  local copies, waits for them, and re-layouts  32.5 us (18%)
  waiting for transfers between devices  31.6 us (17%)
  starting transfers between devices  31 us (17%)
  blocking collectives  24.9 us (14%)
    pallas_call x2, Pallas kernels, attend(): call(functools.partial(attention_kernel, head), shape((T, 256)), [SM, SM,...  34.2 us
    unnamed x69, local copies, waits for them, and re-layouts  29.5 us
    ppermute x9, waiting for transfers between devices, send(): return lax.ppermute(v, 'seq', way)  25.4 us
    all_to_all x1, blocking collectives, body(): lax.all_to_all(partial.reshape(64, 12, 384), ('dp', 'zh', 'seq'), 0, 0, t...  24.9 us
    ppermute x9, starting transfers between devices, send(): return lax.ppermute(v, 'seq', way)  11.3 us
    all_to_all x2, starting transfers between devices, send_back(): lax.all_to_all(grads.reshape(SEQ, ROWS, 256), 'seq', 0, 0, tiled=True)  9.1 us
    pallas_call x1, Pallas kernels, body(): call(input_gradient_kernel, (shape((ROWS, 1024)), shape((ROWS, D), F32)),...  8.92 us
    pallas_call x2, Pallas kernels, project(): call(functools.partial(project_kernel, len(rows)), shape((T // 2, 384)),...  7.46 us
  transfers between devices with their start and end apart: 19, of which 8 were waited for; matrix products, arithmetic and copies ran while one was open for 2% of the time, Pallas kernels for 27%

profile of v2, /device:TPU:0, one launch (start us, length us, event | category | flops | bytes accessed | tf_op | source)
XLA Modules:
  0.0 180.0 jit_solution(13491619306963892414)
XLA Ops:
  2.2 2.1 %collective-permute-start.2 = (bf16[256,1536]{1,0:T(8,128)(2,1)S(1)}, bf16[256,1536]{1,0:T(8,128)(2,1)}, u32[]{:S(2)}, u32[]{:S(2)}) collective-permute-start(bf16[256,1536]{1,0:T(8,128)(2,1)S(1)} %shard_map.67.refs_4_.refs_0_), channel_id=1, source_target_pairs={{0,4},{1,5},{2,6},{3,7},{4,0},{5,1},{6,2},{7,3},{8,12},{9,13},{10,... | collective-permute-start | bytes 2359304 | tf_op jit(solution)/shard_map/ppermute | solution.py:241
  4.3 3.0 %collective-permute-start.1 = (bf16[256,1536]{1,0:T(8,128)(2,1)S(1)}, bf16[256,1536]{1,0:T(8,128)(2,1)S(1)}, u32[]{:S(2)}, u32[]{:S(2)}) collective-permute-start(bf16[256,1536]{1,0:T(8,128)(2,1)S(1)} %shard_map.67.refs_4_.refs_0_), channel_id=1, source_target_pairs={{0,3},{1,0},{2,1},{3,2},{4,7},{5,4},{6,5},{7,6},{8,11},{9,8},{10,9... | collective-permute-start | bytes 2359304 | tf_op jit(solution)/shard_map/ppermute | solution.py:241
  7.3 2.5 %collective-permute-start.14 = (bf16[384,3072]{1,0:T(8,128)(2,1)}, bf16[384,3072]{1,0:T(8,128)(2,1)}, u32[]{:S(2)}, u32[]{:S(2)}) collective-permute-start(bf16[384,3072]{1,0:T(8,128)(2,1)} %w0_ref.1), channel_id=1, source_target_pairs={{0,20},{1,21},{2,22},{3,23},{4,16},{5,17},{6,18},{7,19},{16,4},{17... | collective-permute-start | bytes 7077896 | tf_op jit(solution)/shard_map/ppermute | solution.py:264
  9.9 1.7 copy-done
  12.7 9.3 %collective-permute-done.2.refs_7_.refs_3_ = bf16[256,1536]{1,0:T(8,128)(2,1)} collective-permute-done((bf16[256,1536]{1,0:T(8,128)(2,1)S(1)}, bf16[256,1536]{1,0:T(8,128)(2,1)}, u32[]{:S(2)}, u32[]{:S(2)}) %collective-permute-start.2) | collective-permute-done | bytes 786464 | tf_op jit(solution)/shard_map/ppermute | solution.py:241
  22.0 1.9 %collective-permute-done.1.refs_6_.refs_2_ = bf16[256,1536]{1,0:T(8,128)(2,1)S(1)} collective-permute-done((bf16[256,1536]{1,0:T(8,128)(2,1)S(1)}, bf16[256,1536]{1,0:T(8,128)(2,1)S(1)}, u32[]{:S(2)}, u32[]{:S(2)}) %collective-permute-start.1) | collective-permute-done | bytes 786464 | tf_op jit(solution)/shard_map/ppermute | solution.py:241
  23.9 3.4 %collective-permute-done.refs_5_.refs_1_ = bf16[256,1536]{1,0:T(8,128)(2,1)S(1)} collective-permute-done((bf16[256,1536]{1,0:T(8,128)(2,1)S(1)}, bf16[256,1536]{1,0:T(8,128)(2,1)S(1)}, u32[]{:S(2)}, u32[]{:S(2)}) %collective-permute-start) | collective-permute-done | bytes 786464 | tf_op jit(solution)/shard_map/ppermute | solution.py:241
  27.7 3.6 %collective-permute-start.4 = (bf16[384,384]{1,0:T(8,128)(2,1)S(1)}, bf16[384,384]{1,0:T(8,128)(2,1)S(1)}, u32[]{:S(2)}, u32[]{:S(2)}) collective-permute-start(bf16[384,384]{1,0:T(8,128)(2,1)S(1)} %shard_map.68.refs_0_), channel_id=1, source_target_pairs={{0,16},{16,0},{1,17},{17,1},{2,18},{18,2},{3,19},{19,3},{4,20},{20... | collective-permute-start | bytes 884744 | tf_op jit(solution)/shard_map/ppermute | solution.py:258
  31.3 1.8 %collective-permute-start.6 = (bf16[128,1536]{1,0:T(8,128)(2,1)S(1)}, bf16[128,1536]{1,0:T(8,128)(2,1)}, u32[]{:S(2)}, u32[]{:S(2)}) collective-permute-start(bf16[128,1536]{1,0:T(8,128)(2,1)S(1)} %slice.6), channel_id=1, source_target_pairs={{0,1},{1,2},{2,3},{3,0},{4,5},{5,6},{6,7},{7,4},{8,9},{9,10},{10,1... | collective-permute-start | bytes 1179656 | tf_op jit(solution)/shard_map/ppermute | solution.py:241
  33.1 3.8 %collective-permute-done.4.refs_2_ = bf16[384,384]{1,0:T(8,128)(2,1)S(1)} collective-permute-done((bf16[384,384]{1,0:T(8,128)(2,1)S(1)}, bf16[384,384]{1,0:T(8,128)(2,1)S(1)}, u32[]{:S(2)}, u32[]{:S(2)}) %collective-permute-start.4) | collective-permute-done | bytes 294944 | tf_op jit(solution)/shard_map/ppermute | solution.py:258
  38.0 1.6 collective-permute-start.8
  40.4 4.2 %collective-permute-done.6.refs_4_ = bf16[128,1536]{1,0:T(8,128)(2,1)} collective-permute-done((bf16[128,1536]{1,0:T(8,128)(2,1)S(1)}, bf16[128,1536]{1,0:T(8,128)(2,1)}, u32[]{:S(2)}, u32[]{:S(2)}) %collective-permute-start.6) | collective-permute-done | bytes 393248 | tf_op jit(solution)/shard_map/ppermute | solution.py:241
  45.3 2.0 %collective-permute-start.10 = (bf16[128,1536]{1,0:T(8,128)(2,1)}, bf16[128,1536]{1,0:T(8,128)(2,1)}, u32[]{:S(2)}, u32[]{:S(2)}) collective-permute-start(bf16[128,1536]{1,0:T(8,128)(2,1)} %collective-permute-done.6.refs_4_), channel_id=1, source_target_pairs={{0,4},{1,5},{2,6},{3,7},{4,0},{5,1},{6,2},{7,3},{8,12},{9,13},{10,... | collective-permute-start | bytes 1179656 | tf_op jit(solution)/shard_map/ppermute | solution.py:241
  47.3 4.1 %all-to-all-start = ((bf16[8,256,128]{2,1,0:T(8,128)(2,1)}), bf16[8,256,128]{2,1,0:T(8,128)(2,1)}, u32[]{:S(2)}, u32[]{:S(2)}) async-start(bf16[8,256,128]{2,1,0:T(8,128)(2,1)} %bitcast.25), calls=%async_computation | async-start | bytes 1048576 | tf_op jit(solution)/shard_map/all_to_all | solution.py:297
  52.4 1.1 copy-done.8
  53.5 1.1 copy-done.11
  57.6 3.4 %shard_map.69.near_ref = bf16[1024,384]{1,0:T(8,128)(2,1)S(1)} custom-call(s32[4]{0:T(128)S(1)} %pad_add_fusion.owner_ref.pos_ref, bf16[384,384]{1,0:T(8,128)(2,1)S(1)} %shard_map.68.refs_0_, bf16[384,384]{1,0:T(8,128)(2,1)S(1)} %copy-done.18, bf16[384,384]{1,0:T(8,128)(2,1)S(1)} %copy-done.16, bf16[384,384]{1,0:T(8,128)(2,1)S(1)} %copy-done.20, ...), custom_call_target="tpu_custom_call" | custom-call | flops 1207959552 | bytes 1048576 | tf_op jit(solution)/shard_map/pallas_call | solution.py:301
  62.0 6.6 %collective-permute-done.10.refs_8_ = bf16[128,1536]{1,0:T(8,128)(2,1)} collective-permute-done((bf16[128,1536]{1,0:T(8,128)(2,1)}, bf16[128,1536]{1,0:T(8,128)(2,1)}, u32[]{:S(2)}, u32[]{:S(2)}) %collective-permute-start.10) | collective-permute-done | bytes 393248 | tf_op jit(solution)/shard_map/ppermute | solution.py:241
  68.6 4.1 %shard_map.70.far_ref = bf16[1024,384]{1,0:T(8,128)(2,1)S(1)} custom-call(s32[4]{0:T(128)S(1)} %pad_add_fusion.owner_ref.pos_ref, bf16[384,384]{1,0:T(8,128)(2,1)S(1)} %shard_map.68.refs_0_, bf16[384,384]{1,0:T(8,128)(2,1)S(1)} %copy-done.18, bf16[384,384]{1,0:T(8,128)(2,1)S(1)} %copy-done.16, bf16[384,384]{1,0:T(8,128)(2,1)S(1)} %copy-done.20, ...), custom_call_target="tpu_custom_call" | custom-call | flops 1207959552 | bytes 1048576 | tf_op jit(solution)/shard_map/pallas_call | solution.py:301
  73.6 1.1 copy-done.26
  75.9 17.1 %shard_map.72.first_ref = bf16[2048,256]{1,0:T(8,128)(2,1)S(1)} custom-call(s32[9]{0:T(128)S(1)} %stack.59.pos_ref, s32[1]{0:T(128)S(6)} %copy.12.len_ref, bf16[1024,384]{1,0:T(8,128)(2,1)S(1)} %copy-done.26, bf16[1024,384]{1,0:T(8,128)(2,1)S(1)} %copy-done.29, bf16[2048,128]{1,0:T(8,128)(2,1)} %bitcast.16.up_ref), custom_call_target="tpu_custom_call" | custom-call | flops 10737418240 | bytes 1048576 | tf_op jit(solution)/shard_map/pallas_call | solution.py:311
  94.0 3.6 %all-to-all-start.1 = ((bf16[8,256,256]{2,1,0:T(8,128)(2,1)}), bf16[8,256,256]{2,1,0:T(8,128)(2,1)S(1)}, u32[]{:S(2)}, u32[]{:S(2)}) async-start(bf16[8,256,256]{2,1,0:T(8,128)(2,1)} %bitcast.28), calls=%async_computation.1 | async-start | bytes 2097152 | tf_op jit(solution)/shard_map/all_to_all | solution.py:331
  99.9 17.1 %shard_map.71.second_ref = bf16[2048,256]{1,0:T(8,128)(2,1)S(1)} custom-call(s32[9]{0:T(128)S(1)} %stack.59.pos_ref, s32[1]{0:T(128)S(6)} %copy.12.len_ref, bf16[1024,384]{1,0:T(8,128)(2,1)S(1)} %copy-done.27, bf16[1024,384]{1,0:T(8,128)(2,1)S(1)} %copy-done.30, bf16[2048,128]{1,0:T(8,128)(2,1)} %bitcast.16.up_ref), custom_call_target="tpu_custom_call" | custom-call | flops 10737418240 | bytes 1048576 | tf_op jit(solution)/shard_map/pallas_call | solution.py:311
  118.1 5.5 %all-to-all-start.2 = ((bf16[8,256,256]{2,1,0:T(8,128)(2,1)}), bf16[8,256,256]{2,1,0:T(8,128)(2,1)}, u32[]{:S(2)}, u32[]{:S(2)}) async-start(bf16[8,256,256]{2,1,0:T(8,128)(2,1)} %bitcast.29), calls=%async_computation.2 | async-start | bytes 2097152 | tf_op jit(solution)/shard_map/all_to_all | solution.py:331
  127.0 1.2 copy-done.22
  128.2 1.2 copy-done.24
  129.4 6.2 %shard_map.73 = (f32[768,384]{1,0:T(8,128)S(1)}, bf16[768,384]{1,0:T(8,128)(2,1)S(1)}) custom-call(s32[9]{0:T(128)S(1)} %stack.59.pos_ref, bf16[2048,256]{1,0:T(8,128)(2,1)S(1)} %copy-done.22, bf16[2048,256]{1,0:T(8,128)(2,1)S(1)} %copy-done.24, bf16[256,1536]{1,0:T(8,128)(2,1)S(1)} %copy-done.5, bf16[256,1536]{1,0:T(8,128)(2,1)S(1)} %copy-done.12, ...), custom_call_target="tpu_custom_call" | custom-call | flops 2415919104 | bytes 1048576 | tf_op jit(solution)/shard_map/pallas_call | solution.py:338
  136.9 1.8 collective-permute-done.12.got_ref
  140.1 1.3 copy-done.14
  143.4 2.0 %reshape.21 = bf16[64,12,384]{2,1,0:T(8,128)(2,1)} reshape(bf16[768,384]{1,0:T(8,128)(2,1)} %copy-done.6) | data formatting | bytes 1179648 | tf_op jit(solution)/shard_map/reshape | solution.py:349
  145.4 24.9 %all_to_all.20.parts_ref = bf16[64,12,384]{2,1,0:T(8,128)(2,1)S(1)} all-to-all(bf16[64,12,384]{2,1,0:T(8,128)(2,1)} %reshape.21), channel_id=1, replica_groups=mesh['dp'=4,'zh'=2,'core'=2,'seq'=8] {'dp','zh','seq'}, dimensions={0} | all-to-all | bytes 1179648 | tf_op jit(solution)/shard_map/all_to_all | solution.py:348
  171.1 8.9 %shard_map.74 = (bf16[256,1024]{1,0:T(8,128)(2,1)}, f32[256,1536]{1,0:T(8,128)}) custom-call(s32[4]{0:T(128)S(1)} %pad_add_fusion.owner_ref.pos_ref, bf16[8,256,256]{2,1,0:T(8,128)(2,1)S(1)} %all-to-all-done.1.first_ref, bf16[8,256,256]{2,1,0:T(8,128)(2,1)} %all-to-all-done.2.second_ref, bf16[384,3072]{1,0:T(8,128)(2,1)S(1)} %copy-done.1, ...), custom_call_target="tpu_custom_call" | custom-call | flops 2415919104 | bytes 1048576 | tf_op jit(solution)/shard_map/pallas_call | solution.py:352
  (92 shorter events, 25.0 us)
Async XLA Ops:
  0.6 1.1 copy-start.2
  1.8 10.0 %copy-start.33 = (bf16[1,256,1024]{2,1,0:T(8,128)(2,1)S(1)}, bf16[1,256,1024]{2,1,0:T(8,128)(2,1)}, u32[]{:S(2)}) copy-start(bf16[1,256,1024]{2,1,0:T(8,128)(2,1)} %param.7) | copy-start | bytes 1572868
  2.2 50.2 %copy-start.4 = (bf16[256,1536]{1,0:T(8,128)(2,1)}, bf16[256,1536]{1,0:T(8,128)(2,1)S(1)}, u32[]{:S(2)}) copy-start(bf16[256,1536]{1,0:T(8,128)(2,1)S(1)} %shard_map.67.refs_4_.refs_0_) | copy-start | bytes 2359300
  2.2 19.7 %collective-permute-start.2 = (bf16[256,1536]{1,0:T(8,128)(2,1)S(1)}, bf16[256,1536]{1,0:T(8,128)(2,1)}, u32[]{:S(2)}, u32[]{:S(2)}) collective-permute-start(bf16[256,1536]{1,0:T(8,128)(2,1)S(1)} %shard_map.67.refs_4_.refs_0_), channel_id=1, source_target_pairs={{0,4},{1,5},{2,6},{3,7},{4,0},{5,1},{6,2},{7,3},{8,12},{9,13},{10,... | collective-permute-start | bytes 2359304 | tf_op jit(solution)/shard_map/ppermute | solution.py:241
  4.3 19.5 %collective-permute-start.1 = (bf16[256,1536]{1,0:T(8,128)(2,1)S(1)}, bf16[256,1536]{1,0:T(8,128)(2,1)S(1)}, u32[]{:S(2)}, u32[]{:S(2)}) collective-permute-start(bf16[256,1536]{1,0:T(8,128)(2,1)S(1)} %shard_map.67.refs_4_.refs_0_), channel_id=1, source_target_pairs={{0,3},{1,0},{2,1},{3,2},{4,7},{5,4},{6,5},{7,6},{8,11},{9,8},{10,9... | collective-permute-start | bytes 2359304 | tf_op jit(solution)/shard_map/ppermute | solution.py:241
  7.3 19.9 %collective-permute-start = (bf16[256,1536]{1,0:T(8,128)(2,1)S(1)}, bf16[256,1536]{1,0:T(8,128)(2,1)S(1)}, u32[]{:S(2)}, u32[]{:S(2)}) collective-permute-start(bf16[256,1536]{1,0:T(8,128)(2,1)S(1)} %shard_map.67.refs_4_.refs_0_), channel_id=1, source_target_pairs={{0,1},{1,2},{2,3},{3,0},{4,5},{5,6},{6,7},{7,4},{8,9},{9,10},{10,1... | collective-permute-start | bytes 2359304 | tf_op jit(solution)/shard_map/ppermute | solution.py:241
  7.3 90.2 %collective-permute-start.14 = (bf16[384,3072]{1,0:T(8,128)(2,1)}, bf16[384,3072]{1,0:T(8,128)(2,1)}, u32[]{:S(2)}, u32[]{:S(2)}) collective-permute-start(bf16[384,3072]{1,0:T(8,128)(2,1)} %w0_ref.1), channel_id=1, source_target_pairs={{0,20},{1,21},{2,22},{3,23},{4,16},{5,17},{6,18},{7,19},{16,4},{17... | collective-permute-start | bytes 7077896 | tf_op jit(solution)/shard_map/ppermute | solution.py:264
  9.9 1.7 copy-start
  23.9 28.4 %copy-start.7 = (bf16[256,1536]{1,0:T(8,128)(2,1)}, bf16[256,1536]{1,0:T(8,128)(2,1)S(1)}, u32[]{:S(2)}) copy-start(bf16[256,1536]{1,0:T(8,128)(2,1)S(1)} %collective-permute-done.1.refs_6_.refs_2_) | copy-start | bytes 2359300
  27.3 25.0 %copy-start.10 = (bf16[256,1536]{1,0:T(8,128)(2,1)}, bf16[256,1536]{1,0:T(8,128)(2,1)S(1)}, u32[]{:S(2)}) copy-start(bf16[256,1536]{1,0:T(8,128)(2,1)S(1)} %collective-permute-done.refs_5_.refs_1_) | copy-start | bytes 2359300
  27.3 12.3 %collective-permute-start.7 = (bf16[128,1536]{1,0:T(8,128)(2,1)S(1)}, bf16[128,1536]{1,0:T(8,128)(2,1)}, u32[]{:S(2)}, u32[]{:S(2)}) collective-permute-start(bf16[128,1536]{1,0:T(8,128)(2,1)S(1)} %slice.7), channel_id=1, source_target_pairs={{0,3},{1,0},{2,1},{3,2},{4,7},{5,4},{6,5},{7,6},{8,11},{9,8},{10,9... | collective-permute-start | bytes 1179656 | tf_op jit(solution)/shard_map/ppermute | solution.py:241
  27.7 9.2 %collective-permute-start.4 = (bf16[384,384]{1,0:T(8,128)(2,1)S(1)}, bf16[384,384]{1,0:T(8,128)(2,1)S(1)}, u32[]{:S(2)}, u32[]{:S(2)}) collective-permute-start(bf16[384,384]{1,0:T(8,128)(2,1)S(1)} %shard_map.68.refs_0_), channel_id=1, source_target_pairs={{0,16},{16,0},{1,17},{17,1},{2,18},{18,2},{3,19},{19,3},{4,20},{20... | collective-permute-start | bytes 884744 | tf_op jit(solution)/shard_map/ppermute | solution.py:258
  31.2 6.0 %collective-permute-start.3 = (bf16[384,384]{1,0:T(8,128)(2,1)S(1)}, bf16[384,384]{1,0:T(8,128)(2,1)S(1)}, u32[]{:S(2)}, u32[]{:S(2)}) collective-permute-start(bf16[384,384]{1,0:T(8,128)(2,1)S(1)} %shard_map.68.refs_0_), channel_id=1, source_target_pairs={{0,8},{8,0},{1,9},{9,1},{2,10},{10,2},{3,11},{11,3},{4,12},{12,4},... | collective-permute-start | bytes 884744 | tf_op jit(solution)/shard_map/ppermute | solution.py:254
  31.3 13.3 %collective-permute-start.6 = (bf16[128,1536]{1,0:T(8,128)(2,1)S(1)}, bf16[128,1536]{1,0:T(8,128)(2,1)}, u32[]{:S(2)}, u32[]{:S(2)}) collective-permute-start(bf16[128,1536]{1,0:T(8,128)(2,1)S(1)} %slice.6), channel_id=1, source_target_pairs={{0,1},{1,2},{2,3},{3,0},{4,5},{5,6},{6,7},{7,4},{8,9},{9,10},{10,1... | collective-permute-start | bytes 1179656 | tf_op jit(solution)/shard_map/ppermute | solution.py:241
  36.9 31.7 %collective-permute-start.9 = (bf16[256,1536]{1,0:T(8,128)(2,1)}, bf16[256,1536]{1,0:T(8,128)(2,1)}, u32[]{:S(2)}, u32[]{:S(2)}) collective-permute-start(bf16[256,1536]{1,0:T(8,128)(2,1)} %collective-permute-done.2.refs_7_.refs_3_), channel_id=1, source_target_pairs={{0,3},{1,0},{2,1},{3,2},{4,7},{5,4},{6,5},{7,6},{8,11},{9,8},{10,9... | collective-permute-start | bytes 2359304 | tf_op jit(solution)/shard_map/ppermute | solution.py:241
  38.0 30.6 %collective-permute-start.8 = (bf16[256,1536]{1,0:T(8,128)(2,1)}, bf16[256,1536]{1,0:T(8,128)(2,1)}, u32[]{:S(2)}, u32[]{:S(2)}) collective-permute-start(bf16[256,1536]{1,0:T(8,128)(2,1)} %collective-permute-done.2.refs_7_.refs_3_), channel_id=1, source_target_pairs={{0,1},{1,2},{2,3},{3,0},{4,5},{5,6},{6,7},{7,4},{8,9},{9,10},{10,1... | collective-permute-start | bytes 2359304 | tf_op jit(solution)/shard_map/ppermute | solution.py:241
  39.6 4.9 %collective-permute-start.5 = (bf16[384,384]{1,0:T(8,128)(2,1)S(1)}, bf16[384,384]{1,0:T(8,128)(2,1)S(1)}, u32[]{:S(2)}, u32[]{:S(2)}) collective-permute-start(bf16[384,384]{1,0:T(8,128)(2,1)S(1)} %collective-permute-done.4.refs_2_), channel_id=1, source_target_pairs={{0,8},{8,0},{1,9},{9,1},{2,10},{10,2},{3,11},{11,3},{4,12},{12,4},... | collective-permute-start | bytes 884744 | tf_op jit(solution)/shard_map/ppermute | solution.py:254
  44.6 17.4 %collective-permute-start.11 = (bf16[128,1536]{1,0:T(8,128)(2,1)}, bf16[128,1536]{1,0:T(8,128)(2,1)}, u32[]{:S(2)}, u32[]{:S(2)}) collective-permute-start(bf16[128,1536]{1,0:T(8,128)(2,1)} %collective-permute-done.7.refs_5_), channel_id=1, source_target_pairs={{0,4},{1,5},{2,6},{3,7},{4,0},{5,1},{6,2},{7,3},{8,12},{9,13},{10,... | collective-permute-start | bytes 1179656 | tf_op jit(solution)/shard_map/ppermute | solution.py:241
  45.3 23.3 %collective-permute-start.10 = (bf16[128,1536]{1,0:T(8,128)(2,1)}, bf16[128,1536]{1,0:T(8,128)(2,1)}, u32[]{:S(2)}, u32[]{:S(2)}) collective-permute-start(bf16[128,1536]{1,0:T(8,128)(2,1)} %collective-permute-done.6.refs_4_), channel_id=1, source_target_pairs={{0,4},{1,5},{2,6},{3,7},{4,0},{5,1},{6,2},{7,3},{8,12},{9,13},{10,... | collective-permute-start | bytes 1179656 | tf_op jit(solution)/shard_map/ppermute | solution.py:241
  47.3 26.3 %all-to-all-start = ((bf16[8,256,128]{2,1,0:T(8,128)(2,1)}), bf16[8,256,128]{2,1,0:T(8,128)(2,1)}, u32[]{:S(2)}, u32[]{:S(2)}) async-start(bf16[8,256,128]{2,1,0:T(8,128)(2,1)} %bitcast.25), calls=%async_computation | async-start | bytes 1048576 | tf_op jit(solution)/shard_map/all_to_all | solution.py:297
  52.4 1.1 copy-start.8
  57.5 4.4 %copy-start.1 = (bf16[384,3072]{1,0:T(8,128)(2,1)S(1)}, bf16[384,3072]{1,0:T(8,128)(2,1)}, u32[]{:S(2)}) copy-start(bf16[384,3072]{1,0:T(8,128)(2,1)} %w0_ref.1) | copy-start | bytes 7077892
  61.9 109.1 %collective-permute-start.13 = (bf16[384,3072]{1,0:T(8,128)(2,1)S(1)}, bf16[384,3072]{1,0:T(8,128)(2,1)}, u32[]{:S(2)}, u32[]{:S(2)}) collective-permute-start(bf16[384,3072]{1,0:T(8,128)(2,1)S(1)} %copy-done.1), channel_id=1, source_target_pairs={{0,8},{8,0},{1,9},{9,1},{2,10},{10,2},{3,11},{11,3},{4,12},{12,4},... | collective-permute-start | bytes 7077896 | tf_op jit(solution)/shard_map/ppermute | solution.py:254
  73.6 1.1 copy-start.26
  94.0 24.1 %all-to-all-start.1 = ((bf16[8,256,256]{2,1,0:T(8,128)(2,1)}), bf16[8,256,256]{2,1,0:T(8,128)(2,1)S(1)}, u32[]{:S(2)}, u32[]{:S(2)}) async-start(bf16[8,256,256]{2,1,0:T(8,128)(2,1)} %bitcast.28), calls=%async_computation.1 | async-start | bytes 2097152 | tf_op jit(solution)/shard_map/all_to_all | solution.py:331
  97.6 73.5 %collective-permute-start.15 = (bf16[384,3072]{1,0:T(8,128)(2,1)}, bf16[384,3072]{1,0:T(8,128)(2,1)}, u32[]{:S(2)}, u32[]{:S(2)}) collective-permute-start(bf16[384,3072]{1,0:T(8,128)(2,1)} %collective-permute-done.14.w2_ref), channel_id=1, source_target_pairs={{0,8},{8,0},{1,9},{9,1},{2,10},{10,2},{3,11},{11,3},{4,12},{12,4},... | collective-permute-start | bytes 7077896 | tf_op jit(solution)/shard_map/ppermute | solution.py:254
  118.1 22.0 %all-to-all-start.2 = ((bf16[8,256,256]{2,1,0:T(8,128)(2,1)}), bf16[8,256,256]{2,1,0:T(8,128)(2,1)}, u32[]{:S(2)}, u32[]{:S(2)}) async-start(bf16[8,256,256]{2,1,0:T(8,128)(2,1)} %bitcast.29), calls=%async_computation.2 | async-start | bytes 2097152 | tf_op jit(solution)/shard_map/all_to_all | solution.py:331
  127.0 1.2 copy-start.22
  128.2 1.2 copy-start.24
  136.7 2.0 %collective-permute-start.12 = (bf16[768,384]{1,0:T(8,128)(2,1)S(1)}, bf16[768,384]{1,0:T(8,128)(2,1)S(1)}, u32[]{:S(2)}, u32[]{:S(2)}) collective-permute-start(bf16[768,384]{1,0:T(8,128)(2,1)S(1)} %get-tuple-element.23), channel_id=1, source_target_pairs={{0,8},{8,0},{1,9},{9,1},{2,10},{10,2},{3,11},{11,3},{4,12},{12,4},... | collective-permute-start | bytes 1769480 | tf_op jit(solution)/shard_map/ppermute | solution.py:254
  140.1 1.3 copy-start.14
  145.4 25.7 %copy-start.3 = (bf16[1,256,1536]{2,1,0:T(8,128)(2,1)S(1)}, bf16[1,256,1536]{2,1,0:T(8,128)(2,1)}, u32[]{:S(2)}) copy-start(bf16[1,256,1536]{2,1,0:T(8,128)(2,1)} %param.4) | copy-start | bytes 2359300
  (21 other events, 20.7 us)

commit v3 on v2

--- a/solution.py
+++ b/solution.py
@@ -21,6 +21,7 @@
 NC = T // CH
 VM = pl.BlockSpec(memory_space=pltpu.VMEM)
 SM = pl.BlockSpec(memory_space=pltpu.SMEM)
+ANY = pl.BlockSpec(memory_space=pl.ANY)
 
 
 def dot(a, b, dims=((1,), (0,))):
@@ -37,41 +38,45 @@
     out_ref[...] = standardize(x_ref[...].astype(F32))[0].astype(BF)
 
 
-def columns_kernel(me_ref, w_ref, out_ref):
-    s = me_ref[0] * GW
-    q, k, v = (
-        w_ref[:, pl.ds(pl.multiple_of(kind * 1024 + s, GW), GW)].astype(F32) for kind in range(3)
-    )
-    low = lax.broadcasted_iota(jnp.int32, k.shape, 1) < HD
-    out_ref[:, 0:128] = jnp.where(low, k, pltpu.roll(v, HD, 1)).astype(BF)
-    out_ref[:, 128:256] = jnp.where(low, pltpu.roll(k, HD, 1), v).astype(BF)
-    out_ref[:, 256:384] = q.astype(BF)
+def columns_kernel(y_ref, w_ref, out_ref):
+    for z in range(2):
+        s = (z * 4 + y_ref[0]) * GW
+        q, k, v = (
+            w_ref[:, pl.ds(pl.multiple_of(kind * 1024 + s, GW), GW)].astype(F32) for kind in range(3)
+        )
+        low = lax.broadcasted_iota(jnp.int32, k.shape, 1) < HD
+        at = z * 384
+        out_ref[:, at : at + 128] = jnp.where(low, k, pltpu.roll(v, HD, 1)).astype(BF)
+        out_ref[:, at + 128 : at + 256] = jnp.where(low, pltpu.roll(k, HD, 1), v).astype(BF)
+        out_ref[:, at + 256 : at + 384] = q.astype(BF)
 
 
 def project_kernel(n, owner_ref, *refs):
-    weights, blocks, out_ref = refs[:4], refs[4 : 4 + n], refs[4 + n]
-    first = 0
-    for block in blocks:
-        count = block.shape[0]
-        total = None
-        for f in range(4):
-            rows = pl.ds(pl.multiple_of(owner_ref[f] * 384, 384), 384)
-            t = dot(block[:, rows], weights[f][...])
-            total = t if total is None else total + t
-        out_ref[first : first + count, :] = total.astype(BF)
-        first += count
+    weights, blocks, outs = refs[:4], refs[4 : 4 + n], refs[4 + n :]
+    for j in (1, 0):
+        cols = pl.ds(pl.multiple_of((owner_ref[4] ^ j) * 384, 384), 384)
+        first = 0
+        for block in blocks:
+            count = block.shape[0]
+            total = None
+            for f in range(4):
+                rows = pl.ds(pl.multiple_of(owner_ref[f] * 384, 384), 384)
+                t = dot(block[:, rows], weights[f][:, cols])
+                total = t if total is None else total + t
+            outs[j][first : first + count, :] = total.astype(BF)
+            first += count
 
 
 def attention_kernel(
-    head, pos_ref, len_ref, near_ref, far_ref, up_ref, out_ref, kv, ka, vt, kt, qt, ut, s_ref, e_ref, acc
+    head, pos_ref, len_ref, near_ref, far_ref, other_ref, last_ref, up_ref, out_ref, kv, ka, vt, kt, qt, ut, s_ref, e_ref, acc
 ):
     length = len_ref[0]
     hrows = slice(head * HD, (head + 1) * HD)
     lane = lax.broadcasted_iota(jnp.int32, (BQ, 128), 1)
     for b in range(SEQ):
         r = slice(b * BQ, (b + 1) * BQ)
-        source = near_ref if b < 4 else far_ref
-        own = slice(b % 4 * BQ, (b % 4 + 1) * BQ)
+        source = (near_ref, far_ref, other_ref, last_ref)[b // 4 * 2 + (b % 4 == 3)]
+        own = slice(b % 4 % 3 * BQ, (b % 4 % 3 + 1) * BQ)
         first = pl.multiple_of(pos_ref[b] * BQ, BQ)
         mine = source[own, head * 128 : (head + 1) * 128]
         kv[r, :] = mine
@@ -147,25 +152,33 @@
         out_ref[rows, 128:256] = acc[b * BQ : (b + 1) * BQ, :].astype(BF)
 
 
+def fetch(pairs, sems):
+    copies = [pltpu.make_async_copy(a, b, sems.at[i]) for i, (a, b) in enumerate(pairs)]
+    for copy in copies:
+        copy.start()
+    return copies
+
+
 def weight_gradient_kernel(pos_ref, first_ref, second_ref, *refs):
-    blocks, (keep_ref, send_ref, acc) = refs[:-3], refs[-3:]
-    at = [0] * SEQ
-    which = 0
-    for i, block in enumerate(blocks):
+    sources, (keep_ref, send_ref, acc, held, sems) = refs[:-5], refs[-5:]
+    at = [sum(b.shape[0] for b in sources[:i]) for i in range(len(sources))]
+    spots = [pl.ds(a, b.shape[0]) for a, b in zip(at, sources)]
+    copies = fetch([(b, held.at[spot]) for b, spot in zip(sources, spots)], sems)
+    for i, block in enumerate(sources):
         count = block.shape[0]
-        rows = pl.ds(pl.multiple_of(pos_ref[which] * ROWS + at[which], 128), count)
+        first = pos_ref[at[i] // ROWS] * ROWS + at[i] % ROWS
+        rows = pl.ds(pl.multiple_of(first, 128), count)
         both = [g[rows, :].astype(F32).T.astype(BF) for g in (first_ref, second_ref)]
         parts = [g[128:256] for g in both] + [g[0:HD] for g in both]
         flipped = jnp.concatenate(parts, axis=0)
+        copies[i].wait()
         for c in range(3):
             cs = slice(c * 512, (c + 1) * 512)
-            t = dot(flipped, block[:, cs])
+            t = dot(flipped, held[at[i] : at[i] + count, cs])
             if i == 0:
                 acc[:, cs] = t
             else:
                 acc[:, cs] += t
-        at[which] += count
-        which += at[which] == ROWS
     core = pos_ref[SEQ]
     for c in range(4):
         flipped = acc[:, c * 384 : (c + 1) * 384].T
@@ -183,8 +196,22 @@
                     send_ref[r, :] = halves[k][i].astype(BF)
 
 
-def add_kernel(keep_ref, got_ref, out_ref):
-    out_ref[...] = (keep_ref[...] + got_ref[...].astype(F32)).astype(BF)
+def add_kernel(me_ref, keep_ref, got_ref, own_ref, *outs):
+    for d in range(8):
+        rows = pl.ds(pl.multiple_of((me_ref[0] ^ d) * 96, 96), 96)
+        t = keep_ref[rows, :] + got_ref[rows, :].astype(F32)
+        if d == 0:
+            own_ref[...] = t
+        else:
+            outs[d - 1][...] = t.astype(BF)
+
+
+def sum_kernel(own_ref, *refs):
+    t = own_ref[...]
+    for ref in refs[:-1]:
+        t = t + ref[...].astype(F32)
+    for s in range(SEQ):
+        refs[-1][s] = t[s * 12 : (s + 1) * 12]
 
 
 def join(first, second, part):
@@ -196,10 +223,7 @@
 
 def combine_kernel(parts_ref, out_ref):
     for s in range(SEQ):
-        total = None
-        for r in range(8):
-            t = parts_ref[r * SEQ + s].astype(F32)
-            total = t if total is None else total + t
+        total = parts_ref[s]
         at = s * GW
         low, high = total[:, 0:128], total[:, 128:256]
         out_ref[:, at : at + GW] = total[:, 256:384]
@@ -208,8 +232,9 @@
 
 
 def input_gradient_kernel(
-    pos_ref, first_ref, second_ref, w0_ref, w1_ref, w2_ref, w3_ref, x_ref, ctx_ref, out_ref, packed
+    pos_ref, first_ref, second_ref, w0, w1, w2, w3, x_ref, ctx_ref, out_ref, packed, held, sems
 ):
+    copies = fetch([(w, held.at[f]) for f, w in enumerate((w0, w1, w2, w3))], sems)
     for s in range(SEQ):
         at = s * GW
         a = [first_ref[s, :, i * 128 : (i + 1) * 128].astype(F32) for i in range(2)]
@@ -218,9 +243,10 @@
         packed[:, at : at + GW] = join(a[0], b[0], 0).astype(BF)
         packed[:, 1024 + at : 1024 + at + GW] = join(a[1], b[1], 0).astype(BF)
         packed[:, 2048 + at : 2048 + at + GW] = join(a[1], b[1], 1).astype(BF)
-    for f, w_ref in enumerate((w0_ref, w1_ref, w2_ref, w3_ref)):
+    for f in range(4):
         to = pl.ds(pl.multiple_of(pos_ref[f] * 384, 384), 384)
-        out_ref[:, to] = dot(packed[...], w_ref[...], ((1,), (1,)))
+        copies[f].wait()
+        out_ref[:, to] = dot(packed[...], held[f], ((1,), (1,)))
     standard, inv_std = standardize(x_ref[...].astype(F32))
     ng = out_ref[...]
     row_mean = jnp.mean(ng, axis=1, keepdims=True)
@@ -232,40 +258,27 @@
     return jax.ShapeDtypeStruct(dims, dtype)
 
 
-def gather_rows(x, extra):
-    up = [(i, (i // 4) * 4 + (i % 4 + 1) % 4) for i in range(8)]
-    down = [(i, (i // 4) * 4 + (i % 4 + 3) % 4) for i in range(8)]
-    across = [(i, i ^ 4) for i in range(8)]
-
-    def send(v, way):
-        return lax.ppermute(v, "seq", way)
-
-    half = ROWS // 2
-    below, above, other = send(x, up), send(x, down), send(x, across)
-    below, above, other, extra = lax.optimization_barrier((below, above, other, extra))
-    far = [send(below[:half], up), send(above[half:], down)]
-    other_below, other_above = send(other, up), send(other, down)
-    other_far = [send(v, across) for v in far]
-    offsets = [(0, 0), (0, 3), (0, 1), (1, 0), (0, 2), (1, 3), (1, 1), (1, 2)]
-    return offsets, [x, below, above, other], [*far, other_below, other_above, *other_far], extra
+UP = [(i, (i // 4) * 4 + (i % 4 + 1) % 4) for i in range(8)]
+DOWN = [(i, (i // 4) * 4 + (i % 4 + 3) % 4) for i in range(8)]
+ACROSS = [(i, i ^ 4) for i in range(8)]
+SWAP = [(f * 8 + s, (f ^ 1) * 8 + (s ^ 4)) for f in range(2) for s in range(8)]
+OFFSETS = [(dz, dy) for dz in range(2) for dy in (0, 3, 1, 2)]
+tie = lax.optimization_barrier
+
+
+def send(v, way):
+    return lax.ppermute(v, "seq", way)
 
 
 def sibling(v):
     return lax.ppermute(v, "core", [(0, 1), (1, 0)])
 
 
-def gather_columns(mine):
-    over = lax.ppermute(mine, "zh", [(0, 1), (1, 0)])
-    return [mine, sibling(mine), over, sibling(over)]
-
-
-def gather_weight(w):
-    swap = [(f * 8 + s, (f ^ 1) * 8 + (s ^ 4)) for f in range(2) for s in range(8)]
-    over = lax.ppermute(w, ("zh", "seq"), swap)
-    return [w, sibling(w), over, sibling(over)]
-
-
-def call(kernel, out, in_specs, flops=0, scratch=(), transcendentals=0, vmem=32):
+def swap(v):
+    return lax.ppermute(v, ("zh", "seq"), SWAP)
+
+
+def call(kernel, out, in_specs, flops=0, scratch=(), transcendentals=0, vmem=56):
     return pl.pallas_call(
         kernel,
         out_shape=out,
@@ -284,34 +297,45 @@
     me = lax.axis_index("seq")
     core = lax.axis_index("core")
     fsdp = lax.axis_index("zh") * 2 + core
+    half = ROWS // 2
     normed = call(norm_kernel, shape((ROWS, D)), [VM])(x)
-    mine = call(columns_kernel, shape((384, 384)), [SM, VM])(me[None].astype(jnp.int32), projection)
+    mine = call(columns_kernel, shape((384, 768)), [SM, VM])(
+        (me % 4)[None].astype(jnp.int32), projection
+    )
     upstream = cotangent[0].reshape(ROWS, SEQ, GW).transpose(1, 0, 2)
-    offsets, near, far, (mine, upstream) = gather_rows(normed, (mine, upstream))
-    blocks = near + far
-    index = [(me // 4 ^ dz) * 4 + (me % 4 + dy) % 4 for dz, dy in offsets]
+    index = [(me // 4 ^ dz) * 4 + (me % 4 + dy) % 4 for dz, dy in OFFSETS]
     place = jnp.stack(index + [core]).astype(jnp.int32)
-    owners = jnp.stack([fsdp ^ i for i in range(4)]).astype(jnp.int32)
-
-    columns = gather_columns(mine)
+    owners = jnp.stack([fsdp ^ i for i in range(4)] + [me // 4]).astype(jnp.int32)
+
+    below, above, other = send(normed, UP), send(normed, DOWN), send(normed, ACROSS)
+    mine, upstream, place, owners, below, above = tie((mine, upstream, place, owners, below, above))
+    over = swap(mine)
+    columns = [mine, sibling(mine), over, sibling(over)]
+    far = [send(below[:half], UP), send(above[half:], DOWN)]
+
+    def project(rows):
+        count = sum(r.shape[0] for r in rows)
+        kept, sent = call(
+            functools.partial(project_kernel, len(rows)),
+            (shape((count, 384)), shape((count, 384))),
+            [SM] + [VM] * (4 + len(rows)),
+            4 * count * D * 384,
+        )(owners, *columns, *rows)
+        return kept, send(sent, ACROSS)
+
+    near_kept, near_got = project([normed, below, above])
+    far, other, upstream = tie((far, other, upstream))
+    far_kept, far_got = project(far)
     upstream = lax.all_to_all(upstream, "seq", 0, 0, tiled=True).reshape(T, GW)
-    weights = gather_weight(projection)
-
-    def project(rows):
-        return call(
-            functools.partial(project_kernel, len(rows)),
-            shape((T // 2, 384)),
-            [SM] + [VM] * (4 + len(rows)),
-            T * D * 384,
-        )(owners, *columns, *rows)
-
-    near_packed, far_packed = project(near), project(far)
+    other_below, other_above = send(other, UP), send(other, DOWN)
+    weight, columns[2] = tie((projection, over))
+    weight_over = swap(weight)
 
     def attend(head):
         return call(
             functools.partial(attention_kernel, head),
             shape((T, 256)),
-            [SM, SM, VM, VM, VM],
+            [SM, SM] + [VM] * 5,
             20 * 2 * T * T * HD,
             [
                 pltpu.VMEM((T, 128), BF),
@@ -325,36 +349,54 @@
                 pltpu.VMEM((T, 128), F32),
             ],
             T * T,
-        )(place, lengths, near_packed, far_packed, upstream)
+        )(place, lengths, near_kept, far_kept, near_got, far_got, upstream)
 
     def send_back(grads):
         return lax.all_to_all(grads.reshape(SEQ, ROWS, 256), "seq", 0, 0, tiled=True)
 
     first = attend(0)
+    first, other_below, other_above = tie((first, other_below, other_above))
     back0 = send_back(first)
+    other_far = [send(other_below[:half], UP), send(other_above[half:], DOWN)]
+    weights = [projection, sibling(projection), weight_over, sibling(weight_over)]
+    blocks = [normed, below, above, *far, other, other_below, other_above, *other_far]
     second = attend(1)
-    second, back0 = lax.optimization_barrier((second, back0))
+    second, back0 = tie((second, back0))
     back1 = send_back(second)
-    keep, send = call(
+    keep, out = call(
         weight_gradient_kernel,
         (shape((768, 384), F32), shape((768, 384))),
-        [SM] + [VM] * (2 + len(blocks)),
+        [SM, VM, VM] + [ANY] * len(blocks),
         2 * T * D * 384,
-        [pltpu.VMEM((384, D), F32)],
+        [
+            pltpu.VMEM((384, D), F32),
+            pltpu.VMEM((T, D), BF),
+            pltpu.SemaphoreType.DMA((len(blocks),)),
+        ],
     )(place, first, second, *blocks)
-    got = sibling(send)
-    got, back1 = lax.optimization_barrier((got, back1))
-    partial = call(add_kernel, shape((768, 384)), [VM, VM])(keep, got)
-    partial = lax.all_to_all(
-        partial.reshape(64, 12, 384), ("dp", "zh", "seq"), 0, 0, tiled=True
-    )
-    projection_gradient = call(combine_kernel, shape((12, 3072), F32), [VM])(partial)
+    got = sibling(out)
+    group = lax.axis_index("dp") * 2 + lax.axis_index("zh")
+    own, *outs = call(
+        add_kernel, (shape((96, 384), F32),) + (shape((96, 384)),) * 7, [SM, VM, VM]
+    )(group[None].astype(jnp.int32), keep, got)
+    outs = [
+        lax.ppermute(v, ("dp", "zh"), [(i, i ^ (d + 1)) for i in range(8)])
+        for d, v in enumerate(outs)
+    ]
+    outs, back1 = tie((outs, back1))
+    summed = call(sum_kernel, shape((SEQ, 12, 384), F32), [VM] * 8)(own, *outs)
+    summed = lax.all_to_all(summed, "seq", 0, 0, tiled=True)
+    projection_gradient = call(combine_kernel, shape((12, 3072), F32), [VM])(summed)
     context, input_gradient = call(
         input_gradient_kernel,
         (shape((ROWS, 1024)), shape((ROWS, D), F32)),
-        [SM] + [VM] * 7,
+        [SM, VM, VM] + [ANY] * 4 + [VM],
         2 * ROWS * D * 3072,
-        [pltpu.VMEM((ROWS, 3072), BF)],
+        [
+            pltpu.VMEM((ROWS, 3072), BF),
+            pltpu.VMEM((4, 384, 3072), BF),
+            pltpu.SemaphoreType.DMA((4,)),
+        ],
     )(owners, back0, back1, *weights, x)
     return (context[None], input_gradient[None], projection_gradient)
 

time: 181 us -> 212 us (1.17)
  starting transfers between devices: 31 us -> 54.6 us
  waiting for transfers between devices: 31.6 us -> 53.4 us
  local copies, waits for them, and re-layouts: 32.5 us -> 12.1 us
  Pallas kernels: 58.3 us -> 76.9 us
  blocking collectives: 24.9 us -> 12.1 us
    unnamed x69 -> x35, local copies, waits for them, and re-layouts: 29.5 us -> 4.32 us
    ppermute x2 -> x9, waiting for transfers between devices: 3.8 us -> 24.2 us  [the longest x2 17.5 us: swap(): return lax.ppermute(v, ('zh', 'seq'), SWAP)]
    ppermute x2 -> x9, starting transfers between devices: 6.11 us -> 23.9 us  [the longest x7 16.9 us: body(): lax.ppermute(v, ('dp', 'zh'), [(i, i ^ d + 1) for i in range(8)])]
    pallas_call x7 -> x8, Pallas kernels: 42.8 us -> 56.1 us  [the longest x2 37.4 us: attend(): call(functools.partial(attention_kernel, head), shape((T, 256)), [SM, SM]...]
    all_to_all x1, blocking collectives: 24.9 us -> 12.1 us  [body(): summed = lax.all_to_all(summed, 'seq', 0, 0, tiled=True)]
    ppermute x9 -> x11, starting transfers between devices: 11.3 us -> 18.1 us  [send(): return lax.ppermute(v, 'seq', way)]
    slice x2 -> x4, local copies, waits for them, and re-layouts: 0.05 us -> 5.58 us  [the longest x2 3.53 us: body(): other_far = [send(other_below[:half], UP), send(other_above[half:], DOWN)]]
    pallas_call x1, Pallas kernels: 6.2 us -> 9.02 us  [body(): call(weight_gradient_kernel, (shape((768, 384), F32), shape((768, 384))),...]
  transfers between devices with their start and end apart: 19 -> 28, of which waited for: 8 -> 9; matrix products, arithmetic and copies ran while one was open for 2% -> 4% of each run, Pallas kernels for 27% -> 31%
where the time goes in v3:
time: 212 us; the launch traced here: 211 us
  Pallas kernels  76.9 us (36%)
  starting transfers between devices  54.6 us (26%)
  waiting for transfers between devices  53.4 us (25%)
  local copies, waits for them, and re-layouts  12.1 us (6%)
  blocking collectives  12.1 us (6%)
    pallas_call x2, Pallas kernels, attend(): call(functools.partial(attention_kernel, head), shape((T, 256)), [SM, SM]...  37.4 us
    ppermute x11, waiting for transfers between devices, send(): return lax.ppermute(v, 'seq', way)  27 us
    ppermute x11, starting transfers between devices, send(): return lax.ppermute(v, 'seq', way)  18.1 us
    ppermute x2, waiting for transfers between devices, swap(): return lax.ppermute(v, ('zh', 'seq'), SWAP)  17.5 us
    ppermute x7, starting transfers between devices, body(): lax.ppermute(v, ('dp', 'zh'), [(i, i ^ d + 1) for i in range(8)])  16.9 us
    all_to_all x1, blocking collectives, body(): summed = lax.all_to_all(summed, 'seq', 0, 0, tiled=True)  12.1 us
    pallas_call x2, Pallas kernels, project(): call(functools.partial(project_kernel, len(rows)), (shape((count, 384)),...  10.1 us
    pallas_call x1, Pallas kernels, body(): call(input_gradient_kernel, (shape((ROWS, 1024)), shape((ROWS, D), F32)),...  9.27 us
  transfers between devices with their start and end apart: 28, of which 9 were waited for; matrix products, arithmetic and copies ran while one was open for 4% of the time, Pallas kernels for 31%

profile of v3, /device:TPU:0, one launch (start us, length us, event | category | flops | bytes accessed | tf_op | source)
XLA Modules:
  0.0 210.7 jit_solution(6811896403322907926)
XLA Ops:
  0.6 2.5 %shard_map.68.refs_4_.refs_0_ = bf16[256,1536]{1,0:T(8,128)(2,1)} custom-call(bf16[256,1536]{1,0:T(8,128)(2,1)} %bitcast.28), custom_call_target="tpu_custom_call" | custom-call | bytes 1048576 | tf_op jit(solution)/shard_map/pallas_call | solution.py:301
  8.5 2.7 %shard_map.67.refs_0_ = bf16[384,768]{1,0:T(8,128)(2,1)} custom-call(s32[1]{0:T(128)} %bitcast.y_ref, bf16[384,3072]{1,0:T(8,128)(2,1)} %w0.1), custom_call_target="tpu_custom_call" | custom-call | bytes 1048576 | tf_op jit(solution)/shard_map/pallas_call | solution.py:302
  12.5 11.5 %collective-permute-done.refs_5_.refs_1_ = bf16[256,1536]{1,0:T(8,128)(2,1)} collective-permute-done((bf16[256,1536]{1,0:T(8,128)(2,1)}, bf16[256,1536]{1,0:T(8,128)(2,1)}, u32[]{:S(2)}, u32[]{:S(2)}) %collective-permute-start) | collective-permute-done | bytes 786464 | tf_op jit(solution)/shard_map/ppermute | solution.py:270
  24.1 4.0 %collective-permute-start.3 = (bf16[384,768]{1,0:T(8,128)(2,1)}, bf16[384,768]{1,0:T(8,128)(2,1)S(1)}, u32[]{:S(2)}, u32[]{:S(2)}) collective-permute-start(bf16[384,768]{1,0:T(8,128)(2,1)} %shard_map.67.refs_0_), channel_id=1, source_target_pairs={{0,20},{1,21},{2,22},{3,23},{4,16},{5,17},{6,18},{7,19},{16,4},{17... | collective-permute-start | bytes 1769480 | tf_op jit(solution)/shard_map/ppermute | solution.py:278
  28.1 12.7 %collective-permute-done.3.refs_2_ = bf16[384,768]{1,0:T(8,128)(2,1)S(1)} collective-permute-done((bf16[384,768]{1,0:T(8,128)(2,1)}, bf16[384,768]{1,0:T(8,128)(2,1)S(1)}, u32[]{:S(2)}, u32[]{:S(2)}) %collective-permute-start.3) | collective-permute-done | bytes 589856 | tf_op jit(solution)/shard_map/ppermute | solution.py:278
  40.9 3.0 %collective-permute-start.23 = (bf16[384,3072]{1,0:T(8,128)(2,1)S(1)}, bf16[384,3072]{1,0:T(8,128)(2,1)}, u32[]{:S(2)}, u32[]{:S(2)}) collective-permute-start(bf16[384,3072]{1,0:T(8,128)(2,1)S(1)} %copy-done), channel_id=1, source_target_pairs={{0,20},{1,21},{2,22},{3,23},{4,16},{5,17},{6,18},{7,19},{16,4},{17... | collective-permute-start | bytes 7077896 | tf_op jit(solution)/shard_map/ppermute | solution.py:278
  47.7 2.1 collective-permute-start.6
  50.6 6.3 %shard_map.69 = (bf16[768,384]{1,0:T(8,128)(2,1)}, bf16[768,384]{1,0:T(8,128)(2,1)}) custom-call(s32[5]{0:T(128)} %stack.63.owner_ref.pos_ref, bf16[384,768]{1,0:T(8,128)(2,1)} %shard_map.67.refs_0_, bf16[384,768]{1,0:T(8,128)(2,1)} %copy-done.4, bf16[384,768]{1,0:T(8,128)(2,1)} %copy-done.3, bf16[384,768]{1,0:T(8,128)(2,1)} %copy-done.5, ...), custom_call_target="tpu_custom_call" | custom-call | flops 1811939328 | bytes 1048576 | tf_op jit(solution)/shard_map/pallas_call | solution.py:318
  56.9 2.0 collective-permute-start.8
  58.9 5.9 %collective-permute-done.7.refs_5_ = bf16[256,1536]{1,0:T(8,128)(2,1)} collective-permute-done((bf16[256,1536]{1,0:T(8,128)(2,1)S(1)}, bf16[256,1536]{1,0:T(8,128)(2,1)}, u32[]{:S(2)}, u32[]{:S(2)}) %collective-permute-start.7) | collective-permute-done | bytes 786464 | tf_op jit(solution)/shard_map/ppermute | solution.py:270
  64.8 3.9 %all-to-all-start = ((bf16[8,256,128]{2,1,0:T(8,128)(2,1)}), bf16[8,256,128]{2,1,0:T(8,128)(2,1)S(1)}, u32[]{:S(2)}, u32[]{:S(2)}) async-start(bf16[8,256,128]{2,1,0:T(8,128)(2,1)} %bitcast.27), calls=%async_computation | async-start | bytes 1048576 | tf_op jit(solution)/shard_map/all_to_all | solution.py:329
  68.8 3.8 %shard_map.70 = (bf16[256,384]{1,0:T(8,128)(2,1)}, bf16[256,384]{1,0:T(8,128)(2,1)}) custom-call(s32[5]{0:T(128)} %stack.63.owner_ref.pos_ref, bf16[384,768]{1,0:T(8,128)(2,1)} %shard_map.67.refs_0_, bf16[384,768]{1,0:T(8,128)(2,1)} %copy-done.4, bf16[384,768]{1,0:T(8,128)(2,1)} %copy-done.3, bf16[384,768]{1,0:T(8,128)(2,1)} %copy-done.5, ...), custom_call_target="tpu_custom_call" | custom-call | flops 603979776 | bytes 1048576 | tf_op jit(solution)/shard_map/pallas_call | solution.py:318
  72.5 2.0 collective-permute-start.9
  76.7 9.5 %collective-permute-done.9.last_ref = bf16[256,384]{1,0:T(8,128)(2,1)S(1)} collective-permute-done((bf16[256,384]{1,0:T(8,128)(2,1)}, bf16[256,384]{1,0:T(8,128)(2,1)S(1)}, u32[]{:S(2)}, u32[]{:S(2)}) %collective-permute-start.9) | collective-permute-done | bytes 196640 | tf_op jit(solution)/shard_map/ppermute | solution.py:270
  86.2 2.6 %collective-permute-start.11 = (bf16[256,1536]{1,0:T(8,128)(2,1)}, bf16[256,1536]{1,0:T(8,128)(2,1)}, u32[]{:S(2)}, u32[]{:S(2)}) collective-permute-start(bf16[256,1536]{1,0:T(8,128)(2,1)} %collective-permute-done.7.refs_5_), channel_id=1, source_target_pairs={{0,3},{1,0},{2,1},{3,2},{4,7},{5,4},{6,5},{7,6},{8,11},{9,8},{10,9... | collective-permute-start | bytes 2359304 | tf_op jit(solution)/shard_map/ppermute | solution.py:270
  88.9 4.8 %collective-permute-done.23.w2 = bf16[384,3072]{1,0:T(8,128)(2,1)} collective-permute-done((bf16[384,3072]{1,0:T(8,128)(2,1)S(1)}, bf16[384,3072]{1,0:T(8,128)(2,1)}, u32[]{:S(2)}, u32[]{:S(2)}) %collective-permute-start.23) | collective-permute-done | bytes 2359328 | tf_op jit(solution)/shard_map/ppermute | solution.py:278
  94.5 18.7 %shard_map.72.first_ref = bf16[2048,256]{1,0:T(8,128)(2,1)} custom-call(s32[9]{0:T(128)} %stack.57.pos_ref, s32[1]{0:T(128)S(6)} %copy.11.len_ref, bf16[768,384]{1,0:T(8,128)(2,1)} %get-tuple-element.48.near_ref, bf16[256,384]{1,0:T(8,128)(2,1)} %get-tuple-element.52.far_ref, bf16[768,384]{1,0:T(8,128)(2,1)} %collective-permute-done.8.other_ref, ...), custom_call_target="tpu_custom_call" | custom-call | flops 10737418240 | bytes 1048576 | tf_op jit(solution)/shard_map/pallas_call | solution.py:335
  113.2 3.6 %all-to-all-start.1 = ((bf16[8,256,256]{2,1,0:T(8,128)(2,1)}), bf16[8,256,256]{2,1,0:T(8,128)(2,1)S(1)}, u32[]{:S(2)}, u32[]{:S(2)}) async-start(bf16[8,256,256]{2,1,0:T(8,128)(2,1)} %bitcast.32), calls=%async_computation.1 | async-start | bytes 2097152 | tf_op jit(solution)/shard_map/all_to_all | solution.py:355
  118.6 2.0 collective-permute-start.12
  123.6 18.7 %shard_map.71.second_ref = bf16[2048,256]{1,0:T(8,128)(2,1)} custom-call(s32[9]{0:T(128)} %stack.57.pos_ref, s32[1]{0:T(128)S(6)} %copy.11.len_ref, bf16[768,384]{1,0:T(8,128)(2,1)} %get-tuple-element.48.near_ref, bf16[256,384]{1,0:T(8,128)(2,1)} %get-tuple-element.52.far_ref, bf16[768,384]{1,0:T(8,128)(2,1)} %collective-permute-done.8.other_ref, ...), custom_call_target="tpu_custom_call" | custom-call | flops 10737418240 | bytes 1048576 | tf_op jit(solution)/shard_map/pallas_call | solution.py:335
  142.3 4.5 %all-to-all-start.2 = ((bf16[8,256,256]{2,1,0:T(8,128)(2,1)}), bf16[8,256,256]{2,1,0:T(8,128)(2,1)}, u32[]{:S(2)}, u32[]{:S(2)}) async-start(bf16[8,256,256]{2,1,0:T(8,128)(2,1)} %bitcast.31), calls=%async_computation.2 | async-start | bytes 2097152 | tf_op jit(solution)/shard_map/all_to_all | solution.py:355
  146.8 9.0 %shard_map.73 = (f32[768,384]{1,0:T(8,128)}, bf16[768,384]{1,0:T(8,128)(2,1)}) custom-call(s32[9]{0:T(128)} %stack.57.pos_ref, bf16[2048,256]{1,0:T(8,128)(2,1)} %shard_map.72.first_ref, bf16[2048,256]{1,0:T(8,128)(2,1)} %shard_map.71.second_ref, bf16[256,1536]{1,0:T(8,128)(2,1)} %shard_map.68.refs_4_.refs_0_, ...), custom_call_target="tpu_custom_call" | custom-call | flops 2415919104 | bytes 1048576 | tf_op jit(solution)/shard_map/pallas_call | solution.py:366
  155.9 2.2 %collective-permute-done.14.got_ref = bf16[768,384]{1,0:T(8,128)(2,1)S(1)} collective-permute-done((bf16[768,384]{1,0:T(8,128)(2,1)}, bf16[768,384]{1,0:T(8,128)(2,1)S(1)}, u32[]{:S(2)}, u32[]{:S(2)}) %collective-permute-start.14) | collective-permute-done | bytes 589856 | tf_op jit(solution)/shard_map/ppermute | solution.py:274
  159.0 2.3 %shard_map.74 = (f32[96,384]{1,0:T(8,128)}, bf16[96,384]{1,0:T(8,128)(2,1)}, bf16[96,384]{1,0:T(8,128)(2,1)}, bf16[96,384]{1,0:T(8,128)(2,1)}, bf16[96,384]{1,0:...) custom-call(s32[1]{0:T(128)} %bitcast.19.me_ref, ...), custom_call_target="tpu_custom_call" | custom-call | bytes 1048576 | tf_op jit(solution)/shard_map/pallas_call | solution.py:379
  161.3 3.6 %collective-permute-start.15 = (bf16[96,384]{1,0:T(8,128)(2,1)}, bf16[96,384]{1,0:T(8,128)(2,1)S(1)}, u32[]{:S(2)}, u32[]{:S(2)}) collective-permute-start(bf16[96,384]{1,0:T(8,128)(2,1)} %get-tuple-element.64), channel_id=1, source_target_pairs={{0,16},{16,0},{32,48},{48,32},{64,80},{80,64},{96,112},{112,96},{1... | collective-permute-start | bytes 221192 | tf_op jit(solution)/shard_map/ppermute | solution.py:383
  167.6 3.0 %collective-permute-start.18 = (bf16[96,384]{1,0:T(8,128)(2,1)}, bf16[96,384]{1,0:T(8,128)(2,1)S(1)}, u32[]{:S(2)}, u32[]{:S(2)}) collective-permute-start(bf16[96,384]{1,0:T(8,128)(2,1)} %get-tuple-element.67), channel_id=1, source_target_pairs={{0,64},{16,80},{32,96},{48,112},{64,0},{80,16},{96,32},{112,48},{1... | collective-permute-start | bytes 221192 | tf_op jit(solution)/shard_map/ppermute | solution.py:383
  170.6 3.2 %collective-permute-start.19 = (bf16[96,384]{1,0:T(8,128)(2,1)}, bf16[96,384]{1,0:T(8,128)(2,1)S(1)}, u32[]{:S(2)}, u32[]{:S(2)}) collective-permute-start(bf16[96,384]{1,0:T(8,128)(2,1)} %get-tuple-element.68), channel_id=1, source_target_pairs={{0,80},{16,64},{32,112},{48,96},{64,16},{80,0},{96,48},{112,32},{1... | collective-permute-start | bytes 221192 | tf_op jit(solution)/shard_map/ppermute | solution.py:383
  173.9 2.8 %collective-permute-start.20 = (bf16[96,384]{1,0:T(8,128)(2,1)}, bf16[96,384]{1,0:T(8,128)(2,1)S(1)}, u32[]{:S(2)}, u32[]{:S(2)}) collective-permute-start(bf16[96,384]{1,0:T(8,128)(2,1)} %get-tuple-element.69), channel_id=1, source_target_pairs={{0,96},{16,112},{32,64},{48,80},{64,32},{80,48},{96,0},{112,16},{1... | collective-permute-start | bytes 221192 | tf_op jit(solution)/shard_map/ppermute | solution.py:383
  176.7 2.8 %collective-permute-start.21 = (bf16[96,384]{1,0:T(8,128)(2,1)}, bf16[96,384]{1,0:T(8,128)(2,1)S(1)}, u32[]{:S(2)}, u32[]{:S(2)}) collective-permute-start(bf16[96,384]{1,0:T(8,128)(2,1)} %get-tuple-element.70), channel_id=1, source_target_pairs={{0,112},{16,96},{32,80},{48,64},{64,48},{80,32},{96,16},{112,0},{1... | collective-permute-start | bytes 221192 | tf_op jit(solution)/shard_map/ppermute | solution.py:383
  181.0 3.8 %collective-permute-done.21.refs_6_ = bf16[96,384]{1,0:T(8,128)(2,1)S(1)} collective-permute-done((bf16[96,384]{1,0:T(8,128)(2,1)}, bf16[96,384]{1,0:T(8,128)(2,1)S(1)}, u32[]{:S(2)}, u32[]{:S(2)}) %collective-permute-start.21) | collective-permute-done | bytes 73760 | tf_op jit(solution)/shard_map/ppermute | solution.py:383
  187.4 12.1 %all_to_all.20.parts_ref = f32[8,12,384]{2,1,0:T(8,128)} all-to-all(f32[8,12,384]{2,1,0:T(8,128)} %shard_map.76), channel_id=1, replica_groups=mesh['dp'=4,'zh'=2,'core'=2,'seq'=8] {'seq'}, dimensions={0} | all-to-all | bytes 294912 | tf_op jit(solution)/shard_map/all_to_all | solution.py:388
  201.2 9.3 %shard_map.75 = (bf16[256,1024]{1,0:T(8,128)(2,1)}, f32[256,1536]{1,0:T(8,128)}) custom-call(s32[5]{0:T(128)} %stack.63.owner_ref.pos_ref, bf16[8,256,256]{2,1,0:T(8,128)(2,1)} %copy-done.1, bf16[8,256,256]{2,1,0:T(8,128)(2,1)} %all-to-all-done.2.second_ref, bf16[384,3072]{1,0:T(8,128)(2,1)} %w0.1, bf16[384,3072]{1,0:T(8,128)(2,1)} %collective-permute-done.22.w1, ...), custom_call_target="tpu_custom_call" | custom-call | flops 2415919104 | bytes 1048576 | tf_op jit(solution)/shard_map/pallas_call | solution.py:390
  (78 shorter events, 28.0 us)
Async XLA Ops:
  3.1 21.0 %collective-permute-start = (bf16[256,1536]{1,0:T(8,128)(2,1)}, bf16[256,1536]{1,0:T(8,128)(2,1)}, u32[]{:S(2)}, u32[]{:S(2)}) collective-permute-start(bf16[256,1536]{1,0:T(8,128)(2,1)} %shard_map.68.refs_4_.refs_0_), channel_id=1, source_target_pairs={{0,1},{1,2},{2,3},{3,0},{4,5},{5,6},{6,7},{7,4},{8,9},{9,10},{10,1... | collective-permute-start | bytes 2359304 | tf_op jit(solution)/shard_map/ppermute | solution.py:270
  4.8 19.3 %collective-permute-start.1 = (bf16[256,1536]{1,0:T(8,128)(2,1)}, bf16[256,1536]{1,0:T(8,128)(2,1)}, u32[]{:S(2)}, u32[]{:S(2)}) collective-permute-start(bf16[256,1536]{1,0:T(8,128)(2,1)} %shard_map.68.refs_4_.refs_0_), channel_id=1, source_target_pairs={{0,3},{1,0},{2,1},{3,2},{4,7},{5,4},{6,5},{7,6},{8,11},{9,8},{10,9... | collective-permute-start | bytes 2359304 | tf_op jit(solution)/shard_map/ppermute | solution.py:270
  6.4 34.5 %copy-start = (bf16[384,3072]{1,0:T(8,128)(2,1)S(1)}, bf16[384,3072]{1,0:T(8,128)(2,1)}, u32[]{:S(2)}) copy-start(bf16[384,3072]{1,0:T(8,128)(2,1)} %w0.1) | copy-start | bytes 7077892
  6.4 38.0 %copy-start.2 = (bf16[256,1536]{1,0:T(8,128)(2,1)S(1)}, bf16[256,1536]{1,0:T(8,128)(2,1)}, u32[]{:S(2)}) copy-start(bf16[256,1536]{1,0:T(8,128)(2,1)} %shard_map.68.refs_4_.refs_0_) | copy-start | bytes 2359300
  24.1 16.8 %collective-permute-start.3 = (bf16[384,768]{1,0:T(8,128)(2,1)}, bf16[384,768]{1,0:T(8,128)(2,1)S(1)}, u32[]{:S(2)}, u32[]{:S(2)}) collective-permute-start(bf16[384,768]{1,0:T(8,128)(2,1)} %shard_map.67.refs_0_), channel_id=1, source_target_pairs={{0,20},{1,21},{2,22},{3,23},{4,16},{5,17},{6,18},{7,19},{16,4},{17... | collective-permute-start | bytes 1769480 | tf_op jit(solution)/shard_map/ppermute | solution.py:278
  40.9 52.8 %collective-permute-start.23 = (bf16[384,3072]{1,0:T(8,128)(2,1)S(1)}, bf16[384,3072]{1,0:T(8,128)(2,1)}, u32[]{:S(2)}, u32[]{:S(2)}) collective-permute-start(bf16[384,3072]{1,0:T(8,128)(2,1)S(1)} %copy-done), channel_id=1, source_target_pairs={{0,20},{1,21},{2,22},{3,23},{4,16},{5,17},{6,18},{7,19},{16,4},{17... | collective-permute-start | bytes 7077896 | tf_op jit(solution)/shard_map/ppermute | solution.py:278
  43.8 3.8 %collective-permute-start.2 = (bf16[384,768]{1,0:T(8,128)(2,1)}, bf16[384,768]{1,0:T(8,128)(2,1)S(1)}, u32[]{:S(2)}, u32[]{:S(2)}) collective-permute-start(bf16[384,768]{1,0:T(8,128)(2,1)} %shard_map.67.refs_0_), channel_id=1, source_target_pairs={{0,8},{8,0},{1,9},{9,1},{2,10},{10,2},{3,11},{11,3},{4,12},{12,4},... | collective-permute-start | bytes 1769480 | tf_op jit(solution)/shard_map/ppermute | solution.py:274
  43.8 6.0 %collective-permute-start.4 = (bf16[384,768]{1,0:T(8,128)(2,1)S(1)}, bf16[384,768]{1,0:T(8,128)(2,1)S(1)}, u32[]{:S(2)}, u32[]{:S(2)}) collective-permute-start(bf16[384,768]{1,0:T(8,128)(2,1)S(1)} %collective-permute-done.3.refs_2_), channel_id=1, source_target_pairs={{0,8},{8,0},{1,9},{9,1},{2,10},{10,2},{3,11},{11,3},{4,12},{12,4},... | collective-permute-start | bytes 1769480 | tf_op jit(solution)/shard_map/ppermute | solution.py:274
  44.3 20.5 %collective-permute-start.7 = (bf16[256,1536]{1,0:T(8,128)(2,1)S(1)}, bf16[256,1536]{1,0:T(8,128)(2,1)}, u32[]{:S(2)}, u32[]{:S(2)}) collective-permute-start(bf16[256,1536]{1,0:T(8,128)(2,1)S(1)} %copy-done.2), channel_id=1, source_target_pairs={{0,4},{1,5},{2,6},{3,7},{4,0},{5,1},{6,2},{7,3},{8,12},{9,13},{10,... | collective-permute-start | bytes 2359304 | tf_op jit(solution)/shard_map/ppermute | solution.py:270
  45.4 19.5 %collective-permute-start.5 = (bf16[128,1536]{1,0:T(8,128)(2,1)S(1)}, bf16[128,1536]{1,0:T(8,128)(2,1)S(1)}, u32[]{:S(2)}, u32[]{:S(2)}) collective-permute-start(bf16[128,1536]{1,0:T(8,128)(2,1)S(1)} %slice.12), channel_id=1, source_target_pairs={{0,1},{1,2},{2,3},{3,0},{4,5},{5,6},{6,7},{7,4},{8,9},{9,10},{10,1... | collective-permute-start | bytes 1179656 | tf_op jit(solution)/shard_map/ppermute | solution.py:270
  47.7 17.2 %collective-permute-start.6 = (bf16[128,1536]{1,0:T(8,128)(2,1)S(1)}, bf16[128,1536]{1,0:T(8,128)(2,1)}, u32[]{:S(2)}, u32[]{:S(2)}) collective-permute-start(bf16[128,1536]{1,0:T(8,128)(2,1)S(1)} %slice.13), channel_id=1, source_target_pairs={{0,3},{1,0},{2,1},{3,2},{4,7},{5,4},{6,5},{7,6},{8,11},{9,8},{10,9... | collective-permute-start | bytes 1179656 | tf_op jit(solution)/shard_map/ppermute | solution.py:270
  56.9 36.8 %collective-permute-start.8 = (bf16[768,384]{1,0:T(8,128)(2,1)}, bf16[768,384]{1,0:T(8,128)(2,1)}, u32[]{:S(2)}, u32[]{:S(2)}) collective-permute-start(bf16[768,384]{1,0:T(8,128)(2,1)} %get-tuple-element.53), channel_id=1, source_target_pairs={{0,4},{1,5},{2,6},{3,7},{4,0},{5,1},{6,2},{7,3},{8,12},{9,13},{10,... | collective-permute-start | bytes 1769480 | tf_op jit(solution)/shard_map/ppermute | solution.py:270
  64.8 28.9 %all-to-all-start = ((bf16[8,256,128]{2,1,0:T(8,128)(2,1)}), bf16[8,256,128]{2,1,0:T(8,128)(2,1)S(1)}, u32[]{:S(2)}, u32[]{:S(2)}) async-start(bf16[8,256,128]{2,1,0:T(8,128)(2,1)} %bitcast.27), calls=%async_computation | async-start | bytes 1048576 | tf_op jit(solution)/shard_map/all_to_all | solution.py:329
  72.5 13.7 %collective-permute-start.9 = (bf16[256,384]{1,0:T(8,128)(2,1)}, bf16[256,384]{1,0:T(8,128)(2,1)S(1)}, u32[]{:S(2)}, u32[]{:S(2)}) collective-permute-start(bf16[256,384]{1,0:T(8,128)(2,1)} %get-tuple-element.54), channel_id=1, source_target_pairs={{0,4},{1,5},{2,6},{3,7},{4,0},{5,1},{6,2},{7,3},{8,12},{9,13},{10,... | collective-permute-start | bytes 589832 | tf_op jit(solution)/shard_map/ppermute | solution.py:270
  74.5 126.7 %collective-permute-start.22 = (bf16[384,3072]{1,0:T(8,128)(2,1)S(1)}, bf16[384,3072]{1,0:T(8,128)(2,1)}, u32[]{:S(2)}, u32[]{:S(2)}) collective-permute-start(bf16[384,3072]{1,0:T(8,128)(2,1)S(1)} %copy-done), channel_id=1, source_target_pairs={{0,8},{8,0},{1,9},{9,1},{2,10},{10,2},{3,11},{11,3},{4,12},{12,4},... | collective-permute-start | bytes 7077896 | tf_op jit(solution)/shard_map/ppermute | solution.py:274
  75.2 38.0 %collective-permute-start.10 = (bf16[256,1536]{1,0:T(8,128)(2,1)}, bf16[256,1536]{1,0:T(8,128)(2,1)}, u32[]{:S(2)}, u32[]{:S(2)}) collective-permute-start(bf16[256,1536]{1,0:T(8,128)(2,1)} %collective-permute-done.7.refs_5_), channel_id=1, source_target_pairs={{0,1},{1,2},{2,3},{3,0},{4,5},{5,6},{6,7},{7,4},{8,9},{9,10},{10,1... | collective-permute-start | bytes 2359304 | tf_op jit(solution)/shard_map/ppermute | solution.py:270
  86.2 26.9 %collective-permute-start.11 = (bf16[256,1536]{1,0:T(8,128)(2,1)}, bf16[256,1536]{1,0:T(8,128)(2,1)}, u32[]{:S(2)}, u32[]{:S(2)}) collective-permute-start(bf16[256,1536]{1,0:T(8,128)(2,1)} %collective-permute-done.7.refs_5_), channel_id=1, source_target_pairs={{0,3},{1,0},{2,1},{3,2},{4,7},{5,4},{6,5},{7,6},{8,11},{9,8},{10,9... | collective-permute-start | bytes 2359304 | tf_op jit(solution)/shard_map/ppermute | solution.py:270
  93.7 107.5 %collective-permute-start.24 = (bf16[384,3072]{1,0:T(8,128)(2,1)}, bf16[384,3072]{1,0:T(8,128)(2,1)}, u32[]{:S(2)}, u32[]{:S(2)}) collective-permute-start(bf16[384,3072]{1,0:T(8,128)(2,1)} %collective-permute-done.23.w2), channel_id=1, source_target_pairs={{0,8},{8,0},{1,9},{9,1},{2,10},{10,2},{3,11},{11,3},{4,12},{12,4},... | collective-permute-start | bytes 7077896 | tf_op jit(solution)/shard_map/ppermute | solution.py:274
  113.2 29.1 %all-to-all-start.1 = ((bf16[8,256,256]{2,1,0:T(8,128)(2,1)}), bf16[8,256,256]{2,1,0:T(8,128)(2,1)S(1)}, u32[]{:S(2)}, u32[]{:S(2)}) async-start(bf16[8,256,256]{2,1,0:T(8,128)(2,1)} %bitcast.32), calls=%async_computation.1 | async-start | bytes 2097152 | tf_op jit(solution)/shard_map/all_to_all | solution.py:355
  118.6 28.2 %collective-permute-start.12 = (bf16[128,1536]{1,0:T(8,128)(2,1)}, bf16[128,1536]{1,0:T(8,128)(2,1)}, u32[]{:S(2)}, u32[]{:S(2)}) collective-permute-start(bf16[128,1536]{1,0:T(8,128)(2,1)} %slice.14), channel_id=1, source_target_pairs={{0,1},{1,2},{2,3},{3,0},{4,5},{5,6},{6,7},{7,4},{8,9},{9,10},{10,1... | collective-permute-start | bytes 1179656 | tf_op jit(solution)/shard_map/ppermute | solution.py:270
  122.4 24.4 %collective-permute-start.13 = (bf16[128,1536]{1,0:T(8,128)(2,1)}, bf16[128,1536]{1,0:T(8,128)(2,1)}, u32[]{:S(2)}, u32[]{:S(2)}) collective-permute-start(bf16[128,1536]{1,0:T(8,128)(2,1)} %slice.15), channel_id=1, source_target_pairs={{0,3},{1,0},{2,1},{3,2},{4,7},{5,4},{6,5},{7,6},{8,11},{9,8},{10,9... | collective-permute-start | bytes 1179656 | tf_op jit(solution)/shard_map/ppermute | solution.py:270
  142.3 42.5 %all-to-all-start.2 = ((bf16[8,256,256]{2,1,0:T(8,128)(2,1)}), bf16[8,256,256]{2,1,0:T(8,128)(2,1)}, u32[]{:S(2)}, u32[]{:S(2)}) async-start(bf16[8,256,256]{2,1,0:T(8,128)(2,1)} %bitcast.31), calls=%async_computation.2 | async-start | bytes 2097152 | tf_op jit(solution)/shard_map/all_to_all | solution.py:355
  155.8 2.3 %collective-permute-start.14 = (bf16[768,384]{1,0:T(8,128)(2,1)}, bf16[768,384]{1,0:T(8,128)(2,1)S(1)}, u32[]{:S(2)}, u32[]{:S(2)}) collective-permute-start(bf16[768,384]{1,0:T(8,128)(2,1)} %get-tuple-element.63), channel_id=1, source_target_pairs={{0,8},{8,0},{1,9},{9,1},{2,10},{10,2},{3,11},{11,3},{4,12},{12,4},... | collective-permute-start | bytes 1769480 | tf_op jit(solution)/shard_map/ppermute | solution.py:274
  161.3 6.3 %collective-permute-start.15 = (bf16[96,384]{1,0:T(8,128)(2,1)}, bf16[96,384]{1,0:T(8,128)(2,1)S(1)}, u32[]{:S(2)}, u32[]{:S(2)}) collective-permute-start(bf16[96,384]{1,0:T(8,128)(2,1)} %get-tuple-element.64), channel_id=1, source_target_pairs={{0,16},{16,0},{32,48},{48,32},{64,80},{80,64},{96,112},{112,96},{1... | collective-permute-start | bytes 221192 | tf_op jit(solution)/shard_map/ppermute | solution.py:383
  164.8 5.8 %collective-permute-start.16 = (bf16[96,384]{1,0:T(8,128)(2,1)}, bf16[96,384]{1,0:T(8,128)(2,1)S(1)}, u32[]{:S(2)}, u32[]{:S(2)}) collective-permute-start(bf16[96,384]{1,0:T(8,128)(2,1)} %get-tuple-element.65), channel_id=1, source_target_pairs={{0,32},{16,48},{32,0},{48,16},{64,96},{80,112},{96,64},{112,80},{1... | collective-permute-start | bytes 221192 | tf_op jit(solution)/shard_map/ppermute | solution.py:383
  166.4 7.5 %collective-permute-start.17 = (bf16[96,384]{1,0:T(8,128)(2,1)}, bf16[96,384]{1,0:T(8,128)(2,1)S(1)}, u32[]{:S(2)}, u32[]{:S(2)}) collective-permute-start(bf16[96,384]{1,0:T(8,128)(2,1)} %get-tuple-element.66), channel_id=1, source_target_pairs={{0,48},{16,32},{32,16},{48,0},{64,112},{80,96},{96,80},{112,64},{1... | collective-permute-start | bytes 221192 | tf_op jit(solution)/shard_map/ppermute | solution.py:383
  167.6 17.2 %copy-start.9 = (bf16[96,384]{1,0:T(8,128)(2,1)}, bf16[96,384]{1,0:T(8,128)(2,1)S(1)}, u32[]{:S(2)}) copy-start(bf16[96,384]{1,0:T(8,128)(2,1)S(1)} %collective-permute-done.15.refs_0_) | copy-start | bytes 221188
  167.6 9.0 %collective-permute-start.18 = (bf16[96,384]{1,0:T(8,128)(2,1)}, bf16[96,384]{1,0:T(8,128)(2,1)S(1)}, u32[]{:S(2)}, u32[]{:S(2)}) collective-permute-start(bf16[96,384]{1,0:T(8,128)(2,1)} %get-tuple-element.67), channel_id=1, source_target_pairs={{0,64},{16,80},{32,96},{48,112},{64,0},{80,16},{96,32},{112,48},{1... | collective-permute-start | bytes 221192 | tf_op jit(solution)/shard_map/ppermute | solution.py:383
  170.6 14.2 %copy-start.10 = (bf16[96,384]{1,0:T(8,128)(2,1)}, bf16[96,384]{1,0:T(8,128)(2,1)S(1)}, u32[]{:S(2)}) copy-start(bf16[96,384]{1,0:T(8,128)(2,1)S(1)} %collective-permute-done.16.refs_1_) | copy-start | bytes 221188
  170.6 8.8 %collective-permute-start.19 = (bf16[96,384]{1,0:T(8,128)(2,1)}, bf16[96,384]{1,0:T(8,128)(2,1)S(1)}, u32[]{:S(2)}, u32[]{:S(2)}) collective-permute-start(bf16[96,384]{1,0:T(8,128)(2,1)} %get-tuple-element.68), channel_id=1, source_target_pairs={{0,80},{16,64},{32,112},{48,96},{64,16},{80,0},{96,48},{112,32},{1... | collective-permute-start | bytes 221192 | tf_op jit(solution)/shard_map/ppermute | solution.py:383
  173.9 7.1 %collective-permute-start.20 = (bf16[96,384]{1,0:T(8,128)(2,1)}, bf16[96,384]{1,0:T(8,128)(2,1)S(1)}, u32[]{:S(2)}, u32[]{:S(2)}) collective-permute-start(bf16[96,384]{1,0:T(8,128)(2,1)} %get-tuple-element.69), channel_id=1, source_target_pairs={{0,96},{16,112},{32,64},{48,80},{64,32},{80,48},{96,0},{112,16},{1... | collective-permute-start | bytes 221192 | tf_op jit(solution)/shard_map/ppermute | solution.py:383
  176.7 8.2 %collective-permute-start.21 = (bf16[96,384]{1,0:T(8,128)(2,1)}, bf16[96,384]{1,0:T(8,128)(2,1)S(1)}, u32[]{:S(2)}, u32[]{:S(2)}) collective-permute-start(bf16[96,384]{1,0:T(8,128)(2,1)} %get-tuple-element.70), channel_id=1, source_target_pairs={{0,112},{16,96},{32,80},{48,64},{64,48},{80,32},{96,16},{112,0},{1... | collective-permute-start | bytes 221192 | tf_op jit(solution)/shard_map/ppermute | solution.py:383
  (13 other events, 67.6 us)

commit v4 on v3

--- a/solution.py
+++ b/solution.py
@@ -34,49 +34,57 @@
     return centered * inv_std, inv_std
 
 
-def norm_kernel(x_ref, out_ref):
-    out_ref[...] = standardize(x_ref[...].astype(F32))[0].astype(BF)
-
-
-def columns_kernel(y_ref, w_ref, out_ref):
+def fetch(pairs, sems):
+    copies = [pltpu.make_async_copy(a, b, sems.at[i]) for i, (a, b) in enumerate(pairs)]
+    for copy in copies:
+        copy.start()
+    return copies
+
+
+def prepare_kernel(y_ref, x_ref, w_ref, normed_ref, columns_ref, held, sems):
+    pairs = []
     for z in range(2):
-        s = (z * 4 + y_ref[0]) * GW
-        q, k, v = (
-            w_ref[:, pl.ds(pl.multiple_of(kind * 1024 + s, GW), GW)].astype(F32) for kind in range(3)
-        )
+        for kind in range(3):
+            first = pl.multiple_of(kind * 1024 + (z * 4 + y_ref[0]) * GW, GW)
+            pairs.append((w_ref.at[:, pl.ds(first, GW)], held.at[z * 3 + kind]))
+    copies = fetch(pairs, sems)
+    normed_ref[...] = standardize(x_ref[...].astype(F32))[0].astype(BF)
+    for copy in copies:
+        copy.wait()
+    for z in range(2):
+        k, v = (held[z * 3 + kind].astype(F32) for kind in (1, 2))
         low = lax.broadcasted_iota(jnp.int32, k.shape, 1) < HD
         at = z * 384
-        out_ref[:, at : at + 128] = jnp.where(low, k, pltpu.roll(v, HD, 1)).astype(BF)
-        out_ref[:, at + 128 : at + 256] = jnp.where(low, pltpu.roll(k, HD, 1), v).astype(BF)
-        out_ref[:, at + 256 : at + 384] = q.astype(BF)
-
-
-def project_kernel(n, owner_ref, *refs):
-    weights, blocks, outs = refs[:4], refs[4 : 4 + n], refs[4 + n :]
-    for j in (1, 0):
-        cols = pl.ds(pl.multiple_of((owner_ref[4] ^ j) * 384, 384), 384)
-        first = 0
-        for block in blocks:
-            count = block.shape[0]
-            total = None
-            for f in range(4):
-                rows = pl.ds(pl.multiple_of(owner_ref[f] * 384, 384), 384)
-                t = dot(block[:, rows], weights[f][:, cols])
-                total = t if total is None else total + t
-            outs[j][first : first + count, :] = total.astype(BF)
-            first += count
+        columns_ref[:, at : at + 128] = jnp.where(low, k, pltpu.roll(v, HD, 1)).astype(BF)
+        columns_ref[:, at + 128 : at + 256] = jnp.where(low, pltpu.roll(k, HD, 1), v).astype(BF)
+        columns_ref[:, at + 256 : at + 384] = held[z * 3]
+
+
+def project_kernel(n, owner_ref, group_ref, *refs):
+    weights, blocks, out_ref = refs[:4], refs[4 : 4 + n], refs[4 + n]
+    cols = pl.ds(pl.multiple_of(group_ref[0] * 384, 384), 384)
+    first = 0
+    for block in blocks:
+        count = block.shape[0]
+        total = None
+        for f in range(4):
+            rows = pl.ds(pl.multiple_of(owner_ref[f] * 384, 384), 384)
+            t = dot(block[:, rows], weights[f][:, cols])
+            total = t if total is None else total + t
+        out_ref[first : first + count, :] = total.astype(BF)
+        first += count
 
 
 def attention_kernel(
-    head, pos_ref, len_ref, near_ref, far_ref, other_ref, last_ref, up_ref, out_ref, kv, ka, vt, kt, qt, ut, s_ref, e_ref, acc
+    head, pos_ref, len_ref, kept_ref, other_ref, last_ref, up_ref, out_ref, kv, ka, vt, kt, qt, ut, s_ref, e_ref, acc
 ):
     length = len_ref[0]
     hrows = slice(head * HD, (head + 1) * HD)
     lane = lax.broadcasted_iota(jnp.int32, (BQ, 128), 1)
     for b in range(SEQ):
         r = slice(b * BQ, (b + 1) * BQ)
-        source = (near_ref, far_ref, other_ref, last_ref)[b // 4 * 2 + (b % 4 == 3)]
-        own = slice(b % 4 % 3 * BQ, (b % 4 % 3 + 1) * BQ)
+        source = kept_ref if b < 4 else last_ref if b == 7 else other_ref
+        own = slice(b % 4 * BQ, (b % 4 + 1) * BQ) if b < 7 else slice(0, BQ)
         first = pl.multiple_of(pos_ref[b] * BQ, BQ)
         mine = source[own, head * 128 : (head + 1) * 128]
         kv[r, :] = mine
@@ -152,13 +160,6 @@
         out_ref[rows, 128:256] = acc[b * BQ : (b + 1) * BQ, :].astype(BF)
 
 
-def fetch(pairs, sems):
-    copies = [pltpu.make_async_copy(a, b, sems.at[i]) for i, (a, b) in enumerate(pairs)]
-    for copy in copies:
-        copy.start()
-    return copies
-
-
 def weight_gradient_kernel(pos_ref, first_ref, second_ref, *refs):
     sources, (keep_ref, send_ref, acc, held, sems) = refs[:-5], refs[-5:]
     at = [sum(b.shape[0] for b in sources[:i]) for i in range(len(sources))]
@@ -196,24 +197,6 @@
                     send_ref[r, :] = halves[k][i].astype(BF)
 
 
-def add_kernel(me_ref, keep_ref, got_ref, own_ref, *outs):
-    for d in range(8):
-        rows = pl.ds(pl.multiple_of((me_ref[0] ^ d) * 96, 96), 96)
-        t = keep_ref[rows, :] + got_ref[rows, :].astype(F32)
-        if d == 0:
-            own_ref[...] = t
-        else:
-            outs[d - 1][...] = t.astype(BF)
-
-
-def sum_kernel(own_ref, *refs):
-    t = own_ref[...]
-    for ref in refs[:-1]:
-        t = t + ref[...].astype(F32)
-    for s in range(SEQ):
-        refs[-1][s] = t[s * 12 : (s + 1) * 12]
-
-
 def join(first, second, part):
     low = lax.broadcasted_iota(jnp.int32, first.shape, first.ndim - 1) < HD
     if part == 0:
@@ -221,9 +204,20 @@
     return jnp.where(low, pltpu.roll(first, HD, first.ndim - 1), second)
 
 
+def add_kernel(keep_ref, got_ref, out_ref):
+    for i in range(64 // 8):
+        rows = slice(i * 96, (i + 1) * 96)
+        t = keep_ref[rows, :] + got_ref[rows, :].astype(F32)
+        for s in range(SEQ):
+            out_ref[i * SEQ + s] = t[s * 12 : (s + 1) * 12].astype(BF)
+
+
 def combine_kernel(parts_ref, out_ref):
     for s in range(SEQ):
-        total = parts_ref[s]
+        total = None
+        for r in range(8):
+            t = parts_ref[r * SEQ + s].astype(F32)
+            total = t if total is None else total + t
         at = s * GW
         low, high = total[:, 0:128], total[:, 128:256]
         out_ref[:, at : at + GW] = total[:, 256:384]
@@ -263,6 +257,7 @@
 ACROSS = [(i, i ^ 4) for i in range(8)]
 SWAP = [(f * 8 + s, (f ^ 1) * 8 + (s ^ 4)) for f in range(2) for s in range(8)]
 OFFSETS = [(dz, dy) for dz in range(2) for dy in (0, 3, 1, 2)]
+HEAD_FLOPS = (10**9, 10**10)
 tie = lax.optimization_barrier
 
 
@@ -298,45 +293,52 @@
     core = lax.axis_index("core")
     fsdp = lax.axis_index("zh") * 2 + core
     half = ROWS // 2
-    normed = call(norm_kernel, shape((ROWS, D)), [VM])(x)
-    mine = call(columns_kernel, shape((384, 768)), [SM, VM])(
-        (me % 4)[None].astype(jnp.int32), projection
-    )
+    normed, mine = call(
+        prepare_kernel,
+        (shape((ROWS, D)), shape((384, 768))),
+        [SM, VM, ANY],
+        scratch=[pltpu.VMEM((6, 384, GW), BF), pltpu.SemaphoreType.DMA((6,))],
+    )((me % 4)[None].astype(jnp.int32), x, projection)
     upstream = cotangent[0].reshape(ROWS, SEQ, GW).transpose(1, 0, 2)
     index = [(me // 4 ^ dz) * 4 + (me % 4 + dy) % 4 for dz, dy in OFFSETS]
     place = jnp.stack(index + [core]).astype(jnp.int32)
-    owners = jnp.stack([fsdp ^ i for i in range(4)] + [me // 4]).astype(jnp.int32)
+    owners = jnp.stack([fsdp ^ i for i in range(4)]).astype(jnp.int32)
 
     below, above, other = send(normed, UP), send(normed, DOWN), send(normed, ACROSS)
-    mine, upstream, place, owners, below, above = tie((mine, upstream, place, owners, below, above))
-    over = swap(mine)
-    columns = [mine, sibling(mine), over, sibling(over)]
+    over, beside = swap(mine), sibling(mine)
+    upstream, place, owners, below, above, other, over, beside = tie(
+        (upstream, place, owners, below, above, other, over, beside)
+    )
     far = [send(below[:half], UP), send(above[half:], DOWN)]
-
-    def project(rows):
+    columns = [mine, beside, over, sibling(over)]
+
+    def project(rows, group):
         count = sum(r.shape[0] for r in rows)
-        kept, sent = call(
+        return call(
             functools.partial(project_kernel, len(rows)),
-            (shape((count, 384)), shape((count, 384))),
-            [SM] + [VM] * (4 + len(rows)),
-            4 * count * D * 384,
-        )(owners, *columns, *rows)
-        return kept, send(sent, ACROSS)
-
-    near_kept, near_got = project([normed, below, above])
-    far, other, upstream = tie((far, other, upstream))
-    far_kept, far_got = project(far)
+            shape((count, 384)),
+            [SM, SM] + [VM] * (4 + len(rows)),
+            2 * count * D * 384,
+        )(owners, group, *columns, *rows)
+
+    here = (me // 4)[None].astype(jnp.int32)
+    near = project([normed, below, above], 1 - here)
+    _, far, other, upstream = tie((near, far, other, upstream))
+    near_got = send(near, ACROSS)
     upstream = lax.all_to_all(upstream, "seq", 0, 0, tiled=True).reshape(T, GW)
     other_below, other_above = send(other, UP), send(other, DOWN)
-    weight, columns[2] = tie((projection, over))
+    last = project(far, 1 - here)
+    last, far, weight = tie((last, far, projection))
+    far_got = send(last, ACROSS)
+    kept = project([normed, below, above, *far], here)
     weight_over = swap(weight)
 
     def attend(head):
         return call(
             functools.partial(attention_kernel, head),
             shape((T, 256)),
-            [SM, SM] + [VM] * 5,
-            20 * 2 * T * T * HD,
+            [SM, SM] + [VM] * 4,
+            HEAD_FLOPS[head],
             [
                 pltpu.VMEM((T, 128), BF),
                 pltpu.VMEM((T, 128), BF),
@@ -349,19 +351,21 @@
                 pltpu.VMEM((T, 128), F32),
             ],
             T * T,
-        )(place, lengths, near_kept, far_kept, near_got, far_got, upstream)
+        )(place, lengths, kept, near_got, far_got, upstream)
 
     def send_back(grads):
         return lax.all_to_all(grads.reshape(SEQ, ROWS, 256), "seq", 0, 0, tiled=True)
 
     first = attend(0)
-    first, other_below, other_above = tie((first, other_below, other_above))
+    first, other_below, other_above, weight = tie((first, other_below, other_above, weight))
     back0 = send_back(first)
     other_far = [send(other_below[:half], UP), send(other_above[half:], DOWN)]
-    weights = [projection, sibling(projection), weight_over, sibling(weight_over)]
+    beside = sibling(weight)
+    second = attend(1)
+    second, back0, weight_over, beside, other_far = tie(
+        (second, back0, weight_over, beside, other_far)
+    )
     blocks = [normed, below, above, *far, other, other_below, other_above, *other_far]
-    second = attend(1)
-    second, back0 = tie((second, back0))
     back1 = send_back(second)
     keep, out = call(
         weight_gradient_kernel,
@@ -375,18 +379,10 @@
         ],
     )(place, first, second, *blocks)
     got = sibling(out)
-    group = lax.axis_index("dp") * 2 + lax.axis_index("zh")
-    own, *outs = call(
-        add_kernel, (shape((96, 384), F32),) + (shape((96, 384)),) * 7, [SM, VM, VM]
-    )(group[None].astype(jnp.int32), keep, got)
-    outs = [
-        lax.ppermute(v, ("dp", "zh"), [(i, i ^ (d + 1)) for i in range(8)])
-        for d, v in enumerate(outs)
-    ]
-    outs, back1 = tie((outs, back1))
-    summed = call(sum_kernel, shape((SEQ, 12, 384), F32), [VM] * 8)(own, *outs)
-    summed = lax.all_to_all(summed, "seq", 0, 0, tiled=True)
-    projection_gradient = call(combine_kernel, shape((12, 3072), F32), [VM])(summed)
+    partial = call(add_kernel, shape((64, 12, 384)), [VM, VM])(keep, got)
+    partial, back1, weight_over = tie((partial, back1, weight_over))
+    weights = [projection, beside, weight_over, sibling(weight_over)]
+    partial = lax.all_to_all(partial, ("dp", "zh", "seq"), 0, 0, tiled=True)
     context, input_gradient = call(
         input_gradient_kernel,
         (shape((ROWS, 1024)), shape((ROWS, D), F32)),
@@ -398,6 +394,8 @@
             pltpu.SemaphoreType.DMA((4,)),
         ],
     )(owners, back0, back1, *weights, x)
+    partial, context, input_gradient = tie((partial, context, input_gradient))
+    projection_gradient = call(combine_kernel, shape((12, 3072), F32), [VM])(partial)
     return (context[None], input_gradient[None], projection_gradient)
 
 

time: 212 us -> 168 us (0.79)
  waiting for transfers between devices: 53.4 us -> 36 us
  blocking collectives: 12.1 us -> 0 us
  starting transfers between devices: 54.6 us -> 43 us
  local copies, waits for them, and re-layouts: 12.1 us -> 9.13 us
    ppermute x7 -> x0, starting transfers between devices: 16.9 us -> none  [body(): lax.ppermute(v, ('dp', 'zh'), [(i, i ^ d + 1) for i in range(8)])]
    ppermute x11, waiting for transfers between devices: 27 us -> 13.6 us  [send(): return lax.ppermute(v, 'seq', way)]
    all_to_all x1 -> x0, blocking collectives: 12.1 us -> none  [body(): summed = lax.all_to_all(summed, 'seq', 0, 0, tiled=True)]
    all_to_all x0 -> x1, starting transfers between devices: none -> 10.2 us  [body(): partial = lax.all_to_all(partial, ('dp', 'zh', 'seq'), 0, 0, tiled=True)]
    all_to_all x0 -> x1, waiting for transfers between devices: none -> 7.09 us  [body(): partial = lax.all_to_all(partial, ('dp', 'zh', 'seq'), 0, 0, tiled=True)]
    ppermute x7 -> x0, waiting for transfers between devices: 6.65 us -> none  [body(): lax.ppermute(v, ('dp', 'zh'), [(i, i ^ d + 1) for i in range(8)])]
    ppermute x2, waiting for transfers between devices: 17.5 us -> 11.3 us  [swap(): return lax.ppermute(v, ('zh', 'seq'), SWAP)]
    ppermute x11, starting transfers between devices: 18.1 us -> 15 us  [send(): return lax.ppermute(v, 'seq', way)]
  transfers between devices with their start and end apart: 28 -> 22, of which waited for: 9 -> 9; matrix products, arithmetic and copies ran while one was open for 4% -> 3% of each run, Pallas kernels for 31% -> 43%
where the time goes in v4:
time: 168 us; the launch traced here: 167 us
  Pallas kernels  76.7 us (46%)
  starting transfers between devices  43 us (26%)
  waiting for transfers between devices  36 us (21%)
  local copies, waits for them, and re-layouts  9.13 us (5%)
    pallas_call x2, Pallas kernels, attend(): call(functools.partial(attention_kernel, head), shape((T, 256)), [SM, SM]...  37.2 us
    ppermute x11, starting transfers between devices, send(): return lax.ppermute(v, 'seq', way)  15 us
    ppermute x11, waiting for transfers between devices, send(): return lax.ppermute(v, 'seq', way)  13.6 us
    pallas_call x3, Pallas kernels, project(): call(functools.partial(project_kernel, len(rows)), shape((count, 384)), [...  13.6 us
    ppermute x2, waiting for transfers between devices, swap(): return lax.ppermute(v, ('zh', 'seq'), SWAP)  11.3 us
    all_to_all x1, starting transfers between devices, body(): partial = lax.all_to_all(partial, ('dp', 'zh', 'seq'), 0, 0, tiled=True)  10.2 us
    pallas_call x1, Pallas kernels, body(): call(input_gradient_kernel, (shape((ROWS, 1024)), shape((ROWS, D), F32)),...  9.27 us
    all_to_all x2, starting transfers between devices, send_back(): lax.all_to_all(grads.reshape(SEQ, ROWS, 256), 'seq', 0, 0, tiled=True)  9.02 us
  transfers between devices with their start and end apart: 22, of which 9 were waited for; matrix products, arithmetic and copies ran while one was open for 3% of the time, Pallas kernels for 43%

profile of v4, /device:TPU:0, one launch (start us, length us, event | category | flops | bytes accessed | tf_op | source)
XLA Modules:
  0.0 167.0 jit_solution(8962530942953542323)
XLA Ops:
  0.6 3.4 %shard_map.67 = (bf16[256,1536]{1,0:T(8,128)(2,1)}, bf16[384,768]{1,0:T(8,128)(2,1)}) custom-call(s32[1]{0:T(128)} %bitcast.14.y_ref, bf16[256,1536]{1,0:T(8,128)(2,1)} %bitcast.27, bf16[384,3072]{1,0:T(8,128)(2,1)} %w0.1), custom_call_target="tpu_custom_call" | custom-call | bytes 1048576 | tf_op jit(solution)/shard_map/pallas_call | solution.py:296
  4.1 2.1 %collective-permute-start.2 = (bf16[256,1536]{1,0:T(8,128)(2,1)}, bf16[256,1536]{1,0:T(8,128)(2,1)}, u32[]{:S(2)}, u32[]{:S(2)}) collective-permute-start(bf16[256,1536]{1,0:T(8,128)(2,1)} %get-tuple-element.41.refs_4_.refs_0_), channel_id=1, source_target_pairs={{0,4},{1,5},{2,6},{3,7},{4,0},{5,1},{6,2},{7,3},{8,12},{9,13},{10,... | collective-permute-start | bytes 2359304 | tf_op jit(solution)/shard_map/ppermute | solution.py:265
  6.2 3.0 %collective-permute-start.1 = (bf16[256,1536]{1,0:T(8,128)(2,1)}, bf16[256,1536]{1,0:T(8,128)(2,1)S(1)}, u32[]{:S(2)}, u32[]{:S(2)}) collective-permute-start(bf16[256,1536]{1,0:T(8,128)(2,1)} %get-tuple-element.41.refs_4_.refs_0_), channel_id=1, source_target_pairs={{0,3},{1,0},{2,1},{3,2},{4,7},{5,4},{6,5},{7,6},{8,11},{9,8},{10,9... | collective-permute-start | bytes 2359304 | tf_op jit(solution)/shard_map/ppermute | solution.py:265
  9.2 2.5 %collective-permute-start.3 = (bf16[384,768]{1,0:T(8,128)(2,1)}, bf16[384,768]{1,0:T(8,128)(2,1)S(1)}, u32[]{:S(2)}, u32[]{:S(2)}) collective-permute-start(bf16[384,768]{1,0:T(8,128)(2,1)} %get-tuple-element.42.refs_0_), channel_id=1, source_target_pairs={{0,20},{1,21},{2,22},{3,23},{4,16},{5,17},{6,18},{7,19},{16,4},{17... | collective-permute-start | bytes 1769480 | tf_op jit(solution)/shard_map/ppermute | solution.py:273
  11.7 1.1 copy.8
  15.1 11.3 %collective-permute-done.3.refs_2_ = bf16[384,768]{1,0:T(8,128)(2,1)S(1)} collective-permute-done((bf16[384,768]{1,0:T(8,128)(2,1)}, bf16[384,768]{1,0:T(8,128)(2,1)S(1)}, u32[]{:S(2)}, u32[]{:S(2)}) %collective-permute-start.3) | collective-permute-done | bytes 589856 | tf_op jit(solution)/shard_map/ppermute | solution.py:273
  26.4 3.0 %collective-permute-done.refs_5_.refs_1_ = bf16[256,1536]{1,0:T(8,128)(2,1)S(1)} collective-permute-done((bf16[256,1536]{1,0:T(8,128)(2,1)}, bf16[256,1536]{1,0:T(8,128)(2,1)S(1)}, u32[]{:S(2)}, u32[]{:S(2)}) %collective-permute-start) | collective-permute-done | bytes 786464 | tf_op jit(solution)/shard_map/ppermute | solution.py:265
  29.9 1.6 collective-permute-start.6
  32.4 4.8 %shard_map.68 = bf16[768,384]{1,0:T(8,128)(2,1)} custom-call(s32[4]{0:T(128)} %pad_add_fusion.owner_ref.pos_ref, s32[1]{0:T(128)S(6)} %sub.17.group_ref, bf16[384,768]{1,0:T(8,128)(2,1)} %get-tuple-element.42.refs_0_, bf16[384,768]{1,0:T(8,128)(2,1)} %copy-done.1, bf16[384,768]{1,0:T(8,128)(2,1)} %copy-done.2, bf16[384,768]{1,0:T(8,128)(2,1)} %copy-done.3, ...), custom_call_target="tpu_custom_call" | custom-call | flops 905969664 | bytes 1048576 | tf_op jit(solution)/shard_map/pallas_call | solution.py:317
  37.2 3.9 %collective-permute-done.7.refs_5_.refs_8_.refs_4_ = bf16[128,1536]{1,0:T(8,128)(2,1)} collective-permute-done((bf16[128,1536]{1,0:T(8,128)(2,1)S(1)}, bf16[128,1536]{1,0:T(8,128)(2,1)}, u32[]{:S(2)}, u32[]{:S(2)}) %collective-permute-start.7) | collective-permute-done | bytes 393248 | tf_op jit(solution)/shard_map/ppermute | solution.py:265
  41.1 1.3 collective-permute-done.6.refs_4_.refs_7_.refs_3_
  42.7 1.7 %collective-permute-start.10 = (bf16[256,1536]{1,0:T(8,128)(2,1)}, bf16[256,1536]{1,0:T(8,128)(2,1)}, u32[]{:S(2)}, u32[]{:S(2)}) collective-permute-start(bf16[256,1536]{1,0:T(8,128)(2,1)} %collective-permute-done.2.refs_5_), channel_id=1, source_target_pairs={{0,1},{1,2},{2,3},{3,0},{4,5},{5,6},{6,7},{7,4},{8,9},{9,10},{10,1... | collective-permute-start | bytes 2359304 | tf_op jit(solution)/shard_map/ppermute | solution.py:265
  45.0 3.6 %all-to-all-start = ((bf16[8,256,128]{2,1,0:T(8,128)(2,1)}), bf16[8,256,128]{2,1,0:T(8,128)(2,1)S(1)}, u32[]{:S(2)}, u32[]{:S(2)}) async-start(bf16[8,256,128]{2,1,0:T(8,128)(2,1)} %bitcast.29), calls=%async_computation | async-start | bytes 1048576 | tf_op jit(solution)/shard_map/all_to_all | solution.py:328
  48.7 3.2 %shard_map.69 = bf16[256,384]{1,0:T(8,128)(2,1)} custom-call(s32[4]{0:T(128)} %pad_add_fusion.owner_ref.pos_ref, s32[1]{0:T(128)S(6)} %sub.17.group_ref, bf16[384,768]{1,0:T(8,128)(2,1)} %get-tuple-element.42.refs_0_, bf16[384,768]{1,0:T(8,128)(2,1)} %copy-done.1, bf16[384,768]{1,0:T(8,128)(2,1)} %copy-done.2, bf16[384,768]{1,0:T(8,128)(2,1)} %copy-done.3, ...), custom_call_target="tpu_custom_call" | custom-call | flops 301989888 | bytes 1048576 | tf_op jit(solution)/shard_map/pallas_call | solution.py:317
  51.9 2.0 %collective-permute-start.9 = (bf16[256,384]{1,0:T(8,128)(2,1)}, bf16[256,384]{1,0:T(8,128)(2,1)}, u32[]{:S(2)}, u32[]{:S(2)}) collective-permute-start(bf16[256,384]{1,0:T(8,128)(2,1)} %shard_map.69), channel_id=1, source_target_pairs={{0,4},{1,5},{2,6},{3,7},{4,0},{5,1},{6,2},{7,3},{8,12},{9,13},{10,... | collective-permute-start | bytes 589832 | tf_op jit(solution)/shard_map/ppermute | solution.py:265
  54.5 2.4 %collective-permute-start.12 = (bf16[384,3072]{1,0:T(8,128)(2,1)S(1)}, bf16[384,3072]{1,0:T(8,128)(2,1)}, u32[]{:S(2)}, u32[]{:S(2)}) collective-permute-start(bf16[384,3072]{1,0:T(8,128)(2,1)S(1)} %copy-done), channel_id=1, source_target_pairs={{0,20},{1,21},{2,22},{3,23},{4,16},{5,17},{6,18},{7,19},{16,4},{17... | collective-permute-start | bytes 7077896 | tf_op jit(solution)/shard_map/ppermute | solution.py:273
  56.9 5.6 %shard_map.70.kept_ref = bf16[1024,384]{1,0:T(8,128)(2,1)} custom-call(s32[4]{0:T(128)} %pad_add_fusion.owner_ref.pos_ref, s32[1]{0:T(128)} %bitcast.16.group_ref, bf16[384,768]{1,0:T(8,128)(2,1)} %get-tuple-element.42.refs_0_, bf16[384,768]{1,0:T(8,128)(2,1)} %copy-done.1, bf16[384,768]{1,0:T(8,128)(2,1)} %copy-done.2, bf16[384,768]{1,0:T(8,128)(2,1)} %copy-done.3, ...), custom_call_target="tpu_custom_call" | custom-call | flops 1207959552 | bytes 1048576 | tf_op jit(solution)/shard_map/pallas_call | solution.py:317
  62.5 5.5 %collective-permute-done.9.last_ref = bf16[256,384]{1,0:T(8,128)(2,1)} collective-permute-done((bf16[256,384]{1,0:T(8,128)(2,1)}, bf16[256,384]{1,0:T(8,128)(2,1)}, u32[]{:S(2)}, u32[]{:S(2)}) %collective-permute-start.9) | collective-permute-done | bytes 196640 | tf_op jit(solution)/shard_map/ppermute | solution.py:265
  69.6 18.6 %shard_map.71.first_ref = bf16[2048,256]{1,0:T(8,128)(2,1)} custom-call(s32[9]{0:T(128)} %stack.54.pos_ref, s32[1]{0:T(128)S(6)} %copy.11.len_ref, bf16[1024,384]{1,0:T(8,128)(2,1)} %shard_map.70.kept_ref, bf16[768,384]{1,0:T(8,128)(2,1)} %copy-done.11, bf16[256,384]{1,0:T(8,128)(2,1)} %collective-permute-done.9.last_ref, bf16[2048,128]{1,0:T(8,128)(2,1)} %bitcast.34), custom_call_target="tpu_custom_call" | custom-call | flops 1000000000 | bytes 1048576 | tf_op jit(solution)/shard_map/pallas_call | solution.py:337
  88.3 3.6 %all-to-all-start.1 = ((bf16[8,256,256]{2,1,0:T(8,128)(2,1)}), bf16[8,256,256]{2,1,0:T(8,128)(2,1)S(1)}, u32[]{:S(2)}, u32[]{:S(2)}) async-start(bf16[8,256,256]{2,1,0:T(8,128)(2,1)} %bitcast.31), calls=%async_computation.1 | async-start | bytes 2097152 | tf_op jit(solution)/shard_map/all_to_all | solution.py:357
  93.0 1.0 slice.15
  94.0 3.2 %collective-permute-start.15 = (bf16[128,1536]{1,0:T(8,128)(2,1)S(1)}, bf16[128,1536]{1,0:T(8,128)(2,1)S(1)}, u32[]{:S(2)}, u32[]{:S(2)}) collective-permute-start(bf16[128,1536]{1,0:T(8,128)(2,1)S(1)} %slice.15), channel_id=1, source_target_pairs={{0,3},{1,0},{2,1},{3,2},{4,7},{5,4},{6,5},{7,6},{8,11},{9,8},{10,9... | collective-permute-start | bytes 1179656 | tf_op jit(solution)/shard_map/ppermute | solution.py:265
  97.2 18.6 %shard_map.72.second_ref = bf16[2048,256]{1,0:T(8,128)(2,1)} custom-call(s32[9]{0:T(128)} %stack.54.pos_ref, s32[1]{0:T(128)S(6)} %copy.11.len_ref, bf16[1024,384]{1,0:T(8,128)(2,1)} %shard_map.70.kept_ref, bf16[768,384]{1,0:T(8,128)(2,1)} %copy-done.11, bf16[256,384]{1,0:T(8,128)(2,1)} %collective-permute-done.9.last_ref, bf16[2048,128]{1,0:T(8,128)(2,1)} %bitcast.35), custom_call_target="tpu_custom_call" | custom-call | flops 10000000000 | bytes 1048576 | tf_op jit(solution)/shard_map/pallas_call | solution.py:337
  116.6 5.5 %all-to-all-start.2 = ((bf16[8,256,256]{2,1,0:T(8,128)(2,1)}), bf16[8,256,256]{2,1,0:T(8,128)(2,1)S(1)}, u32[]{:S(2)}, u32[]{:S(2)}) async-start(bf16[8,256,256]{2,1,0:T(8,128)(2,1)} %bitcast.32), calls=%async_computation.2 | async-start | bytes 2097152 | tf_op jit(solution)/shard_map/all_to_all | solution.py:357
  122.1 8.8 %shard_map.73 = (f32[768,384]{1,0:T(8,128)}, bf16[768,384]{1,0:T(8,128)(2,1)}) custom-call(s32[9]{0:T(128)} %stack.54.pos_ref, bf16[2048,256]{1,0:T(8,128)(2,1)} %shard_map.71.first_ref, bf16[2048,256]{1,0:T(8,128)(2,1)} %shard_map.72.second_ref, bf16[256,1536]{1,0:T(8,128)(2,1)} %get-tuple-element.41.refs_4_.refs_0_, bf16[256,1536]{1,0:T(8,128)(2,1)} %copy-done.5, ...), custom_call_target="tpu_custom_call" | custom-call | flops 2415919104 | bytes 1048576 | tf_op jit(solution)/shard_map/pallas_call | solution.py:370
  131.0 2.2 %collective-permute-done.16.got_ref = bf16[768,384]{1,0:T(8,128)(2,1)S(1)} collective-permute-done((bf16[768,384]{1,0:T(8,128)(2,1)}, bf16[768,384]{1,0:T(8,128)(2,1)S(1)}, u32[]{:S(2)}, u32[]{:S(2)}) %collective-permute-start.16) | collective-permute-done | bytes 589856 | tf_op jit(solution)/shard_map/ppermute | solution.py:269
  134.0 2.5 %shard_map.74 = bf16[64,12,384]{2,1,0:T(8,128)(2,1)} custom-call(f32[768,384]{1,0:T(8,128)} %get-tuple-element.66.keep_ref, bf16[768,384]{1,0:T(8,128)(2,1)} %copy-done.9), custom_call_target="tpu_custom_call" | custom-call | bytes 1048576 | tf_op jit(solution)/shard_map/pallas_call | solution.py:382
  136.4 1.1 all-to-all-done.2.second_ref
  137.6 10.2 %all-to-all-start.3 = ((bf16[64,12,384]{2,1,0:T(8,128)(2,1)}), bf16[64,12,384]{2,1,0:T(8,128)(2,1)S(1)}, u32[]{:S(2)}, u32[]{:S(2)}) async-start(bf16[64,12,384]{2,1,0:T(8,128)(2,1)} %shard_map.74), calls=%async_computation.3 | async-start | bytes 1572864 | tf_op jit(solution)/shard_map/all_to_all | solution.py:385
  147.8 9.3 %shard_map.75 = (bf16[256,1024]{1,0:T(8,128)(2,1)}, f32[256,1536]{1,0:T(8,128)}) custom-call(s32[4]{0:T(128)} %pad_add_fusion.owner_ref.pos_ref, bf16[8,256,256]{2,1,0:T(8,128)(2,1)} %copy-done.6, bf16[8,256,256]{2,1,0:T(8,128)(2,1)} %copy-done.7, bf16[384,3072]{1,0:T(8,128)(2,1)} %w0.1, bf16[384,3072]{1,0:T(8,128)(2,1)} %collective-permute-done.13.w1, ...), custom_call_target="tpu_custom_call" | custom-call | flops 2415919104 | bytes 1048576 | tf_op jit(solution)/shard_map/pallas_call | solution.py:386
  157.1 7.1 %all-to-all-done.3.parts_ref = bf16[64,12,384]{2,1,0:T(8,128)(2,1)S(1)} async-done(((bf16[64,12,384]{2,1,0:T(8,128)(2,1)}), bf16[64,12,384]{2,1,0:T(8,128)(2,1)S(1)}, u32[]{:S(2)}, u32[]{:S(2)}) %all-to-all-start.3) | async-done | bytes 589856 | tf_op jit(solution)/shard_map/all_to_all | solution.py:385
  165.1 1.9 %shard_map.76 = f32[12,3072]{1,0:T(8,128)} custom-call(bf16[64,12,384]{2,1,0:T(8,128)(2,1)} %copy-done.8), custom_call_target="tpu_custom_call" | custom-call | bytes 1048576 | tf_op jit(solution)/shard_map/pallas_call | solution.py:398
  (56 shorter events, 9.9 us)
Async XLA Ops:
  4.1 22.3 %collective-permute-start.2 = (bf16[256,1536]{1,0:T(8,128)(2,1)}, bf16[256,1536]{1,0:T(8,128)(2,1)}, u32[]{:S(2)}, u32[]{:S(2)}) collective-permute-start(bf16[256,1536]{1,0:T(8,128)(2,1)} %get-tuple-element.41.refs_4_.refs_0_), channel_id=1, source_target_pairs={{0,4},{1,5},{2,6},{3,7},{4,0},{5,1},{6,2},{7,3},{8,12},{9,13},{10,... | collective-permute-start | bytes 2359304 | tf_op jit(solution)/shard_map/ppermute | solution.py:265
  6.2 20.2 %collective-permute-start.1 = (bf16[256,1536]{1,0:T(8,128)(2,1)}, bf16[256,1536]{1,0:T(8,128)(2,1)S(1)}, u32[]{:S(2)}, u32[]{:S(2)}) collective-permute-start(bf16[256,1536]{1,0:T(8,128)(2,1)} %get-tuple-element.41.refs_4_.refs_0_), channel_id=1, source_target_pairs={{0,3},{1,0},{2,1},{3,2},{4,7},{5,4},{6,5},{7,6},{8,11},{9,8},{10,9... | collective-permute-start | bytes 2359304 | tf_op jit(solution)/shard_map/ppermute | solution.py:265
  9.2 20.1 %collective-permute-start = (bf16[256,1536]{1,0:T(8,128)(2,1)}, bf16[256,1536]{1,0:T(8,128)(2,1)S(1)}, u32[]{:S(2)}, u32[]{:S(2)}) collective-permute-start(bf16[256,1536]{1,0:T(8,128)(2,1)} %get-tuple-element.41.refs_4_.refs_0_), channel_id=1, source_target_pairs={{0,1},{1,2},{2,3},{3,0},{4,5},{5,6},{6,7},{7,4},{8,9},{9,10},{10,1... | collective-permute-start | bytes 2359304 | tf_op jit(solution)/shard_map/ppermute | solution.py:265
  9.2 5.9 %collective-permute-start.4 = (bf16[384,768]{1,0:T(8,128)(2,1)}, bf16[384,768]{1,0:T(8,128)(2,1)S(1)}, u32[]{:S(2)}, u32[]{:S(2)}) collective-permute-start(bf16[384,768]{1,0:T(8,128)(2,1)} %get-tuple-element.42.refs_0_), channel_id=1, source_target_pairs={{0,8},{8,0},{1,9},{9,1},{2,10},{10,2},{3,11},{11,3},{4,12},{12,4},... | collective-permute-start | bytes 1769480 | tf_op jit(solution)/shard_map/ppermute | solution.py:269
  9.2 17.2 %collective-permute-start.3 = (bf16[384,768]{1,0:T(8,128)(2,1)}, bf16[384,768]{1,0:T(8,128)(2,1)S(1)}, u32[]{:S(2)}, u32[]{:S(2)}) collective-permute-start(bf16[384,768]{1,0:T(8,128)(2,1)} %get-tuple-element.42.refs_0_), channel_id=1, source_target_pairs={{0,20},{1,21},{2,22},{3,23},{4,16},{5,17},{6,18},{7,19},{16,4},{17... | collective-permute-start | bytes 1769480 | tf_op jit(solution)/shard_map/ppermute | solution.py:273
  15.1 16.5 %copy-start.1 = (bf16[384,768]{1,0:T(8,128)(2,1)}, bf16[384,768]{1,0:T(8,128)(2,1)S(1)}, u32[]{:S(2)}) copy-start(bf16[384,768]{1,0:T(8,128)(2,1)S(1)} %collective-permute-done.4.refs_1_) | copy-start | bytes 1769476
  26.4 5.1 %copy-start.2 = (bf16[384,768]{1,0:T(8,128)(2,1)}, bf16[384,768]{1,0:T(8,128)(2,1)S(1)}, u32[]{:S(2)}) copy-start(bf16[384,768]{1,0:T(8,128)(2,1)S(1)} %collective-permute-done.3.refs_2_) | copy-start | bytes 1769476
  26.4 5.1 %copy-start.4 = (bf16[256,1536]{1,0:T(8,128)(2,1)}, bf16[256,1536]{1,0:T(8,128)(2,1)S(1)}, u32[]{:S(2)}) copy-start(bf16[256,1536]{1,0:T(8,128)(2,1)S(1)} %collective-permute-done.1.refs_6_.refs_2_) | copy-start | bytes 2359300
  29.3 2.2 %copy-start.5 = (bf16[256,1536]{1,0:T(8,128)(2,1)}, bf16[256,1536]{1,0:T(8,128)(2,1)S(1)}, u32[]{:S(2)}) copy-start(bf16[256,1536]{1,0:T(8,128)(2,1)S(1)} %collective-permute-done.refs_5_.refs_1_) | copy-start | bytes 2359300
  29.3 2.2 %collective-permute-start.5 = (bf16[384,768]{1,0:T(8,128)(2,1)S(1)}, bf16[384,768]{1,0:T(8,128)(2,1)S(1)}, u32[]{:S(2)}, u32[]{:S(2)}) collective-permute-start(bf16[384,768]{1,0:T(8,128)(2,1)S(1)} %collective-permute-done.3.refs_2_), channel_id=1, source_target_pairs={{0,8},{8,0},{1,9},{9,1},{2,10},{10,2},{3,11},{11,3},{4,12},{12,4},... | collective-permute-start | bytes 1769480 | tf_op jit(solution)/shard_map/ppermute | solution.py:269
  29.4 11.7 %collective-permute-start.7 = (bf16[128,1536]{1,0:T(8,128)(2,1)S(1)}, bf16[128,1536]{1,0:T(8,128)(2,1)}, u32[]{:S(2)}, u32[]{:S(2)}) collective-permute-start(bf16[128,1536]{1,0:T(8,128)(2,1)S(1)} %slice.13), channel_id=1, source_target_pairs={{0,3},{1,0},{2,1},{3,2},{4,7},{5,4},{6,5},{7,6},{8,11},{9,8},{10,9... | collective-permute-start | bytes 1179656 | tf_op jit(solution)/shard_map/ppermute | solution.py:265
  29.9 12.5 %collective-permute-start.6 = (bf16[128,1536]{1,0:T(8,128)(2,1)S(1)}, bf16[128,1536]{1,0:T(8,128)(2,1)}, u32[]{:S(2)}, u32[]{:S(2)}) collective-permute-start(bf16[128,1536]{1,0:T(8,128)(2,1)S(1)} %slice.12), channel_id=1, source_target_pairs={{0,1},{1,2},{2,3},{3,0},{4,5},{5,6},{6,7},{7,4},{8,9},{9,10},{10,1... | collective-permute-start | bytes 1179656 | tf_op jit(solution)/shard_map/ppermute | solution.py:265
  31.5 0.9 copy-start.3
  37.2 17.3 %copy-start = (bf16[384,3072]{1,0:T(8,128)(2,1)S(1)}, bf16[384,3072]{1,0:T(8,128)(2,1)}, u32[]{:S(2)}) copy-start(bf16[384,3072]{1,0:T(8,128)(2,1)} %w0.1) | copy-start | bytes 7077892
  42.4 45.8 %collective-permute-start.11 = (bf16[256,1536]{1,0:T(8,128)(2,1)}, bf16[256,1536]{1,0:T(8,128)(2,1)}, u32[]{:S(2)}, u32[]{:S(2)}) collective-permute-start(bf16[256,1536]{1,0:T(8,128)(2,1)} %collective-permute-done.2.refs_5_), channel_id=1, source_target_pairs={{0,3},{1,0},{2,1},{3,2},{4,7},{5,4},{6,5},{7,6},{8,11},{9,8},{10,9... | collective-permute-start | bytes 2359304 | tf_op jit(solution)/shard_map/ppermute | solution.py:265
  42.7 45.6 %collective-permute-start.10 = (bf16[256,1536]{1,0:T(8,128)(2,1)}, bf16[256,1536]{1,0:T(8,128)(2,1)}, u32[]{:S(2)}, u32[]{:S(2)}) collective-permute-start(bf16[256,1536]{1,0:T(8,128)(2,1)} %collective-permute-done.2.refs_5_), channel_id=1, source_target_pairs={{0,1},{1,2},{2,3},{3,0},{4,5},{5,6},{6,7},{7,4},{8,9},{9,10},{10,1... | collective-permute-start | bytes 2359304 | tf_op jit(solution)/shard_map/ppermute | solution.py:265
  44.4 24.2 %collective-permute-start.8 = (bf16[768,384]{1,0:T(8,128)(2,1)}, bf16[768,384]{1,0:T(8,128)(2,1)S(1)}, u32[]{:S(2)}, u32[]{:S(2)}) collective-permute-start(bf16[768,384]{1,0:T(8,128)(2,1)} %shard_map.68), channel_id=1, source_target_pairs={{0,4},{1,5},{2,6},{3,7},{4,0},{5,1},{6,2},{7,3},{8,12},{9,13},{10,... | collective-permute-start | bytes 1769480 | tf_op jit(solution)/shard_map/ppermute | solution.py:265
  45.0 23.6 %all-to-all-start = ((bf16[8,256,128]{2,1,0:T(8,128)(2,1)}), bf16[8,256,128]{2,1,0:T(8,128)(2,1)S(1)}, u32[]{:S(2)}, u32[]{:S(2)}) async-start(bf16[8,256,128]{2,1,0:T(8,128)(2,1)} %bitcast.29), calls=%async_computation | async-start | bytes 1048576 | tf_op jit(solution)/shard_map/all_to_all | solution.py:328
  51.9 16.1 %collective-permute-start.9 = (bf16[256,384]{1,0:T(8,128)(2,1)}, bf16[256,384]{1,0:T(8,128)(2,1)}, u32[]{:S(2)}, u32[]{:S(2)}) collective-permute-start(bf16[256,384]{1,0:T(8,128)(2,1)} %shard_map.69), channel_id=1, source_target_pairs={{0,4},{1,5},{2,6},{3,7},{4,0},{5,1},{6,2},{7,3},{8,12},{9,13},{10,... | collective-permute-start | bytes 589832 | tf_op jit(solution)/shard_map/ppermute | solution.py:265
  54.5 62.0 %collective-permute-start.12 = (bf16[384,3072]{1,0:T(8,128)(2,1)S(1)}, bf16[384,3072]{1,0:T(8,128)(2,1)}, u32[]{:S(2)}, u32[]{:S(2)}) collective-permute-start(bf16[384,3072]{1,0:T(8,128)(2,1)S(1)} %copy-done), channel_id=1, source_target_pairs={{0,20},{1,21},{2,22},{3,23},{4,16},{5,17},{6,18},{7,19},{16,4},{17... | collective-permute-start | bytes 7077896 | tf_op jit(solution)/shard_map/ppermute | solution.py:273
  68.6 1.0 copy-start.11
  88.3 28.3 %collective-permute-start.13 = (bf16[384,3072]{1,0:T(8,128)(2,1)S(1)}, bf16[384,3072]{1,0:T(8,128)(2,1)}, u32[]{:S(2)}, u32[]{:S(2)}) collective-permute-start(bf16[384,3072]{1,0:T(8,128)(2,1)S(1)} %copy-done), channel_id=1, source_target_pairs={{0,8},{8,0},{1,9},{9,1},{2,10},{10,2},{3,11},{11,3},{4,12},{12,4},... | collective-permute-start | bytes 7077896 | tf_op jit(solution)/shard_map/ppermute | solution.py:269
  88.3 28.2 %all-to-all-start.1 = ((bf16[8,256,256]{2,1,0:T(8,128)(2,1)}), bf16[8,256,256]{2,1,0:T(8,128)(2,1)S(1)}, u32[]{:S(2)}, u32[]{:S(2)}) async-start(bf16[8,256,256]{2,1,0:T(8,128)(2,1)} %bitcast.31), calls=%async_computation.1 | async-start | bytes 2097152 | tf_op jit(solution)/shard_map/all_to_all | solution.py:357
  94.0 21.8 %collective-permute-start.15 = (bf16[128,1536]{1,0:T(8,128)(2,1)S(1)}, bf16[128,1536]{1,0:T(8,128)(2,1)S(1)}, u32[]{:S(2)}, u32[]{:S(2)}) collective-permute-start(bf16[128,1536]{1,0:T(8,128)(2,1)S(1)} %slice.15), channel_id=1, source_target_pairs={{0,3},{1,0},{2,1},{3,2},{4,7},{5,4},{6,5},{7,6},{8,11},{9,8},{10,9... | collective-permute-start | bytes 1179656 | tf_op jit(solution)/shard_map/ppermute | solution.py:265
  97.2 19.4 %collective-permute-start.14 = (bf16[128,1536]{1,0:T(8,128)(2,1)S(1)}, bf16[128,1536]{1,0:T(8,128)(2,1)}, u32[]{:S(2)}, u32[]{:S(2)}) collective-permute-start(bf16[128,1536]{1,0:T(8,128)(2,1)S(1)} %slice.14), channel_id=1, source_target_pairs={{0,1},{1,2},{2,3},{3,0},{4,5},{5,6},{6,7},{7,4},{8,9},{9,10},{10,1... | collective-permute-start | bytes 1179656 | tf_op jit(solution)/shard_map/ppermute | solution.py:265
  116.6 14.3 %copy-start.6 = (bf16[8,256,256]{2,1,0:T(8,128)(2,1)}, bf16[8,256,256]{2,1,0:T(8,128)(2,1)S(1)}, u32[]{:S(2)}) copy-start(bf16[8,256,256]{2,1,0:T(8,128)(2,1)S(1)} %all-to-all-done.1.first_ref) | copy-start | bytes 3145732
  116.6 21.0 %all-to-all-start.2 = ((bf16[8,256,256]{2,1,0:T(8,128)(2,1)}), bf16[8,256,256]{2,1,0:T(8,128)(2,1)S(1)}, u32[]{:S(2)}, u32[]{:S(2)}) async-start(bf16[8,256,256]{2,1,0:T(8,128)(2,1)} %bitcast.32), calls=%async_computation.2 | async-start | bytes 2097152 | tf_op jit(solution)/shard_map/all_to_all | solution.py:357
  130.9 2.3 %collective-permute-start.16 = (bf16[768,384]{1,0:T(8,128)(2,1)}, bf16[768,384]{1,0:T(8,128)(2,1)S(1)}, u32[]{:S(2)}, u32[]{:S(2)}) collective-permute-start(bf16[768,384]{1,0:T(8,128)(2,1)} %get-tuple-element.67), channel_id=1, source_target_pairs={{0,8},{8,0},{1,9},{9,1},{2,10},{10,2},{3,11},{11,3},{4,12},{12,4},... | collective-permute-start | bytes 1769480 | tf_op jit(solution)/shard_map/ppermute | solution.py:269
  137.6 10.2 %copy-start.7 = (bf16[8,256,256]{2,1,0:T(8,128)(2,1)}, bf16[8,256,256]{2,1,0:T(8,128)(2,1)S(1)}, u32[]{:S(2)}) copy-start(bf16[8,256,256]{2,1,0:T(8,128)(2,1)S(1)} %all-to-all-done.2.second_ref) | copy-start | bytes 3145732
  137.6 10.2 %collective-permute-start.17 = (bf16[384,3072]{1,0:T(8,128)(2,1)}, bf16[384,3072]{1,0:T(8,128)(2,1)}, u32[]{:S(2)}, u32[]{:S(2)}) collective-permute-start(bf16[384,3072]{1,0:T(8,128)(2,1)} %collective-permute-done.12.w2), channel_id=1, source_target_pairs={{0,8},{8,0},{1,9},{9,1},{2,10},{10,2},{3,11},{11,3},{4,12},{12,4},... | collective-permute-start | bytes 7077896 | tf_op jit(solution)/shard_map/ppermute | solution.py:269
  137.6 26.6 %all-to-all-start.3 = ((bf16[64,12,384]{2,1,0:T(8,128)(2,1)}), bf16[64,12,384]{2,1,0:T(8,128)(2,1)S(1)}, u32[]{:S(2)}, u32[]{:S(2)}) async-start(bf16[64,12,384]{2,1,0:T(8,128)(2,1)} %shard_map.74), calls=%async_computation.3 | async-start | bytes 1572864 | tf_op jit(solution)/shard_map/all_to_all | solution.py:385
  164.2 0.9 copy-start.8
  (3 other events, 2.4 us)

commit v5 on v4

--- a/solution.py
+++ b/solution.py
@@ -61,30 +61,34 @@
 
 
 def project_kernel(n, owner_ref, group_ref, *refs):
-    weights, blocks, out_ref = refs[:4], refs[4 : 4 + n], refs[4 + n]
-    cols = pl.ds(pl.multiple_of(group_ref[0] * 384, 384), 384)
-    first = 0
-    for block in blocks:
-        count = block.shape[0]
-        total = None
-        for f in range(4):
-            rows = pl.ds(pl.multiple_of(owner_ref[f] * 384, 384), 384)
-            t = dot(block[:, rows], weights[f][:, cols])
-            total = t if total is None else total + t
-        out_ref[first : first + count, :] = total.astype(BF)
-        first += count
+    weights, blocks, outs = refs[:4], refs[4 : 4 + n], refs[4 + n :]
+    for j, out_ref in enumerate(outs):
+        cols = pl.ds(pl.multiple_of(group_ref[j] * 384, 384), 384)
+        first = 0
+        for block in blocks:
+            count = block.shape[0]
+            total = None
+            for f in range(4):
+                rows = pl.ds(pl.multiple_of(owner_ref[f] * 384, 384), 384)
+                t = dot(block[:, rows], weights[f][:, cols])
+                total = t if total is None else total + t
+            out_ref[first : first + count, :] = total.astype(BF)
+            first += count
 
 
 def attention_kernel(
-    head, pos_ref, len_ref, kept_ref, other_ref, last_ref, up_ref, out_ref, kv, ka, vt, kt, qt, ut, s_ref, e_ref, acc
+    head, pos_ref, len_ref, kept_ref, far_ref, other_ref, last_ref, up_ref, out_ref, kv, ka, vt, kt, qt, ut, s_ref, e_ref, acc
 ):
     length = len_ref[0]
     hrows = slice(head * HD, (head + 1) * HD)
     lane = lax.broadcasted_iota(jnp.int32, (BQ, 128), 1)
     for b in range(SEQ):
         r = slice(b * BQ, (b + 1) * BQ)
-        source = kept_ref if b < 4 else last_ref if b == 7 else other_ref
-        own = slice(b % 4 * BQ, (b % 4 + 1) * BQ) if b < 7 else slice(0, BQ)
+        source, at = (
+            (kept_ref, 0), (kept_ref, 1), (kept_ref, 2), (far_ref, 0),
+            (kept_ref, 3), (other_ref, 0), (other_ref, 1), (last_ref, 0),
+        )[b]
+        own = slice(at * BQ, (at + 1) * BQ)
         first = pl.multiple_of(pos_ref[b] * BQ, BQ)
         mine = source[own, head * 128 : (head + 1) * 128]
         kv[r, :] = mine
@@ -161,28 +165,21 @@
 
 
 def weight_gradient_kernel(pos_ref, first_ref, second_ref, *refs):
-    sources, (keep_ref, send_ref, acc, held, sems) = refs[:-5], refs[-5:]
+    sources, (keep_ref, send_ref, flipped_ref, held, sems) = refs[:-5], refs[-5:]
     at = [sum(b.shape[0] for b in sources[:i]) for i in range(len(sources))]
     spots = [pl.ds(a, b.shape[0]) for a, b in zip(at, sources)]
     copies = fetch([(b, held.at[spot]) for b, spot in zip(sources, spots)], sems)
-    for i, block in enumerate(sources):
-        count = block.shape[0]
-        first = pos_ref[at[i] // ROWS] * ROWS + at[i] % ROWS
-        rows = pl.ds(pl.multiple_of(first, 128), count)
+    for b in range(SEQ):
+        rows = pl.ds(pl.multiple_of(pos_ref[b] * ROWS, ROWS), ROWS)
+        cols = slice(b * ROWS, (b + 1) * ROWS)
         both = [g[rows, :].astype(F32).T.astype(BF) for g in (first_ref, second_ref)]
         parts = [g[128:256] for g in both] + [g[0:HD] for g in both]
-        flipped = jnp.concatenate(parts, axis=0)
-        copies[i].wait()
-        for c in range(3):
-            cs = slice(c * 512, (c + 1) * 512)
-            t = dot(flipped, held[at[i] : at[i] + count, cs])
-            if i == 0:
-                acc[:, cs] = t
-            else:
-                acc[:, cs] += t
+        flipped_ref[:, cols] = jnp.concatenate(parts, axis=0)
+    for copy in copies:
+        copy.wait()
     core = pos_ref[SEQ]
     for c in range(4):
-        flipped = acc[:, c * 384 : (c + 1) * 384].T
+        flipped = dot(flipped_ref[...], held[:, c * 384 : (c + 1) * 384]).T
         halves = [[flipped[i * 96 : (i + 1) * 96] for i in (k, k + 2)] for k in range(2)]
         for k in range(2):
             for i in range(2):
@@ -254,6 +251,7 @@
 
 UP = [(i, (i // 4) * 4 + (i % 4 + 1) % 4) for i in range(8)]
 DOWN = [(i, (i // 4) * 4 + (i % 4 + 3) % 4) for i in range(8)]
+FAR = [(i, (i // 4) * 4 + (i % 4 + 2) % 4) for i in range(8)]
 ACROSS = [(i, i ^ 4) for i in range(8)]
 SWAP = [(f * 8 + s, (f ^ 1) * 8 + (s ^ 4)) for f in range(2) for s in range(8)]
 OFFSETS = [(dz, dy) for dz in range(2) for dy in (0, 3, 1, 2)]
@@ -312,32 +310,34 @@
     far = [send(below[:half], UP), send(above[half:], DOWN)]
     columns = [mine, beside, over, sibling(over)]
 
-    def project(rows, group):
-        count = sum(r.shape[0] for r in rows)
+    def project(rows, groups, count):
+        height = sum(r.shape[0] for r in rows)
         return call(
             functools.partial(project_kernel, len(rows)),
-            shape((count, 384)),
+            (shape((height, 384)),) * count,
             [SM, SM] + [VM] * (4 + len(rows)),
-            2 * count * D * 384,
-        )(owners, group, *columns, *rows)
-
-    here = (me // 4)[None].astype(jnp.int32)
-    near = project([normed, below, above], 1 - here)
-    _, far, other, upstream = tie((near, far, other, upstream))
+        )(owners, groups, *columns, *rows)
+
+    here = me // 4
+    groups = jnp.stack([1 - here, here]).astype(jnp.int32)
+    (near,) = project([below, above], groups, 1)
     near_got = send(near, ACROSS)
+    _, upstream, turned = tie((near, upstream, groups[::-1]))
+    (kept,) = project([normed, below, above, other], turned, 1)
     upstream = lax.all_to_all(upstream, "seq", 0, 0, tiled=True).reshape(T, GW)
-    other_below, other_above = send(other, UP), send(other, DOWN)
-    last = project(far, 1 - here)
-    last, far, weight = tie((last, far, projection))
+    _, far = tie((kept, far))
+    last, far_kept = project(far, groups, 2)
     far_got = send(last, ACROSS)
-    kept = project([normed, below, above, *far], here)
+    _, weight, other_late = tie((last, projection, other))
+    other_below, other_above = send(other_late, UP), send(other_late, DOWN)
+    other_far = send(other_late, FAR)
     weight_over = swap(weight)
 
     def attend(head):
         return call(
             functools.partial(attention_kernel, head),
             shape((T, 256)),
-            [SM, SM] + [VM] * 4,
+            [SM, SM] + [VM] * 5,
             HEAD_FLOPS[head],
             [
                 pltpu.VMEM((T, 128), BF),
@@ -351,21 +351,20 @@
                 pltpu.VMEM((T, 128), F32),
             ],
             T * T,
-        )(place, lengths, kept, near_got, far_got, upstream)
+        )(place, lengths, kept, far_kept, near_got, far_got, upstream)
 
     def send_back(grads):
         return lax.all_to_all(grads.reshape(SEQ, ROWS, 256), "seq", 0, 0, tiled=True)
 
     first = attend(0)
-    first, other_below, other_above, weight = tie((first, other_below, other_above, weight))
+    first, weight = tie((first, weight))
     back0 = send_back(first)
-    other_far = [send(other_below[:half], UP), send(other_above[half:], DOWN)]
     beside = sibling(weight)
     second = attend(1)
-    second, back0, weight_over, beside, other_far = tie(
-        (second, back0, weight_over, beside, other_far)
+    second, back0, weight_over, beside, other_below, other_above, other_far = tie(
+        (second, back0, weight_over, beside, other_below, other_above, other_far)
     )
-    blocks = [normed, below, above, *far, other, other_below, other_above, *other_far]
+    blocks = [normed, below, above, *far, other, other_below, other_above, other_far]
     back1 = send_back(second)
     keep, out = call(
         weight_gradient_kernel,
@@ -373,7 +372,7 @@
         [SM, VM, VM] + [ANY] * len(blocks),
         2 * T * D * 384,
         [
-            pltpu.VMEM((384, D), F32),
+            pltpu.VMEM((384, T), BF),
             pltpu.VMEM((T, D), BF),
             pltpu.SemaphoreType.DMA((len(blocks),)),
         ],

time: 168 us -> 185 us (1.10)
  waiting for transfers between devices: 36 us -> 51 us
  starting transfers between devices: 43 us -> 45.6 us
  Pallas kernels: 76.7 us -> 78.6 us
    all_to_all x2, waiting for transfers between devices: 1.12 us -> 10.5 us  [send_back(): lax.all_to_all(grads.reshape(SEQ, ROWS, 256), 'seq', 0, 0, tiled=True)]
    ppermute x11 -> x10, waiting for transfers between devices: 13.6 us -> 18.8 us  [send(): return lax.ppermute(v, 'seq', way)]
    slice x2 -> x0, local copies, waits for them, and re-layouts: 2.05 us -> none  [body(): other_far = [send(other_below[:half], UP), send(other_above[half:], DOWN)]]
    ppermute x2, starting transfers between devices: 4.89 us -> 6.76 us  [swap(): return lax.ppermute(v, ('zh', 'seq'), SWAP)]
    unnamed x27 -> x31, local copies, waits for them, and re-layouts: 5.49 us -> 3.63 us
    ppermute x11 -> x10, starting transfers between devices: 15 us -> 14.2 us  [send(): return lax.ppermute(v, 'seq', way)]
  transfers between devices with their start and end apart: 22 -> 21, of which waited for: 9 -> 7; matrix products, arithmetic and copies ran while one was open for 3% -> 2% of each run, Pallas kernels for 43% -> 40%
where the time goes in v5:
time: 185 us
  Pallas kernels  78.6 us (42%)
  waiting for transfers between devices  51 us (28%)
  starting transfers between devices  45.6 us (25%)
  local copies, waits for them, and re-layouts  7.32 us (4%)
    pallas_call x2, Pallas kernels, attend(): call(functools.partial(attention_kernel, head), shape((T, 256)), [SM, SM]...  37.4 us
    ppermute x10, waiting for transfers between devices, send(): return lax.ppermute(v, 'seq', way)  18.8 us
    ppermute x10, starting transfers between devices, send(): return lax.ppermute(v, 'seq', way)  14.2 us
    pallas_call x3, Pallas kernels, project(): call(functools.partial(project_kernel, len(rows)), (shape((height, 384)),...  13.4 us
    ppermute x2, waiting for transfers between devices, swap(): return lax.ppermute(v, ('zh', 'seq'), SWAP)  12.4 us
    all_to_all x1, starting transfers between devices, body(): partial = lax.all_to_all(partial, ('dp', 'zh', 'seq'), 0, 0, tiled=True)  11.3 us
    pallas_call x1, Pallas kernels, body(): call(weight_gradient_kernel, (shape((768, 384), F32), shape((768, 384))),...  10.6 us
    all_to_all x2, waiting for transfers between devices, send_back(): lax.all_to_all(grads.reshape(SEQ, ROWS, 256), 'seq', 0, 0, tiled=True)  10.5 us
  transfers between devices with their start and end apart: 21, of which 7 were waited for; matrix products, arithmetic and copies ran while one was open for 2% of the time, Pallas kernels for 40%

profile of v5, /device:TPU:0, one launch (start us, length us, event | category | flops | bytes accessed | tf_op | source)
XLA Modules:
  0.0 184.8 jit_solution(14831128955327736270)
XLA Ops:
  0.7 3.5 %shard_map.67 = (bf16[256,1536]{1,0:T(8,128)(2,1)}, bf16[384,768]{1,0:T(8,128)(2,1)}) custom-call(s32[1]{0:T(128)} %bitcast.14.y_ref, bf16[256,1536]{1,0:T(8,128)(2,1)} %bitcast.28, bf16[384,3072]{1,0:T(8,128)(2,1)} %w0.1), custom_call_target="tpu_custom_call" | custom-call | bytes 1048576 | tf_op jit(solution)/shard_map/pallas_call | solution.py:294
  4.2 2.1 %collective-permute-start.2 = (bf16[256,1536]{1,0:T(8,128)(2,1)}, bf16[256,1536]{1,0:T(8,128)(2,1)}, u32[]{:S(2)}, u32[]{:S(2)}) collective-permute-start(bf16[256,1536]{1,0:T(8,128)(2,1)} %get-tuple-element.40.refs_4_.refs_0_), channel_id=1, source_target_pairs={{0,4},{1,5},{2,6},{3,7},{4,0},{5,1},{6,2},{7,3},{8,12},{9,13},{10,... | collective-permute-start | bytes 2359304 | tf_op jit(solution)/shard_map/ppermute | solution.py:263
  6.3 3.0 %collective-permute-start.1 = (bf16[256,1536]{1,0:T(8,128)(2,1)}, bf16[256,1536]{1,0:T(8,128)(2,1)S(1)}, u32[]{:S(2)}, u32[]{:S(2)}) collective-permute-start(bf16[256,1536]{1,0:T(8,128)(2,1)} %get-tuple-element.40.refs_4_.refs_0_), channel_id=1, source_target_pairs={{0,3},{1,0},{2,1},{3,2},{4,7},{5,4},{6,5},{7,6},{8,11},{9,8},{10,9... | collective-permute-start | bytes 2359304 | tf_op jit(solution)/shard_map/ppermute | solution.py:263
  9.3 2.5 %collective-permute-start.3 = (bf16[384,768]{1,0:T(8,128)(2,1)}, bf16[384,768]{1,0:T(8,128)(2,1)S(1)}, u32[]{:S(2)}, u32[]{:S(2)}) collective-permute-start(bf16[384,768]{1,0:T(8,128)(2,1)} %get-tuple-element.41.refs_0_), channel_id=1, source_target_pairs={{0,20},{1,21},{2,22},{3,23},{4,16},{5,17},{6,18},{7,19},{16,4},{17... | collective-permute-start | bytes 1769480 | tf_op jit(solution)/shard_map/ppermute | solution.py:271
  11.9 0.9 copy.10
  14.0 12.4 %collective-permute-done.3.refs_2_ = bf16[384,768]{1,0:T(8,128)(2,1)S(1)} collective-permute-done((bf16[384,768]{1,0:T(8,128)(2,1)}, bf16[384,768]{1,0:T(8,128)(2,1)S(1)}, u32[]{:S(2)}, u32[]{:S(2)}) %collective-permute-start.3) | collective-permute-done | bytes 589856 | tf_op jit(solution)/shard_map/ppermute | solution.py:271
  26.5 3.0 %collective-permute-done.refs_4_.refs_5_.refs_1_ = bf16[256,1536]{1,0:T(8,128)(2,1)S(1)} collective-permute-done((bf16[256,1536]{1,0:T(8,128)(2,1)}, bf16[256,1536]{1,0:T(8,128)(2,1)S(1)}, u32[]{:S(2)}, u32[]{:S(2)}) %collective-permute-start) | collective-permute-done | bytes 786464 | tf_op jit(solution)/shard_map/ppermute | solution.py:263
  31.6 1.5 collective-permute-start.6
  34.6 4.0 %shard_map.68 = bf16[512,384]{1,0:T(8,128)(2,1)} custom-call(s32[4]{0:T(128)} %pad_add_fusion.owner_ref.pos_ref, s32[2]{0:T(128)} %copy-done.12, bf16[384,768]{1,0:T(8,128)(2,1)} %get-tuple-element.41.refs_0_, bf16[384,768]{1,0:T(8,128)(2,1)} %copy-done.1, bf16[384,768]{1,0:T(8,128)(2,1)} %copy-done.2, bf16[384,768]{1,0:T(8,128)(2,1)} %copy-done.3, ...), custom_call_target="tpu_custom_call" | custom-call | bytes 1048576 | tf_op jit(solution)/shard_map/pallas_call | solution.py:315
  38.6 3.5 %all-to-all-start = ((bf16[8,256,128]{2,1,0:T(8,128)(2,1)}), bf16[8,256,128]{2,1,0:T(8,128)(2,1)S(1)}, u32[]{:S(2)}, u32[]{:S(2)}) async-start(bf16[8,256,128]{2,1,0:T(8,128)(2,1)} %bitcast.30), calls=%async_computation | async-start | bytes 1048576 | tf_op jit(solution)/shard_map/all_to_all | solution.py:327
  42.1 1.9 %collective-permute-start.8 = (bf16[512,384]{1,0:T(8,128)(2,1)}, bf16[512,384]{1,0:T(8,128)(2,1)S(1)}, u32[]{:S(2)}, u32[]{:S(2)}) collective-permute-start(bf16[512,384]{1,0:T(8,128)(2,1)} %shard_map.68), channel_id=1, source_target_pairs={{0,4},{1,5},{2,6},{3,7},{4,0},{5,1},{6,2},{7,3},{8,12},{9,13},{10,... | collective-permute-start | bytes 1179656 | tf_op jit(solution)/shard_map/ppermute | solution.py:263
  44.0 5.6 %shard_map.69.kept_ref = bf16[1024,384]{1,0:T(8,128)(2,1)} custom-call(s32[4]{0:T(128)} %pad_add_fusion.owner_ref.pos_ref, s32[2]{0:T(128)} %rev.3.group_ref, bf16[384,768]{1,0:T(8,128)(2,1)} %get-tuple-element.41.refs_0_, bf16[384,768]{1,0:T(8,128)(2,1)} %copy-done.1, bf16[384,768]{1,0:T(8,128)(2,1)} %copy-done.2, bf16[384,768]{1,0:T(8,128)(2,1)} %copy-done.3, ...), custom_call_target="tpu_custom_call" | custom-call | bytes 1048576 | tf_op jit(solution)/shard_map/pallas_call | solution.py:315
  49.6 3.9 %shard_map.70 = (bf16[256,384]{1,0:T(8,128)(2,1)}, bf16[256,384]{1,0:T(8,128)(2,1)}) custom-call(s32[4]{0:T(128)} %pad_add_fusion.owner_ref.pos_ref, s32[2]{0:T(128)} %copy-done.12, bf16[384,768]{1,0:T(8,128)(2,1)} %get-tuple-element.41.refs_0_, bf16[384,768]{1,0:T(8,128)(2,1)} %copy-done.1, bf16[384,768]{1,0:T(8,128)(2,1)} %copy-done.2, ...), custom_call_target="tpu_custom_call" | custom-call | bytes 1048576 | tf_op jit(solution)/shard_map/pallas_call | solution.py:315
  54.4 4.2 %collective-permute-start.10 = (bf16[384,3072]{1,0:T(8,128)(2,1)S(1)}, bf16[384,3072]{1,0:T(8,128)(2,1)}, u32[]{:S(2)}, u32[]{:S(2)}) collective-permute-start(bf16[384,3072]{1,0:T(8,128)(2,1)S(1)} %copy-done), channel_id=1, source_target_pairs={{0,20},{1,21},{2,22},{3,23},{4,16},{5,17},{6,18},{7,19},{16,4},{17... | collective-permute-start | bytes 7077896 | tf_op jit(solution)/shard_map/ppermute | solution.py:271
  58.6 4.4 %collective-permute-done.9.last_ref = bf16[256,384]{1,0:T(8,128)(2,1)S(1)} collective-permute-done((bf16[256,384]{1,0:T(8,128)(2,1)}, bf16[256,384]{1,0:T(8,128)(2,1)S(1)}, u32[]{:S(2)}, u32[]{:S(2)}) %collective-permute-start.9) | collective-permute-done | bytes 196640 | tf_op jit(solution)/shard_map/ppermute | solution.py:263
  64.0 18.7 %shard_map.71.first_ref = bf16[2048,256]{1,0:T(8,128)(2,1)} custom-call(s32[9]{0:T(128)} %stack.63.pos_ref, s32[1]{0:T(128)S(6)} %copy.11.len_ref, bf16[1024,384]{1,0:T(8,128)(2,1)} %shard_map.69.kept_ref, bf16[256,384]{1,0:T(8,128)(2,1)} %get-tuple-element.53.far_ref, bf16[512,384]{1,0:T(8,128)(2,1)} %copy-done.13, bf16[256,384]{1,0:T(8,128)(2,1)} %copy-done.14, ...), custom_call_target="tpu_custom_call" | custom-call | flops 1000000000 | bytes 1048576 | tf_op jit(solution)/shard_map/pallas_call | solution.py:337
  82.7 3.0 %collective-permute-start.14 = (bf16[256,1536]{1,0:T(8,128)(2,1)}, bf16[256,1536]{1,0:T(8,128)(2,1)}, u32[]{:S(2)}, u32[]{:S(2)}) collective-permute-start(bf16[256,1536]{1,0:T(8,128)(2,1)} %collective-permute-done.2.refs_7_.refs_5_), channel_id=1, source_target_pairs={{0,2},{1,3},{2,0},{3,1},{4,6},{5,7},{6,4},{7,5},{8,10},{9,11},{10,... | collective-permute-start | bytes 2359304 | tf_op jit(solution)/shard_map/ppermute | solution.py:263
  85.6 1.2 collective-permute-start.13
  86.8 0.8 collective-permute-start.12
  87.7 4.0 %all-to-all-start.1 = ((bf16[8,256,256]{2,1,0:T(8,128)(2,1)}), bf16[8,256,256]{2,1,0:T(8,128)(2,1)S(1)}, u32[]{:S(2)}, u32[]{:S(2)}) async-start(bf16[8,256,256]{2,1,0:T(8,128)(2,1)} %bitcast.32), calls=%async_computation.1 | async-start | bytes 2097152 | tf_op jit(solution)/shard_map/all_to_all | solution.py:357
  91.7 18.7 %shard_map.72.second_ref = bf16[2048,256]{1,0:T(8,128)(2,1)} custom-call(s32[9]{0:T(128)} %stack.63.pos_ref, s32[1]{0:T(128)S(6)} %copy.11.len_ref, bf16[1024,384]{1,0:T(8,128)(2,1)} %shard_map.69.kept_ref, bf16[256,384]{1,0:T(8,128)(2,1)} %get-tuple-element.53.far_ref, bf16[512,384]{1,0:T(8,128)(2,1)} %copy-done.13, bf16[256,384]{1,0:T(8,128)(2,1)} %copy-done.14, ...), custom_call_target="tpu_custom_call" | custom-call | flops 10000000000 | bytes 1048576 | tf_op jit(solution)/shard_map/pallas_call | solution.py:337
  110.4 11.4 %collective-permute-done.13.refs_7_ = bf16[256,1536]{1,0:T(8,128)(2,1)} collective-permute-done((bf16[256,1536]{1,0:T(8,128)(2,1)}, bf16[256,1536]{1,0:T(8,128)(2,1)}, u32[]{:S(2)}, u32[]{:S(2)}) %collective-permute-start.13) | collective-permute-done | bytes 786464 | tf_op jit(solution)/shard_map/ppermute | solution.py:263
  121.8 10.5 %all-to-all-done.1.first_ref = bf16[8,256,256]{2,1,0:T(8,128)(2,1)S(1)} async-done(((bf16[8,256,256]{2,1,0:T(8,128)(2,1)}), bf16[8,256,256]{2,1,0:T(8,128)(2,1)S(1)}, u32[]{:S(2)}, u32[]{:S(2)}) %all-to-all-start.1) | async-done | bytes 1048608 | tf_op jit(solution)/shard_map/all_to_all | solution.py:357
  132.3 5.6 %all-to-all-start.2 = ((bf16[8,256,256]{2,1,0:T(8,128)(2,1)}), bf16[8,256,256]{2,1,0:T(8,128)(2,1)S(1)}, u32[]{:S(2)}, u32[]{:S(2)}) async-start(bf16[8,256,256]{2,1,0:T(8,128)(2,1)} %bitcast.33), calls=%async_computation.2 | async-start | bytes 2097152 | tf_op jit(solution)/shard_map/all_to_all | solution.py:357
  137.9 10.6 %shard_map.73 = (f32[768,384]{1,0:T(8,128)}, bf16[768,384]{1,0:T(8,128)(2,1)}) custom-call(s32[9]{0:T(128)} %stack.63.pos_ref, bf16[2048,256]{1,0:T(8,128)(2,1)} %shard_map.71.first_ref, bf16[2048,256]{1,0:T(8,128)(2,1)} %shard_map.72.second_ref, bf16[256,1536]{1,0:T(8,128)(2,1)} %get-tuple-element.40.refs_4_.refs_0_, bf16[256,1536]{1,0:T(8,128)(2,1)} %copy-done.5, ...), custom_call_target="tpu_custom_call" | custom-call | flops 2415919104 | bytes 1048576 | tf_op jit(solution)/shard_map/pallas_call | solution.py:369
  148.6 2.2 %collective-permute-done.15.got_ref = bf16[768,384]{1,0:T(8,128)(2,1)S(1)} collective-permute-done((bf16[768,384]{1,0:T(8,128)(2,1)}, bf16[768,384]{1,0:T(8,128)(2,1)S(1)}, u32[]{:S(2)}, u32[]{:S(2)}) %collective-permute-start.15) | collective-permute-done | bytes 589856 | tf_op jit(solution)/shard_map/ppermute | solution.py:267
  151.6 2.5 %shard_map.74 = bf16[64,12,384]{2,1,0:T(8,128)(2,1)} custom-call(f32[768,384]{1,0:T(8,128)} %get-tuple-element.64.keep_ref, bf16[768,384]{1,0:T(8,128)(2,1)} %copy-done.9), custom_call_target="tpu_custom_call" | custom-call | bytes 1048576 | tf_op jit(solution)/shard_map/pallas_call | solution.py:381
  154.2 11.3 %all-to-all-start.3 = ((bf16[64,12,384]{2,1,0:T(8,128)(2,1)}), bf16[64,12,384]{2,1,0:T(8,128)(2,1)S(1)}, u32[]{:S(2)}, u32[]{:S(2)}) async-start(bf16[64,12,384]{2,1,0:T(8,128)(2,1)} %shard_map.74), calls=%async_computation.3 | async-start | bytes 1572864 | tf_op jit(solution)/shard_map/all_to_all | solution.py:384
  165.5 9.3 %shard_map.75 = (bf16[256,1024]{1,0:T(8,128)(2,1)}, f32[256,1536]{1,0:T(8,128)}) custom-call(s32[4]{0:T(128)} %pad_add_fusion.owner_ref.pos_ref, bf16[8,256,256]{2,1,0:T(8,128)(2,1)} %copy-done.6, bf16[8,256,256]{2,1,0:T(8,128)(2,1)} %copy-done.7, bf16[384,3072]{1,0:T(8,128)(2,1)} %w0.1, bf16[384,3072]{1,0:T(8,128)(2,1)} %collective-permute-done.11.w1, ...), custom_call_target="tpu_custom_call" | custom-call | flops 2415919104 | bytes 1048576 | tf_op jit(solution)/shard_map/pallas_call | solution.py:385
  174.8 7.1 %all-to-all-done.3.parts_ref = bf16[64,12,384]{2,1,0:T(8,128)(2,1)S(1)} async-done(((bf16[64,12,384]{2,1,0:T(8,128)(2,1)}), bf16[64,12,384]{2,1,0:T(8,128)(2,1)S(1)}, u32[]{:S(2)}, u32[]{:S(2)}) %all-to-all-start.3) | async-done | bytes 589856 | tf_op jit(solution)/shard_map/all_to_all | solution.py:384
  181.9 0.9 copy-done.8
  182.8 1.9 %shard_map.76 = f32[12,3072]{1,0:T(8,128)} custom-call(bf16[64,12,384]{2,1,0:T(8,128)(2,1)} %copy-done.8), custom_call_target="tpu_custom_call" | custom-call | bytes 1048576 | tf_op jit(solution)/shard_map/pallas_call | solution.py:397
  (58 shorter events, 7.3 us)
Async XLA Ops:
  0.6 11.2 %copy-start.10 = (bf16[1,256,1024]{2,1,0:T(8,128)(2,1)S(1)}, bf16[1,256,1024]{2,1,0:T(8,128)(2,1)}, u32[]{:S(2)}) copy-start(bf16[1,256,1024]{2,1,0:T(8,128)(2,1)} %param.7) | copy-start | bytes 1572868
  4.2 22.3 %collective-permute-start.2 = (bf16[256,1536]{1,0:T(8,128)(2,1)}, bf16[256,1536]{1,0:T(8,128)(2,1)}, u32[]{:S(2)}, u32[]{:S(2)}) collective-permute-start(bf16[256,1536]{1,0:T(8,128)(2,1)} %get-tuple-element.40.refs_4_.refs_0_), channel_id=1, source_target_pairs={{0,4},{1,5},{2,6},{3,7},{4,0},{5,1},{6,2},{7,3},{8,12},{9,13},{10,... | collective-permute-start | bytes 2359304 | tf_op jit(solution)/shard_map/ppermute | solution.py:263
  6.3 20.2 %collective-permute-start.1 = (bf16[256,1536]{1,0:T(8,128)(2,1)}, bf16[256,1536]{1,0:T(8,128)(2,1)S(1)}, u32[]{:S(2)}, u32[]{:S(2)}) collective-permute-start(bf16[256,1536]{1,0:T(8,128)(2,1)} %get-tuple-element.40.refs_4_.refs_0_), channel_id=1, source_target_pairs={{0,3},{1,0},{2,1},{3,2},{4,7},{5,4},{6,5},{7,6},{8,11},{9,8},{10,9... | collective-permute-start | bytes 2359304 | tf_op jit(solution)/shard_map/ppermute | solution.py:263
  9.3 20.1 %collective-permute-start = (bf16[256,1536]{1,0:T(8,128)(2,1)}, bf16[256,1536]{1,0:T(8,128)(2,1)S(1)}, u32[]{:S(2)}, u32[]{:S(2)}) collective-permute-start(bf16[256,1536]{1,0:T(8,128)(2,1)} %get-tuple-element.40.refs_4_.refs_0_), channel_id=1, source_target_pairs={{0,1},{1,2},{2,3},{3,0},{4,5},{5,6},{6,7},{7,4},{8,9},{9,10},{10,1... | collective-permute-start | bytes 2359304 | tf_op jit(solution)/shard_map/ppermute | solution.py:263
  9.3 4.7 %collective-permute-start.4 = (bf16[384,768]{1,0:T(8,128)(2,1)}, bf16[384,768]{1,0:T(8,128)(2,1)S(1)}, u32[]{:S(2)}, u32[]{:S(2)}) collective-permute-start(bf16[384,768]{1,0:T(8,128)(2,1)} %get-tuple-element.41.refs_0_), channel_id=1, source_target_pairs={{0,8},{8,0},{1,9},{9,1},{2,10},{10,2},{3,11},{11,3},{4,12},{12,4},... | collective-permute-start | bytes 1769480 | tf_op jit(solution)/shard_map/ppermute | solution.py:267
  9.3 17.2 %collective-permute-start.3 = (bf16[384,768]{1,0:T(8,128)(2,1)}, bf16[384,768]{1,0:T(8,128)(2,1)S(1)}, u32[]{:S(2)}, u32[]{:S(2)}) collective-permute-start(bf16[384,768]{1,0:T(8,128)(2,1)} %get-tuple-element.41.refs_0_), channel_id=1, source_target_pairs={{0,20},{1,21},{2,22},{3,23},{4,16},{5,17},{6,18},{7,19},{16,4},{17... | collective-permute-start | bytes 1769480 | tf_op jit(solution)/shard_map/ppermute | solution.py:271
  14.0 19.8 %copy-start.1 = (bf16[384,768]{1,0:T(8,128)(2,1)}, bf16[384,768]{1,0:T(8,128)(2,1)S(1)}, u32[]{:S(2)}) copy-start(bf16[384,768]{1,0:T(8,128)(2,1)S(1)} %collective-permute-done.4.refs_1_) | copy-start | bytes 1769476
  26.4 7.3 %copy-start.2 = (bf16[384,768]{1,0:T(8,128)(2,1)}, bf16[384,768]{1,0:T(8,128)(2,1)S(1)}, u32[]{:S(2)}) copy-start(bf16[384,768]{1,0:T(8,128)(2,1)S(1)} %collective-permute-done.3.refs_2_) | copy-start | bytes 1769476
  26.5 7.3 %copy-start.4 = (bf16[256,1536]{1,0:T(8,128)(2,1)}, bf16[256,1536]{1,0:T(8,128)(2,1)S(1)}, u32[]{:S(2)}) copy-start(bf16[256,1536]{1,0:T(8,128)(2,1)S(1)} %collective-permute-done.1.refs_5_.refs_6_.refs_2_) | copy-start | bytes 2359300
  29.4 4.4 %copy-start.5 = (bf16[256,1536]{1,0:T(8,128)(2,1)}, bf16[256,1536]{1,0:T(8,128)(2,1)S(1)}, u32[]{:S(2)}) copy-start(bf16[256,1536]{1,0:T(8,128)(2,1)S(1)} %collective-permute-done.refs_4_.refs_5_.refs_1_) | copy-start | bytes 2359300
  29.4 4.3 %collective-permute-start.5 = (bf16[384,768]{1,0:T(8,128)(2,1)S(1)}, bf16[384,768]{1,0:T(8,128)(2,1)S(1)}, u32[]{:S(2)}, u32[]{:S(2)}) collective-permute-start(bf16[384,768]{1,0:T(8,128)(2,1)S(1)} %collective-permute-done.3.refs_2_), channel_id=1, source_target_pairs={{0,8},{8,0},{1,9},{9,1},{2,10},{10,2},{3,11},{11,3},{4,12},{12,4},... | collective-permute-start | bytes 1769480 | tf_op jit(solution)/shard_map/ppermute | solution.py:267
  31.1 18.5 %collective-permute-start.7 = (bf16[128,1536]{1,0:T(8,128)(2,1)}, bf16[128,1536]{1,0:T(8,128)(2,1)}, u32[]{:S(2)}, u32[]{:S(2)}) collective-permute-start(bf16[128,1536]{1,0:T(8,128)(2,1)} %slice.7), channel_id=1, source_target_pairs={{0,3},{1,0},{2,1},{3,2},{4,7},{5,4},{6,5},{7,6},{8,11},{9,8},{10,9... | collective-permute-start | bytes 1179656 | tf_op jit(solution)/shard_map/ppermute | solution.py:263
  31.6 18.0 %collective-permute-start.6 = (bf16[128,1536]{1,0:T(8,128)(2,1)}, bf16[128,1536]{1,0:T(8,128)(2,1)}, u32[]{:S(2)}, u32[]{:S(2)}) collective-permute-start(bf16[128,1536]{1,0:T(8,128)(2,1)} %slice.6), channel_id=1, source_target_pairs={{0,1},{1,2},{2,3},{3,0},{4,5},{5,6},{6,7},{7,4},{8,9},{9,10},{10,1... | collective-permute-start | bytes 1179656 | tf_op jit(solution)/shard_map/ppermute | solution.py:263
  33.8 0.8 copy-start.3
  38.6 24.4 %all-to-all-start = ((bf16[8,256,128]{2,1,0:T(8,128)(2,1)}), bf16[8,256,128]{2,1,0:T(8,128)(2,1)S(1)}, u32[]{:S(2)}, u32[]{:S(2)}) async-start(bf16[8,256,128]{2,1,0:T(8,128)(2,1)} %bitcast.30), calls=%async_computation | async-start | bytes 1048576 | tf_op jit(solution)/shard_map/all_to_all | solution.py:327
  42.1 20.9 %collective-permute-start.8 = (bf16[512,384]{1,0:T(8,128)(2,1)}, bf16[512,384]{1,0:T(8,128)(2,1)S(1)}, u32[]{:S(2)}, u32[]{:S(2)}) collective-permute-start(bf16[512,384]{1,0:T(8,128)(2,1)} %shard_map.68), channel_id=1, source_target_pairs={{0,4},{1,5},{2,6},{3,7},{4,0},{5,1},{6,2},{7,3},{8,12},{9,13},{10,... | collective-permute-start | bytes 1179656 | tf_op jit(solution)/shard_map/ppermute | solution.py:263
  49.6 4.8 %copy-start = (bf16[384,3072]{1,0:T(8,128)(2,1)S(1)}, bf16[384,3072]{1,0:T(8,128)(2,1)}, u32[]{:S(2)}) copy-start(bf16[384,3072]{1,0:T(8,128)(2,1)} %w0.1) | copy-start | bytes 7077892
  53.5 9.4 %collective-permute-start.9 = (bf16[256,384]{1,0:T(8,128)(2,1)}, bf16[256,384]{1,0:T(8,128)(2,1)S(1)}, u32[]{:S(2)}, u32[]{:S(2)}) collective-permute-start(bf16[256,384]{1,0:T(8,128)(2,1)} %get-tuple-element.54), channel_id=1, source_target_pairs={{0,4},{1,5},{2,6},{3,7},{4,0},{5,1},{6,2},{7,3},{8,12},{9,13},{10,... | collective-permute-start | bytes 589832 | tf_op jit(solution)/shard_map/ppermute | solution.py:263
  54.4 78.0 %collective-permute-start.10 = (bf16[384,3072]{1,0:T(8,128)(2,1)S(1)}, bf16[384,3072]{1,0:T(8,128)(2,1)}, u32[]{:S(2)}, u32[]{:S(2)}) collective-permute-start(bf16[384,3072]{1,0:T(8,128)(2,1)S(1)} %copy-done), channel_id=1, source_target_pairs={{0,20},{1,21},{2,22},{3,23},{4,16},{5,17},{6,18},{7,19},{16,4},{17... | collective-permute-start | bytes 7077896 | tf_op jit(solution)/shard_map/ppermute | solution.py:271
  63.0 1.0 copy-start.11
  82.7 49.7 %collective-permute-start.11 = (bf16[384,3072]{1,0:T(8,128)(2,1)S(1)}, bf16[384,3072]{1,0:T(8,128)(2,1)}, u32[]{:S(2)}, u32[]{:S(2)}) collective-permute-start(bf16[384,3072]{1,0:T(8,128)(2,1)S(1)} %copy-done), channel_id=1, source_target_pairs={{0,8},{8,0},{1,9},{9,1},{2,10},{10,2},{3,11},{11,3},{4,12},{12,4},... | collective-permute-start | bytes 7077896 | tf_op jit(solution)/shard_map/ppermute | solution.py:267
  82.7 27.7 %collective-permute-start.14 = (bf16[256,1536]{1,0:T(8,128)(2,1)}, bf16[256,1536]{1,0:T(8,128)(2,1)}, u32[]{:S(2)}, u32[]{:S(2)}) collective-permute-start(bf16[256,1536]{1,0:T(8,128)(2,1)} %collective-permute-done.2.refs_7_.refs_5_), channel_id=1, source_target_pairs={{0,2},{1,3},{2,0},{3,1},{4,6},{5,7},{6,4},{7,5},{8,10},{9,11},{10,... | collective-permute-start | bytes 2359304 | tf_op jit(solution)/shard_map/ppermute | solution.py:263
  85.6 36.1 %collective-permute-start.13 = (bf16[256,1536]{1,0:T(8,128)(2,1)}, bf16[256,1536]{1,0:T(8,128)(2,1)}, u32[]{:S(2)}, u32[]{:S(2)}) collective-permute-start(bf16[256,1536]{1,0:T(8,128)(2,1)} %collective-permute-done.2.refs_7_.refs_5_), channel_id=1, source_target_pairs={{0,3},{1,0},{2,1},{3,2},{4,7},{5,4},{6,5},{7,6},{8,11},{9,8},{10,9... | collective-permute-start | bytes 2359304 | tf_op jit(solution)/shard_map/ppermute | solution.py:263
  86.8 35.0 %collective-permute-start.12 = (bf16[256,1536]{1,0:T(8,128)(2,1)}, bf16[256,1536]{1,0:T(8,128)(2,1)}, u32[]{:S(2)}, u32[]{:S(2)}) collective-permute-start(bf16[256,1536]{1,0:T(8,128)(2,1)} %collective-permute-done.2.refs_7_.refs_5_), channel_id=1, source_target_pairs={{0,1},{1,2},{2,3},{3,0},{4,5},{5,6},{6,7},{7,4},{8,9},{9,10},{10,1... | collective-permute-start | bytes 2359304 | tf_op jit(solution)/shard_map/ppermute | solution.py:263
  87.7 44.7 %all-to-all-start.1 = ((bf16[8,256,256]{2,1,0:T(8,128)(2,1)}), bf16[8,256,256]{2,1,0:T(8,128)(2,1)S(1)}, u32[]{:S(2)}, u32[]{:S(2)}) async-start(bf16[8,256,256]{2,1,0:T(8,128)(2,1)} %bitcast.32), calls=%async_computation.1 | async-start | bytes 2097152 | tf_op jit(solution)/shard_map/all_to_all | solution.py:357
  132.3 16.2 %copy-start.6 = (bf16[8,256,256]{2,1,0:T(8,128)(2,1)}, bf16[8,256,256]{2,1,0:T(8,128)(2,1)S(1)}, u32[]{:S(2)}) copy-start(bf16[8,256,256]{2,1,0:T(8,128)(2,1)S(1)} %all-to-all-done.1.first_ref) | copy-start | bytes 3145732
  132.3 21.7 %all-to-all-start.2 = ((bf16[8,256,256]{2,1,0:T(8,128)(2,1)}), bf16[8,256,256]{2,1,0:T(8,128)(2,1)S(1)}, u32[]{:S(2)}, u32[]{:S(2)}) async-start(bf16[8,256,256]{2,1,0:T(8,128)(2,1)} %bitcast.33), calls=%async_computation.2 | async-start | bytes 2097152 | tf_op jit(solution)/shard_map/all_to_all | solution.py:357
  148.5 2.3 %collective-permute-start.15 = (bf16[768,384]{1,0:T(8,128)(2,1)}, bf16[768,384]{1,0:T(8,128)(2,1)S(1)}, u32[]{:S(2)}, u32[]{:S(2)}) collective-permute-start(bf16[768,384]{1,0:T(8,128)(2,1)} %get-tuple-element.65), channel_id=1, source_target_pairs={{0,8},{8,0},{1,9},{9,1},{2,10},{10,2},{3,11},{11,3},{4,12},{12,4},... | collective-permute-start | bytes 1769480 | tf_op jit(solution)/shard_map/ppermute | solution.py:267
  154.1 11.5 %copy-start.7 = (bf16[8,256,256]{2,1,0:T(8,128)(2,1)}, bf16[8,256,256]{2,1,0:T(8,128)(2,1)S(1)}, u32[]{:S(2)}) copy-start(bf16[8,256,256]{2,1,0:T(8,128)(2,1)S(1)} %all-to-all-done.2.second_ref) | copy-start | bytes 3145732
  154.1 11.5 %collective-permute-start.16 = (bf16[384,3072]{1,0:T(8,128)(2,1)}, bf16[384,3072]{1,0:T(8,128)(2,1)}, u32[]{:S(2)}, u32[]{:S(2)}) collective-permute-start(bf16[384,3072]{1,0:T(8,128)(2,1)} %collective-permute-done.10.w2), channel_id=1, source_target_pairs={{0,8},{8,0},{1,9},{9,1},{2,10},{10,2},{3,11},{11,3},{4,12},{12,4},... | collective-permute-start | bytes 7077896 | tf_op jit(solution)/shard_map/ppermute | solution.py:267
  154.2 27.7 %all-to-all-start.3 = ((bf16[64,12,384]{2,1,0:T(8,128)(2,1)}), bf16[64,12,384]{2,1,0:T(8,128)(2,1)S(1)}, u32[]{:S(2)}, u32[]{:S(2)}) async-start(bf16[64,12,384]{2,1,0:T(8,128)(2,1)} %shard_map.74), calls=%async_computation.3 | async-start | bytes 1572864 | tf_op jit(solution)/shard_map/all_to_all | solution.py:384
  181.9 0.9 copy-start.8
  (4 other events, 2.9 us)

commit v6 on v5

--- a/solution.py
+++ b/solution.py
@@ -165,7 +165,7 @@
 
 
 def weight_gradient_kernel(pos_ref, first_ref, second_ref, *refs):
-    sources, (keep_ref, send_ref, flipped_ref, held, sems) = refs[:-5], refs[-5:]
+    sources, (keep_ref, send_ref, flipped_ref, held, acc, sems) = refs[:-6], refs[-6:]
     at = [sum(b.shape[0] for b in sources[:i]) for i in range(len(sources))]
     spots = [pl.ds(a, b.shape[0]) for a, b in zip(at, sources)]
     copies = fetch([(b, held.at[spot]) for b, spot in zip(sources, spots)], sems)
@@ -175,11 +175,18 @@
         both = [g[rows, :].astype(F32).T.astype(BF) for g in (first_ref, second_ref)]
         parts = [g[128:256] for g in both] + [g[0:HD] for g in both]
         flipped_ref[:, cols] = jnp.concatenate(parts, axis=0)
-    for copy in copies:
-        copy.wait()
+    for half in range(2):
+        rows = slice(half * T // 2, (half + 1) * T // 2)
+        for i, copy in enumerate(copies):
+            if at[i] // (T // 2) == half:
+                copy.wait()
+        for c in range(3):
+            cs = slice(c * 512, (c + 1) * 512)
+            t = dot(flipped_ref[:, rows], held[rows, cs])
+            acc[:, cs] = t if half == 0 else acc[:, cs] + t
     core = pos_ref[SEQ]
     for c in range(4):
-        flipped = dot(flipped_ref[...], held[:, c * 384 : (c + 1) * 384]).T
+        flipped = acc[:, c * 384 : (c + 1) * 384].T
         halves = [[flipped[i * 96 : (i + 1) * 96] for i in (k, k + 2)] for k in range(2)]
         for k in range(2):
             for i in range(2):
@@ -302,10 +309,12 @@
     place = jnp.stack(index + [core]).astype(jnp.int32)
     owners = jnp.stack([fsdp ^ i for i in range(4)]).astype(jnp.int32)
 
-    below, above, other = send(normed, UP), send(normed, DOWN), send(normed, ACROSS)
-    over, beside = swap(mine), sibling(mine)
-    upstream, place, owners, below, above, other, over, beside = tie(
-        (upstream, place, owners, below, above, other, over, beside)
+    beside, other = sibling(mine), send(normed, ACROSS)
+    above, below = send(normed, DOWN), send(normed, UP)
+    over = swap(mine)
+    upstream = lax.all_to_all(tie((upstream, normed))[0], "seq", 0, 0, tiled=True).reshape(T, GW)
+    beside, other, above, below, over, upstream, place, owners = tie(
+        (beside, other, above, below, over, upstream, place, owners)
     )
     far = [send(below[:half], UP), send(above[half:], DOWN)]
     columns = [mine, beside, over, sibling(over)]
@@ -322,16 +331,14 @@
     groups = jnp.stack([1 - here, here]).astype(jnp.int32)
     (near,) = project([below, above], groups, 1)
     near_got = send(near, ACROSS)
-    _, upstream, turned = tie((near, upstream, groups[::-1]))
+    _, turned = tie((near, groups[::-1]))
     (kept,) = project([normed, below, above, other], turned, 1)
-    upstream = lax.all_to_all(upstream, "seq", 0, 0, tiled=True).reshape(T, GW)
     _, far = tie((kept, far))
     last, far_kept = project(far, groups, 2)
+    _, weight, other_late, near_got = tie((last, projection, other, near_got))
+    other_below, other_above = send(other_late, UP), send(other_late, DOWN)
+    weight_over = swap(weight)
     far_got = send(last, ACROSS)
-    _, weight, other_late = tie((last, projection, other))
-    other_below, other_above = send(other_late, UP), send(other_late, DOWN)
-    other_far = send(other_late, FAR)
-    weight_over = swap(weight)
 
     def attend(head):
         return call(
@@ -357,12 +364,15 @@
         return lax.all_to_all(grads.reshape(SEQ, ROWS, 256), "seq", 0, 0, tiled=True)
 
     first = attend(0)
-    first, weight = tie((first, weight))
+    other_below, other_above, other_late, first, weight = tie(
+        (other_below, other_above, other_late, first, weight)
+    )
+    other_far = send(other_late, FAR)
     back0 = send_back(first)
     beside = sibling(weight)
     second = attend(1)
-    second, back0, weight_over, beside, other_below, other_above, other_far = tie(
-        (second, back0, weight_over, beside, other_below, other_above, other_far)
+    second, back0, weight_over, beside, other_far = tie(
+        (second, back0, weight_over, beside, other_far)
     )
     blocks = [normed, below, above, *far, other, other_below, other_above, other_far]
     back1 = send_back(second)
@@ -374,6 +384,7 @@
         [
             pltpu.VMEM((384, T), BF),
             pltpu.VMEM((T, D), BF),
+            pltpu.VMEM((384, D), F32),
             pltpu.SemaphoreType.DMA((len(blocks),)),
         ],
     )(place, first, second, *blocks)

time: 185 us -> 169 us (0.914)
  waiting for transfers between devices: 51 us -> 34.7 us
  Pallas kernels: 78.6 us -> 76.3 us
    all_to_all x1, waiting for transfers between devices: 0.01 us -> 14.5 us  [body(): lax.all_to_all(tie((upstream, normed))[0], 'seq', 0, 0, tiled=True)]
    ppermute x2, waiting for transfers between devices: 12.4 us -> 0.01 us  [swap(): return lax.ppermute(v, ('zh', 'seq'), SWAP)]
    all_to_all x2, waiting for transfers between devices: 10.5 us -> 0.27 us  [send_back(): lax.all_to_all(grads.reshape(SEQ, ROWS, 256), 'seq', 0, 0, tiled=True)]
    ppermute x10, waiting for transfers between devices: 18.8 us -> 10.6 us  [send(): return lax.ppermute(v, 'seq', way)]
    pallas_call x1, Pallas kernels: 10.6 us -> 8.29 us  [body(): call(weight_gradient_kernel, (shape((768, 384), F32), shape((768, 384))),...]
    ppermute x10, starting transfers between devices: 14.2 us -> 16.3 us  [send(): return lax.ppermute(v, 'seq', way)]
    unnamed x31 -> x35, local copies, waits for them, and re-layouts: 3.63 us -> 5.1 us
  transfers between devices with their start and end apart: 21 -> 21, of which waited for: 7 -> 6; matrix products, arithmetic and copies ran while one was open for 2% -> 3% of each run, Pallas kernels for 40% -> 42%
where the time goes in v6:
time: 169 us; the launch traced here: 168 us
  Pallas kernels  76.3 us (45%)
  starting transfers between devices  45.7 us (27%)
  waiting for transfers between devices  34.7 us (21%)
  local copies, waits for them, and re-layouts  9.02 us (5%)
    pallas_call x2, Pallas kernels, attend(): call(functools.partial(attention_kernel, head), shape((T, 256)), [SM, SM]...  37.4 us
    ppermute x10, starting transfers between devices, send(): return lax.ppermute(v, 'seq', way)  16.3 us
    all_to_all x1, waiting for transfers between devices, body(): lax.all_to_all(tie((upstream, normed))[0], 'seq', 0, 0, tiled=True)  14.5 us
    pallas_call x3, Pallas kernels, project(): call(functools.partial(project_kernel, len(rows)), (shape((height, 384)),...  13.4 us
    all_to_all x1, starting transfers between devices, body(): partial = lax.all_to_all(partial, ('dp', 'zh', 'seq'), 0, 0, tiled=True)  11.1 us
    ppermute x10, waiting for transfers between devices, send(): return lax.ppermute(v, 'seq', way)  10.6 us
    pallas_call x1, Pallas kernels, body(): call(input_gradient_kernel, (shape((ROWS, 1024)), shape((ROWS, D), F32)),...  9.28 us
    pallas_call x1, Pallas kernels, body(): call(weight_gradient_kernel, (shape((768, 384), F32), shape((768, 384))),...  8.29 us
  transfers between devices with their start and end apart: 21, of which 6 were waited for; matrix products, arithmetic and copies ran while one was open for 3% of the time, Pallas kernels for 42%

profile of v6, /device:TPU:0, one launch (start us, length us, event | category | flops | bytes accessed | tf_op | source)
XLA Modules:
  0.0 168.5 jit_solution(12439885894804172802)
XLA Ops:
  0.7 3.5 %shard_map.67 = (bf16[256,1536]{1,0:T(8,128)(2,1)}, bf16[384,768]{1,0:T(8,128)(2,1)}) custom-call(s32[1]{0:T(128)} %bitcast.y_ref, bf16[256,1536]{1,0:T(8,128)(2,1)} %bitcast.28, bf16[384,3072]{1,0:T(8,128)(2,1)} %w0.1), custom_call_target="tpu_custom_call" | custom-call | bytes 1048576 | tf_op jit(solution)/shard_map/pallas_call | solution.py:301
  4.2 1.7 %collective-permute-start.3 = (bf16[256,1536]{1,0:T(8,128)(2,1)}, bf16[256,1536]{1,0:T(8,128)(2,1)S(1)}, u32[]{:S(2)}, u32[]{:S(2)}) collective-permute-start(bf16[256,1536]{1,0:T(8,128)(2,1)} %get-tuple-element.43.refs_4_.refs_0_), channel_id=1, source_target_pairs={{0,1},{1,2},{2,3},{3,0},{4,5},{5,6},{6,7},{7,4},{8,9},{9,10},{10,1... | collective-permute-start | bytes 2359304 | tf_op jit(solution)/shard_map/ppermute | solution.py:270
  5.9 1.6 collective-permute-start.2
  7.5 2.0 %collective-permute-start.1 = (bf16[256,1536]{1,0:T(8,128)(2,1)}, bf16[256,1536]{1,0:T(8,128)(2,1)}, u32[]{:S(2)}, u32[]{:S(2)}) collective-permute-start(bf16[256,1536]{1,0:T(8,128)(2,1)} %get-tuple-element.43.refs_4_.refs_0_), channel_id=1, source_target_pairs={{0,4},{1,5},{2,6},{3,7},{4,0},{5,1},{6,2},{7,3},{8,12},{9,13},{10,... | collective-permute-start | bytes 2359304 | tf_op jit(solution)/shard_map/ppermute | solution.py:270
  9.5 2.5 %collective-permute-start.4 = (bf16[384,768]{1,0:T(8,128)(2,1)}, bf16[384,768]{1,0:T(8,128)(2,1)S(1)}, u32[]{:S(2)}, u32[]{:S(2)}) collective-permute-start(bf16[384,768]{1,0:T(8,128)(2,1)} %get-tuple-element.42.refs_0_), channel_id=1, source_target_pairs={{0,20},{1,21},{2,22},{3,23},{4,16},{5,17},{6,18},{7,19},{16,4},{17... | collective-permute-start | bytes 1769480 | tf_op jit(solution)/shard_map/ppermute | solution.py:278
  12.1 0.9 copy.10
  13.0 3.7 %all-to-all-start = ((bf16[8,256,128]{2,1,0:T(8,128)(2,1)}), bf16[8,256,128]{2,1,0:T(8,128)(2,1)S(1)}, u32[]{:S(2)}, u32[]{:S(2)}) async-start(bf16[8,256,128]{2,1,0:T(8,128)(2,1)} %bitcast.27), calls=%async_computation | async-start | bytes 1048576 | tf_op jit(solution)/shard_map/all_to_all | solution.py:315
  17.9 14.5 %all-to-all-done = bf16[8,256,128]{2,1,0:T(8,128)(2,1)S(1)} async-done(((bf16[8,256,128]{2,1,0:T(8,128)(2,1)}), bf16[8,256,128]{2,1,0:T(8,128)(2,1)S(1)}, u32[]{:S(2)}, u32[]{:S(2)}) %all-to-all-start) | async-done | bytes 524320 | tf_op jit(solution)/shard_map/all_to_all | solution.py:315
  33.2 1.0 slice.6
  35.1 1.7 %collective-permute-start.7 = (bf16[128,1536]{1,0:T(8,128)(2,1)}, bf16[128,1536]{1,0:T(8,128)(2,1)}, u32[]{:S(2)}, u32[]{:S(2)}) collective-permute-start(bf16[128,1536]{1,0:T(8,128)(2,1)} %slice.7), channel_id=1, source_target_pairs={{0,3},{1,0},{2,1},{3,2},{4,7},{5,4},{6,5},{7,6},{8,11},{9,8},{10,9... | collective-permute-start | bytes 1179656 | tf_op jit(solution)/shard_map/ppermute | solution.py:270
  38.6 3.9 %shard_map.68 = bf16[512,384]{1,0:T(8,128)(2,1)} custom-call(s32[4]{0:T(128)} %pad_add_fusion.owner_ref.pos_ref, s32[2]{0:T(128)} %pad_add_fusion.1.group_ref, bf16[384,768]{1,0:T(8,128)(2,1)} %get-tuple-element.42.refs_0_, bf16[384,768]{1,0:T(8,128)(2,1)} %copy-done.2, bf16[384,768]{1,0:T(8,128)(2,1)} %copy-done.1, bf16[384,768]{1,0:T(8,128)(2,1)} %copy-done.3, ...), custom_call_target="tpu_custom_call" | custom-call | bytes 1048576 | tf_op jit(solution)/shard_map/pallas_call | solution.py:324
  42.5 1.7 %collective-permute-start.8 = (bf16[512,384]{1,0:T(8,128)(2,1)}, bf16[512,384]{1,0:T(8,128)(2,1)S(1)}, u32[]{:S(2)}, u32[]{:S(2)}) collective-permute-start(bf16[512,384]{1,0:T(8,128)(2,1)} %shard_map.68), channel_id=1, source_target_pairs={{0,4},{1,5},{2,6},{3,7},{4,0},{5,1},{6,2},{7,3},{8,12},{9,13},{10,... | collective-permute-start | bytes 1179656 | tf_op jit(solution)/shard_map/ppermute | solution.py:270
  44.9 5.6 %shard_map.69.kept_ref = bf16[1024,384]{1,0:T(8,128)(2,1)} custom-call(s32[4]{0:T(128)} %pad_add_fusion.owner_ref.pos_ref, s32[2]{0:T(128)} %rev.3.group_ref, bf16[384,768]{1,0:T(8,128)(2,1)} %get-tuple-element.42.refs_0_, bf16[384,768]{1,0:T(8,128)(2,1)} %copy-done.2, bf16[384,768]{1,0:T(8,128)(2,1)} %copy-done.1, bf16[384,768]{1,0:T(8,128)(2,1)} %copy-done.3, ...), custom_call_target="tpu_custom_call" | custom-call | bytes 1048576 | tf_op jit(solution)/shard_map/pallas_call | solution.py:324
  50.4 3.9 %shard_map.70 = (bf16[256,384]{1,0:T(8,128)(2,1)}, bf16[256,384]{1,0:T(8,128)(2,1)}) custom-call(s32[4]{0:T(128)} %pad_add_fusion.owner_ref.pos_ref, s32[2]{0:T(128)} %pad_add_fusion.1.group_ref, bf16[384,768]{1,0:T(8,128)(2,1)} %get-tuple-element.42.refs_0_, bf16[384,768]{1,0:T(8,128)(2,1)} %copy-done.2, bf16[384,768]{1,0:T(8,128)(2,1)} %copy-done.1, ...), custom_call_target="tpu_custom_call" | custom-call | bytes 1048576 | tf_op jit(solution)/shard_map/pallas_call | solution.py:324
  54.4 2.9 %collective-permute-start.10 = (bf16[256,1536]{1,0:T(8,128)(2,1)}, bf16[256,1536]{1,0:T(8,128)(2,1)S(1)}, u32[]{:S(2)}, u32[]{:S(2)}) collective-permute-start(bf16[256,1536]{1,0:T(8,128)(2,1)} %collective-permute-done.1.refs_7_.refs_5_), channel_id=1, source_target_pairs={{0,3},{1,0},{2,1},{3,2},{4,7},{5,4},{6,5},{7,6},{8,11},{9,8},{10,9... | collective-permute-start | bytes 2359304 | tf_op jit(solution)/shard_map/ppermute | solution.py:270
  58.7 3.7 %collective-permute-start.12 = (bf16[384,3072]{1,0:T(8,128)(2,1)S(1)}, bf16[384,3072]{1,0:T(8,128)(2,1)}, u32[]{:S(2)}, u32[]{:S(2)}) collective-permute-start(bf16[384,3072]{1,0:T(8,128)(2,1)S(1)} %copy-done), channel_id=1, source_target_pairs={{0,20},{1,21},{2,22},{3,23},{4,16},{5,17},{6,18},{7,19},{16,4},{17... | collective-permute-start | bytes 7077896 | tf_op jit(solution)/shard_map/ppermute | solution.py:278
  62.4 1.1 collective-permute-done.11.last_ref
  64.1 18.7 %shard_map.71.first_ref = bf16[2048,256]{1,0:T(8,128)(2,1)} custom-call(s32[9]{0:T(128)} %stack.63.pos_ref, s32[1]{0:T(128)S(6)} %copy.11.len_ref, bf16[1024,384]{1,0:T(8,128)(2,1)} %shard_map.69.kept_ref, bf16[256,384]{1,0:T(8,128)(2,1)} %get-tuple-element.57.far_ref, bf16[512,384]{1,0:T(8,128)(2,1)} %copy-done.15, bf16[256,384]{1,0:T(8,128)(2,1)} %copy-done.16, ...), custom_call_target="tpu_custom_call" | custom-call | flops 1000000000 | bytes 1048576 | tf_op jit(solution)/shard_map/pallas_call | solution.py:344
  84.0 4.4 %all-to-all-start.1 = ((bf16[8,256,256]{2,1,0:T(8,128)(2,1)}), bf16[8,256,256]{2,1,0:T(8,128)(2,1)S(1)}, u32[]{:S(2)}, u32[]{:S(2)}) async-start(bf16[8,256,256]{2,1,0:T(8,128)(2,1)} %bitcast.31), calls=%async_computation.1 | async-start | bytes 2097152 | tf_op jit(solution)/shard_map/all_to_all | solution.py:364
  88.4 3.5 %collective-permute-start.14 = (bf16[256,1536]{1,0:T(8,128)(2,1)}, bf16[256,1536]{1,0:T(8,128)(2,1)}, u32[]{:S(2)}, u32[]{:S(2)}) collective-permute-start(bf16[256,1536]{1,0:T(8,128)(2,1)} %collective-permute-done.1.refs_7_.refs_5_), channel_id=1, source_target_pairs={{0,2},{1,3},{2,0},{3,1},{4,6},{5,7},{6,4},{7,5},{8,10},{9,11},{10,... | collective-permute-start | bytes 2359304 | tf_op jit(solution)/shard_map/ppermute | solution.py:270
  92.0 18.6 %shard_map.72.second_ref = bf16[2048,256]{1,0:T(8,128)(2,1)} custom-call(s32[9]{0:T(128)} %stack.63.pos_ref, s32[1]{0:T(128)S(6)} %copy.11.len_ref, bf16[1024,384]{1,0:T(8,128)(2,1)} %shard_map.69.kept_ref, bf16[256,384]{1,0:T(8,128)(2,1)} %get-tuple-element.57.far_ref, bf16[512,384]{1,0:T(8,128)(2,1)} %copy-done.15, bf16[256,384]{1,0:T(8,128)(2,1)} %copy-done.16, ...), custom_call_target="tpu_custom_call" | custom-call | flops 10000000000 | bytes 1048576 | tf_op jit(solution)/shard_map/pallas_call | solution.py:344
  110.6 9.6 %collective-permute-done.14.refs_8_ = bf16[256,1536]{1,0:T(8,128)(2,1)} collective-permute-done((bf16[256,1536]{1,0:T(8,128)(2,1)}, bf16[256,1536]{1,0:T(8,128)(2,1)}, u32[]{:S(2)}, u32[]{:S(2)}) %collective-permute-start.14) | collective-permute-done | bytes 786464 | tf_op jit(solution)/shard_map/ppermute | solution.py:270
  120.2 3.6 %all-to-all-start.2 = ((bf16[8,256,256]{2,1,0:T(8,128)(2,1)}), bf16[8,256,256]{2,1,0:T(8,128)(2,1)S(1)}, u32[]{:S(2)}, u32[]{:S(2)}) async-start(bf16[8,256,256]{2,1,0:T(8,128)(2,1)} %bitcast.32), calls=%async_computation.2 | async-start | bytes 2097152 | tf_op jit(solution)/shard_map/all_to_all | solution.py:364
  123.8 8.3 %shard_map.73 = (f32[768,384]{1,0:T(8,128)}, bf16[768,384]{1,0:T(8,128)(2,1)}) custom-call(s32[9]{0:T(128)} %stack.63.pos_ref, bf16[2048,256]{1,0:T(8,128)(2,1)} %shard_map.71.first_ref, bf16[2048,256]{1,0:T(8,128)(2,1)} %shard_map.72.second_ref, bf16[256,1536]{1,0:T(8,128)(2,1)} %get-tuple-element.43.refs_4_.refs_0_, bf16[256,1536]{1,0:T(8,128)(2,1)} %copy-done.4, ...), custom_call_target="tpu_custom_call" | custom-call | flops 2415919104 | bytes 1048576 | tf_op jit(solution)/shard_map/pallas_call | solution.py:379
  132.4 2.2 %collective-permute-done.15.got_ref = bf16[768,384]{1,0:T(8,128)(2,1)S(1)} collective-permute-done((bf16[768,384]{1,0:T(8,128)(2,1)}, bf16[768,384]{1,0:T(8,128)(2,1)S(1)}, u32[]{:S(2)}, u32[]{:S(2)}) %collective-permute-start.15) | collective-permute-done | bytes 589856 | tf_op jit(solution)/shard_map/ppermute | solution.py:274
  134.6 0.8 copy-done.9
  135.4 2.5 %shard_map.74 = bf16[64,12,384]{2,1,0:T(8,128)(2,1)} custom-call(f32[768,384]{1,0:T(8,128)} %get-tuple-element.68.keep_ref, bf16[768,384]{1,0:T(8,128)(2,1)} %copy-done.9), custom_call_target="tpu_custom_call" | custom-call | bytes 1048576 | tf_op jit(solution)/shard_map/pallas_call | solution.py:392
  138.1 11.1 %all-to-all-start.3 = ((bf16[64,12,384]{2,1,0:T(8,128)(2,1)}), bf16[64,12,384]{2,1,0:T(8,128)(2,1)S(1)}, u32[]{:S(2)}, u32[]{:S(2)}) async-start(bf16[64,12,384]{2,1,0:T(8,128)(2,1)} %shard_map.74), calls=%async_computation.3 | async-start | bytes 1572864 | tf_op jit(solution)/shard_map/all_to_all | solution.py:395
  149.3 9.3 %shard_map.75 = (bf16[256,1024]{1,0:T(8,128)(2,1)}, f32[256,1536]{1,0:T(8,128)}) custom-call(s32[4]{0:T(128)} %pad_add_fusion.owner_ref.pos_ref, bf16[8,256,256]{2,1,0:T(8,128)(2,1)} %copy-done.6, bf16[8,256,256]{2,1,0:T(8,128)(2,1)} %copy-done.7, bf16[384,3072]{1,0:T(8,128)(2,1)} %w0.1, bf16[384,3072]{1,0:T(8,128)(2,1)} %collective-permute-done.13.w1, ...), custom_call_target="tpu_custom_call" | custom-call | flops 2415919104 | bytes 1048576 | tf_op jit(solution)/shard_map/pallas_call | solution.py:396
  158.6 7.1 %all-to-all-done.3.parts_ref = bf16[64,12,384]{2,1,0:T(8,128)(2,1)S(1)} async-done(((bf16[64,12,384]{2,1,0:T(8,128)(2,1)}), bf16[64,12,384]{2,1,0:T(8,128)(2,1)S(1)}, u32[]{:S(2)}, u32[]{:S(2)}) %all-to-all-start.3) | async-done | bytes 589856 | tf_op jit(solution)/shard_map/all_to_all | solution.py:395
  165.7 0.9 copy-done.8
  166.5 1.9 %shard_map.76 = f32[12,3072]{1,0:T(8,128)} custom-call(bf16[64,12,384]{2,1,0:T(8,128)(2,1)} %copy-done.8), custom_call_target="tpu_custom_call" | custom-call | bytes 1048576 | tf_op jit(solution)/shard_map/pallas_call | solution.py:408
  (62 shorter events, 8.4 us)
Async XLA Ops:
  0.6 11.4 %copy-start.10 = (bf16[1,256,1024]{2,1,0:T(8,128)(2,1)S(1)}, bf16[1,256,1024]{2,1,0:T(8,128)(2,1)}, u32[]{:S(2)}) copy-start(bf16[1,256,1024]{2,1,0:T(8,128)(2,1)} %param.7) | copy-start | bytes 1572868
  4.2 28.3 %collective-permute-start.3 = (bf16[256,1536]{1,0:T(8,128)(2,1)}, bf16[256,1536]{1,0:T(8,128)(2,1)S(1)}, u32[]{:S(2)}, u32[]{:S(2)}) collective-permute-start(bf16[256,1536]{1,0:T(8,128)(2,1)} %get-tuple-element.43.refs_4_.refs_0_), channel_id=1, source_target_pairs={{0,1},{1,2},{2,3},{3,0},{4,5},{5,6},{6,7},{7,4},{8,9},{9,10},{10,1... | collective-permute-start | bytes 2359304 | tf_op jit(solution)/shard_map/ppermute | solution.py:270
  5.9 26.6 %collective-permute-start.2 = (bf16[256,1536]{1,0:T(8,128)(2,1)}, bf16[256,1536]{1,0:T(8,128)(2,1)S(1)}, u32[]{:S(2)}, u32[]{:S(2)}) collective-permute-start(bf16[256,1536]{1,0:T(8,128)(2,1)} %get-tuple-element.43.refs_4_.refs_0_), channel_id=1, source_target_pairs={{0,3},{1,0},{2,1},{3,2},{4,7},{5,4},{6,5},{7,6},{8,11},{9,8},{10,9... | collective-permute-start | bytes 2359304 | tf_op jit(solution)/shard_map/ppermute | solution.py:270
  7.5 25.0 %collective-permute-start.1 = (bf16[256,1536]{1,0:T(8,128)(2,1)}, bf16[256,1536]{1,0:T(8,128)(2,1)}, u32[]{:S(2)}, u32[]{:S(2)}) collective-permute-start(bf16[256,1536]{1,0:T(8,128)(2,1)} %get-tuple-element.43.refs_4_.refs_0_), channel_id=1, source_target_pairs={{0,4},{1,5},{2,6},{3,7},{4,0},{5,1},{6,2},{7,3},{8,12},{9,13},{10,... | collective-permute-start | bytes 2359304 | tf_op jit(solution)/shard_map/ppermute | solution.py:270
  9.5 23.0 %collective-permute-start.4 = (bf16[384,768]{1,0:T(8,128)(2,1)}, bf16[384,768]{1,0:T(8,128)(2,1)S(1)}, u32[]{:S(2)}, u32[]{:S(2)}) collective-permute-start(bf16[384,768]{1,0:T(8,128)(2,1)} %get-tuple-element.42.refs_0_), channel_id=1, source_target_pairs={{0,20},{1,21},{2,22},{3,23},{4,16},{5,17},{6,18},{7,19},{16,4},{17... | collective-permute-start | bytes 1769480 | tf_op jit(solution)/shard_map/ppermute | solution.py:278
  12.0 20.5 %collective-permute-start = (bf16[384,768]{1,0:T(8,128)(2,1)}, bf16[384,768]{1,0:T(8,128)(2,1)S(1)}, u32[]{:S(2)}, u32[]{:S(2)}) collective-permute-start(bf16[384,768]{1,0:T(8,128)(2,1)} %get-tuple-element.42.refs_0_), channel_id=1, source_target_pairs={{0,8},{8,0},{1,9},{9,1},{2,10},{10,2},{3,11},{11,3},{4,12},{12,4},... | collective-permute-start | bytes 1769480 | tf_op jit(solution)/shard_map/ppermute | solution.py:274
  13.0 19.5 %all-to-all-start = ((bf16[8,256,128]{2,1,0:T(8,128)(2,1)}), bf16[8,256,128]{2,1,0:T(8,128)(2,1)S(1)}, u32[]{:S(2)}, u32[]{:S(2)}) async-start(bf16[8,256,128]{2,1,0:T(8,128)(2,1)} %bitcast.27), calls=%async_computation | async-start | bytes 1048576 | tf_op jit(solution)/shard_map/all_to_all | solution.py:315
  32.4 5.3 %copy-start.1 = (bf16[384,768]{1,0:T(8,128)(2,1)}, bf16[384,768]{1,0:T(8,128)(2,1)S(1)}, u32[]{:S(2)}) copy-start(bf16[384,768]{1,0:T(8,128)(2,1)S(1)} %collective-permute-done.4.refs_2_) | copy-start | bytes 1769476
  32.5 5.3 %copy-start.2 = (bf16[384,768]{1,0:T(8,128)(2,1)}, bf16[384,768]{1,0:T(8,128)(2,1)S(1)}, u32[]{:S(2)}) copy-start(bf16[384,768]{1,0:T(8,128)(2,1)S(1)} %collective-permute-done.refs_1_) | copy-start | bytes 1769476
  32.5 5.3 %copy-start.4 = (bf16[256,1536]{1,0:T(8,128)(2,1)}, bf16[256,1536]{1,0:T(8,128)(2,1)S(1)}, u32[]{:S(2)}) copy-start(bf16[256,1536]{1,0:T(8,128)(2,1)S(1)} %collective-permute-done.3.refs_4_.refs_5_.refs_1_) | copy-start | bytes 2359300
  32.5 5.3 %copy-start.5 = (bf16[256,1536]{1,0:T(8,128)(2,1)}, bf16[256,1536]{1,0:T(8,128)(2,1)S(1)}, u32[]{:S(2)}) copy-start(bf16[256,1536]{1,0:T(8,128)(2,1)S(1)} %collective-permute-done.2.refs_5_.refs_6_.refs_2_) | copy-start | bytes 2359300
  33.2 4.5 %collective-permute-start.5 = (bf16[384,768]{1,0:T(8,128)(2,1)S(1)}, bf16[384,768]{1,0:T(8,128)(2,1)S(1)}, u32[]{:S(2)}, u32[]{:S(2)}) collective-permute-start(bf16[384,768]{1,0:T(8,128)(2,1)S(1)} %collective-permute-done.4.refs_2_), channel_id=1, source_target_pairs={{0,8},{8,0},{1,9},{9,1},{2,10},{10,2},{3,11},{11,3},{4,12},{12,4},... | collective-permute-start | bytes 1769480 | tf_op jit(solution)/shard_map/ppermute | solution.py:274
  35.1 15.4 %collective-permute-start.7 = (bf16[128,1536]{1,0:T(8,128)(2,1)}, bf16[128,1536]{1,0:T(8,128)(2,1)}, u32[]{:S(2)}, u32[]{:S(2)}) collective-permute-start(bf16[128,1536]{1,0:T(8,128)(2,1)} %slice.7), channel_id=1, source_target_pairs={{0,3},{1,0},{2,1},{3,2},{4,7},{5,4},{6,5},{7,6},{8,11},{9,8},{10,9... | collective-permute-start | bytes 1179656 | tf_op jit(solution)/shard_map/ppermute | solution.py:270
  36.8 13.7 %collective-permute-start.6 = (bf16[128,1536]{1,0:T(8,128)(2,1)}, bf16[128,1536]{1,0:T(8,128)(2,1)}, u32[]{:S(2)}, u32[]{:S(2)}) collective-permute-start(bf16[128,1536]{1,0:T(8,128)(2,1)} %slice.6), channel_id=1, source_target_pairs={{0,1},{1,2},{2,3},{3,0},{4,5},{5,6},{6,7},{7,4},{8,9},{9,10},{10,1... | collective-permute-start | bytes 1179656 | tf_op jit(solution)/shard_map/ppermute | solution.py:270
  37.7 6.5 %copy-start.12 = (s32[2]{0:T(128)S(1)}, s32[2]{0:T(128)}, u32[]{:S(2)}) copy-start(s32[2]{0:T(128)} %pad_add_fusion.1.group_ref) | copy-start | bytes 28
  42.5 11.8 %collective-permute-start.8 = (bf16[512,384]{1,0:T(8,128)(2,1)}, bf16[512,384]{1,0:T(8,128)(2,1)S(1)}, u32[]{:S(2)}, u32[]{:S(2)}) collective-permute-start(bf16[512,384]{1,0:T(8,128)(2,1)} %shard_map.68), channel_id=1, source_target_pairs={{0,4},{1,5},{2,6},{3,7},{4,0},{5,1},{6,2},{7,3},{8,12},{9,13},{10,... | collective-permute-start | bytes 1179656 | tf_op jit(solution)/shard_map/ppermute | solution.py:270
  50.4 8.3 %copy-start = (bf16[384,3072]{1,0:T(8,128)(2,1)S(1)}, bf16[384,3072]{1,0:T(8,128)(2,1)}, u32[]{:S(2)}) copy-start(bf16[384,3072]{1,0:T(8,128)(2,1)} %w0.1) | copy-start | bytes 7077892
  54.4 9.1 %copy-start.15 = (bf16[512,384]{1,0:T(8,128)(2,1)}, bf16[512,384]{1,0:T(8,128)(2,1)S(1)}, u32[]{:S(2)}) copy-start(bf16[512,384]{1,0:T(8,128)(2,1)S(1)} %collective-permute-done.8.other_ref) | copy-start | bytes 1179652
  54.4 28.5 %collective-permute-start.10 = (bf16[256,1536]{1,0:T(8,128)(2,1)}, bf16[256,1536]{1,0:T(8,128)(2,1)S(1)}, u32[]{:S(2)}, u32[]{:S(2)}) collective-permute-start(bf16[256,1536]{1,0:T(8,128)(2,1)} %collective-permute-done.1.refs_7_.refs_5_), channel_id=1, source_target_pairs={{0,3},{1,0},{2,1},{3,2},{4,7},{5,4},{6,5},{7,6},{8,11},{9,8},{10,9... | collective-permute-start | bytes 2359304 | tf_op jit(solution)/shard_map/ppermute | solution.py:270
  57.3 25.6 %collective-permute-start.9 = (bf16[256,1536]{1,0:T(8,128)(2,1)}, bf16[256,1536]{1,0:T(8,128)(2,1)S(1)}, u32[]{:S(2)}, u32[]{:S(2)}) collective-permute-start(bf16[256,1536]{1,0:T(8,128)(2,1)} %collective-permute-done.1.refs_7_.refs_5_), channel_id=1, source_target_pairs={{0,1},{1,2},{2,3},{3,0},{4,5},{5,6},{6,7},{7,4},{8,9},{9,10},{10,1... | collective-permute-start | bytes 2359304 | tf_op jit(solution)/shard_map/ppermute | solution.py:270
  57.3 6.1 %collective-permute-start.11 = (bf16[256,384]{1,0:T(8,128)(2,1)}, bf16[256,384]{1,0:T(8,128)(2,1)S(1)}, u32[]{:S(2)}, u32[]{:S(2)}) collective-permute-start(bf16[256,384]{1,0:T(8,128)(2,1)} %get-tuple-element.55), channel_id=1, source_target_pairs={{0,4},{1,5},{2,6},{3,7},{4,0},{5,1},{6,2},{7,3},{8,12},{9,13},{10,... | collective-permute-start | bytes 589832 | tf_op jit(solution)/shard_map/ppermute | solution.py:270
  58.7 61.5 %collective-permute-start.12 = (bf16[384,3072]{1,0:T(8,128)(2,1)S(1)}, bf16[384,3072]{1,0:T(8,128)(2,1)}, u32[]{:S(2)}, u32[]{:S(2)}) collective-permute-start(bf16[384,3072]{1,0:T(8,128)(2,1)S(1)} %copy-done), channel_id=1, source_target_pairs={{0,20},{1,21},{2,22},{3,23},{4,16},{5,17},{6,18},{7,19},{16,4},{17... | collective-permute-start | bytes 7077896 | tf_op jit(solution)/shard_map/ppermute | solution.py:278
  82.9 1.1 copy-start.14
  82.9 37.3 %collective-permute-start.13 = (bf16[384,3072]{1,0:T(8,128)(2,1)S(1)}, bf16[384,3072]{1,0:T(8,128)(2,1)}, u32[]{:S(2)}, u32[]{:S(2)}) collective-permute-start(bf16[384,3072]{1,0:T(8,128)(2,1)S(1)} %copy-done), channel_id=1, source_target_pairs={{0,8},{8,0},{1,9},{9,1},{2,10},{10,2},{3,11},{11,3},{4,12},{12,4},... | collective-permute-start | bytes 7077896 | tf_op jit(solution)/shard_map/ppermute | solution.py:274
  84.0 36.1 %all-to-all-start.1 = ((bf16[8,256,256]{2,1,0:T(8,128)(2,1)}), bf16[8,256,256]{2,1,0:T(8,128)(2,1)S(1)}, u32[]{:S(2)}, u32[]{:S(2)}) async-start(bf16[8,256,256]{2,1,0:T(8,128)(2,1)} %bitcast.31), calls=%async_computation.1 | async-start | bytes 2097152 | tf_op jit(solution)/shard_map/all_to_all | solution.py:364
  88.4 31.7 %collective-permute-start.14 = (bf16[256,1536]{1,0:T(8,128)(2,1)}, bf16[256,1536]{1,0:T(8,128)(2,1)}, u32[]{:S(2)}, u32[]{:S(2)}) collective-permute-start(bf16[256,1536]{1,0:T(8,128)(2,1)} %collective-permute-done.1.refs_7_.refs_5_), channel_id=1, source_target_pairs={{0,2},{1,3},{2,0},{3,1},{4,6},{5,7},{6,4},{7,5},{8,10},{9,11},{10,... | collective-permute-start | bytes 2359304 | tf_op jit(solution)/shard_map/ppermute | solution.py:270
  120.2 11.9 %copy-start.6 = (bf16[8,256,256]{2,1,0:T(8,128)(2,1)}, bf16[8,256,256]{2,1,0:T(8,128)(2,1)S(1)}, u32[]{:S(2)}) copy-start(bf16[8,256,256]{2,1,0:T(8,128)(2,1)S(1)} %all-to-all-done.1.first_ref) | copy-start | bytes 3145732
  120.2 18.0 %all-to-all-start.2 = ((bf16[8,256,256]{2,1,0:T(8,128)(2,1)}), bf16[8,256,256]{2,1,0:T(8,128)(2,1)S(1)}, u32[]{:S(2)}, u32[]{:S(2)}) async-start(bf16[8,256,256]{2,1,0:T(8,128)(2,1)} %bitcast.32), calls=%async_computation.2 | async-start | bytes 2097152 | tf_op jit(solution)/shard_map/all_to_all | solution.py:364
  132.1 2.5 %collective-permute-start.15 = (bf16[768,384]{1,0:T(8,128)(2,1)}, bf16[768,384]{1,0:T(8,128)(2,1)S(1)}, u32[]{:S(2)}, u32[]{:S(2)}) collective-permute-start(bf16[768,384]{1,0:T(8,128)(2,1)} %get-tuple-element.69), channel_id=1, source_target_pairs={{0,8},{8,0},{1,9},{9,1},{2,10},{10,2},{3,11},{11,3},{4,12},{12,4},... | collective-permute-start | bytes 1769480 | tf_op jit(solution)/shard_map/ppermute | solution.py:274
  138.1 11.1 %copy-start.7 = (bf16[8,256,256]{2,1,0:T(8,128)(2,1)}, bf16[8,256,256]{2,1,0:T(8,128)(2,1)S(1)}, u32[]{:S(2)}) copy-start(bf16[8,256,256]{2,1,0:T(8,128)(2,1)S(1)} %all-to-all-done.2.second_ref) | copy-start | bytes 3145732
  138.1 11.1 %collective-permute-start.16 = (bf16[384,3072]{1,0:T(8,128)(2,1)}, bf16[384,3072]{1,0:T(8,128)(2,1)}, u32[]{:S(2)}, u32[]{:S(2)}) collective-permute-start(bf16[384,3072]{1,0:T(8,128)(2,1)} %collective-permute-done.12.w2), channel_id=1, source_target_pairs={{0,8},{8,0},{1,9},{9,1},{2,10},{10,2},{3,11},{11,3},{4,12},{12,4},... | collective-permute-start | bytes 7077896 | tf_op jit(solution)/shard_map/ppermute | solution.py:274
  138.1 27.5 %all-to-all-start.3 = ((bf16[64,12,384]{2,1,0:T(8,128)(2,1)}), bf16[64,12,384]{2,1,0:T(8,128)(2,1)S(1)}, u32[]{:S(2)}, u32[]{:S(2)}) async-start(bf16[64,12,384]{2,1,0:T(8,128)(2,1)} %shard_map.74), calls=%async_computation.3 | async-start | bytes 1572864 | tf_op jit(solution)/shard_map/all_to_all | solution.py:395
  (6 other events, 4.9 us)

commit v7 on v6

--- a/solution.py
+++ b/solution.py
@@ -230,9 +230,10 @@
 
 
 def input_gradient_kernel(
-    pos_ref, first_ref, second_ref, w0, w1, w2, w3, x_ref, ctx_ref, out_ref, packed, held, sems
+    pos_ref, first_ref, second_ref, w0, w1, w2, w3, w4, w5, x_ref, ctx_ref, out_ref, packed, held, sems
 ):
-    copies = fetch([(w, held.at[f]) for f, w in enumerate((w0, w1, w2, w3))], sems)
+    halves = [held.at[f, :, pl.ds(p * 1536, 1536)] for f in (2, 3) for p in range(2)]
+    copies = fetch(list(zip((w0, w1, w2, w3, w4, w5), [held.at[0], held.at[1]] + halves)), sems)
     for s in range(SEQ):
         at = s * GW
         a = [first_ref[s, :, i * 128 : (i + 1) * 128].astype(F32) for i in range(2)]
@@ -241,10 +242,20 @@
         packed[:, at : at + GW] = join(a[0], b[0], 0).astype(BF)
         packed[:, 1024 + at : 1024 + at + GW] = join(a[1], b[1], 0).astype(BF)
         packed[:, 2048 + at : 2048 + at + GW] = join(a[1], b[1], 1).astype(BF)
+    nt = ((1,), (1,))
     for f in range(4):
         to = pl.ds(pl.multiple_of(pos_ref[f] * 384, 384), 384)
-        copies[f].wait()
-        out_ref[:, to] = dot(packed[...], held[f], ((1,), (1,)))
+        if f < 2:
+            copies[f].wait()
+            out_ref[:, to] = dot(packed[...], held[f], nt)
+        else:
+            total = None
+            for p in range(2):
+                copies[2 * f - 2 + p].wait()
+                cols = pl.ds(pl.multiple_of((pos_ref[4] ^ p) * 1536, 1536), 1536)
+                t = dot(packed[:, cols], held[f, :, p * 1536 : (p + 1) * 1536], nt)
+                total = t if p == 0 else total + t
+            out_ref[:, to] = total
     standard, inv_std = standardize(x_ref[...].astype(F32))
     ng = out_ref[...]
     row_mean = jnp.mean(ng, axis=1, keepdims=True)
@@ -258,7 +269,6 @@
 
 UP = [(i, (i // 4) * 4 + (i % 4 + 1) % 4) for i in range(8)]
 DOWN = [(i, (i // 4) * 4 + (i % 4 + 3) % 4) for i in range(8)]
-FAR = [(i, (i // 4) * 4 + (i % 4 + 2) % 4) for i in range(8)]
 ACROSS = [(i, i ^ 4) for i in range(8)]
 SWAP = [(f * 8 + s, (f ^ 1) * 8 + (s ^ 4)) for f in range(2) for s in range(8)]
 OFFSETS = [(dz, dy) for dz in range(2) for dy in (0, 3, 1, 2)]
@@ -307,14 +317,16 @@
     upstream = cotangent[0].reshape(ROWS, SEQ, GW).transpose(1, 0, 2)
     index = [(me // 4 ^ dz) * 4 + (me % 4 + dy) % 4 for dz, dy in OFFSETS]
     place = jnp.stack(index + [core]).astype(jnp.int32)
-    owners = jnp.stack([fsdp ^ i for i in range(4)]).astype(jnp.int32)
+    owners = jnp.stack([fsdp ^ i for i in range(4)] + [lax.axis_index("dp") % 2]).astype(jnp.int32)
 
     beside, other = sibling(mine), send(normed, ACROSS)
     above, below = send(normed, DOWN), send(normed, UP)
     over = swap(mine)
     upstream = lax.all_to_all(tie((upstream, normed))[0], "seq", 0, 0, tiled=True).reshape(T, GW)
-    beside, other, above, below, over, upstream, place, owners = tie(
-        (beside, other, above, below, over, upstream, place, owners)
+    parity = lax.axis_index("dp") % 2
+    weight_half = lax.dynamic_slice_in_dim(projection, parity * 1536, 1536, 1)
+    beside, other, above, below, over, upstream, place, owners, weight_half = tie(
+        (beside, other, above, below, over, upstream, place, owners, weight_half)
     )
     far = [send(below[:half], UP), send(above[half:], DOWN)]
     columns = [mine, beside, over, sibling(over)]
@@ -335,10 +347,11 @@
     (kept,) = project([normed, below, above, other], turned, 1)
     _, far = tie((kept, far))
     last, far_kept = project(far, groups, 2)
-    _, weight, other_late, near_got = tie((last, projection, other, near_got))
+    _, other_late, near_got = tie((last, other, near_got))
     other_below, other_above = send(other_late, UP), send(other_late, DOWN)
-    weight_over = swap(weight)
-    far_got = send(last, ACROSS)
+    weight_half = swap(weight_half)
+    far_got, far_late = tie((send(last, ACROSS), far))
+    other_far = [send(v, ACROSS) for v in far_late]
 
     def attend(head):
         return call(
@@ -364,17 +377,15 @@
         return lax.all_to_all(grads.reshape(SEQ, ROWS, 256), "seq", 0, 0, tiled=True)
 
     first = attend(0)
-    other_below, other_above, other_late, first, weight = tie(
-        (other_below, other_above, other_late, first, weight)
+    other_below, other_above, other_far, first, weight, weight_half = tie(
+        (other_below, other_above, other_far, first, projection, weight_half)
     )
-    other_far = send(other_late, FAR)
+    weight_rest = lax.ppermute(weight_half, "dp", [(i, i ^ 1) for i in range(4)])
     back0 = send_back(first)
     beside = sibling(weight)
     second = attend(1)
-    second, back0, weight_over, beside, other_far = tie(
-        (second, back0, weight_over, beside, other_far)
-    )
-    blocks = [normed, below, above, *far, other, other_below, other_above, other_far]
+    second, back0, beside = tie((second, back0, beside))
+    blocks = [normed, below, above, *far, other, other_below, other_above, *other_far]
     back1 = send_back(second)
     keep, out = call(
         weight_gradient_kernel,
@@ -390,18 +401,19 @@
     )(place, first, second, *blocks)
     got = sibling(out)
     partial = call(add_kernel, shape((64, 12, 384)), [VM, VM])(keep, got)
-    partial, back1, weight_over = tie((partial, back1, weight_over))
-    weights = [projection, beside, weight_over, sibling(weight_over)]
+    partial, back1, weight_half, weight_rest = tie((partial, back1, weight_half, weight_rest))
+    weights = [projection, beside, weight_half, weight_rest]
+    weights += [sibling(weight_half), sibling(weight_rest)]
     partial = lax.all_to_all(partial, ("dp", "zh", "seq"), 0, 0, tiled=True)
     context, input_gradient = call(
         input_gradient_kernel,
         (shape((ROWS, 1024)), shape((ROWS, D), F32)),
-        [SM, VM, VM] + [ANY] * 4 + [VM],
+        [SM, VM, VM] + [ANY] * 6 + [VM],
         2 * ROWS * D * 3072,
         [
             pltpu.VMEM((ROWS, 3072), BF),
             pltpu.VMEM((4, 384, 3072), BF),
-            pltpu.SemaphoreType.DMA((4,)),
+            pltpu.SemaphoreType.DMA((6,)),
         ],
     )(owners, back0, back1, *weights, x)
     partial, context, input_gradient = tie((partial, context, input_gradient))

time: 169 us -> 165 us (0.976)
  waiting for transfers between devices: 34.7 us -> 28.4 us
  local copies, waits for them, and re-layouts: 9.02 us -> 11.2 us
    ppermute x10 -> x11, waiting for transfers between devices: 10.6 us -> 4.86 us  [send(): return lax.ppermute(v, 'seq', way)]
    all_to_all x1, starting transfers between devices: 11.1 us -> 8.9 us  [body(): partial = lax.all_to_all(partial, ('dp', 'zh', 'seq'), 0, 0, tiled=True)]
    slice x2, local copies, waits for them, and re-layouts: 1.81 us -> 3.83 us  [body(): far = [send(below[:half], UP), send(above[half:], DOWN)]]
    unnamed x35 -> x33, local copies, waits for them, and re-layouts: 5.1 us -> 3.55 us
    ppermute x10 -> x11, starting transfers between devices: 16.3 us -> 15.1 us  [send(): return lax.ppermute(v, 'seq', way)]
  transfers between devices with their start and end apart: 21 -> 24, of which waited for: 6 -> 4; matrix products, arithmetic and copies ran while one was open for 3% -> 5% of each run, Pallas kernels for 42% -> 43%
where the time goes in v7:
time: 165 us; the launch traced here: 164 us
  Pallas kernels  76.7 us (46%)
  starting transfers between devices  45.7 us (28%)
  waiting for transfers between devices  28.4 us (17%)
  local copies, waits for them, and re-layouts  11.2 us (7%)
    pallas_call x2, Pallas kernels, attend(): call(functools.partial(attention_kernel, head), shape((T, 256)), [SM, SM]...  37.4 us
    ppermute x11, starting transfers between devices, send(): return lax.ppermute(v, 'seq', way)  15.1 us
    all_to_all x1, waiting for transfers between devices, body(): lax.all_to_all(tie((upstream, normed))[0], 'seq', 0, 0, tiled=True)  14.8 us
    pallas_call x3, Pallas kernels, project(): call(functools.partial(project_kernel, len(rows)), (shape((height, 384)),...  13.3 us
    pallas_call x1, Pallas kernels, body(): call(input_gradient_kernel, (shape((ROWS, 1024)), shape((ROWS, D), F32)),...  9.59 us
    all_to_all x2, starting transfers between devices, send_back(): lax.all_to_all(grads.reshape(SEQ, ROWS, 256), 'seq', 0, 0, tiled=True)  9.12 us
    all_to_all x1, starting transfers between devices, body(): partial = lax.all_to_all(partial, ('dp', 'zh', 'seq'), 0, 0, tiled=True)  8.9 us
    pallas_call x1, Pallas kernels, body(): call(weight_gradient_kernel, (shape((768, 384), F32), shape((768, 384))),...  8.44 us
  transfers between devices with their start and end apart: 24, of which 4 were waited for; matrix products, arithmetic and copies ran while one was open for 5% of the time, Pallas kernels for 43%

profile of v7, /device:TPU:0, one launch (start us, length us, event | category | flops | bytes accessed | tf_op | source)
XLA Modules:
  0.0 164.3 jit_solution(12544024488523387651)
XLA Ops:
  0.7 3.5 %shard_map.67 = (bf16[256,1536]{1,0:T(8,128)(2,1)}, bf16[384,768]{1,0:T(8,128)(2,1)}) custom-call(s32[1]{0:T(128)} %bitcast.y_ref, bf16[256,1536]{1,0:T(8,128)(2,1)} %bitcast.29, bf16[384,3072]{1,0:T(8,128)(2,1)} %w0.1), custom_call_target="tpu_custom_call" | custom-call | bytes 1048576 | tf_op jit(solution)/shard_map/pallas_call | solution.py:311
  4.1 2.1 %collective-permute-start.1 = (bf16[256,1536]{1,0:T(8,128)(2,1)}, bf16[256,1536]{1,0:T(8,128)(2,1)}, u32[]{:S(2)}, u32[]{:S(2)}) collective-permute-start(bf16[256,1536]{1,0:T(8,128)(2,1)} %get-tuple-element.47.refs_4_.refs_0_), channel_id=1, source_target_pairs={{0,4},{1,5},{2,6},{3,7},{4,0},{5,1},{6,2},{7,3},{8,12},{9,13},{10,... | collective-permute-start | bytes 2359304 | tf_op jit(solution)/shard_map/ppermute | solution.py:280
  6.2 3.0 %collective-permute-start.2 = (bf16[256,1536]{1,0:T(8,128)(2,1)}, bf16[256,1536]{1,0:T(8,128)(2,1)}, u32[]{:S(2)}, u32[]{:S(2)}) collective-permute-start(bf16[256,1536]{1,0:T(8,128)(2,1)} %get-tuple-element.47.refs_4_.refs_0_), channel_id=1, source_target_pairs={{0,3},{1,0},{2,1},{3,2},{4,7},{5,4},{6,5},{7,6},{8,11},{9,8},{10,9... | collective-permute-start | bytes 2359304 | tf_op jit(solution)/shard_map/ppermute | solution.py:280
  9.2 2.5 %collective-permute-start.4 = (bf16[384,768]{1,0:T(8,128)(2,1)}, bf16[384,768]{1,0:T(8,128)(2,1)S(1)}, u32[]{:S(2)}, u32[]{:S(2)}) collective-permute-start(bf16[384,768]{1,0:T(8,128)(2,1)} %get-tuple-element.46.refs_0_), channel_id=1, source_target_pairs={{0,20},{1,21},{2,22},{3,23},{4,16},{5,17},{6,18},{7,19},{16,4},{17... | collective-permute-start | bytes 1769480 | tf_op jit(solution)/shard_map/ppermute | solution.py:288
  12.7 5.0 %all-to-all-start = ((bf16[8,256,128]{2,1,0:T(8,128)(2,1)}), bf16[8,256,128]{2,1,0:T(8,128)(2,1)}, u32[]{:S(2)}, u32[]{:S(2)}) async-start(bf16[8,256,128]{2,1,0:T(8,128)(2,1)} %bitcast.31), calls=%async_computation | async-start | bytes 1048576 | tf_op jit(solution)/shard_map/all_to_all | solution.py:325
  19.0 1.1 constant_dynamic-slice_fusion
  20.1 14.8 %all-to-all-done = bf16[8,256,128]{2,1,0:T(8,128)(2,1)} async-done(((bf16[8,256,128]{2,1,0:T(8,128)(2,1)}), bf16[8,256,128]{2,1,0:T(8,128)(2,1)}, u32[]{:S(2)}, u32[]{:S(2)}) %all-to-all-start) | async-done | bytes 524320 | tf_op jit(solution)/shard_map/all_to_all | solution.py:325
  35.0 2.1 %slice.6 = bf16[128,1536]{1,0:T(8,128)(2,1)} slice(bf16[256,1536]{1,0:T(8,128)(2,1)} %collective-permute-done.3.refs_4_.refs_5_.refs_1_), slice={[0:128], [0:1536]} | slice | bytes 786432 | tf_op jit(solution)/shard_map/slice | solution.py:331
  37.1 1.8 %slice.7 = bf16[128,1536]{1,0:T(8,128)(2,1)} slice(bf16[256,1536]{1,0:T(8,128)(2,1)} %collective-permute-done.2.refs_5_.refs_6_.refs_2_), slice={[128:256], [0:1536]} | slice | bytes 786432 | tf_op jit(solution)/shard_map/slice | solution.py:331
  38.9 3.2 %collective-permute-start.7 = (bf16[128,1536]{1,0:T(8,128)(2,1)}, bf16[128,1536]{1,0:T(8,128)(2,1)}, u32[]{:S(2)}, u32[]{:S(2)}) collective-permute-start(bf16[128,1536]{1,0:T(8,128)(2,1)} %slice.7), channel_id=1, source_target_pairs={{0,3},{1,0},{2,1},{3,2},{4,7},{5,4},{6,5},{7,6},{8,11},{9,8},{10,9... | collective-permute-start | bytes 1179656 | tf_op jit(solution)/shard_map/ppermute | solution.py:280
  42.8 3.9 %shard_map.68 = bf16[512,384]{1,0:T(8,128)(2,1)} custom-call(s32[5]{0:T(128)} %stack.72.owner_ref.pos_ref, s32[2]{0:T(128)} %pad_add_fusion.group_ref, bf16[384,768]{1,0:T(8,128)(2,1)} %get-tuple-element.46.refs_0_, bf16[384,768]{1,0:T(8,128)(2,1)} %copy-done.1, bf16[384,768]{1,0:T(8,128)(2,1)} %copy-done.2, ...), custom_call_target="tpu_custom_call" | custom-call | bytes 1048576 | tf_op jit(solution)/shard_map/pallas_call | solution.py:336
  46.7 1.7 %collective-permute-start.8 = (bf16[512,384]{1,0:T(8,128)(2,1)}, bf16[512,384]{1,0:T(8,128)(2,1)}, u32[]{:S(2)}, u32[]{:S(2)}) collective-permute-start(bf16[512,384]{1,0:T(8,128)(2,1)} %shard_map.68), channel_id=1, source_target_pairs={{0,4},{1,5},{2,6},{3,7},{4,0},{5,1},{6,2},{7,3},{8,12},{9,13},{10,... | collective-permute-start | bytes 1179656 | tf_op jit(solution)/shard_map/ppermute | solution.py:280
  48.4 2.5 %collective-permute-start.14 = (bf16[384,1536]{1,0:T(8,128)(2,1)}, bf16[384,1536]{1,0:T(8,128)(2,1)S(1)}, u32[]{:S(2)}, u32[]{:S(2)}) collective-permute-start(bf16[384,1536]{1,0:T(8,128)(2,1)} %constant_dynamic-slice_fusion), channel_id=1, source_target_pairs={{0,20},{1,21},{2,22},{3,23},{4,16},{5,17},{6,18},{7,19},{16,4},{17... | collective-permute-start | bytes 3538952 | tf_op jit(solution)/shard_map/ppermute | solution.py:288
  51.5 5.6 %shard_map.69.kept_ref = bf16[1024,384]{1,0:T(8,128)(2,1)} custom-call(s32[5]{0:T(128)} %stack.72.owner_ref.pos_ref, s32[2]{0:T(128)} %rev.3.group_ref, bf16[384,768]{1,0:T(8,128)(2,1)} %get-tuple-element.46.refs_0_, bf16[384,768]{1,0:T(8,128)(2,1)} %copy-done.1, bf16[384,768]{1,0:T(8,128)(2,1)} %copy-done.2, ...), custom_call_target="tpu_custom_call" | custom-call | bytes 1048576 | tf_op jit(solution)/shard_map/pallas_call | solution.py:336
  57.1 3.7 %shard_map.70 = (bf16[256,384]{1,0:T(8,128)(2,1)}, bf16[256,384]{1,0:T(8,128)(2,1)}) custom-call(s32[5]{0:T(128)} %stack.72.owner_ref.pos_ref, s32[2]{0:T(128)} %pad_add_fusion.group_ref, bf16[384,768]{1,0:T(8,128)(2,1)} %get-tuple-element.46.refs_0_, bf16[384,768]{1,0:T(8,128)(2,1)} %copy-done.1, bf16[384,768]{1,0:T(8,128)(2,1)} %copy-done.2, ...), custom_call_target="tpu_custom_call" | custom-call | bytes 1048576 | tf_op jit(solution)/shard_map/pallas_call | solution.py:336
  60.8 2.0 %collective-permute-start.9 = (bf16[256,1536]{1,0:T(8,128)(2,1)}, bf16[256,1536]{1,0:T(8,128)(2,1)S(1)}, u32[]{:S(2)}, u32[]{:S(2)}) collective-permute-start(bf16[256,1536]{1,0:T(8,128)(2,1)} %collective-permute-done.1.refs_7_.refs_5_), channel_id=1, source_target_pairs={{0,1},{1,2},{2,3},{3,0},{4,5},{5,6},{6,7},{7,4},{8,9},{9,10},{10,1... | collective-permute-start | bytes 2359304 | tf_op jit(solution)/shard_map/ppermute | solution.py:280
  62.9 1.0 collective-permute-start.11
  63.9 4.8 %collective-permute-done.11.last_ref = bf16[256,384]{1,0:T(8,128)(2,1)S(1)} collective-permute-done((bf16[256,384]{1,0:T(8,128)(2,1)}, bf16[256,384]{1,0:T(8,128)(2,1)S(1)}, u32[]{:S(2)}, u32[]{:S(2)}) %collective-permute-start.11) | collective-permute-done | bytes 196640 | tf_op jit(solution)/shard_map/ppermute | solution.py:280
  68.7 1.0 collective-permute-start.12
  71.4 18.7 %shard_map.71.first_ref = bf16[2048,256]{1,0:T(8,128)(2,1)} custom-call(s32[9]{0:T(128)} %stack.66.pos_ref, s32[1]{0:T(128)S(6)} %copy.11.len_ref, bf16[1024,384]{1,0:T(8,128)(2,1)} %shard_map.69.kept_ref, bf16[256,384]{1,0:T(8,128)(2,1)} %get-tuple-element.63.far_ref, bf16[512,384]{1,0:T(8,128)(2,1)} %collective-permute-done.8.other_ref, ...), custom_call_target="tpu_custom_call" | custom-call | flops 1000000000 | bytes 1048576 | tf_op jit(solution)/shard_map/pallas_call | solution.py:357
  90.3 1.1 copy-done.13
  92.0 3.6 %all-to-all-start.1 = ((bf16[8,256,256]{2,1,0:T(8,128)(2,1)}), bf16[8,256,256]{2,1,0:T(8,128)(2,1)S(1)}, u32[]{:S(2)}, u32[]{:S(2)}) async-start(bf16[8,256,256]{2,1,0:T(8,128)(2,1)} %bitcast.33), calls=%async_computation.1 | async-start | bytes 2097152 | tf_op jit(solution)/shard_map/all_to_all | solution.py:377
  95.5 1.5 collective-permute-start.17
  97.1 18.7 %shard_map.72.second_ref = bf16[2048,256]{1,0:T(8,128)(2,1)} custom-call(s32[9]{0:T(128)} %stack.66.pos_ref, s32[1]{0:T(128)S(6)} %copy.11.len_ref, bf16[1024,384]{1,0:T(8,128)(2,1)} %shard_map.69.kept_ref, bf16[256,384]{1,0:T(8,128)(2,1)} %get-tuple-element.63.far_ref, bf16[512,384]{1,0:T(8,128)(2,1)} %collective-permute-done.8.other_ref, ...), custom_call_target="tpu_custom_call" | custom-call | flops 10000000000 | bytes 1048576 | tf_op jit(solution)/shard_map/pallas_call | solution.py:357
  115.8 5.6 %all-to-all-start.2 = ((bf16[8,256,256]{2,1,0:T(8,128)(2,1)}), bf16[8,256,256]{2,1,0:T(8,128)(2,1)S(1)}, u32[]{:S(2)}, u32[]{:S(2)}) async-start(bf16[8,256,256]{2,1,0:T(8,128)(2,1)} %bitcast.34), calls=%async_computation.2 | async-start | bytes 2097152 | tf_op jit(solution)/shard_map/all_to_all | solution.py:377
  121.3 8.4 %shard_map.73 = (f32[768,384]{1,0:T(8,128)}, bf16[768,384]{1,0:T(8,128)(2,1)}) custom-call(s32[9]{0:T(128)} %stack.66.pos_ref, bf16[2048,256]{1,0:T(8,128)(2,1)} %shard_map.71.first_ref, bf16[2048,256]{1,0:T(8,128)(2,1)} %shard_map.72.second_ref, bf16[256,1536]{1,0:T(8,128)(2,1)} %get-tuple-element.47.refs_4_.refs_0_, ...), custom_call_target="tpu_custom_call" | custom-call | flops 2415919104 | bytes 1048576 | tf_op jit(solution)/shard_map/pallas_call | solution.py:390
  130.1 2.2 %collective-permute-done.16.got_ref = bf16[768,384]{1,0:T(8,128)(2,1)S(1)} collective-permute-done((bf16[768,384]{1,0:T(8,128)(2,1)}, bf16[768,384]{1,0:T(8,128)(2,1)S(1)}, u32[]{:S(2)}, u32[]{:S(2)}) %collective-permute-start.16) | collective-permute-done | bytes 589856 | tf_op jit(solution)/shard_map/ppermute | solution.py:284
  133.2 2.6 %shard_map.74 = bf16[64,12,384]{2,1,0:T(8,128)(2,1)} custom-call(f32[768,384]{1,0:T(8,128)} %get-tuple-element.75.keep_ref, bf16[768,384]{1,0:T(8,128)(2,1)} %copy-done.8), custom_call_target="tpu_custom_call" | custom-call | bytes 1048576 | tf_op jit(solution)/shard_map/pallas_call | solution.py:403
  136.4 8.9 %all-to-all-start.3 = ((bf16[64,12,384]{2,1,0:T(8,128)(2,1)}), bf16[64,12,384]{2,1,0:T(8,128)(2,1)S(1)}, u32[]{:S(2)}, u32[]{:S(2)}) async-start(bf16[64,12,384]{2,1,0:T(8,128)(2,1)} %shard_map.74), calls=%async_computation.3 | async-start | bytes 1572864 | tf_op jit(solution)/shard_map/all_to_all | solution.py:407
  145.3 9.6 %shard_map.75 = (bf16[256,1024]{1,0:T(8,128)(2,1)}, f32[256,1536]{1,0:T(8,128)}) custom-call(s32[5]{0:T(128)} %stack.72.owner_ref.pos_ref, bf16[8,256,256]{2,1,0:T(8,128)(2,1)} %copy-done.3, bf16[8,256,256]{2,1,0:T(8,128)(2,1)} %copy-done.4, bf16[384,3072]{1,0:T(8,128)(2,1)} %w0.1, bf16[384,3072]{1,0:T(8,128)(2,1)} %collective-permute-done.15.w1, ...), custom_call_target="tpu_custom_call" | custom-call | flops 2415919104 | bytes 1048576 | tf_op jit(solution)/shard_map/pallas_call | solution.py:408
  154.9 6.5 %all-to-all-done.3.parts_ref = bf16[64,12,384]{2,1,0:T(8,128)(2,1)S(1)} async-done(((bf16[64,12,384]{2,1,0:T(8,128)(2,1)}), bf16[64,12,384]{2,1,0:T(8,128)(2,1)S(1)}, u32[]{:S(2)}, u32[]{:S(2)}) %all-to-all-start.3) | async-done | bytes 589856 | tf_op jit(solution)/shard_map/all_to_all | solution.py:407
  162.4 1.9 %shard_map.76 = f32[12,3072]{1,0:T(8,128)} custom-call(bf16[64,12,384]{2,1,0:T(8,128)(2,1)} %copy-done.5), custom_call_target="tpu_custom_call" | custom-call | bytes 1048576 | tf_op jit(solution)/shard_map/pallas_call | solution.py:420
  (67 shorter events, 8.0 us)
Async XLA Ops:
  0.6 11.1 %copy-start.9 = (bf16[1,256,1024]{2,1,0:T(8,128)(2,1)S(1)}, bf16[1,256,1024]{2,1,0:T(8,128)(2,1)}, u32[]{:S(2)}) copy-start(bf16[1,256,1024]{2,1,0:T(8,128)(2,1)} %param.7) | copy-start | bytes 1572868
  4.1 30.8 %collective-permute-start.1 = (bf16[256,1536]{1,0:T(8,128)(2,1)}, bf16[256,1536]{1,0:T(8,128)(2,1)}, u32[]{:S(2)}, u32[]{:S(2)}) collective-permute-start(bf16[256,1536]{1,0:T(8,128)(2,1)} %get-tuple-element.47.refs_4_.refs_0_), channel_id=1, source_target_pairs={{0,4},{1,5},{2,6},{3,7},{4,0},{5,1},{6,2},{7,3},{8,12},{9,13},{10,... | collective-permute-start | bytes 2359304 | tf_op jit(solution)/shard_map/ppermute | solution.py:280
  6.2 28.7 %collective-permute-start.2 = (bf16[256,1536]{1,0:T(8,128)(2,1)}, bf16[256,1536]{1,0:T(8,128)(2,1)}, u32[]{:S(2)}, u32[]{:S(2)}) collective-permute-start(bf16[256,1536]{1,0:T(8,128)(2,1)} %get-tuple-element.47.refs_4_.refs_0_), channel_id=1, source_target_pairs={{0,3},{1,0},{2,1},{3,2},{4,7},{5,4},{6,5},{7,6},{8,11},{9,8},{10,9... | collective-permute-start | bytes 2359304 | tf_op jit(solution)/shard_map/ppermute | solution.py:280
  9.2 25.7 %collective-permute-start.3 = (bf16[256,1536]{1,0:T(8,128)(2,1)}, bf16[256,1536]{1,0:T(8,128)(2,1)}, u32[]{:S(2)}, u32[]{:S(2)}) collective-permute-start(bf16[256,1536]{1,0:T(8,128)(2,1)} %get-tuple-element.47.refs_4_.refs_0_), channel_id=1, source_target_pairs={{0,1},{1,2},{2,3},{3,0},{4,5},{5,6},{6,7},{7,4},{8,9},{9,10},{10,1... | collective-permute-start | bytes 2359304 | tf_op jit(solution)/shard_map/ppermute | solution.py:280
  9.2 25.7 %collective-permute-start = (bf16[384,768]{1,0:T(8,128)(2,1)}, bf16[384,768]{1,0:T(8,128)(2,1)S(1)}, u32[]{:S(2)}, u32[]{:S(2)}) collective-permute-start(bf16[384,768]{1,0:T(8,128)(2,1)} %get-tuple-element.46.refs_0_), channel_id=1, source_target_pairs={{0,8},{8,0},{1,9},{9,1},{2,10},{10,2},{3,11},{11,3},{4,12},{12,4},... | collective-permute-start | bytes 1769480 | tf_op jit(solution)/shard_map/ppermute | solution.py:284
  9.2 25.7 %collective-permute-start.4 = (bf16[384,768]{1,0:T(8,128)(2,1)}, bf16[384,768]{1,0:T(8,128)(2,1)S(1)}, u32[]{:S(2)}, u32[]{:S(2)}) collective-permute-start(bf16[384,768]{1,0:T(8,128)(2,1)} %get-tuple-element.46.refs_0_), channel_id=1, source_target_pairs={{0,20},{1,21},{2,22},{3,23},{4,16},{5,17},{6,18},{7,19},{16,4},{17... | collective-permute-start | bytes 1769480 | tf_op jit(solution)/shard_map/ppermute | solution.py:288
  11.8 7.2 %copy-start = (bf16[384,3072]{1,0:T(8,128)(2,1)S(1)}, bf16[384,3072]{1,0:T(8,128)(2,1)}, u32[]{:S(2)}) copy-start(bf16[384,3072]{1,0:T(8,128)(2,1)} %w0.1) | copy-start | bytes 7077892
  12.7 22.1 %all-to-all-start = ((bf16[8,256,128]{2,1,0:T(8,128)(2,1)}), bf16[8,256,128]{2,1,0:T(8,128)(2,1)}, u32[]{:S(2)}, u32[]{:S(2)}) async-start(bf16[8,256,128]{2,1,0:T(8,128)(2,1)} %bitcast.31), calls=%async_computation | async-start | bytes 1048576 | tf_op jit(solution)/shard_map/all_to_all | solution.py:325
  34.9 7.9 %copy-start.1 = (bf16[384,768]{1,0:T(8,128)(2,1)}, bf16[384,768]{1,0:T(8,128)(2,1)S(1)}, u32[]{:S(2)}) copy-start(bf16[384,768]{1,0:T(8,128)(2,1)S(1)} %collective-permute-done.refs_1_) | copy-start | bytes 1769476
  34.9 7.8 %copy-start.2 = (bf16[384,768]{1,0:T(8,128)(2,1)}, bf16[384,768]{1,0:T(8,128)(2,1)S(1)}, u32[]{:S(2)}) copy-start(bf16[384,768]{1,0:T(8,128)(2,1)S(1)} %collective-permute-done.4.refs_2_) | copy-start | bytes 1769476
  34.9 7.8 %collective-permute-start.5 = (bf16[384,768]{1,0:T(8,128)(2,1)S(1)}, bf16[384,768]{1,0:T(8,128)(2,1)}, u32[]{:S(2)}, u32[]{:S(2)}) collective-permute-start(bf16[384,768]{1,0:T(8,128)(2,1)S(1)} %collective-permute-done.4.refs_2_), channel_id=1, source_target_pairs={{0,8},{8,0},{1,9},{9,1},{2,10},{10,2},{3,11},{11,3},{4,12},{12,4},... | collective-permute-start | bytes 1769480 | tf_op jit(solution)/shard_map/ppermute | solution.py:284
  37.1 20.0 %collective-permute-start.6 = (bf16[128,1536]{1,0:T(8,128)(2,1)}, bf16[128,1536]{1,0:T(8,128)(2,1)}, u32[]{:S(2)}, u32[]{:S(2)}) collective-permute-start(bf16[128,1536]{1,0:T(8,128)(2,1)} %slice.6), channel_id=1, source_target_pairs={{0,1},{1,2},{2,3},{3,0},{4,5},{5,6},{6,7},{7,4},{8,9},{9,10},{10,1... | collective-permute-start | bytes 1179656 | tf_op jit(solution)/shard_map/ppermute | solution.py:280
  38.9 18.2 %collective-permute-start.7 = (bf16[128,1536]{1,0:T(8,128)(2,1)}, bf16[128,1536]{1,0:T(8,128)(2,1)}, u32[]{:S(2)}, u32[]{:S(2)}) collective-permute-start(bf16[128,1536]{1,0:T(8,128)(2,1)} %slice.7), channel_id=1, source_target_pairs={{0,3},{1,0},{2,1},{3,2},{4,7},{5,4},{6,5},{7,6},{8,11},{9,8},{10,9... | collective-permute-start | bytes 1179656 | tf_op jit(solution)/shard_map/ppermute | solution.py:280
  42.7 8.1 %copy-start.10 = (s32[2]{0:T(128)S(1)}, s32[2]{0:T(128)}, u32[]{:S(2)}) copy-start(s32[2]{0:T(128)} %pad_add_fusion.group_ref) | copy-start | bytes 28
  46.7 14.1 %collective-permute-start.8 = (bf16[512,384]{1,0:T(8,128)(2,1)}, bf16[512,384]{1,0:T(8,128)(2,1)}, u32[]{:S(2)}, u32[]{:S(2)}) collective-permute-start(bf16[512,384]{1,0:T(8,128)(2,1)} %shard_map.68), channel_id=1, source_target_pairs={{0,4},{1,5},{2,6},{3,7},{4,0},{5,1},{6,2},{7,3},{8,12},{9,13},{10,... | collective-permute-start | bytes 1179656 | tf_op jit(solution)/shard_map/ppermute | solution.py:280
  48.4 41.8 %collective-permute-start.14 = (bf16[384,1536]{1,0:T(8,128)(2,1)}, bf16[384,1536]{1,0:T(8,128)(2,1)S(1)}, u32[]{:S(2)}, u32[]{:S(2)}) collective-permute-start(bf16[384,1536]{1,0:T(8,128)(2,1)} %constant_dynamic-slice_fusion), channel_id=1, source_target_pairs={{0,20},{1,21},{2,22},{3,23},{4,16},{5,17},{6,18},{7,19},{16,4},{17... | collective-permute-start | bytes 3538952 | tf_op jit(solution)/shard_map/ppermute | solution.py:288
  60.8 29.4 %collective-permute-start.10 = (bf16[256,1536]{1,0:T(8,128)(2,1)}, bf16[256,1536]{1,0:T(8,128)(2,1)S(1)}, u32[]{:S(2)}, u32[]{:S(2)}) collective-permute-start(bf16[256,1536]{1,0:T(8,128)(2,1)} %collective-permute-done.1.refs_7_.refs_5_), channel_id=1, source_target_pairs={{0,3},{1,0},{2,1},{3,2},{4,7},{5,4},{6,5},{7,6},{8,11},{9,8},{10,9... | collective-permute-start | bytes 2359304 | tf_op jit(solution)/shard_map/ppermute | solution.py:280
  60.8 29.4 %collective-permute-start.9 = (bf16[256,1536]{1,0:T(8,128)(2,1)}, bf16[256,1536]{1,0:T(8,128)(2,1)S(1)}, u32[]{:S(2)}, u32[]{:S(2)}) collective-permute-start(bf16[256,1536]{1,0:T(8,128)(2,1)} %collective-permute-done.1.refs_7_.refs_5_), channel_id=1, source_target_pairs={{0,1},{1,2},{2,3},{3,0},{4,5},{5,6},{6,7},{7,4},{8,9},{9,10},{10,1... | collective-permute-start | bytes 2359304 | tf_op jit(solution)/shard_map/ppermute | solution.py:280
  62.9 5.9 %collective-permute-start.11 = (bf16[256,384]{1,0:T(8,128)(2,1)}, bf16[256,384]{1,0:T(8,128)(2,1)S(1)}, u32[]{:S(2)}, u32[]{:S(2)}) collective-permute-start(bf16[256,384]{1,0:T(8,128)(2,1)} %get-tuple-element.59), channel_id=1, source_target_pairs={{0,4},{1,5},{2,6},{3,7},{4,0},{5,1},{6,2},{7,3},{8,12},{9,13},{10,... | collective-permute-start | bytes 589832 | tf_op jit(solution)/shard_map/ppermute | solution.py:280
  68.7 2.7 %copy-start.15 = (bf16[256,384]{1,0:T(8,128)(2,1)}, bf16[256,384]{1,0:T(8,128)(2,1)S(1)}, u32[]{:S(2)}) copy-start(bf16[256,384]{1,0:T(8,128)(2,1)S(1)} %collective-permute-done.11.last_ref) | copy-start | bytes 589828
  68.7 21.4 %collective-permute-start.12 = (bf16[128,1536]{1,0:T(8,128)(2,1)}, bf16[128,1536]{1,0:T(8,128)(2,1)S(1)}, u32[]{:S(2)}, u32[]{:S(2)}) collective-permute-start(bf16[128,1536]{1,0:T(8,128)(2,1)} %collective-permute-done.6.refs_4_.refs_3_), channel_id=1, source_target_pairs={{0,4},{1,5},{2,6},{3,7},{4,0},{5,1},{6,2},{7,3},{8,12},{9,13},{10,... | collective-permute-start | bytes 1179656 | tf_op jit(solution)/shard_map/ppermute | solution.py:280
  69.8 20.4 %collective-permute-start.13 = (bf16[128,1536]{1,0:T(8,128)(2,1)}, bf16[128,1536]{1,0:T(8,128)(2,1)S(1)}, u32[]{:S(2)}, u32[]{:S(2)}) collective-permute-start(bf16[128,1536]{1,0:T(8,128)(2,1)} %collective-permute-done.7.refs_5_.refs_4_), channel_id=1, source_target_pairs={{0,4},{1,5},{2,6},{3,7},{4,0},{5,1},{6,2},{7,3},{8,12},{9,13},{10,... | collective-permute-start | bytes 1179656 | tf_op jit(solution)/shard_map/ppermute | solution.py:280
  90.3 25.5 %collective-permute-start.15 = (bf16[384,3072]{1,0:T(8,128)(2,1)S(1)}, bf16[384,3072]{1,0:T(8,128)(2,1)}, u32[]{:S(2)}, u32[]{:S(2)}) collective-permute-start(bf16[384,3072]{1,0:T(8,128)(2,1)S(1)} %copy-done), channel_id=1, source_target_pairs={{0,8},{8,0},{1,9},{9,1},{2,10},{10,2},{3,11},{11,3},{4,12},{12,4},... | collective-permute-start | bytes 7077896 | tf_op jit(solution)/shard_map/ppermute | solution.py:284
  92.0 23.8 %all-to-all-start.1 = ((bf16[8,256,256]{2,1,0:T(8,128)(2,1)}), bf16[8,256,256]{2,1,0:T(8,128)(2,1)S(1)}, u32[]{:S(2)}, u32[]{:S(2)}) async-start(bf16[8,256,256]{2,1,0:T(8,128)(2,1)} %bitcast.33), calls=%async_computation.1 | async-start | bytes 2097152 | tf_op jit(solution)/shard_map/all_to_all | solution.py:377
  95.5 40.2 %collective-permute-start.17 = (bf16[384,1536]{1,0:T(8,128)(2,1)}, bf16[384,1536]{1,0:T(8,128)(2,1)}, u32[]{:S(2)}, u32[]{:S(2)}) collective-permute-start(bf16[384,1536]{1,0:T(8,128)(2,1)} %copy-done.6), channel_id=1, source_target_pairs={{0,32},{32,0},{64,96},{96,64},{1,33},{33,1},{65,97},{97,65},{2,34}... | collective-permute-start | bytes 3538952 | tf_op jit(solution)/shard_map/ppermute | solution.py:383
  115.8 14.0 %copy-start.3 = (bf16[8,256,256]{2,1,0:T(8,128)(2,1)}, bf16[8,256,256]{2,1,0:T(8,128)(2,1)S(1)}, u32[]{:S(2)}) copy-start(bf16[8,256,256]{2,1,0:T(8,128)(2,1)S(1)} %all-to-all-done.1.first_ref) | copy-start | bytes 3145732
  115.8 20.0 %all-to-all-start.2 = ((bf16[8,256,256]{2,1,0:T(8,128)(2,1)}), bf16[8,256,256]{2,1,0:T(8,128)(2,1)S(1)}, u32[]{:S(2)}, u32[]{:S(2)}) async-start(bf16[8,256,256]{2,1,0:T(8,128)(2,1)} %bitcast.34), calls=%async_computation.2 | async-start | bytes 2097152 | tf_op jit(solution)/shard_map/all_to_all | solution.py:377
  129.8 2.5 %collective-permute-start.16 = (bf16[768,384]{1,0:T(8,128)(2,1)}, bf16[768,384]{1,0:T(8,128)(2,1)S(1)}, u32[]{:S(2)}, u32[]{:S(2)}) collective-permute-start(bf16[768,384]{1,0:T(8,128)(2,1)} %get-tuple-element.76), channel_id=1, source_target_pairs={{0,8},{8,0},{1,9},{9,1},{2,10},{10,2},{3,11},{11,3},{4,12},{12,4},... | collective-permute-start | bytes 1769480 | tf_op jit(solution)/shard_map/ppermute | solution.py:284
  135.8 9.5 %copy-start.4 = (bf16[8,256,256]{2,1,0:T(8,128)(2,1)}, bf16[8,256,256]{2,1,0:T(8,128)(2,1)S(1)}, u32[]{:S(2)}) copy-start(bf16[8,256,256]{2,1,0:T(8,128)(2,1)S(1)} %all-to-all-done.2.second_ref) | copy-start | bytes 3145732
  135.8 9.5 %collective-permute-start.18 = (bf16[384,1536]{1,0:T(8,128)(2,1)S(1)}, bf16[384,1536]{1,0:T(8,128)(2,1)}, u32[]{:S(2)}, u32[]{:S(2)}) collective-permute-start(bf16[384,1536]{1,0:T(8,128)(2,1)S(1)} %copy-done.7), channel_id=1, source_target_pairs={{0,8},{8,0},{1,9},{9,1},{2,10},{10,2},{3,11},{11,3},{4,12},{12,4},... | collective-permute-start | bytes 3538952 | tf_op jit(solution)/shard_map/ppermute | solution.py:284
  136.0 9.3 %collective-permute-start.19 = (bf16[384,1536]{1,0:T(8,128)(2,1)}, bf16[384,1536]{1,0:T(8,128)(2,1)}, u32[]{:S(2)}, u32[]{:S(2)}) collective-permute-start(bf16[384,1536]{1,0:T(8,128)(2,1)} %collective-permute-done.17.w3), channel_id=1, source_target_pairs={{0,8},{8,0},{1,9},{9,1},{2,10},{10,2},{3,11},{11,3},{4,12},{12,4},... | collective-permute-start | bytes 3538952 | tf_op jit(solution)/shard_map/ppermute | solution.py:284
  136.4 25.1 %all-to-all-start.3 = ((bf16[64,12,384]{2,1,0:T(8,128)(2,1)}), bf16[64,12,384]{2,1,0:T(8,128)(2,1)S(1)}, u32[]{:S(2)}, u32[]{:S(2)}) async-start(bf16[64,12,384]{2,1,0:T(8,128)(2,1)} %shard_map.74), calls=%async_computation.3 | async-start | bytes 1572864 | tf_op jit(solution)/shard_map/all_to_all | solution.py:407
  (8 other events, 11.5 us)

commit v8 on v7

--- a/solution.py
+++ b/solution.py
@@ -61,19 +61,24 @@
 
 
 def project_kernel(n, owner_ref, group_ref, *refs):
-    weights, blocks, outs = refs[:4], refs[4 : 4 + n], refs[4 + n :]
-    for j, out_ref in enumerate(outs):
+    weights, blocks, outs = refs[:4], refs[4 : 4 + n], refs[4 + n : -3]
+    held_weight, held, sems = refs[-3:]
+    pairs = []
+    for j in range(len(outs)):
         cols = pl.ds(pl.multiple_of(group_ref[j] * 384, 384), 384)
-        first = 0
-        for block in blocks:
-            count = block.shape[0]
-            total = None
-            for f in range(4):
-                rows = pl.ds(pl.multiple_of(owner_ref[f] * 384, 384), 384)
-                t = dot(block[:, rows], weights[f][:, cols])
-                total = t if total is None else total + t
-            out_ref[first : first + count, :] = total.astype(BF)
-            first += count
+        for f in range(4):
+            rows = pl.ds(pl.multiple_of(owner_ref[f] * 384, 384), 384)
+            pairs.append((weights[f].at[:, cols], held_weight.at[j, rows, :]))
+    at = [sum(b.shape[0] for b in blocks[:i]) for i in range(n)]
+    spots = [pl.ds(a, b.shape[0]) for a, b in zip(at, blocks)]
+    pairs += [(b, held.at[spot]) for b, spot in zip(blocks, spots)]
+    copies = fetch(pairs, sems)
+    for copy in copies[: -n]:
+        copy.wait()
+    for i in range(n):
+        copies[i - n].wait()
+        for j, out_ref in enumerate(outs):
+            out_ref[spots[i], :] = dot(held[spots[i], :], held_weight[j]).astype(BF)
 
 
 def attention_kernel(
@@ -108,57 +113,78 @@
     ones_row = jnp.where(lax.broadcasted_iota(jnp.int32, (HD, BQ), 0) == 0, 1.0, 0.0).astype(BF)
     nt = ((1,), (1,))
 
-    def step(i, carry):
-        contexts, ups, queries, inners = [], [], [], []
+    def scores(start, j, c):
+        r = slice(c * CH, (c + 1) * CH)
+        qa = jnp.concatenate([qt[:, pl.ds(start, BQ)], ones_row], axis=0)
+        s = dot(ka[r, :], qa)
+        s_ref[j, r, :] = s
+        return jnp.max(s.reshape(CH // 8, 8, BQ), axis=0)
+
+    def weigh(peak, j, c):
+        r = slice(c * CH, (c + 1) * CH)
+        e = jnp.exp(s_ref[j, r, :] - peak).astype(BF)
+        e_ref[j, r, :] = e
+        return dot(vt[:, r], e)
+
+    def finish(total, start):
+        cols = pl.ds(start, BQ)
+        inverse = 1.0 / total[HD : HD + 1]
+        context = total[0:HD] * inverse
+        up = (ut[:, cols].astype(F32) * inverse).astype(BF)
+        inner = jnp.sum(up.astype(F32) * context, axis=0, keepdims=True)
+        up = jnp.concatenate([zeros, up], axis=0)
+        query = jnp.concatenate([qt[:, cols], zeros], axis=0)
+        return context, up, query, inner
+
+    def back(state, j, c):
+        r = slice(c * CH, (c + 1) * CH)
+        context, up, query, inner = state
+        e = e_ref[j, r, :]
+        ds = (e.astype(F32) * (dot(kv[r, :], up) - inner)).astype(BF)
+        acc[r, :] += dot(ds, query, nt) + dot(e, up, nt)
+        return dot(kt[:, r], ds)
+
+    def write(block, context, dq):
+        first = pl.multiple_of(pos_ref[block] * BQ, BQ)
+        col = lax.broadcasted_iota(jnp.int32, (HD, BQ), 1) + first
+        context = jnp.where(col < length, context, 0.0)
+        both = jnp.concatenate([dq * 0.125, context], axis=0)
+        out_ref[pl.ds(first, BQ), 0:128] = both.T.astype(BF)
+
+    def add(a, b):
+        return b if a is None else a + b
+
+    def top(peak):
+        return jnp.max(peak, axis=0, keepdims=True)
+
+    def step(i, peak):
         starts = [pl.multiple_of((2 * i + j) * BQ, BQ) for j in range(2)]
-        for j in range(2):
-            cols = pl.ds(starts[j], BQ)
-            qh = qt[:, cols]
-            qa = jnp.concatenate([qh, ones_row], axis=0)
-            peak = None
-            for c in range(NC):
-                r = slice(c * CH, (c + 1) * CH)
-                s = dot(ka[r, :], qa)
-                s_ref[j, r, :] = s
-                t = jnp.max(s.reshape(CH // 8, 8, BQ), axis=0)
-                peak = t if peak is None else jnp.maximum(peak, t)
-            peak = jnp.max(peak, axis=0, keepdims=True)
-            total = None
-            for c in range(NC):
-                r = slice(c * CH, (c + 1) * CH)
-                e = jnp.exp(s_ref[j, r, :] - peak).astype(BF)
-                e_ref[j, r, :] = e
-                t = dot(vt[:, r], e)
-                total = t if total is None else total + t
-            inverse = 1.0 / total[HD : HD + 1]
-            context = total[0:HD] * inverse
-            up = (ut[:, cols].astype(F32) * inverse).astype(BF)
-            inner = jnp.sum(up.astype(F32) * context, axis=0, keepdims=True)
-            contexts.append(context)
-            ups.append(jnp.concatenate([zeros, up], axis=0))
-            queries.append(jnp.concatenate([qh, zeros], axis=0))
-            inners.append(inner)
-        dq = [None, None]
+        after = pl.multiple_of(lax.rem(2 * i + 2, SEQ) * BQ, BQ)
+        peak, peak1, total, total1 = top(peak), None, None, None
         for c in range(NC):
-            r = slice(c * CH, (c + 1) * CH)
-            total = acc[r, :]
-            for j in range(2):
-                dp = dot(kv[r, :], ups[j])
-                e = e_ref[j, r, :]
-                ds = (e.astype(F32) * (dp - inners[j])).astype(BF)
-                t = dot(kt[:, r], ds)
-                dq[j] = t if dq[j] is None else dq[j] + t
-                total = total + (dot(ds, queries[j], nt) + dot(e, ups[j], nt))
-            acc[r, :] = total
-        for j in range(2):
-            first = pl.multiple_of(pos_ref[2 * i + j] * BQ, BQ)
-            col = lax.broadcasted_iota(jnp.int32, (HD, BQ), 1) + first
-            context = jnp.where(col < length, contexts[j], 0.0)
-            both = jnp.concatenate([dq[j] * 0.125, context], axis=0)
-            out_ref[pl.ds(first, BQ), 0:128] = both.T.astype(BF)
-        return carry
-
-    lax.fori_loop(0, T // BQ // 2, step, 0)
+            t = scores(starts[1], 1, c)
+            peak1 = t if c == 0 else jnp.maximum(peak1, t)
+            total = add(total, weigh(peak, 0, c))
+        state = finish(total, starts[0])
+        peak1, dq = top(peak1), None
+        for c in range(NC):
+            total1 = add(total1, weigh(peak1, 1, c))
+            dq = add(dq, back(state, 0, c))
+        state1 = finish(total1, starts[1])
+        write(2 * i, state[0], dq)
+        dq = None
+        for c in range(NC):
+            t = scores(after, 0, c)
+            peak = t if c == 0 else jnp.maximum(peak, t)
+            dq = add(dq, back(state1, 1, c))
+        write(2 * i + 1, state1[0], dq)
+        return peak
+
+    peak = None
+    for c in range(NC):
+        t = scores(0, 0, c)
+        peak = t if c == 0 else jnp.maximum(peak, t)
+    lax.fori_loop(0, SEQ // 2, step, peak)
     for b in range(SEQ):
         rows = pl.ds(pl.multiple_of(pos_ref[b] * BQ, BQ), BQ)
         out_ref[rows, 128:256] = acc[b * BQ : (b + 1) * BQ, :].astype(BF)
@@ -336,7 +362,12 @@
         return call(
             functools.partial(project_kernel, len(rows)),
             (shape((height, 384)),) * count,
-            [SM, SM] + [VM] * (4 + len(rows)),
+            [SM, SM] + [ANY] * (4 + len(rows)),
+            scratch=[
+                pltpu.VMEM((count, D, 384), BF),
+                pltpu.VMEM((height, D), BF),
+                pltpu.SemaphoreType.DMA((4 * count + len(rows),)),
+            ],
         )(owners, groups, *columns, *rows)
 
     here = me // 4

time: 165 us -> 163 us (0.988)
  Pallas kernels: 76.7 us -> 74.3 us
    pallas_call x2, Pallas kernels: 37.4 us -> 34.3 us  [attend(): call(functools.partial(attention_kernel, head), shape((T, 256)), [SM, SM]...]
  transfers between devices with their start and end apart: 24 -> 24, of which waited for: 4 -> 4; matrix products, arithmetic and copies ran while one was open for 5% -> 5% of each run, Pallas kernels for 43% -> 42%
where the time goes in v8:
time: 163 us; the launch traced here: 162 us
  Pallas kernels  74.3 us (46%)
  starting transfers between devices  45.8 us (28%)
  waiting for transfers between devices  28.5 us (17%)
  local copies, waits for them, and re-layouts  11.2 us (7%)
    pallas_call x2, Pallas kernels, attend(): call(functools.partial(attention_kernel, head), shape((T, 256)), [SM, SM]...  34.3 us
    ppermute x11, starting transfers between devices, send(): return lax.ppermute(v, 'seq', way)  15.2 us
    all_to_all x1, waiting for transfers between devices, body(): lax.all_to_all(tie((upstream, normed))[0], 'seq', 0, 0, tiled=True)  14.8 us
    pallas_call x3, Pallas kernels, project(): call(functools.partial(project_kernel, len(rows)), (shape((height, 384)),...  13.9 us
    pallas_call x1, Pallas kernels, body(): call(input_gradient_kernel, (shape((ROWS, 1024)), shape((ROWS, D), F32)),...  9.59 us
    all_to_all x2, starting transfers between devices, send_back(): lax.all_to_all(grads.reshape(SEQ, ROWS, 256), 'seq', 0, 0, tiled=True)  9.14 us
    all_to_all x1, starting transfers between devices, body(): partial = lax.all_to_all(partial, ('dp', 'zh', 'seq'), 0, 0, tiled=True)  8.85 us
    pallas_call x1, Pallas kernels, body(): call(weight_gradient_kernel, (shape((768, 384), F32), shape((768, 384))),...  8.44 us
  transfers between devices with their start and end apart: 24, of which 4 were waited for; matrix products, arithmetic and copies ran while one was open for 5% of the time, Pallas kernels for 42%

profile of v8, /device:TPU:0, one launch (start us, length us, event | category | flops | bytes accessed | tf_op | source)
XLA Modules:
  0.0 162.1 jit_solution(12794279299463408146)
XLA Ops:
  0.7 3.5 %shard_map.67 = (bf16[256,1536]{1,0:T(8,128)(2,1)}, bf16[384,768]{1,0:T(8,128)(2,1)}) custom-call(s32[1]{0:T(128)} %bitcast.y_ref, bf16[256,1536]{1,0:T(8,128)(2,1)} %bitcast.29, bf16[384,3072]{1,0:T(8,128)(2,1)} %w0.1), custom_call_target="tpu_custom_call" | custom-call | bytes 1048576 | tf_op jit(solution)/shard_map/pallas_call | solution.py:337
  4.1 2.1 %collective-permute-start.1 = (bf16[256,1536]{1,0:T(8,128)(2,1)}, bf16[256,1536]{1,0:T(8,128)(2,1)}, u32[]{:S(2)}, u32[]{:S(2)}) collective-permute-start(bf16[256,1536]{1,0:T(8,128)(2,1)} %get-tuple-element.47.refs_4_.refs_0_), channel_id=1, source_target_pairs={{0,4},{1,5},{2,6},{3,7},{4,0},{5,1},{6,2},{7,3},{8,12},{9,13},{10,... | collective-permute-start | bytes 2359304 | tf_op jit(solution)/shard_map/ppermute | solution.py:306
  6.2 3.0 %collective-permute-start.2 = (bf16[256,1536]{1,0:T(8,128)(2,1)}, bf16[256,1536]{1,0:T(8,128)(2,1)}, u32[]{:S(2)}, u32[]{:S(2)}) collective-permute-start(bf16[256,1536]{1,0:T(8,128)(2,1)} %get-tuple-element.47.refs_4_.refs_0_), channel_id=1, source_target_pairs={{0,3},{1,0},{2,1},{3,2},{4,7},{5,4},{6,5},{7,6},{8,11},{9,8},{10,9... | collective-permute-start | bytes 2359304 | tf_op jit(solution)/shard_map/ppermute | solution.py:306
  9.2 2.5 %collective-permute-start.4 = (bf16[384,768]{1,0:T(8,128)(2,1)}, bf16[384,768]{1,0:T(8,128)(2,1)S(1)}, u32[]{:S(2)}, u32[]{:S(2)}) collective-permute-start(bf16[384,768]{1,0:T(8,128)(2,1)} %get-tuple-element.46.refs_0_), channel_id=1, source_target_pairs={{0,20},{1,21},{2,22},{3,23},{4,16},{5,17},{6,18},{7,19},{16,4},{17... | collective-permute-start | bytes 1769480 | tf_op jit(solution)/shard_map/ppermute | solution.py:314
  12.7 5.0 %all-to-all-start = ((bf16[8,256,128]{2,1,0:T(8,128)(2,1)}), bf16[8,256,128]{2,1,0:T(8,128)(2,1)}, u32[]{:S(2)}, u32[]{:S(2)}) async-start(bf16[8,256,128]{2,1,0:T(8,128)(2,1)} %bitcast.31), calls=%async_computation | async-start | bytes 1048576 | tf_op jit(solution)/shard_map/all_to_all | solution.py:351
  19.0 1.1 constant_dynamic-slice_fusion
  20.1 14.8 %all-to-all-done = bf16[8,256,128]{2,1,0:T(8,128)(2,1)} async-done(((bf16[8,256,128]{2,1,0:T(8,128)(2,1)}), bf16[8,256,128]{2,1,0:T(8,128)(2,1)}, u32[]{:S(2)}, u32[]{:S(2)}) %all-to-all-start) | async-done | bytes 524320 | tf_op jit(solution)/shard_map/all_to_all | solution.py:351
  35.0 2.1 %slice.6 = bf16[128,1536]{1,0:T(8,128)(2,1)} slice(bf16[256,1536]{1,0:T(8,128)(2,1)} %collective-permute-done.3.refs_4_.refs_5_.refs_1_), slice={[0:128], [0:1536]} | slice | bytes 786432 | tf_op jit(solution)/shard_map/slice | solution.py:357
  37.1 1.8 %slice.7 = bf16[128,1536]{1,0:T(8,128)(2,1)} slice(bf16[256,1536]{1,0:T(8,128)(2,1)} %collective-permute-done.2.refs_5_.refs_6_.refs_2_), slice={[128:256], [0:1536]} | slice | bytes 786432 | tf_op jit(solution)/shard_map/slice | solution.py:357
  38.9 3.2 %collective-permute-start.7 = (bf16[128,1536]{1,0:T(8,128)(2,1)}, bf16[128,1536]{1,0:T(8,128)(2,1)}, u32[]{:S(2)}, u32[]{:S(2)}) collective-permute-start(bf16[128,1536]{1,0:T(8,128)(2,1)} %slice.7), channel_id=1, source_target_pairs={{0,3},{1,0},{2,1},{3,2},{4,7},{5,4},{6,5},{7,6},{8,11},{9,8},{10,9... | collective-permute-start | bytes 1179656 | tf_op jit(solution)/shard_map/ppermute | solution.py:306
  42.8 4.2 %shard_map.68 = bf16[512,384]{1,0:T(8,128)(2,1)} custom-call(s32[5]{0:T(128)} %stack.72.owner_ref.pos_ref, s32[2]{0:T(128)} %pad_add_fusion.group_ref, bf16[384,768]{1,0:T(8,128)(2,1)} %get-tuple-element.46.refs_0_, bf16[384,768]{1,0:T(8,128)(2,1)} %copy-done.1, bf16[384,768]{1,0:T(8,128)(2,1)} %copy-done.2, ...), custom_call_target="tpu_custom_call" | custom-call | bytes 1048576 | tf_op jit(solution)/shard_map/pallas_call | solution.py:362
  46.9 1.7 %collective-permute-start.8 = (bf16[512,384]{1,0:T(8,128)(2,1)}, bf16[512,384]{1,0:T(8,128)(2,1)}, u32[]{:S(2)}, u32[]{:S(2)}) collective-permute-start(bf16[512,384]{1,0:T(8,128)(2,1)} %shard_map.68), channel_id=1, source_target_pairs={{0,4},{1,5},{2,6},{3,7},{4,0},{5,1},{6,2},{7,3},{8,12},{9,13},{10,... | collective-permute-start | bytes 1179656 | tf_op jit(solution)/shard_map/ppermute | solution.py:306
  48.7 2.5 %collective-permute-start.14 = (bf16[384,1536]{1,0:T(8,128)(2,1)}, bf16[384,1536]{1,0:T(8,128)(2,1)S(1)}, u32[]{:S(2)}, u32[]{:S(2)}) collective-permute-start(bf16[384,1536]{1,0:T(8,128)(2,1)} %constant_dynamic-slice_fusion), channel_id=1, source_target_pairs={{0,20},{1,21},{2,22},{3,23},{4,16},{5,17},{6,18},{7,19},{16,4},{17... | collective-permute-start | bytes 3538952 | tf_op jit(solution)/shard_map/ppermute | solution.py:314
  51.8 5.4 %shard_map.69.kept_ref = bf16[1024,384]{1,0:T(8,128)(2,1)} custom-call(s32[5]{0:T(128)} %stack.72.owner_ref.pos_ref, s32[2]{0:T(128)} %rev.3.group_ref, bf16[384,768]{1,0:T(8,128)(2,1)} %get-tuple-element.46.refs_0_, bf16[384,768]{1,0:T(8,128)(2,1)} %copy-done.1, bf16[384,768]{1,0:T(8,128)(2,1)} %copy-done.2, ...), custom_call_target="tpu_custom_call" | custom-call | bytes 1048576 | tf_op jit(solution)/shard_map/pallas_call | solution.py:362
  57.3 4.3 %shard_map.70 = (bf16[256,384]{1,0:T(8,128)(2,1)}, bf16[256,384]{1,0:T(8,128)(2,1)}) custom-call(s32[5]{0:T(128)} %stack.72.owner_ref.pos_ref, s32[2]{0:T(128)} %pad_add_fusion.group_ref, bf16[384,768]{1,0:T(8,128)(2,1)} %get-tuple-element.46.refs_0_, bf16[384,768]{1,0:T(8,128)(2,1)} %copy-done.1, bf16[384,768]{1,0:T(8,128)(2,1)} %copy-done.2, ...), custom_call_target="tpu_custom_call" | custom-call | bytes 1048576 | tf_op jit(solution)/shard_map/pallas_call | solution.py:362
  61.7 2.0 %collective-permute-start.9 = (bf16[256,1536]{1,0:T(8,128)(2,1)}, bf16[256,1536]{1,0:T(8,128)(2,1)S(1)}, u32[]{:S(2)}, u32[]{:S(2)}) collective-permute-start(bf16[256,1536]{1,0:T(8,128)(2,1)} %collective-permute-done.1.refs_7_.refs_5_), channel_id=1, source_target_pairs={{0,1},{1,2},{2,3},{3,0},{4,5},{5,6},{6,7},{7,4},{8,9},{9,10},{10,1... | collective-permute-start | bytes 2359304 | tf_op jit(solution)/shard_map/ppermute | solution.py:306
  63.7 1.0 collective-permute-start.11
  64.7 4.9 %collective-permute-done.11.last_ref = bf16[256,384]{1,0:T(8,128)(2,1)S(1)} collective-permute-done((bf16[256,384]{1,0:T(8,128)(2,1)}, bf16[256,384]{1,0:T(8,128)(2,1)S(1)}, u32[]{:S(2)}, u32[]{:S(2)}) %collective-permute-start.11) | collective-permute-done | bytes 196640 | tf_op jit(solution)/shard_map/ppermute | solution.py:306
  70.6 1.0 collective-permute-start.13
  72.3 17.2 %shard_map.71.first_ref = bf16[2048,256]{1,0:T(8,128)(2,1)} custom-call(s32[9]{0:T(128)} %stack.66.pos_ref, s32[1]{0:T(128)S(6)} %copy.11.len_ref, bf16[1024,384]{1,0:T(8,128)(2,1)} %shard_map.69.kept_ref, bf16[256,384]{1,0:T(8,128)(2,1)} %get-tuple-element.63.far_ref, bf16[512,384]{1,0:T(8,128)(2,1)} %collective-permute-done.8.other_ref, ...), custom_call_target="tpu_custom_call" | custom-call | flops 1000000000 | bytes 1048576 | tf_op jit(solution)/shard_map/pallas_call | solution.py:388
  89.6 1.1 copy-done.13
  91.2 3.6 %all-to-all-start.1 = ((bf16[8,256,256]{2,1,0:T(8,128)(2,1)}), bf16[8,256,256]{2,1,0:T(8,128)(2,1)S(1)}, u32[]{:S(2)}, u32[]{:S(2)}) async-start(bf16[8,256,256]{2,1,0:T(8,128)(2,1)} %bitcast.33), calls=%async_computation.1 | async-start | bytes 2097152 | tf_op jit(solution)/shard_map/all_to_all | solution.py:408
  94.8 1.6 collective-permute-start.17
  96.4 17.2 %shard_map.72.second_ref = bf16[2048,256]{1,0:T(8,128)(2,1)} custom-call(s32[9]{0:T(128)} %stack.66.pos_ref, s32[1]{0:T(128)S(6)} %copy.11.len_ref, bf16[1024,384]{1,0:T(8,128)(2,1)} %shard_map.69.kept_ref, bf16[256,384]{1,0:T(8,128)(2,1)} %get-tuple-element.63.far_ref, bf16[512,384]{1,0:T(8,128)(2,1)} %collective-permute-done.8.other_ref, ...), custom_call_target="tpu_custom_call" | custom-call | flops 10000000000 | bytes 1048576 | tf_op jit(solution)/shard_map/pallas_call | solution.py:388
  113.6 5.6 %all-to-all-start.2 = ((bf16[8,256,256]{2,1,0:T(8,128)(2,1)}), bf16[8,256,256]{2,1,0:T(8,128)(2,1)S(1)}, u32[]{:S(2)}, u32[]{:S(2)}) async-start(bf16[8,256,256]{2,1,0:T(8,128)(2,1)} %bitcast.34), calls=%async_computation.2 | async-start | bytes 2097152 | tf_op jit(solution)/shard_map/all_to_all | solution.py:408
  119.1 8.4 %shard_map.73 = (f32[768,384]{1,0:T(8,128)}, bf16[768,384]{1,0:T(8,128)(2,1)}) custom-call(s32[9]{0:T(128)} %stack.66.pos_ref, bf16[2048,256]{1,0:T(8,128)(2,1)} %shard_map.71.first_ref, bf16[2048,256]{1,0:T(8,128)(2,1)} %shard_map.72.second_ref, bf16[256,1536]{1,0:T(8,128)(2,1)} %get-tuple-element.47.refs_4_.refs_0_, ...), custom_call_target="tpu_custom_call" | custom-call | flops 2415919104 | bytes 1048576 | tf_op jit(solution)/shard_map/pallas_call | solution.py:421
  127.9 2.2 %collective-permute-done.16.got_ref = bf16[768,384]{1,0:T(8,128)(2,1)S(1)} collective-permute-done((bf16[768,384]{1,0:T(8,128)(2,1)}, bf16[768,384]{1,0:T(8,128)(2,1)S(1)}, u32[]{:S(2)}, u32[]{:S(2)}) %collective-permute-start.16) | collective-permute-done | bytes 589856 | tf_op jit(solution)/shard_map/ppermute | solution.py:310
  131.0 2.6 %shard_map.74 = bf16[64,12,384]{2,1,0:T(8,128)(2,1)} custom-call(f32[768,384]{1,0:T(8,128)} %get-tuple-element.75.keep_ref, bf16[768,384]{1,0:T(8,128)(2,1)} %copy-done.8), custom_call_target="tpu_custom_call" | custom-call | bytes 1048576 | tf_op jit(solution)/shard_map/pallas_call | solution.py:434
  134.2 8.8 %all-to-all-start.3 = ((bf16[64,12,384]{2,1,0:T(8,128)(2,1)}), bf16[64,12,384]{2,1,0:T(8,128)(2,1)S(1)}, u32[]{:S(2)}, u32[]{:S(2)}) async-start(bf16[64,12,384]{2,1,0:T(8,128)(2,1)} %shard_map.74), calls=%async_computation.3 | async-start | bytes 1572864 | tf_op jit(solution)/shard_map/all_to_all | solution.py:438
  143.1 9.6 %shard_map.75 = (bf16[256,1024]{1,0:T(8,128)(2,1)}, f32[256,1536]{1,0:T(8,128)}) custom-call(s32[5]{0:T(128)} %stack.72.owner_ref.pos_ref, bf16[8,256,256]{2,1,0:T(8,128)(2,1)} %copy-done.3, bf16[8,256,256]{2,1,0:T(8,128)(2,1)} %copy-done.4, bf16[384,3072]{1,0:T(8,128)(2,1)} %w0.1, bf16[384,3072]{1,0:T(8,128)(2,1)} %collective-permute-done.15.w1, ...), custom_call_target="tpu_custom_call" | custom-call | flops 2415919104 | bytes 1048576 | tf_op jit(solution)/shard_map/pallas_call | solution.py:439
  152.7 6.5 %all-to-all-done.3.parts_ref = bf16[64,12,384]{2,1,0:T(8,128)(2,1)S(1)} async-done(((bf16[64,12,384]{2,1,0:T(8,128)(2,1)}), bf16[64,12,384]{2,1,0:T(8,128)(2,1)S(1)}, u32[]{:S(2)}, u32[]{:S(2)}) %all-to-all-start.3) | async-done | bytes 589856 | tf_op jit(solution)/shard_map/all_to_all | solution.py:438
  160.1 1.9 %shard_map.76 = f32[12,3072]{1,0:T(8,128)} custom-call(bf16[64,12,384]{2,1,0:T(8,128)(2,1)} %copy-done.5), custom_call_target="tpu_custom_call" | custom-call | bytes 1048576 | tf_op jit(solution)/shard_map/pallas_call | solution.py:451
  (67 shorter events, 8.1 us)
Async XLA Ops:
  0.6 11.1 %copy-start.9 = (bf16[1,256,1024]{2,1,0:T(8,128)(2,1)S(1)}, bf16[1,256,1024]{2,1,0:T(8,128)(2,1)}, u32[]{:S(2)}) copy-start(bf16[1,256,1024]{2,1,0:T(8,128)(2,1)} %param.7) | copy-start | bytes 1572868
  4.1 30.8 %collective-permute-start.1 = (bf16[256,1536]{1,0:T(8,128)(2,1)}, bf16[256,1536]{1,0:T(8,128)(2,1)}, u32[]{:S(2)}, u32[]{:S(2)}) collective-permute-start(bf16[256,1536]{1,0:T(8,128)(2,1)} %get-tuple-element.47.refs_4_.refs_0_), channel_id=1, source_target_pairs={{0,4},{1,5},{2,6},{3,7},{4,0},{5,1},{6,2},{7,3},{8,12},{9,13},{10,... | collective-permute-start | bytes 2359304 | tf_op jit(solution)/shard_map/ppermute | solution.py:306
  6.2 28.7 %collective-permute-start.2 = (bf16[256,1536]{1,0:T(8,128)(2,1)}, bf16[256,1536]{1,0:T(8,128)(2,1)}, u32[]{:S(2)}, u32[]{:S(2)}) collective-permute-start(bf16[256,1536]{1,0:T(8,128)(2,1)} %get-tuple-element.47.refs_4_.refs_0_), channel_id=1, source_target_pairs={{0,3},{1,0},{2,1},{3,2},{4,7},{5,4},{6,5},{7,6},{8,11},{9,8},{10,9... | collective-permute-start | bytes 2359304 | tf_op jit(solution)/shard_map/ppermute | solution.py:306
  9.2 25.7 %collective-permute-start.3 = (bf16[256,1536]{1,0:T(8,128)(2,1)}, bf16[256,1536]{1,0:T(8,128)(2,1)}, u32[]{:S(2)}, u32[]{:S(2)}) collective-permute-start(bf16[256,1536]{1,0:T(8,128)(2,1)} %get-tuple-element.47.refs_4_.refs_0_), channel_id=1, source_target_pairs={{0,1},{1,2},{2,3},{3,0},{4,5},{5,6},{6,7},{7,4},{8,9},{9,10},{10,1... | collective-permute-start | bytes 2359304 | tf_op jit(solution)/shard_map/ppermute | solution.py:306
  9.2 25.7 %collective-permute-start = (bf16[384,768]{1,0:T(8,128)(2,1)}, bf16[384,768]{1,0:T(8,128)(2,1)S(1)}, u32[]{:S(2)}, u32[]{:S(2)}) collective-permute-start(bf16[384,768]{1,0:T(8,128)(2,1)} %get-tuple-element.46.refs_0_), channel_id=1, source_target_pairs={{0,8},{8,0},{1,9},{9,1},{2,10},{10,2},{3,11},{11,3},{4,12},{12,4},... | collective-permute-start | bytes 1769480 | tf_op jit(solution)/shard_map/ppermute | solution.py:310
  9.2 25.7 %collective-permute-start.4 = (bf16[384,768]{1,0:T(8,128)(2,1)}, bf16[384,768]{1,0:T(8,128)(2,1)S(1)}, u32[]{:S(2)}, u32[]{:S(2)}) collective-permute-start(bf16[384,768]{1,0:T(8,128)(2,1)} %get-tuple-element.46.refs_0_), channel_id=1, source_target_pairs={{0,20},{1,21},{2,22},{3,23},{4,16},{5,17},{6,18},{7,19},{16,4},{17... | collective-permute-start | bytes 1769480 | tf_op jit(solution)/shard_map/ppermute | solution.py:314
  11.8 7.2 %copy-start = (bf16[384,3072]{1,0:T(8,128)(2,1)S(1)}, bf16[384,3072]{1,0:T(8,128)(2,1)}, u32[]{:S(2)}) copy-start(bf16[384,3072]{1,0:T(8,128)(2,1)} %w0.1) | copy-start | bytes 7077892
  12.7 22.1 %all-to-all-start = ((bf16[8,256,128]{2,1,0:T(8,128)(2,1)}), bf16[8,256,128]{2,1,0:T(8,128)(2,1)}, u32[]{:S(2)}, u32[]{:S(2)}) async-start(bf16[8,256,128]{2,1,0:T(8,128)(2,1)} %bitcast.31), calls=%async_computation | async-start | bytes 1048576 | tf_op jit(solution)/shard_map/all_to_all | solution.py:351
  34.9 7.9 %copy-start.1 = (bf16[384,768]{1,0:T(8,128)(2,1)}, bf16[384,768]{1,0:T(8,128)(2,1)S(1)}, u32[]{:S(2)}) copy-start(bf16[384,768]{1,0:T(8,128)(2,1)S(1)} %collective-permute-done.refs_1_) | copy-start | bytes 1769476
  34.9 7.8 %copy-start.2 = (bf16[384,768]{1,0:T(8,128)(2,1)}, bf16[384,768]{1,0:T(8,128)(2,1)S(1)}, u32[]{:S(2)}) copy-start(bf16[384,768]{1,0:T(8,128)(2,1)S(1)} %collective-permute-done.4.refs_2_) | copy-start | bytes 1769476
  34.9 7.8 %collective-permute-start.5 = (bf16[384,768]{1,0:T(8,128)(2,1)S(1)}, bf16[384,768]{1,0:T(8,128)(2,1)}, u32[]{:S(2)}, u32[]{:S(2)}) collective-permute-start(bf16[384,768]{1,0:T(8,128)(2,1)S(1)} %collective-permute-done.4.refs_2_), channel_id=1, source_target_pairs={{0,8},{8,0},{1,9},{9,1},{2,10},{10,2},{3,11},{11,3},{4,12},{12,4},... | collective-permute-start | bytes 1769480 | tf_op jit(solution)/shard_map/ppermute | solution.py:310
  37.1 20.2 %collective-permute-start.6 = (bf16[128,1536]{1,0:T(8,128)(2,1)}, bf16[128,1536]{1,0:T(8,128)(2,1)}, u32[]{:S(2)}, u32[]{:S(2)}) collective-permute-start(bf16[128,1536]{1,0:T(8,128)(2,1)} %slice.6), channel_id=1, source_target_pairs={{0,1},{1,2},{2,3},{3,0},{4,5},{5,6},{6,7},{7,4},{8,9},{9,10},{10,1... | collective-permute-start | bytes 1179656 | tf_op jit(solution)/shard_map/ppermute | solution.py:306
  38.9 18.4 %collective-permute-start.7 = (bf16[128,1536]{1,0:T(8,128)(2,1)}, bf16[128,1536]{1,0:T(8,128)(2,1)}, u32[]{:S(2)}, u32[]{:S(2)}) collective-permute-start(bf16[128,1536]{1,0:T(8,128)(2,1)} %slice.7), channel_id=1, source_target_pairs={{0,3},{1,0},{2,1},{3,2},{4,7},{5,4},{6,5},{7,6},{8,11},{9,8},{10,9... | collective-permute-start | bytes 1179656 | tf_op jit(solution)/shard_map/ppermute | solution.py:306
  42.7 8.5 %copy-start.10 = (s32[2]{0:T(128)S(1)}, s32[2]{0:T(128)}, u32[]{:S(2)}) copy-start(s32[2]{0:T(128)} %pad_add_fusion.group_ref) | copy-start | bytes 28
  46.9 14.7 %collective-permute-start.8 = (bf16[512,384]{1,0:T(8,128)(2,1)}, bf16[512,384]{1,0:T(8,128)(2,1)}, u32[]{:S(2)}, u32[]{:S(2)}) collective-permute-start(bf16[512,384]{1,0:T(8,128)(2,1)} %shard_map.68), channel_id=1, source_target_pairs={{0,4},{1,5},{2,6},{3,7},{4,0},{5,1},{6,2},{7,3},{8,12},{9,13},{10,... | collective-permute-start | bytes 1179656 | tf_op jit(solution)/shard_map/ppermute | solution.py:306
  48.7 40.8 %collective-permute-start.14 = (bf16[384,1536]{1,0:T(8,128)(2,1)}, bf16[384,1536]{1,0:T(8,128)(2,1)S(1)}, u32[]{:S(2)}, u32[]{:S(2)}) collective-permute-start(bf16[384,1536]{1,0:T(8,128)(2,1)} %constant_dynamic-slice_fusion), channel_id=1, source_target_pairs={{0,20},{1,21},{2,22},{3,23},{4,16},{5,17},{6,18},{7,19},{16,4},{17... | collective-permute-start | bytes 3538952 | tf_op jit(solution)/shard_map/ppermute | solution.py:314
  61.6 27.9 %collective-permute-start.10 = (bf16[256,1536]{1,0:T(8,128)(2,1)}, bf16[256,1536]{1,0:T(8,128)(2,1)S(1)}, u32[]{:S(2)}, u32[]{:S(2)}) collective-permute-start(bf16[256,1536]{1,0:T(8,128)(2,1)} %collective-permute-done.1.refs_7_.refs_5_), channel_id=1, source_target_pairs={{0,3},{1,0},{2,1},{3,2},{4,7},{5,4},{6,5},{7,6},{8,11},{9,8},{10,9... | collective-permute-start | bytes 2359304 | tf_op jit(solution)/shard_map/ppermute | solution.py:306
  61.7 27.8 %collective-permute-start.9 = (bf16[256,1536]{1,0:T(8,128)(2,1)}, bf16[256,1536]{1,0:T(8,128)(2,1)S(1)}, u32[]{:S(2)}, u32[]{:S(2)}) collective-permute-start(bf16[256,1536]{1,0:T(8,128)(2,1)} %collective-permute-done.1.refs_7_.refs_5_), channel_id=1, source_target_pairs={{0,1},{1,2},{2,3},{3,0},{4,5},{5,6},{6,7},{7,4},{8,9},{9,10},{10,1... | collective-permute-start | bytes 2359304 | tf_op jit(solution)/shard_map/ppermute | solution.py:306
  63.7 5.9 %collective-permute-start.11 = (bf16[256,384]{1,0:T(8,128)(2,1)}, bf16[256,384]{1,0:T(8,128)(2,1)S(1)}, u32[]{:S(2)}, u32[]{:S(2)}) collective-permute-start(bf16[256,384]{1,0:T(8,128)(2,1)} %get-tuple-element.59), channel_id=1, source_target_pairs={{0,4},{1,5},{2,6},{3,7},{4,0},{5,1},{6,2},{7,3},{8,12},{9,13},{10,... | collective-permute-start | bytes 589832 | tf_op jit(solution)/shard_map/ppermute | solution.py:306
  69.6 2.7 %copy-start.15 = (bf16[256,384]{1,0:T(8,128)(2,1)}, bf16[256,384]{1,0:T(8,128)(2,1)S(1)}, u32[]{:S(2)}) copy-start(bf16[256,384]{1,0:T(8,128)(2,1)S(1)} %collective-permute-done.11.last_ref) | copy-start | bytes 589828
  69.6 19.9 %collective-permute-start.12 = (bf16[128,1536]{1,0:T(8,128)(2,1)}, bf16[128,1536]{1,0:T(8,128)(2,1)S(1)}, u32[]{:S(2)}, u32[]{:S(2)}) collective-permute-start(bf16[128,1536]{1,0:T(8,128)(2,1)} %collective-permute-done.6.refs_4_.refs_3_), channel_id=1, source_target_pairs={{0,4},{1,5},{2,6},{3,7},{4,0},{5,1},{6,2},{7,3},{8,12},{9,13},{10,... | collective-permute-start | bytes 1179656 | tf_op jit(solution)/shard_map/ppermute | solution.py:306
  70.6 18.8 %collective-permute-start.13 = (bf16[128,1536]{1,0:T(8,128)(2,1)}, bf16[128,1536]{1,0:T(8,128)(2,1)S(1)}, u32[]{:S(2)}, u32[]{:S(2)}) collective-permute-start(bf16[128,1536]{1,0:T(8,128)(2,1)} %collective-permute-done.7.refs_5_.refs_4_), channel_id=1, source_target_pairs={{0,4},{1,5},{2,6},{3,7},{4,0},{5,1},{6,2},{7,3},{8,12},{9,13},{10,... | collective-permute-start | bytes 1179656 | tf_op jit(solution)/shard_map/ppermute | solution.py:306
  89.5 24.0 %collective-permute-start.15 = (bf16[384,3072]{1,0:T(8,128)(2,1)S(1)}, bf16[384,3072]{1,0:T(8,128)(2,1)}, u32[]{:S(2)}, u32[]{:S(2)}) collective-permute-start(bf16[384,3072]{1,0:T(8,128)(2,1)S(1)} %copy-done), channel_id=1, source_target_pairs={{0,8},{8,0},{1,9},{9,1},{2,10},{10,2},{3,11},{11,3},{4,12},{12,4},... | collective-permute-start | bytes 7077896 | tf_op jit(solution)/shard_map/ppermute | solution.py:310
  91.2 22.3 %all-to-all-start.1 = ((bf16[8,256,256]{2,1,0:T(8,128)(2,1)}), bf16[8,256,256]{2,1,0:T(8,128)(2,1)S(1)}, u32[]{:S(2)}, u32[]{:S(2)}) async-start(bf16[8,256,256]{2,1,0:T(8,128)(2,1)} %bitcast.33), calls=%async_computation.1 | async-start | bytes 2097152 | tf_op jit(solution)/shard_map/all_to_all | solution.py:408
  94.8 38.8 %collective-permute-start.17 = (bf16[384,1536]{1,0:T(8,128)(2,1)}, bf16[384,1536]{1,0:T(8,128)(2,1)}, u32[]{:S(2)}, u32[]{:S(2)}) collective-permute-start(bf16[384,1536]{1,0:T(8,128)(2,1)} %copy-done.6), channel_id=1, source_target_pairs={{0,32},{32,0},{64,96},{96,64},{1,33},{33,1},{65,97},{97,65},{2,34}... | collective-permute-start | bytes 3538952 | tf_op jit(solution)/shard_map/ppermute | solution.py:414
  113.5 14.0 %copy-start.3 = (bf16[8,256,256]{2,1,0:T(8,128)(2,1)}, bf16[8,256,256]{2,1,0:T(8,128)(2,1)S(1)}, u32[]{:S(2)}) copy-start(bf16[8,256,256]{2,1,0:T(8,128)(2,1)S(1)} %all-to-all-done.1.first_ref) | copy-start | bytes 3145732
  113.6 20.0 %all-to-all-start.2 = ((bf16[8,256,256]{2,1,0:T(8,128)(2,1)}), bf16[8,256,256]{2,1,0:T(8,128)(2,1)S(1)}, u32[]{:S(2)}, u32[]{:S(2)}) async-start(bf16[8,256,256]{2,1,0:T(8,128)(2,1)} %bitcast.34), calls=%async_computation.2 | async-start | bytes 2097152 | tf_op jit(solution)/shard_map/all_to_all | solution.py:408
  127.6 2.5 %collective-permute-start.16 = (bf16[768,384]{1,0:T(8,128)(2,1)}, bf16[768,384]{1,0:T(8,128)(2,1)S(1)}, u32[]{:S(2)}, u32[]{:S(2)}) collective-permute-start(bf16[768,384]{1,0:T(8,128)(2,1)} %get-tuple-element.76), channel_id=1, source_target_pairs={{0,8},{8,0},{1,9},{9,1},{2,10},{10,2},{3,11},{11,3},{4,12},{12,4},... | collective-permute-start | bytes 1769480 | tf_op jit(solution)/shard_map/ppermute | solution.py:310
  133.6 9.5 %copy-start.4 = (bf16[8,256,256]{2,1,0:T(8,128)(2,1)}, bf16[8,256,256]{2,1,0:T(8,128)(2,1)S(1)}, u32[]{:S(2)}) copy-start(bf16[8,256,256]{2,1,0:T(8,128)(2,1)S(1)} %all-to-all-done.2.second_ref) | copy-start | bytes 3145732
  133.6 9.4 %collective-permute-start.18 = (bf16[384,1536]{1,0:T(8,128)(2,1)S(1)}, bf16[384,1536]{1,0:T(8,128)(2,1)}, u32[]{:S(2)}, u32[]{:S(2)}) collective-permute-start(bf16[384,1536]{1,0:T(8,128)(2,1)S(1)} %copy-done.7), channel_id=1, source_target_pairs={{0,8},{8,0},{1,9},{9,1},{2,10},{10,2},{3,11},{11,3},{4,12},{12,4},... | collective-permute-start | bytes 3538952 | tf_op jit(solution)/shard_map/ppermute | solution.py:310
  133.8 9.2 %collective-permute-start.19 = (bf16[384,1536]{1,0:T(8,128)(2,1)}, bf16[384,1536]{1,0:T(8,128)(2,1)}, u32[]{:S(2)}, u32[]{:S(2)}) collective-permute-start(bf16[384,1536]{1,0:T(8,128)(2,1)} %collective-permute-done.17.w3), channel_id=1, source_target_pairs={{0,8},{8,0},{1,9},{9,1},{2,10},{10,2},{3,11},{11,3},{4,12},{12,4},... | collective-permute-start | bytes 3538952 | tf_op jit(solution)/shard_map/ppermute | solution.py:310
  134.2 25.0 %all-to-all-start.3 = ((bf16[64,12,384]{2,1,0:T(8,128)(2,1)}), bf16[64,12,384]{2,1,0:T(8,128)(2,1)S(1)}, u32[]{:S(2)}, u32[]{:S(2)}) async-start(bf16[64,12,384]{2,1,0:T(8,128)(2,1)} %shard_map.74), calls=%async_computation.3 | async-start | bytes 1572864 | tf_op jit(solution)/shard_map/all_to_all | solution.py:438
  (8 other events, 11.5 us)

commit v9 on v8

--- a/solution.py
+++ b/solution.py
@@ -17,7 +17,8 @@
 GW = 128
 EPS = 1e-05
 BQ = 256
-CH = 512
+AQ = 512
+CH = 256
 NC = T // CH
 VM = pl.BlockSpec(memory_space=pltpu.VMEM)
 SM = pl.BlockSpec(memory_space=pltpu.SMEM)
@@ -77,7 +78,7 @@
         copy.wait()
     for i in range(n):
         copies[i - n].wait()
-        for j, out_ref in enumerate(outs):
+        for j, out_ref in enumerate(outs[:2]):
             out_ref[spots[i], :] = dot(held[spots[i], :], held_weight[j]).astype(BF)
 
 
@@ -109,16 +110,16 @@
         u = jnp.where(row < length, up_ref[pl.ds(first, BQ), :].astype(F32), 0.0)
         ut[:, r] = u.T[hrows].astype(BF)
     acc[...] = jnp.zeros_like(acc)
-    zeros = jnp.zeros((HD, BQ), BF)
-    ones_row = jnp.where(lax.broadcasted_iota(jnp.int32, (HD, BQ), 0) == 0, 1.0, 0.0).astype(BF)
+    zeros = jnp.zeros((HD, AQ), BF)
+    ones_row = jnp.where(lax.broadcasted_iota(jnp.int32, (HD, AQ), 0) == 0, 1.0, 0.0).astype(BF)
     nt = ((1,), (1,))
 
     def scores(start, j, c):
         r = slice(c * CH, (c + 1) * CH)
-        qa = jnp.concatenate([qt[:, pl.ds(start, BQ)], ones_row], axis=0)
+        qa = jnp.concatenate([qt[:, pl.ds(start, AQ)], ones_row], axis=0)
         s = dot(ka[r, :], qa)
         s_ref[j, r, :] = s
-        return jnp.max(s.reshape(CH // 8, 8, BQ), axis=0)
+        return jnp.max(s.reshape(CH // 8, 8, AQ), axis=0)
 
     def weigh(peak, j, c):
         r = slice(c * CH, (c + 1) * CH)
@@ -127,7 +128,7 @@
         return dot(vt[:, r], e)
 
     def finish(total, start):
-        cols = pl.ds(start, BQ)
+        cols = pl.ds(start, AQ)
         inverse = 1.0 / total[HD : HD + 1]
         context = total[0:HD] * inverse
         up = (ut[:, cols].astype(F32) * inverse).astype(BF)
@@ -145,11 +146,13 @@
         return dot(kt[:, r], ds)
 
     def write(block, context, dq):
-        first = pl.multiple_of(pos_ref[block] * BQ, BQ)
-        col = lax.broadcasted_iota(jnp.int32, (HD, BQ), 1) + first
-        context = jnp.where(col < length, context, 0.0)
-        both = jnp.concatenate([dq * 0.125, context], axis=0)
-        out_ref[pl.ds(first, BQ), 0:128] = both.T.astype(BF)
+        for p in range(AQ // BQ):
+            part = slice(p * BQ, (p + 1) * BQ)
+            first = pl.multiple_of(pos_ref[block * (AQ // BQ) + p] * BQ, BQ)
+            col = lax.broadcasted_iota(jnp.int32, (HD, BQ), 1) + first
+            kept = jnp.where(col < length, context[:, part], 0.0)
+            both = jnp.concatenate([dq[:, part] * 0.125, kept], axis=0)
+            out_ref[pl.ds(first, BQ), 0:128] = both.T.astype(BF)
 
     def add(a, b):
         return b if a is None else a + b
@@ -158,8 +161,8 @@
         return jnp.max(peak, axis=0, keepdims=True)
 
     def step(i, peak):
-        starts = [pl.multiple_of((2 * i + j) * BQ, BQ) for j in range(2)]
-        after = pl.multiple_of(lax.rem(2 * i + 2, SEQ) * BQ, BQ)
+        starts = [pl.multiple_of((2 * i + j) * AQ, AQ) for j in range(2)]
+        after = pl.multiple_of(lax.rem(2 * i + 2, T // AQ) * AQ, AQ)
         peak, peak1, total, total1 = top(peak), None, None, None
         for c in range(NC):
             t = scores(starts[1], 1, c)
@@ -184,7 +187,7 @@
     for c in range(NC):
         t = scores(0, 0, c)
         peak = t if c == 0 else jnp.maximum(peak, t)
-    lax.fori_loop(0, SEQ // 2, step, peak)
+    lax.fori_loop(0, T // AQ // 2, step, peak)
     for b in range(SEQ):
         rows = pl.ds(pl.multiple_of(pos_ref[b] * BQ, BQ), BQ)
         out_ref[rows, 128:256] = acc[b * BQ : (b + 1) * BQ, :].astype(BF)
@@ -349,10 +352,12 @@
     above, below = send(normed, DOWN), send(normed, UP)
     over = swap(mine)
     upstream = lax.all_to_all(tie((upstream, normed))[0], "seq", 0, 0, tiled=True).reshape(T, GW)
+    here = me // 4
+    groups = jnp.stack([1 - here, here, 1 - here]).astype(jnp.int32)
     parity = lax.axis_index("dp") % 2
     weight_half = lax.dynamic_slice_in_dim(projection, parity * 1536, 1536, 1)
-    beside, other, above, below, over, upstream, place, owners, weight_half = tie(
-        (beside, other, above, below, over, upstream, place, owners, weight_half)
+    beside, other, above, below, over, upstream, place, owners, weight_half, groups, turned = tie(
+        (beside, other, above, below, over, upstream, place, owners, weight_half, groups, groups[1:])
     )
     far = [send(below[:half], UP), send(above[half:], DOWN)]
     columns = [mine, beside, over, sibling(over)]
@@ -370,11 +375,9 @@
             ],
         )(owners, groups, *columns, *rows)
 
-    here = me // 4
-    groups = jnp.stack([1 - here, here]).astype(jnp.int32)
     (near,) = project([below, above], groups, 1)
     near_got = send(near, ACROSS)
-    _, turned = tie((near, groups[::-1]))
+    _, turned = tie((near, turned))
     (kept,) = project([normed, below, above, other], turned, 1)
     _, far = tie((kept, far))
     last, far_kept = project(far, groups, 2)
@@ -397,8 +400,8 @@
                 pltpu.VMEM((HD, T), BF),
                 pltpu.VMEM((HD, T), BF),
                 pltpu.VMEM((HD, T), BF),
-                pltpu.VMEM((2, T, BQ), F32),
-                pltpu.VMEM((2, T, BQ), BF),
+                pltpu.VMEM((2, T, AQ), F32),
+                pltpu.VMEM((2, T, AQ), BF),
                 pltpu.VMEM((T, 128), F32),
             ],
             T * T,

time: 163 us -> 160 us (0.982)
  Pallas kernels: 74.3 us -> 71.8 us
    pallas_call x2, Pallas kernels: 34.3 us -> 31.9 us  [attend(): call(functools.partial(attention_kernel, head), shape((T, 256)), [SM, SM]...]
    unnamed x33 -> x41, local copies, waits for them, and re-layouts: 3.55 us -> 5.83 us
  transfers between devices with their start and end apart: 24 -> 24, of which waited for: 4 -> 4; matrix products, arithmetic and copies ran while one was open for 5% -> 4% of each run, Pallas kernels for 42% -> 42%
where the time goes in v9:
time: 160 us; the launch traced here: 159 us
  Pallas kernels  71.8 us (45%)
  starting transfers between devices  46 us (29%)
  waiting for transfers between devices  27 us (17%)
  local copies, waits for them, and re-layouts  11.4 us (7%)
  between operations  1.66 us (1%)
    pallas_call x2, Pallas kernels, attend(): call(functools.partial(attention_kernel, head), shape((T, 256)), [SM, SM]...  31.9 us
    ppermute x11, starting transfers between devices, send(): return lax.ppermute(v, 'seq', way)  15.3 us
    pallas_call x3, Pallas kernels, project(): call(functools.partial(project_kernel, len(rows)), (shape((height, 384)),...  13.9 us
    all_to_all x1, waiting for transfers between devices, body(): lax.all_to_all(tie((upstream, normed))[0], 'seq', 0, 0, tiled=True)  13.6 us
    pallas_call x1, Pallas kernels, body(): call(input_gradient_kernel, (shape((ROWS, 1024)), shape((ROWS, D), F32)),...  9.59 us
    all_to_all x1, starting transfers between devices, body(): partial = lax.all_to_all(partial, ('dp', 'zh', 'seq'), 0, 0, tiled=True)  9.14 us
    all_to_all x2, starting transfers between devices, send_back(): lax.all_to_all(grads.reshape(SEQ, ROWS, 256), 'seq', 0, 0, tiled=True)  8.9 us
    pallas_call x1, Pallas kernels, body(): call(weight_gradient_kernel, (shape((768, 384), F32), shape((768, 384))),...  8.48 us
  transfers between devices with their start and end apart: 24, of which 4 were waited for; matrix products, arithmetic and copies ran while one was open for 4% of the time, Pallas kernels for 42%

profile of v9, /device:TPU:0, one launch (start us, length us, event | category | flops | bytes accessed | tf_op | source)
XLA Modules:
  0.0 159.2 jit_solution(9386120707477749474)
XLA Ops:
  0.7 3.5 %shard_map.67 = (bf16[256,1536]{1,0:T(8,128)(2,1)}, bf16[384,768]{1,0:T(8,128)(2,1)}) custom-call(s32[1]{0:T(128)} %bitcast.y_ref, bf16[256,1536]{1,0:T(8,128)(2,1)} %bitcast.29, bf16[384,3072]{1,0:T(8,128)(2,1)} %w0.1), custom_call_target="tpu_custom_call" | custom-call | bytes 1048576 | tf_op jit(solution)/shard_map/pallas_call | solution.py:340
  4.2 2.1 %collective-permute-start.1 = (bf16[256,1536]{1,0:T(8,128)(2,1)}, bf16[256,1536]{1,0:T(8,128)(2,1)}, u32[]{:S(2)}, u32[]{:S(2)}) collective-permute-start(bf16[256,1536]{1,0:T(8,128)(2,1)} %get-tuple-element.49.refs_4_.refs_0_), channel_id=1, source_target_pairs={{0,4},{1,5},{2,6},{3,7},{4,0},{5,1},{6,2},{7,3},{8,12},{9,13},{10,... | collective-permute-start | bytes 2359304 | tf_op jit(solution)/shard_map/ppermute | solution.py:309
  6.2 3.0 %collective-permute-start.2 = (bf16[256,1536]{1,0:T(8,128)(2,1)}, bf16[256,1536]{1,0:T(8,128)(2,1)}, u32[]{:S(2)}, u32[]{:S(2)}) collective-permute-start(bf16[256,1536]{1,0:T(8,128)(2,1)} %get-tuple-element.49.refs_4_.refs_0_), channel_id=1, source_target_pairs={{0,3},{1,0},{2,1},{3,2},{4,7},{5,4},{6,5},{7,6},{8,11},{9,8},{10,9... | collective-permute-start | bytes 2359304 | tf_op jit(solution)/shard_map/ppermute | solution.py:309
  9.3 2.5 %collective-permute-start.4 = (bf16[384,768]{1,0:T(8,128)(2,1)}, bf16[384,768]{1,0:T(8,128)(2,1)S(1)}, u32[]{:S(2)}, u32[]{:S(2)}) collective-permute-start(bf16[384,768]{1,0:T(8,128)(2,1)} %get-tuple-element.48.refs_0_), channel_id=1, source_target_pairs={{0,20},{1,21},{2,22},{3,23},{4,16},{5,17},{6,18},{7,19},{16,4},{17... | collective-permute-start | bytes 1769480 | tf_op jit(solution)/shard_map/ppermute | solution.py:317
  12.8 5.0 %all-to-all-start = ((bf16[8,256,128]{2,1,0:T(8,128)(2,1)}), bf16[8,256,128]{2,1,0:T(8,128)(2,1)}, u32[]{:S(2)}, u32[]{:S(2)}) async-start(bf16[8,256,128]{2,1,0:T(8,128)(2,1)} %bitcast.31), calls=%async_computation | async-start | bytes 1048576 | tf_op jit(solution)/shard_map/all_to_all | solution.py:354
  20.2 1.1 constant_dynamic-slice_fusion
  21.3 13.6 %all-to-all-done = bf16[8,256,128]{2,1,0:T(8,128)(2,1)} async-done(((bf16[8,256,128]{2,1,0:T(8,128)(2,1)}), bf16[8,256,128]{2,1,0:T(8,128)(2,1)}, u32[]{:S(2)}, u32[]{:S(2)}) %all-to-all-start) | async-done | bytes 524320 | tf_op jit(solution)/shard_map/all_to_all | solution.py:354
  35.1 1.3 slice.8
  36.5 1.0 slice.9
  37.5 3.3 %collective-permute-start.7 = (bf16[128,1536]{1,0:T(8,128)(2,1)S(1)}, bf16[128,1536]{1,0:T(8,128)(2,1)S(1)}, u32[]{:S(2)}, u32[]{:S(2)}) collective-permute-start(bf16[128,1536]{1,0:T(8,128)(2,1)S(1)} %slice.9), channel_id=1, source_target_pairs={{0,3},{1,0},{2,1},{3,2},{4,7},{5,4},{6,5},{7,6},{8,11},{9,8},{10,9... | collective-permute-start | bytes 1179656 | tf_op jit(solution)/shard_map/ppermute | solution.py:309
  41.6 4.1 %shard_map.68 = bf16[512,384]{1,0:T(8,128)(2,1)} custom-call(s32[5]{0:T(128)} %stack.75.owner_ref.pos_ref, s32[3]{0:T(128)} %pad_add_fusion.group_ref, bf16[384,768]{1,0:T(8,128)(2,1)} %get-tuple-element.48.refs_0_, bf16[384,768]{1,0:T(8,128)(2,1)} %copy-done.1, bf16[384,768]{1,0:T(8,128)(2,1)} %copy-done.2, bf16[384,768]{1,0:T(8,128)(2,1)} %copy-done.3, ...), custom_call_target="tpu_custom_call" | custom-call | bytes 1048576 | tf_op jit(solution)/shard_map/pallas_call | solution.py:367
  45.8 1.7 %collective-permute-start.8 = (bf16[512,384]{1,0:T(8,128)(2,1)}, bf16[512,384]{1,0:T(8,128)(2,1)S(1)}, u32[]{:S(2)}, u32[]{:S(2)}) collective-permute-start(bf16[512,384]{1,0:T(8,128)(2,1)} %shard_map.68), channel_id=1, source_target_pairs={{0,4},{1,5},{2,6},{3,7},{4,0},{5,1},{6,2},{7,3},{8,12},{9,13},{10,... | collective-permute-start | bytes 1179656 | tf_op jit(solution)/shard_map/ppermute | solution.py:309
  47.5 2.5 %collective-permute-start.14 = (bf16[384,1536]{1,0:T(8,128)(2,1)S(1)}, bf16[384,1536]{1,0:T(8,128)(2,1)S(1)}, u32[]{:S(2)}, u32[]{:S(2)}) collective-permute-start(bf16[384,1536]{1,0:T(8,128)(2,1)S(1)} %copy-done.9), channel_id=1, source_target_pairs={{0,20},{1,21},{2,22},{3,23},{4,16},{5,17},{6,18},{7,19},{16,4},{17... | collective-permute-start | bytes 3538952 | tf_op jit(solution)/shard_map/ppermute | solution.py:317
  50.0 5.4 %shard_map.69.kept_ref = bf16[1024,384]{1,0:T(8,128)(2,1)} custom-call(s32[5]{0:T(128)} %stack.75.owner_ref.pos_ref, s32[2]{0:T(128)} %pad_add_fusion.1.group_ref, bf16[384,768]{1,0:T(8,128)(2,1)} %get-tuple-element.48.refs_0_, bf16[384,768]{1,0:T(8,128)(2,1)} %copy-done.1, bf16[384,768]{1,0:T(8,128)(2,1)} %copy-done.2, bf16[384,768]{1,0:T(8,128)(2,1)} %copy-done.3, ...), custom_call_target="tpu_custom_call" | custom-call | bytes 1048576 | tf_op jit(solution)/shard_map/pallas_call | solution.py:367
  57.0 4.3 %shard_map.70 = (bf16[256,384]{1,0:T(8,128)(2,1)}, bf16[256,384]{1,0:T(8,128)(2,1)}) custom-call(s32[5]{0:T(128)} %stack.75.owner_ref.pos_ref, s32[3]{0:T(128)} %pad_add_fusion.group_ref, bf16[384,768]{1,0:T(8,128)(2,1)} %get-tuple-element.48.refs_0_, bf16[384,768]{1,0:T(8,128)(2,1)} %copy-done.1, bf16[384,768]{1,0:T(8,128)(2,1)} %copy-done.2, ...), custom_call_target="tpu_custom_call" | custom-call | bytes 1048576 | tf_op jit(solution)/shard_map/pallas_call | solution.py:367
  61.5 2.0 %collective-permute-start.9 = (bf16[256,1536]{1,0:T(8,128)(2,1)}, bf16[256,1536]{1,0:T(8,128)(2,1)S(1)}, u32[]{:S(2)}, u32[]{:S(2)}) collective-permute-start(bf16[256,1536]{1,0:T(8,128)(2,1)} %collective-permute-done.1.refs_7_.refs_5_), channel_id=1, source_target_pairs={{0,1},{1,2},{2,3},{3,0},{4,5},{5,6},{6,7},{7,4},{8,9},{9,10},{10,1... | collective-permute-start | bytes 2359304 | tf_op jit(solution)/shard_map/ppermute | solution.py:309
  63.5 1.0 collective-permute-start.11
  64.5 4.9 %collective-permute-done.11.last_ref = bf16[256,384]{1,0:T(8,128)(2,1)S(1)} collective-permute-done((bf16[256,384]{1,0:T(8,128)(2,1)}, bf16[256,384]{1,0:T(8,128)(2,1)S(1)}, u32[]{:S(2)}, u32[]{:S(2)}) %collective-permute-start.11) | collective-permute-done | bytes 196640 | tf_op jit(solution)/shard_map/ppermute | solution.py:309
  69.3 1.0 collective-permute-start.12
  72.0 15.9 %shard_map.71.first_ref = bf16[2048,256]{1,0:T(8,128)(2,1)} custom-call(s32[9]{0:T(128)} %stack.69.pos_ref, s32[1]{0:T(128)S(6)} %copy.11.len_ref, bf16[1024,384]{1,0:T(8,128)(2,1)} %shard_map.69.kept_ref, bf16[256,384]{1,0:T(8,128)(2,1)} %get-tuple-element.67.far_ref, bf16[512,384]{1,0:T(8,128)(2,1)} %copy-done.16, bf16[256,384]{1,0:T(8,128)(2,1)} %copy-done.19, ...), custom_call_target="tpu_custom_call" | custom-call | flops 1000000000 | bytes 1048576 | tf_op jit(solution)/shard_map/pallas_call | solution.py:391
  88.1 1.1 copy-done.17
  89.8 3.6 %all-to-all-start.1 = ((bf16[8,256,256]{2,1,0:T(8,128)(2,1)}), bf16[8,256,256]{2,1,0:T(8,128)(2,1)S(1)}, u32[]{:S(2)}, u32[]{:S(2)}) async-start(bf16[8,256,256]{2,1,0:T(8,128)(2,1)} %bitcast.33), calls=%async_computation.1 | async-start | bytes 2097152 | tf_op jit(solution)/shard_map/all_to_all | solution.py:411
  93.4 1.8 %collective-permute-start.17 = (bf16[384,1536]{1,0:T(8,128)(2,1)}, bf16[384,1536]{1,0:T(8,128)(2,1)}, u32[]{:S(2)}, u32[]{:S(2)}) collective-permute-start(bf16[384,1536]{1,0:T(8,128)(2,1)} %copy-done.7), channel_id=1, source_target_pairs={{0,32},{32,0},{64,96},{96,64},{1,33},{33,1},{65,97},{97,65},{2,34}... | collective-permute-start | bytes 3538952 | tf_op jit(solution)/shard_map/ppermute | solution.py:417
  95.2 16.0 %shard_map.72.second_ref = bf16[2048,256]{1,0:T(8,128)(2,1)} custom-call(s32[9]{0:T(128)} %stack.69.pos_ref, s32[1]{0:T(128)S(6)} %copy.11.len_ref, bf16[1024,384]{1,0:T(8,128)(2,1)} %shard_map.69.kept_ref, bf16[256,384]{1,0:T(8,128)(2,1)} %get-tuple-element.67.far_ref, bf16[512,384]{1,0:T(8,128)(2,1)} %copy-done.16, bf16[256,384]{1,0:T(8,128)(2,1)} %copy-done.19, ...), custom_call_target="tpu_custom_call" | custom-call | flops 10000000000 | bytes 1048576 | tf_op jit(solution)/shard_map/pallas_call | solution.py:391
  111.1 5.3 %all-to-all-start.2 = ((bf16[8,256,256]{2,1,0:T(8,128)(2,1)}), bf16[8,256,256]{2,1,0:T(8,128)(2,1)S(1)}, u32[]{:S(2)}, u32[]{:S(2)}) async-start(bf16[8,256,256]{2,1,0:T(8,128)(2,1)} %bitcast.34), calls=%async_computation.2 | async-start | bytes 2097152 | tf_op jit(solution)/shard_map/all_to_all | solution.py:411
  116.5 8.5 %shard_map.73 = (f32[768,384]{1,0:T(8,128)}, bf16[768,384]{1,0:T(8,128)(2,1)}) custom-call(s32[9]{0:T(128)} %stack.69.pos_ref, bf16[2048,256]{1,0:T(8,128)(2,1)} %shard_map.71.first_ref, bf16[2048,256]{1,0:T(8,128)(2,1)} %shard_map.72.second_ref, bf16[256,1536]{1,0:T(8,128)(2,1)} %get-tuple-element.49.refs_4_.refs_0_, ...), custom_call_target="tpu_custom_call" | custom-call | flops 2415919104 | bytes 1048576 | tf_op jit(solution)/shard_map/pallas_call | solution.py:424
  125.1 2.2 %collective-permute-done.16.got_ref = bf16[768,384]{1,0:T(8,128)(2,1)S(1)} collective-permute-done((bf16[768,384]{1,0:T(8,128)(2,1)}, bf16[768,384]{1,0:T(8,128)(2,1)S(1)}, u32[]{:S(2)}, u32[]{:S(2)}) %collective-permute-start.16) | collective-permute-done | bytes 589856 | tf_op jit(solution)/shard_map/ppermute | solution.py:313
  128.1 2.6 %shard_map.74 = bf16[64,12,384]{2,1,0:T(8,128)(2,1)} custom-call(f32[768,384]{1,0:T(8,128)} %get-tuple-element.79.keep_ref, bf16[768,384]{1,0:T(8,128)(2,1)} %copy-done.10), custom_call_target="tpu_custom_call" | custom-call | bytes 1048576 | tf_op jit(solution)/shard_map/pallas_call | solution.py:437
  131.3 9.1 %all-to-all-start.3 = ((bf16[64,12,384]{2,1,0:T(8,128)(2,1)}), bf16[64,12,384]{2,1,0:T(8,128)(2,1)S(1)}, u32[]{:S(2)}, u32[]{:S(2)}) async-start(bf16[64,12,384]{2,1,0:T(8,128)(2,1)} %shard_map.74), calls=%async_computation.3 | async-start | bytes 1572864 | tf_op jit(solution)/shard_map/all_to_all | solution.py:441
  140.4 9.6 %shard_map.75 = (bf16[256,1024]{1,0:T(8,128)(2,1)}, f32[256,1536]{1,0:T(8,128)}) custom-call(s32[5]{0:T(128)} %stack.75.owner_ref.pos_ref, bf16[8,256,256]{2,1,0:T(8,128)(2,1)} %copy-done.4, bf16[8,256,256]{2,1,0:T(8,128)(2,1)} %copy-done.5, bf16[384,3072]{1,0:T(8,128)(2,1)} %w0.1, bf16[384,3072]{1,0:T(8,128)(2,1)} %collective-permute-done.15.w1, ...), custom_call_target="tpu_custom_call" | custom-call | flops 2415919104 | bytes 1048576 | tf_op jit(solution)/shard_map/pallas_call | solution.py:442
  150.0 6.3 %all-to-all-done.3.parts_ref = bf16[64,12,384]{2,1,0:T(8,128)(2,1)S(1)} async-done(((bf16[64,12,384]{2,1,0:T(8,128)(2,1)}), bf16[64,12,384]{2,1,0:T(8,128)(2,1)S(1)}, u32[]{:S(2)}, u32[]{:S(2)}) %all-to-all-start.3) | async-done | bytes 589856 | tf_op jit(solution)/shard_map/all_to_all | solution.py:441
  157.2 1.9 %shard_map.76 = f32[12,3072]{1,0:T(8,128)} custom-call(bf16[64,12,384]{2,1,0:T(8,128)(2,1)} %copy-done.6), custom_call_target="tpu_custom_call" | custom-call | bytes 1048576 | tf_op jit(solution)/shard_map/pallas_call | solution.py:454
  (75 shorter events, 10.1 us)
Async XLA Ops:
  0.6 11.2 %copy-start.11 = (bf16[1,256,1024]{2,1,0:T(8,128)(2,1)S(1)}, bf16[1,256,1024]{2,1,0:T(8,128)(2,1)}, u32[]{:S(2)}) copy-start(bf16[1,256,1024]{2,1,0:T(8,128)(2,1)} %param.7) | copy-start | bytes 1572868
  4.2 30.8 %collective-permute-start.1 = (bf16[256,1536]{1,0:T(8,128)(2,1)}, bf16[256,1536]{1,0:T(8,128)(2,1)}, u32[]{:S(2)}, u32[]{:S(2)}) collective-permute-start(bf16[256,1536]{1,0:T(8,128)(2,1)} %get-tuple-element.49.refs_4_.refs_0_), channel_id=1, source_target_pairs={{0,4},{1,5},{2,6},{3,7},{4,0},{5,1},{6,2},{7,3},{8,12},{9,13},{10,... | collective-permute-start | bytes 2359304 | tf_op jit(solution)/shard_map/ppermute | solution.py:309
  6.2 28.7 %collective-permute-start.2 = (bf16[256,1536]{1,0:T(8,128)(2,1)}, bf16[256,1536]{1,0:T(8,128)(2,1)}, u32[]{:S(2)}, u32[]{:S(2)}) collective-permute-start(bf16[256,1536]{1,0:T(8,128)(2,1)} %get-tuple-element.49.refs_4_.refs_0_), channel_id=1, source_target_pairs={{0,3},{1,0},{2,1},{3,2},{4,7},{5,4},{6,5},{7,6},{8,11},{9,8},{10,9... | collective-permute-start | bytes 2359304 | tf_op jit(solution)/shard_map/ppermute | solution.py:309
  9.3 25.7 %collective-permute-start.3 = (bf16[256,1536]{1,0:T(8,128)(2,1)}, bf16[256,1536]{1,0:T(8,128)(2,1)}, u32[]{:S(2)}, u32[]{:S(2)}) collective-permute-start(bf16[256,1536]{1,0:T(8,128)(2,1)} %get-tuple-element.49.refs_4_.refs_0_), channel_id=1, source_target_pairs={{0,1},{1,2},{2,3},{3,0},{4,5},{5,6},{6,7},{7,4},{8,9},{9,10},{10,1... | collective-permute-start | bytes 2359304 | tf_op jit(solution)/shard_map/ppermute | solution.py:309
  9.3 25.7 %collective-permute-start = (bf16[384,768]{1,0:T(8,128)(2,1)}, bf16[384,768]{1,0:T(8,128)(2,1)S(1)}, u32[]{:S(2)}, u32[]{:S(2)}) collective-permute-start(bf16[384,768]{1,0:T(8,128)(2,1)} %get-tuple-element.48.refs_0_), channel_id=1, source_target_pairs={{0,8},{8,0},{1,9},{9,1},{2,10},{10,2},{3,11},{11,3},{4,12},{12,4},... | collective-permute-start | bytes 1769480 | tf_op jit(solution)/shard_map/ppermute | solution.py:313
  9.3 25.7 %collective-permute-start.4 = (bf16[384,768]{1,0:T(8,128)(2,1)}, bf16[384,768]{1,0:T(8,128)(2,1)S(1)}, u32[]{:S(2)}, u32[]{:S(2)}) collective-permute-start(bf16[384,768]{1,0:T(8,128)(2,1)} %get-tuple-element.48.refs_0_), channel_id=1, source_target_pairs={{0,20},{1,21},{2,22},{3,23},{4,16},{5,17},{6,18},{7,19},{16,4},{17... | collective-permute-start | bytes 1769480 | tf_op jit(solution)/shard_map/ppermute | solution.py:317
  11.8 8.4 %copy-start = (bf16[384,3072]{1,0:T(8,128)(2,1)S(1)}, bf16[384,3072]{1,0:T(8,128)(2,1)}, u32[]{:S(2)}) copy-start(bf16[384,3072]{1,0:T(8,128)(2,1)} %w0.1) | copy-start | bytes 7077892
  12.8 22.1 %all-to-all-start = ((bf16[8,256,128]{2,1,0:T(8,128)(2,1)}), bf16[8,256,128]{2,1,0:T(8,128)(2,1)}, u32[]{:S(2)}, u32[]{:S(2)}) async-start(bf16[8,256,128]{2,1,0:T(8,128)(2,1)} %bitcast.31), calls=%async_computation | async-start | bytes 1048576 | tf_op jit(solution)/shard_map/all_to_all | solution.py:354
  34.9 5.9 %copy-start.1 = (bf16[384,768]{1,0:T(8,128)(2,1)}, bf16[384,768]{1,0:T(8,128)(2,1)S(1)}, u32[]{:S(2)}) copy-start(bf16[384,768]{1,0:T(8,128)(2,1)S(1)} %collective-permute-done.refs_1_) | copy-start | bytes 1769476
  34.9 5.9 %copy-start.2 = (bf16[384,768]{1,0:T(8,128)(2,1)}, bf16[384,768]{1,0:T(8,128)(2,1)S(1)}, u32[]{:S(2)}) copy-start(bf16[384,768]{1,0:T(8,128)(2,1)S(1)} %collective-permute-done.4.refs_2_) | copy-start | bytes 1769476
  35.0 5.8 %collective-permute-start.5 = (bf16[384,768]{1,0:T(8,128)(2,1)S(1)}, bf16[384,768]{1,0:T(8,128)(2,1)S(1)}, u32[]{:S(2)}, u32[]{:S(2)}) collective-permute-start(bf16[384,768]{1,0:T(8,128)(2,1)S(1)} %collective-permute-done.4.refs_2_), channel_id=1, source_target_pairs={{0,8},{8,0},{1,9},{9,1},{2,10},{10,2},{3,11},{11,3},{4,12},{12,4},... | collective-permute-start | bytes 1769480 | tf_op jit(solution)/shard_map/ppermute | solution.py:313
  36.4 19.1 %collective-permute-start.6 = (bf16[128,1536]{1,0:T(8,128)(2,1)S(1)}, bf16[128,1536]{1,0:T(8,128)(2,1)S(1)}, u32[]{:S(2)}, u32[]{:S(2)}) collective-permute-start(bf16[128,1536]{1,0:T(8,128)(2,1)S(1)} %slice.8), channel_id=1, source_target_pairs={{0,1},{1,2},{2,3},{3,0},{4,5},{5,6},{6,7},{7,4},{8,9},{9,10},{10,1... | collective-permute-start | bytes 1179656 | tf_op jit(solution)/shard_map/ppermute | solution.py:309
  37.5 10.0 %copy-start.9 = (bf16[384,1536]{1,0:T(8,128)(2,1)S(1)}, bf16[384,1536]{1,0:T(8,128)(2,1)}, u32[]{:S(2)}) copy-start(bf16[384,1536]{1,0:T(8,128)(2,1)} %constant_dynamic-slice_fusion) | copy-start | bytes 3538948
  37.5 18.0 %collective-permute-start.7 = (bf16[128,1536]{1,0:T(8,128)(2,1)S(1)}, bf16[128,1536]{1,0:T(8,128)(2,1)S(1)}, u32[]{:S(2)}, u32[]{:S(2)}) collective-permute-start(bf16[128,1536]{1,0:T(8,128)(2,1)S(1)} %slice.9), channel_id=1, source_target_pairs={{0,3},{1,0},{2,1},{3,2},{4,7},{5,4},{6,5},{7,6},{8,11},{9,8},{10,9... | collective-permute-start | bytes 1179656 | tf_op jit(solution)/shard_map/ppermute | solution.py:309
  45.8 15.6 %collective-permute-start.8 = (bf16[512,384]{1,0:T(8,128)(2,1)}, bf16[512,384]{1,0:T(8,128)(2,1)S(1)}, u32[]{:S(2)}, u32[]{:S(2)}) collective-permute-start(bf16[512,384]{1,0:T(8,128)(2,1)} %shard_map.68), channel_id=1, source_target_pairs={{0,4},{1,5},{2,6},{3,7},{4,0},{5,1},{6,2},{7,3},{8,12},{9,13},{10,... | collective-permute-start | bytes 1179656 | tf_op jit(solution)/shard_map/ppermute | solution.py:309
  47.5 40.5 %collective-permute-start.14 = (bf16[384,1536]{1,0:T(8,128)(2,1)S(1)}, bf16[384,1536]{1,0:T(8,128)(2,1)S(1)}, u32[]{:S(2)}, u32[]{:S(2)}) collective-permute-start(bf16[384,1536]{1,0:T(8,128)(2,1)S(1)} %copy-done.9), channel_id=1, source_target_pairs={{0,20},{1,21},{2,22},{3,23},{4,16},{5,17},{6,18},{7,19},{16,4},{17... | collective-permute-start | bytes 3538952 | tf_op jit(solution)/shard_map/ppermute | solution.py:317
  61.4 10.7 %copy-start.16 = (bf16[512,384]{1,0:T(8,128)(2,1)}, bf16[512,384]{1,0:T(8,128)(2,1)S(1)}, u32[]{:S(2)}) copy-start(bf16[512,384]{1,0:T(8,128)(2,1)S(1)} %collective-permute-done.8.other_ref) | copy-start | bytes 1179652
  61.4 26.6 %collective-permute-start.10 = (bf16[256,1536]{1,0:T(8,128)(2,1)}, bf16[256,1536]{1,0:T(8,128)(2,1)S(1)}, u32[]{:S(2)}, u32[]{:S(2)}) collective-permute-start(bf16[256,1536]{1,0:T(8,128)(2,1)} %collective-permute-done.1.refs_7_.refs_5_), channel_id=1, source_target_pairs={{0,3},{1,0},{2,1},{3,2},{4,7},{5,4},{6,5},{7,6},{8,11},{9,8},{10,9... | collective-permute-start | bytes 2359304 | tf_op jit(solution)/shard_map/ppermute | solution.py:309
  61.5 26.6 %collective-permute-start.9 = (bf16[256,1536]{1,0:T(8,128)(2,1)}, bf16[256,1536]{1,0:T(8,128)(2,1)S(1)}, u32[]{:S(2)}, u32[]{:S(2)}) collective-permute-start(bf16[256,1536]{1,0:T(8,128)(2,1)} %collective-permute-done.1.refs_7_.refs_5_), channel_id=1, source_target_pairs={{0,1},{1,2},{2,3},{3,0},{4,5},{5,6},{6,7},{7,4},{8,9},{9,10},{10,1... | collective-permute-start | bytes 2359304 | tf_op jit(solution)/shard_map/ppermute | solution.py:309
  63.5 5.9 %collective-permute-start.11 = (bf16[256,384]{1,0:T(8,128)(2,1)}, bf16[256,384]{1,0:T(8,128)(2,1)S(1)}, u32[]{:S(2)}, u32[]{:S(2)}) collective-permute-start(bf16[256,384]{1,0:T(8,128)(2,1)} %get-tuple-element.63), channel_id=1, source_target_pairs={{0,4},{1,5},{2,6},{3,7},{4,0},{5,1},{6,2},{7,3},{8,12},{9,13},{10,... | collective-permute-start | bytes 589832 | tf_op jit(solution)/shard_map/ppermute | solution.py:309
  69.3 18.6 %collective-permute-start.12 = (bf16[128,1536]{1,0:T(8,128)(2,1)}, bf16[128,1536]{1,0:T(8,128)(2,1)S(1)}, u32[]{:S(2)}, u32[]{:S(2)}) collective-permute-start(bf16[128,1536]{1,0:T(8,128)(2,1)} %copy-done.12), channel_id=1, source_target_pairs={{0,4},{1,5},{2,6},{3,7},{4,0},{5,1},{6,2},{7,3},{8,12},{9,13},{10,... | collective-permute-start | bytes 1179656 | tf_op jit(solution)/shard_map/ppermute | solution.py:309
  70.4 17.6 %collective-permute-start.13 = (bf16[128,1536]{1,0:T(8,128)(2,1)}, bf16[128,1536]{1,0:T(8,128)(2,1)S(1)}, u32[]{:S(2)}, u32[]{:S(2)}) collective-permute-start(bf16[128,1536]{1,0:T(8,128)(2,1)} %copy-done.13), channel_id=1, source_target_pairs={{0,4},{1,5},{2,6},{3,7},{4,0},{5,1},{6,2},{7,3},{8,12},{9,13},{10,... | collective-permute-start | bytes 1179656 | tf_op jit(solution)/shard_map/ppermute | solution.py:309
  88.0 23.1 %collective-permute-start.15 = (bf16[384,3072]{1,0:T(8,128)(2,1)S(1)}, bf16[384,3072]{1,0:T(8,128)(2,1)}, u32[]{:S(2)}, u32[]{:S(2)}) collective-permute-start(bf16[384,3072]{1,0:T(8,128)(2,1)S(1)} %copy-done), channel_id=1, source_target_pairs={{0,8},{8,0},{1,9},{9,1},{2,10},{10,2},{3,11},{11,3},{4,12},{12,4},... | collective-permute-start | bytes 7077896 | tf_op jit(solution)/shard_map/ppermute | solution.py:313
  89.8 21.3 %all-to-all-start.1 = ((bf16[8,256,256]{2,1,0:T(8,128)(2,1)}), bf16[8,256,256]{2,1,0:T(8,128)(2,1)S(1)}, u32[]{:S(2)}, u32[]{:S(2)}) async-start(bf16[8,256,256]{2,1,0:T(8,128)(2,1)} %bitcast.33), calls=%async_computation.1 | async-start | bytes 2097152 | tf_op jit(solution)/shard_map/all_to_all | solution.py:411
  93.4 37.3 %collective-permute-start.17 = (bf16[384,1536]{1,0:T(8,128)(2,1)}, bf16[384,1536]{1,0:T(8,128)(2,1)}, u32[]{:S(2)}, u32[]{:S(2)}) collective-permute-start(bf16[384,1536]{1,0:T(8,128)(2,1)} %copy-done.7), channel_id=1, source_target_pairs={{0,32},{32,0},{64,96},{96,64},{1,33},{33,1},{65,97},{97,65},{2,34}... | collective-permute-start | bytes 3538952 | tf_op jit(solution)/shard_map/ppermute | solution.py:417
  111.1 13.8 %copy-start.4 = (bf16[8,256,256]{2,1,0:T(8,128)(2,1)}, bf16[8,256,256]{2,1,0:T(8,128)(2,1)S(1)}, u32[]{:S(2)}) copy-start(bf16[8,256,256]{2,1,0:T(8,128)(2,1)S(1)} %all-to-all-done.1.first_ref) | copy-start | bytes 3145732
  111.1 19.5 %all-to-all-start.2 = ((bf16[8,256,256]{2,1,0:T(8,128)(2,1)}), bf16[8,256,256]{2,1,0:T(8,128)(2,1)S(1)}, u32[]{:S(2)}, u32[]{:S(2)}) async-start(bf16[8,256,256]{2,1,0:T(8,128)(2,1)} %bitcast.34), calls=%async_computation.2 | async-start | bytes 2097152 | tf_op jit(solution)/shard_map/all_to_all | solution.py:411
  125.0 2.3 %collective-permute-start.16 = (bf16[768,384]{1,0:T(8,128)(2,1)}, bf16[768,384]{1,0:T(8,128)(2,1)S(1)}, u32[]{:S(2)}, u32[]{:S(2)}) collective-permute-start(bf16[768,384]{1,0:T(8,128)(2,1)} %get-tuple-element.80), channel_id=1, source_target_pairs={{0,8},{8,0},{1,9},{9,1},{2,10},{10,2},{3,11},{11,3},{4,12},{12,4},... | collective-permute-start | bytes 1769480 | tf_op jit(solution)/shard_map/ppermute | solution.py:313
  130.7 9.8 %copy-start.5 = (bf16[8,256,256]{2,1,0:T(8,128)(2,1)}, bf16[8,256,256]{2,1,0:T(8,128)(2,1)S(1)}, u32[]{:S(2)}) copy-start(bf16[8,256,256]{2,1,0:T(8,128)(2,1)S(1)} %all-to-all-done.2.second_ref) | copy-start | bytes 3145732
  130.7 9.7 %collective-permute-start.18 = (bf16[384,1536]{1,0:T(8,128)(2,1)S(1)}, bf16[384,1536]{1,0:T(8,128)(2,1)}, u32[]{:S(2)}, u32[]{:S(2)}) collective-permute-start(bf16[384,1536]{1,0:T(8,128)(2,1)S(1)} %copy-done.8), channel_id=1, source_target_pairs={{0,8},{8,0},{1,9},{9,1},{2,10},{10,2},{3,11},{11,3},{4,12},{12,4},... | collective-permute-start | bytes 3538952 | tf_op jit(solution)/shard_map/ppermute | solution.py:313
  130.9 9.5 %collective-permute-start.19 = (bf16[384,1536]{1,0:T(8,128)(2,1)}, bf16[384,1536]{1,0:T(8,128)(2,1)}, u32[]{:S(2)}, u32[]{:S(2)}) collective-permute-start(bf16[384,1536]{1,0:T(8,128)(2,1)} %collective-permute-done.17.w3), channel_id=1, source_target_pairs={{0,8},{8,0},{1,9},{9,1},{2,10},{10,2},{3,11},{11,3},{4,12},{12,4},... | collective-permute-start | bytes 3538952 | tf_op jit(solution)/shard_map/ppermute | solution.py:313
  131.3 25.1 %all-to-all-start.3 = ((bf16[64,12,384]{2,1,0:T(8,128)(2,1)}), bf16[64,12,384]{2,1,0:T(8,128)(2,1)S(1)}, u32[]{:S(2)}, u32[]{:S(2)}) async-start(bf16[64,12,384]{2,1,0:T(8,128)(2,1)} %shard_map.74), calls=%async_computation.3 | async-start | bytes 1572864 | tf_op jit(solution)/shard_map/all_to_all | solution.py:441
  (12 other events, 16.7 us)

commit v10 on v9

--- a/solution.py
+++ b/solution.py
@@ -377,14 +377,14 @@
 
     (near,) = project([below, above], groups, 1)
     near_got = send(near, ACROSS)
-    _, turned = tie((near, turned))
+    _, far = tie((near, far))
+    last, far_kept = project(far, groups, 2)
+    _, turned = tie((last, turned))
     (kept,) = project([normed, below, above, other], turned, 1)
-    _, far = tie((kept, far))
-    last, far_kept = project(far, groups, 2)
-    _, other_late, near_got = tie((last, other, near_got))
+    _, other_late = tie((last, other))
     other_below, other_above = send(other_late, UP), send(other_late, DOWN)
     weight_half = swap(weight_half)
-    far_got, far_late = tie((send(last, ACROSS), far))
+    far_got, far_late, kept = tie((send(last, ACROSS), far, kept))
     other_far = [send(v, ACROSS) for v in far_late]
 
     def attend(head):

time: 160 us -> 158 us (0.988)
  waiting for transfers between devices: 27 us -> 22.1 us
  starting transfers between devices: 46 us -> 49.1 us
    ppermute x11, waiting for transfers between devices: 4.89 us -> 0.03 us  [send(): return lax.ppermute(v, 'seq', way)]
    unnamed x41 -> x43, local copies, waits for them, and re-layouts: 5.83 us -> 5.85 us
  transfers between devices with their start and end apart: 24 -> 24, of which waited for: 4 -> 3; matrix products, arithmetic and copies ran while one was open for 4% -> 5% of each run, Pallas kernels for 42% -> 42%
where the time goes in v10:
time: 158 us
  Pallas kernels  71.9 us (46%)
  starting transfers between devices  49.1 us (31%)
  waiting for transfers between devices  22.1 us (14%)
  local copies, waits for them, and re-layouts  11.7 us (7%)
  between operations  1.67 us (1%)
    pallas_call x2, Pallas kernels, attend(): call(functools.partial(attention_kernel, head), shape((T, 256)), [SM, SM]...  31.9 us
    ppermute x11, starting transfers between devices, send(): return lax.ppermute(v, 'seq', way)  16.2 us
    pallas_call x3, Pallas kernels, project(): call(functools.partial(project_kernel, len(rows)), (shape((height, 384)),...  13.9 us
    all_to_all x1, waiting for transfers between devices, body(): lax.all_to_all(tie((upstream, normed))[0], 'seq', 0, 0, tiled=True)  13.6 us
    all_to_all x1, starting transfers between devices, body(): partial = lax.all_to_all(partial, ('dp', 'zh', 'seq'), 0, 0, tiled=True)  10 us
    pallas_call x1, Pallas kernels, body(): call(input_gradient_kernel, (shape((ROWS, 1024)), shape((ROWS, D), F32)),...  9.59 us
    all_to_all x2, starting transfers between devices, send_back(): lax.all_to_all(grads.reshape(SEQ, ROWS, 256), 'seq', 0, 0, tiled=True)  8.9 us
    pallas_call x1, Pallas kernels, body(): call(weight_gradient_kernel, (shape((768, 384), F32), shape((768, 384))),...  8.46 us
  transfers between devices with their start and end apart: 24, of which 3 were waited for; matrix products, arithmetic and copies ran while one was open for 5% of the time, Pallas kernels for 42%

profile of v10, /device:TPU:0, one launch (start us, length us, event | category | flops | bytes accessed | tf_op | source)
XLA Modules:
  0.0 157.6 jit_solution(3329697048530357595)
XLA Ops:
  0.7 3.5 %shard_map.67 = (bf16[256,1536]{1,0:T(8,128)(2,1)}, bf16[384,768]{1,0:T(8,128)(2,1)}) custom-call(s32[1]{0:T(128)} %bitcast.y_ref, bf16[256,1536]{1,0:T(8,128)(2,1)} %bitcast.29, bf16[384,3072]{1,0:T(8,128)(2,1)} %w0.1), custom_call_target="tpu_custom_call" | custom-call | bytes 1048576 | tf_op jit(solution)/shard_map/pallas_call | solution.py:340
  4.1 2.1 %collective-permute-start.1 = (bf16[256,1536]{1,0:T(8,128)(2,1)}, bf16[256,1536]{1,0:T(8,128)(2,1)}, u32[]{:S(2)}, u32[]{:S(2)}) collective-permute-start(bf16[256,1536]{1,0:T(8,128)(2,1)} %get-tuple-element.49.refs_4_.refs_0_), channel_id=1, source_target_pairs={{0,4},{1,5},{2,6},{3,7},{4,0},{5,1},{6,2},{7,3},{8,12},{9,13},{10,... | collective-permute-start | bytes 2359304 | tf_op jit(solution)/shard_map/ppermute | solution.py:309
  6.2 3.0 %collective-permute-start.2 = (bf16[256,1536]{1,0:T(8,128)(2,1)}, bf16[256,1536]{1,0:T(8,128)(2,1)}, u32[]{:S(2)}, u32[]{:S(2)}) collective-permute-start(bf16[256,1536]{1,0:T(8,128)(2,1)} %get-tuple-element.49.refs_4_.refs_0_), channel_id=1, source_target_pairs={{0,3},{1,0},{2,1},{3,2},{4,7},{5,4},{6,5},{7,6},{8,11},{9,8},{10,9... | collective-permute-start | bytes 2359304 | tf_op jit(solution)/shard_map/ppermute | solution.py:309
  9.2 2.5 %collective-permute-start.4 = (bf16[384,768]{1,0:T(8,128)(2,1)}, bf16[384,768]{1,0:T(8,128)(2,1)S(1)}, u32[]{:S(2)}, u32[]{:S(2)}) collective-permute-start(bf16[384,768]{1,0:T(8,128)(2,1)} %get-tuple-element.48.refs_0_), channel_id=1, source_target_pairs={{0,20},{1,21},{2,22},{3,23},{4,16},{5,17},{6,18},{7,19},{16,4},{17... | collective-permute-start | bytes 1769480 | tf_op jit(solution)/shard_map/ppermute | solution.py:317
  11.9 0.9 copy.10
  12.7 5.0 %all-to-all-start = ((bf16[8,256,128]{2,1,0:T(8,128)(2,1)}), bf16[8,256,128]{2,1,0:T(8,128)(2,1)}, u32[]{:S(2)}, u32[]{:S(2)}) async-start(bf16[8,256,128]{2,1,0:T(8,128)(2,1)} %bitcast.31), calls=%async_computation | async-start | bytes 1048576 | tf_op jit(solution)/shard_map/all_to_all | solution.py:354
  20.2 1.1 constant_dynamic-slice_fusion
  21.3 13.6 %all-to-all-done = bf16[8,256,128]{2,1,0:T(8,128)(2,1)} async-done(((bf16[8,256,128]{2,1,0:T(8,128)(2,1)}), bf16[8,256,128]{2,1,0:T(8,128)(2,1)}, u32[]{:S(2)}, u32[]{:S(2)}) %all-to-all-start) | async-done | bytes 524320 | tf_op jit(solution)/shard_map/all_to_all | solution.py:354
  35.0 1.5 slice.8
  36.6 1.0 slice.9
  37.7 3.3 %collective-permute-start.7 = (bf16[128,1536]{1,0:T(8,128)(2,1)S(1)}, bf16[128,1536]{1,0:T(8,128)(2,1)S(1)}, u32[]{:S(2)}, u32[]{:S(2)}) collective-permute-start(bf16[128,1536]{1,0:T(8,128)(2,1)S(1)} %slice.9), channel_id=1, source_target_pairs={{0,3},{1,0},{2,1},{3,2},{4,7},{5,4},{6,5},{7,6},{8,11},{9,8},{10,9... | collective-permute-start | bytes 1179656 | tf_op jit(solution)/shard_map/ppermute | solution.py:309
  41.0 3.8 %collective-permute-start.14 = (bf16[384,1536]{1,0:T(8,128)(2,1)S(1)}, bf16[384,1536]{1,0:T(8,128)(2,1)S(1)}, u32[]{:S(2)}, u32[]{:S(2)}) collective-permute-start(bf16[384,1536]{1,0:T(8,128)(2,1)S(1)} %copy-done.9), channel_id=1, source_target_pairs={{0,20},{1,21},{2,22},{3,23},{4,16},{5,17},{6,18},{7,19},{16,4},{17... | collective-permute-start | bytes 3538952 | tf_op jit(solution)/shard_map/ppermute | solution.py:317
  45.6 4.2 %shard_map.68 = bf16[512,384]{1,0:T(8,128)(2,1)} custom-call(s32[5]{0:T(128)} %stack.75.owner_ref.pos_ref, s32[3]{0:T(128)} %pad_add_fusion.group_ref, bf16[384,768]{1,0:T(8,128)(2,1)} %get-tuple-element.48.refs_0_, bf16[384,768]{1,0:T(8,128)(2,1)} %copy-done.1, bf16[384,768]{1,0:T(8,128)(2,1)} %copy-done.2, bf16[384,768]{1,0:T(8,128)(2,1)} %copy-done.3, ...), custom_call_target="tpu_custom_call" | custom-call | bytes 1048576 | tf_op jit(solution)/shard_map/pallas_call | solution.py:367
  51.4 4.3 %shard_map.69 = (bf16[256,384]{1,0:T(8,128)(2,1)}, bf16[256,384]{1,0:T(8,128)(2,1)}) custom-call(s32[5]{0:T(128)} %stack.75.owner_ref.pos_ref, s32[3]{0:T(128)} %pad_add_fusion.group_ref, bf16[384,768]{1,0:T(8,128)(2,1)} %get-tuple-element.48.refs_0_, bf16[384,768]{1,0:T(8,128)(2,1)} %copy-done.1, bf16[384,768]{1,0:T(8,128)(2,1)} %copy-done.2, ...), custom_call_target="tpu_custom_call" | custom-call | bytes 1048576 | tf_op jit(solution)/shard_map/pallas_call | solution.py:367
  55.8 3.2 %collective-permute-start.9 = (bf16[256,1536]{1,0:T(8,128)(2,1)}, bf16[256,1536]{1,0:T(8,128)(2,1)S(1)}, u32[]{:S(2)}, u32[]{:S(2)}) collective-permute-start(bf16[256,1536]{1,0:T(8,128)(2,1)} %collective-permute-done.1.refs_7_.refs_5_), channel_id=1, source_target_pairs={{0,3},{1,0},{2,1},{3,2},{4,7},{5,4},{6,5},{7,6},{8,11},{9,8},{10,9... | collective-permute-start | bytes 2359304 | tf_op jit(solution)/shard_map/ppermute | solution.py:309
  59.1 2.0 %collective-permute-start.10 = (bf16[256,384]{1,0:T(8,128)(2,1)}, bf16[256,384]{1,0:T(8,128)(2,1)}, u32[]{:S(2)}, u32[]{:S(2)}) collective-permute-start(bf16[256,384]{1,0:T(8,128)(2,1)} %get-tuple-element.60), channel_id=1, source_target_pairs={{0,4},{1,5},{2,6},{3,7},{4,0},{5,1},{6,2},{7,3},{8,12},{9,13},{10,... | collective-permute-start | bytes 589832 | tf_op jit(solution)/shard_map/ppermute | solution.py:309
  61.1 5.4 %shard_map.70.kept_ref = bf16[1024,384]{1,0:T(8,128)(2,1)} custom-call(s32[5]{0:T(128)} %stack.75.owner_ref.pos_ref, s32[2]{0:T(128)} %pad_add_fusion.1.group_ref, bf16[384,768]{1,0:T(8,128)(2,1)} %get-tuple-element.48.refs_0_, bf16[384,768]{1,0:T(8,128)(2,1)} %copy-done.1, bf16[384,768]{1,0:T(8,128)(2,1)} %copy-done.2, bf16[384,768]{1,0:T(8,128)(2,1)} %copy-done.3, ...), custom_call_target="tpu_custom_call" | custom-call | bytes 1048576 | tf_op jit(solution)/shard_map/pallas_call | solution.py:367
  67.1 1.8 %collective-permute-start.12 = (bf16[128,1536]{1,0:T(8,128)(2,1)S(1)}, bf16[128,1536]{1,0:T(8,128)(2,1)S(1)}, u32[]{:S(2)}, u32[]{:S(2)}) collective-permute-start(bf16[128,1536]{1,0:T(8,128)(2,1)S(1)} %copy-done.15), channel_id=1, source_target_pairs={{0,4},{1,5},{2,6},{3,7},{4,0},{5,1},{6,2},{7,3},{8,12},{9,13},{10,... | collective-permute-start | bytes 1179656 | tf_op jit(solution)/shard_map/ppermute | solution.py:309
  69.5 15.9 %shard_map.71.first_ref = bf16[2048,256]{1,0:T(8,128)(2,1)} custom-call(s32[9]{0:T(128)} %stack.69.pos_ref, s32[1]{0:T(128)S(6)} %copy.11.len_ref, bf16[1024,384]{1,0:T(8,128)(2,1)} %shard_map.70.kept_ref, bf16[256,384]{1,0:T(8,128)(2,1)} %get-tuple-element.68.far_ref, bf16[512,384]{1,0:T(8,128)(2,1)} %copy-done.18, ...), custom_call_target="tpu_custom_call" | custom-call | flops 1000000000 | bytes 1048576 | tf_op jit(solution)/shard_map/pallas_call | solution.py:391
  87.3 3.6 %all-to-all-start.1 = ((bf16[8,256,256]{2,1,0:T(8,128)(2,1)}), bf16[8,256,256]{2,1,0:T(8,128)(2,1)S(1)}, u32[]{:S(2)}, u32[]{:S(2)}) async-start(bf16[8,256,256]{2,1,0:T(8,128)(2,1)} %bitcast.33), calls=%async_computation.1 | async-start | bytes 2097152 | tf_op jit(solution)/shard_map/all_to_all | solution.py:411
  90.8 1.8 %collective-permute-start.17 = (bf16[384,1536]{1,0:T(8,128)(2,1)}, bf16[384,1536]{1,0:T(8,128)(2,1)}, u32[]{:S(2)}, u32[]{:S(2)}) collective-permute-start(bf16[384,1536]{1,0:T(8,128)(2,1)} %copy-done.7), channel_id=1, source_target_pairs={{0,32},{32,0},{64,96},{96,64},{1,33},{33,1},{65,97},{97,65},{2,34}... | collective-permute-start | bytes 3538952 | tf_op jit(solution)/shard_map/ppermute | solution.py:417
  92.6 16.0 %shard_map.72.second_ref = bf16[2048,256]{1,0:T(8,128)(2,1)} custom-call(s32[9]{0:T(128)} %stack.69.pos_ref, s32[1]{0:T(128)S(6)} %copy.11.len_ref, bf16[1024,384]{1,0:T(8,128)(2,1)} %shard_map.70.kept_ref, bf16[256,384]{1,0:T(8,128)(2,1)} %get-tuple-element.68.far_ref, bf16[512,384]{1,0:T(8,128)(2,1)} %copy-done.18, ...), custom_call_target="tpu_custom_call" | custom-call | flops 10000000000 | bytes 1048576 | tf_op jit(solution)/shard_map/pallas_call | solution.py:391
  108.6 5.3 %all-to-all-start.2 = ((bf16[8,256,256]{2,1,0:T(8,128)(2,1)}), bf16[8,256,256]{2,1,0:T(8,128)(2,1)S(1)}, u32[]{:S(2)}, u32[]{:S(2)}) async-start(bf16[8,256,256]{2,1,0:T(8,128)(2,1)} %bitcast.34), calls=%async_computation.2 | async-start | bytes 2097152 | tf_op jit(solution)/shard_map/all_to_all | solution.py:411
  114.0 8.5 %shard_map.73 = (f32[768,384]{1,0:T(8,128)}, bf16[768,384]{1,0:T(8,128)(2,1)}) custom-call(s32[9]{0:T(128)} %stack.69.pos_ref, bf16[2048,256]{1,0:T(8,128)(2,1)} %shard_map.71.first_ref, bf16[2048,256]{1,0:T(8,128)(2,1)} %shard_map.72.second_ref, bf16[256,1536]{1,0:T(8,128)(2,1)} %get-tuple-element.49.refs_4_.refs_0_, ...), custom_call_target="tpu_custom_call" | custom-call | flops 2415919104 | bytes 1048576 | tf_op jit(solution)/shard_map/pallas_call | solution.py:424
  122.6 2.2 %collective-permute-done.16.got_ref = bf16[768,384]{1,0:T(8,128)(2,1)S(1)} collective-permute-done((bf16[768,384]{1,0:T(8,128)(2,1)}, bf16[768,384]{1,0:T(8,128)(2,1)S(1)}, u32[]{:S(2)}, u32[]{:S(2)}) %collective-permute-start.16) | collective-permute-done | bytes 589856 | tf_op jit(solution)/shard_map/ppermute | solution.py:313
  124.8 0.9 copy-done.10
  125.6 2.6 %shard_map.74 = bf16[64,12,384]{2,1,0:T(8,128)(2,1)} custom-call(f32[768,384]{1,0:T(8,128)} %get-tuple-element.79.keep_ref, bf16[768,384]{1,0:T(8,128)(2,1)} %copy-done.10), custom_call_target="tpu_custom_call" | custom-call | bytes 1048576 | tf_op jit(solution)/shard_map/pallas_call | solution.py:437
  128.8 10.0 %all-to-all-start.3 = ((bf16[64,12,384]{2,1,0:T(8,128)(2,1)}), bf16[64,12,384]{2,1,0:T(8,128)(2,1)S(1)}, u32[]{:S(2)}, u32[]{:S(2)}) async-start(bf16[64,12,384]{2,1,0:T(8,128)(2,1)} %shard_map.74), calls=%async_computation.3 | async-start | bytes 1572864 | tf_op jit(solution)/shard_map/all_to_all | solution.py:441
  138.9 9.6 %shard_map.75 = (bf16[256,1024]{1,0:T(8,128)(2,1)}, f32[256,1536]{1,0:T(8,128)}) custom-call(s32[5]{0:T(128)} %stack.75.owner_ref.pos_ref, bf16[8,256,256]{2,1,0:T(8,128)(2,1)} %copy-done.4, bf16[8,256,256]{2,1,0:T(8,128)(2,1)} %copy-done.5, bf16[384,3072]{1,0:T(8,128)(2,1)} %w0.1, bf16[384,3072]{1,0:T(8,128)(2,1)} %collective-permute-done.15.w1, ...), custom_call_target="tpu_custom_call" | custom-call | flops 2415919104 | bytes 1048576 | tf_op jit(solution)/shard_map/pallas_call | solution.py:442
  148.5 6.3 %all-to-all-done.3.parts_ref = bf16[64,12,384]{2,1,0:T(8,128)(2,1)S(1)} async-done(((bf16[64,12,384]{2,1,0:T(8,128)(2,1)}), bf16[64,12,384]{2,1,0:T(8,128)(2,1)S(1)}, u32[]{:S(2)}, u32[]{:S(2)}) %all-to-all-start.3) | async-done | bytes 589856 | tf_op jit(solution)/shard_map/all_to_all | solution.py:441
  154.8 0.9 copy-done.6
  155.7 1.9 %shard_map.76 = f32[12,3072]{1,0:T(8,128)} custom-call(bf16[64,12,384]{2,1,0:T(8,128)(2,1)} %copy-done.6), custom_call_target="tpu_custom_call" | custom-call | bytes 1048576 | tf_op jit(solution)/shard_map/pallas_call | solution.py:454
  (77 shorter events, 8.3 us)
Async XLA Ops:
  0.6 11.1 %copy-start.11 = (bf16[1,256,1024]{2,1,0:T(8,128)(2,1)S(1)}, bf16[1,256,1024]{2,1,0:T(8,128)(2,1)}, u32[]{:S(2)}) copy-start(bf16[1,256,1024]{2,1,0:T(8,128)(2,1)} %param.7) | copy-start | bytes 1572868
  4.1 30.8 %collective-permute-start.1 = (bf16[256,1536]{1,0:T(8,128)(2,1)}, bf16[256,1536]{1,0:T(8,128)(2,1)}, u32[]{:S(2)}, u32[]{:S(2)}) collective-permute-start(bf16[256,1536]{1,0:T(8,128)(2,1)} %get-tuple-element.49.refs_4_.refs_0_), channel_id=1, source_target_pairs={{0,4},{1,5},{2,6},{3,7},{4,0},{5,1},{6,2},{7,3},{8,12},{9,13},{10,... | collective-permute-start | bytes 2359304 | tf_op jit(solution)/shard_map/ppermute | solution.py:309
  6.2 28.7 %collective-permute-start.2 = (bf16[256,1536]{1,0:T(8,128)(2,1)}, bf16[256,1536]{1,0:T(8,128)(2,1)}, u32[]{:S(2)}, u32[]{:S(2)}) collective-permute-start(bf16[256,1536]{1,0:T(8,128)(2,1)} %get-tuple-element.49.refs_4_.refs_0_), channel_id=1, source_target_pairs={{0,3},{1,0},{2,1},{3,2},{4,7},{5,4},{6,5},{7,6},{8,11},{9,8},{10,9... | collective-permute-start | bytes 2359304 | tf_op jit(solution)/shard_map/ppermute | solution.py:309
  9.2 25.7 %collective-permute-start.3 = (bf16[256,1536]{1,0:T(8,128)(2,1)}, bf16[256,1536]{1,0:T(8,128)(2,1)}, u32[]{:S(2)}, u32[]{:S(2)}) collective-permute-start(bf16[256,1536]{1,0:T(8,128)(2,1)} %get-tuple-element.49.refs_4_.refs_0_), channel_id=1, source_target_pairs={{0,1},{1,2},{2,3},{3,0},{4,5},{5,6},{6,7},{7,4},{8,9},{9,10},{10,1... | collective-permute-start | bytes 2359304 | tf_op jit(solution)/shard_map/ppermute | solution.py:309
  9.2 25.7 %collective-permute-start = (bf16[384,768]{1,0:T(8,128)(2,1)}, bf16[384,768]{1,0:T(8,128)(2,1)S(1)}, u32[]{:S(2)}, u32[]{:S(2)}) collective-permute-start(bf16[384,768]{1,0:T(8,128)(2,1)} %get-tuple-element.48.refs_0_), channel_id=1, source_target_pairs={{0,8},{8,0},{1,9},{9,1},{2,10},{10,2},{3,11},{11,3},{4,12},{12,4},... | collective-permute-start | bytes 1769480 | tf_op jit(solution)/shard_map/ppermute | solution.py:313
  9.2 25.7 %collective-permute-start.4 = (bf16[384,768]{1,0:T(8,128)(2,1)}, bf16[384,768]{1,0:T(8,128)(2,1)S(1)}, u32[]{:S(2)}, u32[]{:S(2)}) collective-permute-start(bf16[384,768]{1,0:T(8,128)(2,1)} %get-tuple-element.48.refs_0_), channel_id=1, source_target_pairs={{0,20},{1,21},{2,22},{3,23},{4,16},{5,17},{6,18},{7,19},{16,4},{17... | collective-permute-start | bytes 1769480 | tf_op jit(solution)/shard_map/ppermute | solution.py:317
  11.8 8.5 %copy-start = (bf16[384,3072]{1,0:T(8,128)(2,1)S(1)}, bf16[384,3072]{1,0:T(8,128)(2,1)}, u32[]{:S(2)}) copy-start(bf16[384,3072]{1,0:T(8,128)(2,1)} %w0.1) | copy-start | bytes 7077892
  12.7 22.1 %all-to-all-start = ((bf16[8,256,128]{2,1,0:T(8,128)(2,1)}), bf16[8,256,128]{2,1,0:T(8,128)(2,1)}, u32[]{:S(2)}, u32[]{:S(2)}) async-start(bf16[8,256,128]{2,1,0:T(8,128)(2,1)} %bitcast.31), calls=%async_computation | async-start | bytes 1048576 | tf_op jit(solution)/shard_map/all_to_all | solution.py:354
  34.9 9.9 %copy-start.1 = (bf16[384,768]{1,0:T(8,128)(2,1)}, bf16[384,768]{1,0:T(8,128)(2,1)S(1)}, u32[]{:S(2)}) copy-start(bf16[384,768]{1,0:T(8,128)(2,1)S(1)} %collective-permute-done.refs_1_) | copy-start | bytes 1769476
  34.9 9.9 %copy-start.2 = (bf16[384,768]{1,0:T(8,128)(2,1)}, bf16[384,768]{1,0:T(8,128)(2,1)S(1)}, u32[]{:S(2)}) copy-start(bf16[384,768]{1,0:T(8,128)(2,1)S(1)} %collective-permute-done.4.refs_2_) | copy-start | bytes 1769476
  34.9 9.8 %collective-permute-start.5 = (bf16[384,768]{1,0:T(8,128)(2,1)S(1)}, bf16[384,768]{1,0:T(8,128)(2,1)S(1)}, u32[]{:S(2)}, u32[]{:S(2)}) collective-permute-start(bf16[384,768]{1,0:T(8,128)(2,1)S(1)} %collective-permute-done.4.refs_2_), channel_id=1, source_target_pairs={{0,8},{8,0},{1,9},{9,1},{2,10},{10,2},{3,11},{11,3},{4,12},{12,4},... | collective-permute-start | bytes 1769480 | tf_op jit(solution)/shard_map/ppermute | solution.py:313
  36.6 13.3 %collective-permute-start.6 = (bf16[128,1536]{1,0:T(8,128)(2,1)S(1)}, bf16[128,1536]{1,0:T(8,128)(2,1)S(1)}, u32[]{:S(2)}, u32[]{:S(2)}) collective-permute-start(bf16[128,1536]{1,0:T(8,128)(2,1)S(1)} %slice.8), channel_id=1, source_target_pairs={{0,1},{1,2},{2,3},{3,0},{4,5},{5,6},{6,7},{7,4},{8,9},{9,10},{10,1... | collective-permute-start | bytes 1179656 | tf_op jit(solution)/shard_map/ppermute | solution.py:309
  37.7 12.2 %collective-permute-start.7 = (bf16[128,1536]{1,0:T(8,128)(2,1)S(1)}, bf16[128,1536]{1,0:T(8,128)(2,1)S(1)}, u32[]{:S(2)}, u32[]{:S(2)}) collective-permute-start(bf16[128,1536]{1,0:T(8,128)(2,1)S(1)} %slice.9), channel_id=1, source_target_pairs={{0,3},{1,0},{2,1},{3,2},{4,7},{5,4},{6,5},{7,6},{8,11},{9,8},{10,9... | collective-permute-start | bytes 1179656 | tf_op jit(solution)/shard_map/ppermute | solution.py:309
  41.0 44.5 %collective-permute-start.14 = (bf16[384,1536]{1,0:T(8,128)(2,1)S(1)}, bf16[384,1536]{1,0:T(8,128)(2,1)S(1)}, u32[]{:S(2)}, u32[]{:S(2)}) collective-permute-start(bf16[384,1536]{1,0:T(8,128)(2,1)S(1)} %copy-done.9), channel_id=1, source_target_pairs={{0,20},{1,21},{2,22},{3,23},{4,16},{5,17},{6,18},{7,19},{16,4},{17... | collective-permute-start | bytes 3538952 | tf_op jit(solution)/shard_map/ppermute | solution.py:317
  49.8 17.3 %collective-permute-start.13 = (bf16[512,384]{1,0:T(8,128)(2,1)}, bf16[512,384]{1,0:T(8,128)(2,1)S(1)}, u32[]{:S(2)}, u32[]{:S(2)}) collective-permute-start(bf16[512,384]{1,0:T(8,128)(2,1)} %shard_map.68), channel_id=1, source_target_pairs={{0,4},{1,5},{2,6},{3,7},{4,0},{5,1},{6,2},{7,3},{8,12},{9,13},{10,... | collective-permute-start | bytes 1179656 | tf_op jit(solution)/shard_map/ppermute | solution.py:309
  55.7 10.8 %copy-start.13 = (bf16[128,1536]{1,0:T(8,128)(2,1)S(1)}, bf16[128,1536]{1,0:T(8,128)(2,1)}, u32[]{:S(2)}) copy-start(bf16[128,1536]{1,0:T(8,128)(2,1)} %copy-done.12) | copy-start | bytes 1179652
  55.7 11.3 %copy-start.15 = (bf16[128,1536]{1,0:T(8,128)(2,1)S(1)}, bf16[128,1536]{1,0:T(8,128)(2,1)}, u32[]{:S(2)}) copy-start(bf16[128,1536]{1,0:T(8,128)(2,1)} %copy-done.14) | copy-start | bytes 1179652
  55.7 29.8 %collective-permute-start.8 = (bf16[256,1536]{1,0:T(8,128)(2,1)}, bf16[256,1536]{1,0:T(8,128)(2,1)S(1)}, u32[]{:S(2)}, u32[]{:S(2)}) collective-permute-start(bf16[256,1536]{1,0:T(8,128)(2,1)} %collective-permute-done.1.refs_7_.refs_5_), channel_id=1, source_target_pairs={{0,1},{1,2},{2,3},{3,0},{4,5},{5,6},{6,7},{7,4},{8,9},{9,10},{10,1... | collective-permute-start | bytes 2359304 | tf_op jit(solution)/shard_map/ppermute | solution.py:309
  55.8 29.7 %collective-permute-start.9 = (bf16[256,1536]{1,0:T(8,128)(2,1)}, bf16[256,1536]{1,0:T(8,128)(2,1)S(1)}, u32[]{:S(2)}, u32[]{:S(2)}) collective-permute-start(bf16[256,1536]{1,0:T(8,128)(2,1)} %collective-permute-done.1.refs_7_.refs_5_), channel_id=1, source_target_pairs={{0,3},{1,0},{2,1},{3,2},{4,7},{5,4},{6,5},{7,6},{8,11},{9,8},{10,9... | collective-permute-start | bytes 2359304 | tf_op jit(solution)/shard_map/ppermute | solution.py:309
  59.1 7.4 %collective-permute-start.10 = (bf16[256,384]{1,0:T(8,128)(2,1)}, bf16[256,384]{1,0:T(8,128)(2,1)}, u32[]{:S(2)}, u32[]{:S(2)}) collective-permute-start(bf16[256,384]{1,0:T(8,128)(2,1)} %get-tuple-element.60), channel_id=1, source_target_pairs={{0,4},{1,5},{2,6},{3,7},{4,0},{5,1},{6,2},{7,3},{8,12},{9,13},{10,... | collective-permute-start | bytes 589832 | tf_op jit(solution)/shard_map/ppermute | solution.py:309
  66.5 18.9 %collective-permute-start.11 = (bf16[128,1536]{1,0:T(8,128)(2,1)S(1)}, bf16[128,1536]{1,0:T(8,128)(2,1)S(1)}, u32[]{:S(2)}, u32[]{:S(2)}) collective-permute-start(bf16[128,1536]{1,0:T(8,128)(2,1)S(1)} %copy-done.13), channel_id=1, source_target_pairs={{0,4},{1,5},{2,6},{3,7},{4,0},{5,1},{6,2},{7,3},{8,12},{9,13},{10,... | collective-permute-start | bytes 1179656 | tf_op jit(solution)/shard_map/ppermute | solution.py:309
  67.1 18.4 %collective-permute-start.12 = (bf16[128,1536]{1,0:T(8,128)(2,1)S(1)}, bf16[128,1536]{1,0:T(8,128)(2,1)S(1)}, u32[]{:S(2)}, u32[]{:S(2)}) collective-permute-start(bf16[128,1536]{1,0:T(8,128)(2,1)S(1)} %copy-done.15), channel_id=1, source_target_pairs={{0,4},{1,5},{2,6},{3,7},{4,0},{5,1},{6,2},{7,3},{8,12},{9,13},{10,... | collective-permute-start | bytes 1179656 | tf_op jit(solution)/shard_map/ppermute | solution.py:309
  85.5 23.1 %collective-permute-start.15 = (bf16[384,3072]{1,0:T(8,128)(2,1)S(1)}, bf16[384,3072]{1,0:T(8,128)(2,1)}, u32[]{:S(2)}, u32[]{:S(2)}) collective-permute-start(bf16[384,3072]{1,0:T(8,128)(2,1)S(1)} %copy-done), channel_id=1, source_target_pairs={{0,8},{8,0},{1,9},{9,1},{2,10},{10,2},{3,11},{11,3},{4,12},{12,4},... | collective-permute-start | bytes 7077896 | tf_op jit(solution)/shard_map/ppermute | solution.py:313
  87.3 21.4 %all-to-all-start.1 = ((bf16[8,256,256]{2,1,0:T(8,128)(2,1)}), bf16[8,256,256]{2,1,0:T(8,128)(2,1)S(1)}, u32[]{:S(2)}, u32[]{:S(2)}) async-start(bf16[8,256,256]{2,1,0:T(8,128)(2,1)} %bitcast.33), calls=%async_computation.1 | async-start | bytes 2097152 | tf_op jit(solution)/shard_map/all_to_all | solution.py:411
  90.8 37.4 %collective-permute-start.17 = (bf16[384,1536]{1,0:T(8,128)(2,1)}, bf16[384,1536]{1,0:T(8,128)(2,1)}, u32[]{:S(2)}, u32[]{:S(2)}) collective-permute-start(bf16[384,1536]{1,0:T(8,128)(2,1)} %copy-done.7), channel_id=1, source_target_pairs={{0,32},{32,0},{64,96},{96,64},{1,33},{33,1},{65,97},{97,65},{2,34}... | collective-permute-start | bytes 3538952 | tf_op jit(solution)/shard_map/ppermute | solution.py:417
  108.6 13.8 %copy-start.4 = (bf16[8,256,256]{2,1,0:T(8,128)(2,1)}, bf16[8,256,256]{2,1,0:T(8,128)(2,1)S(1)}, u32[]{:S(2)}) copy-start(bf16[8,256,256]{2,1,0:T(8,128)(2,1)S(1)} %all-to-all-done.1.first_ref) | copy-start | bytes 3145732
  108.6 19.6 %all-to-all-start.2 = ((bf16[8,256,256]{2,1,0:T(8,128)(2,1)}), bf16[8,256,256]{2,1,0:T(8,128)(2,1)S(1)}, u32[]{:S(2)}, u32[]{:S(2)}) async-start(bf16[8,256,256]{2,1,0:T(8,128)(2,1)} %bitcast.34), calls=%async_computation.2 | async-start | bytes 2097152 | tf_op jit(solution)/shard_map/all_to_all | solution.py:411
  122.5 2.3 %collective-permute-start.16 = (bf16[768,384]{1,0:T(8,128)(2,1)}, bf16[768,384]{1,0:T(8,128)(2,1)S(1)}, u32[]{:S(2)}, u32[]{:S(2)}) collective-permute-start(bf16[768,384]{1,0:T(8,128)(2,1)} %get-tuple-element.80), channel_id=1, source_target_pairs={{0,8},{8,0},{1,9},{9,1},{2,10},{10,2},{3,11},{11,3},{4,12},{12,4},... | collective-permute-start | bytes 1769480 | tf_op jit(solution)/shard_map/ppermute | solution.py:313
  128.2 10.7 %copy-start.5 = (bf16[8,256,256]{2,1,0:T(8,128)(2,1)}, bf16[8,256,256]{2,1,0:T(8,128)(2,1)S(1)}, u32[]{:S(2)}) copy-start(bf16[8,256,256]{2,1,0:T(8,128)(2,1)S(1)} %all-to-all-done.2.second_ref) | copy-start | bytes 3145732
  128.2 10.6 %collective-permute-start.18 = (bf16[384,1536]{1,0:T(8,128)(2,1)S(1)}, bf16[384,1536]{1,0:T(8,128)(2,1)}, u32[]{:S(2)}, u32[]{:S(2)}) collective-permute-start(bf16[384,1536]{1,0:T(8,128)(2,1)S(1)} %copy-done.8), channel_id=1, source_target_pairs={{0,8},{8,0},{1,9},{9,1},{2,10},{10,2},{3,11},{11,3},{4,12},{12,4},... | collective-permute-start | bytes 3538952 | tf_op jit(solution)/shard_map/ppermute | solution.py:313
  128.5 10.4 %collective-permute-start.19 = (bf16[384,1536]{1,0:T(8,128)(2,1)}, bf16[384,1536]{1,0:T(8,128)(2,1)}, u32[]{:S(2)}, u32[]{:S(2)}) collective-permute-start(bf16[384,1536]{1,0:T(8,128)(2,1)} %collective-permute-done.17.w3), channel_id=1, source_target_pairs={{0,8},{8,0},{1,9},{9,1},{2,10},{10,2},{3,11},{11,3},{4,12},{12,4},... | collective-permute-start | bytes 3538952 | tf_op jit(solution)/shard_map/ppermute | solution.py:313
  128.8 26.0 %all-to-all-start.3 = ((bf16[64,12,384]{2,1,0:T(8,128)(2,1)}), bf16[64,12,384]{2,1,0:T(8,128)(2,1)S(1)}, u32[]{:S(2)}, u32[]{:S(2)}) async-start(bf16[64,12,384]{2,1,0:T(8,128)(2,1)} %shard_map.74), calls=%async_computation.3 | async-start | bytes 1572864 | tf_op jit(solution)/shard_map/all_to_all | solution.py:441
  (13 other events, 21.4 us)

commit v11 on v10

--- a/solution.py
+++ b/solution.py
@@ -242,7 +242,9 @@
         rows = slice(i * 96, (i + 1) * 96)
         t = keep_ref[rows, :] + got_ref[rows, :].astype(F32)
         for s in range(SEQ):
-            out_ref[i * SEQ + s] = t[s * 12 : (s + 1) * 12].astype(BF)
+            part = t[s * 12 : (s + 1) * 12]
+            part = jnp.concatenate([part[:, k * GW : (k + 1) * GW] for k in range(3)], axis=0)
+            out_ref[i * SEQ + s] = part.astype(BF)
 
 
 def combine_kernel(parts_ref, out_ref):
@@ -252,8 +254,8 @@
             t = parts_ref[r * SEQ + s].astype(F32)
             total = t if total is None else total + t
         at = s * GW
-        low, high = total[:, 0:128], total[:, 128:256]
-        out_ref[:, at : at + GW] = total[:, 256:384]
+        low, high = total[0:12], total[12:24]
+        out_ref[:, at : at + GW] = total[24:36]
         out_ref[:, 1024 + at : 1024 + at + GW] = join(low, high, 0)
         out_ref[:, 2048 + at : 2048 + at + GW] = join(low, high, 1)
 
@@ -434,7 +436,7 @@
         ],
     )(place, first, second, *blocks)
     got = sibling(out)
-    partial = call(add_kernel, shape((64, 12, 384)), [VM, VM])(keep, got)
+    partial = call(add_kernel, shape((64, 36, GW)), [VM, VM])(keep, got)
     partial, back1, weight_half, weight_rest = tie((partial, back1, weight_half, weight_rest))
     weights = [projection, beside, weight_half, weight_rest]
     weights += [sibling(weight_half), sibling(weight_rest)]

time: 158 us -> 157 us (level)
  transfers between devices with their start and end apart: 24 -> 24, of which waited for: 3 -> 4; matrix products, arithmetic and copies ran while one was open for 5% -> 5% of each run, Pallas kernels for 42% -> 43%
where the time goes in v11:
time: 157 us; the launch traced here: 156 us
  Pallas kernels  71.8 us (46%)
  starting transfers between devices  49 us (31%)
  waiting for transfers between devices  20.9 us (13%)
  local copies, waits for them, and re-layouts  11.6 us (7%)
  between operations  1.67 us (1%)
    pallas_call x2, Pallas kernels, attend(): call(functools.partial(attention_kernel, head), shape((T, 256)), [SM, SM]...  31.9 us
    ppermute x11, starting transfers between devices, send(): return lax.ppermute(v, 'seq', way)  16.2 us
    pallas_call x3, Pallas kernels, project(): call(functools.partial(project_kernel, len(rows)), (shape((height, 384)),...  13.9 us
    all_to_all x1, waiting for transfers between devices, body(): lax.all_to_all(tie((upstream, normed))[0], 'seq', 0, 0, tiled=True)  13.6 us
    all_to_all x1, starting transfers between devices, body(): partial = lax.all_to_all(partial, ('dp', 'zh', 'seq'), 0, 0, tiled=True)  10 us
    pallas_call x1, Pallas kernels, body(): call(input_gradient_kernel, (shape((ROWS, 1024)), shape((ROWS, D), F32)),...  9.59 us
    all_to_all x2, starting transfers between devices, send_back(): lax.all_to_all(grads.reshape(SEQ, ROWS, 256), 'seq', 0, 0, tiled=True)  8.9 us
    pallas_call x1, Pallas kernels, body(): call(weight_gradient_kernel, (shape((768, 384), F32), shape((768, 384))),...  8.46 us
  transfers between devices with their start and end apart: 24, of which 4 were waited for; matrix products, arithmetic and copies ran while one was open for 5% of the time, Pallas kernels for 43%

profile of v11, /device:TPU:0, one launch (start us, length us, event | category | flops | bytes accessed | tf_op | source)
XLA Modules:
  0.0 156.1 jit_solution(2392167859366601544)
XLA Ops:
  0.7 3.5 %shard_map.67 = (bf16[256,1536]{1,0:T(8,128)(2,1)}, bf16[384,768]{1,0:T(8,128)(2,1)}) custom-call(s32[1]{0:T(128)} %bitcast.y_ref, bf16[256,1536]{1,0:T(8,128)(2,1)} %bitcast.29, bf16[384,3072]{1,0:T(8,128)(2,1)} %w0.1), custom_call_target="tpu_custom_call" | custom-call | bytes 1048576 | tf_op jit(solution)/shard_map/pallas_call | solution.py:342
  4.1 2.1 %collective-permute-start.1 = (bf16[256,1536]{1,0:T(8,128)(2,1)}, bf16[256,1536]{1,0:T(8,128)(2,1)}, u32[]{:S(2)}, u32[]{:S(2)}) collective-permute-start(bf16[256,1536]{1,0:T(8,128)(2,1)} %get-tuple-element.49.refs_4_.refs_0_), channel_id=1, source_target_pairs={{0,4},{1,5},{2,6},{3,7},{4,0},{5,1},{6,2},{7,3},{8,12},{9,13},{10,... | collective-permute-start | bytes 2359304 | tf_op jit(solution)/shard_map/ppermute | solution.py:311
  6.2 3.0 %collective-permute-start.2 = (bf16[256,1536]{1,0:T(8,128)(2,1)}, bf16[256,1536]{1,0:T(8,128)(2,1)}, u32[]{:S(2)}, u32[]{:S(2)}) collective-permute-start(bf16[256,1536]{1,0:T(8,128)(2,1)} %get-tuple-element.49.refs_4_.refs_0_), channel_id=1, source_target_pairs={{0,3},{1,0},{2,1},{3,2},{4,7},{5,4},{6,5},{7,6},{8,11},{9,8},{10,9... | collective-permute-start | bytes 2359304 | tf_op jit(solution)/shard_map/ppermute | solution.py:311
  9.2 2.5 %collective-permute-start.4 = (bf16[384,768]{1,0:T(8,128)(2,1)}, bf16[384,768]{1,0:T(8,128)(2,1)S(1)}, u32[]{:S(2)}, u32[]{:S(2)}) collective-permute-start(bf16[384,768]{1,0:T(8,128)(2,1)} %get-tuple-element.48.refs_0_), channel_id=1, source_target_pairs={{0,20},{1,21},{2,22},{3,23},{4,16},{5,17},{6,18},{7,19},{16,4},{17... | collective-permute-start | bytes 1769480 | tf_op jit(solution)/shard_map/ppermute | solution.py:319
  11.9 0.9 copy.10
  12.7 5.0 %all-to-all-start = ((bf16[8,256,128]{2,1,0:T(8,128)(2,1)}), bf16[8,256,128]{2,1,0:T(8,128)(2,1)}, u32[]{:S(2)}, u32[]{:S(2)}) async-start(bf16[8,256,128]{2,1,0:T(8,128)(2,1)} %bitcast.31), calls=%async_computation | async-start | bytes 1048576 | tf_op jit(solution)/shard_map/all_to_all | solution.py:356
  20.2 1.1 constant_dynamic-slice_fusion
  21.3 13.6 %all-to-all-done = bf16[8,256,128]{2,1,0:T(8,128)(2,1)} async-done(((bf16[8,256,128]{2,1,0:T(8,128)(2,1)}), bf16[8,256,128]{2,1,0:T(8,128)(2,1)}, u32[]{:S(2)}, u32[]{:S(2)}) %all-to-all-start) | async-done | bytes 524320 | tf_op jit(solution)/shard_map/all_to_all | solution.py:356
  35.0 1.5 slice.8
  36.6 1.0 slice.9
  37.7 3.3 %collective-permute-start.7 = (bf16[128,1536]{1,0:T(8,128)(2,1)S(1)}, bf16[128,1536]{1,0:T(8,128)(2,1)S(1)}, u32[]{:S(2)}, u32[]{:S(2)}) collective-permute-start(bf16[128,1536]{1,0:T(8,128)(2,1)S(1)} %slice.9), channel_id=1, source_target_pairs={{0,3},{1,0},{2,1},{3,2},{4,7},{5,4},{6,5},{7,6},{8,11},{9,8},{10,9... | collective-permute-start | bytes 1179656 | tf_op jit(solution)/shard_map/ppermute | solution.py:311
  41.0 3.8 %collective-permute-start.14 = (bf16[384,1536]{1,0:T(8,128)(2,1)S(1)}, bf16[384,1536]{1,0:T(8,128)(2,1)S(1)}, u32[]{:S(2)}, u32[]{:S(2)}) collective-permute-start(bf16[384,1536]{1,0:T(8,128)(2,1)S(1)} %copy-done.9), channel_id=1, source_target_pairs={{0,20},{1,21},{2,22},{3,23},{4,16},{5,17},{6,18},{7,19},{16,4},{17... | collective-permute-start | bytes 3538952 | tf_op jit(solution)/shard_map/ppermute | solution.py:319
  45.6 4.2 %shard_map.68 = bf16[512,384]{1,0:T(8,128)(2,1)} custom-call(s32[5]{0:T(128)} %stack.75.owner_ref.pos_ref, s32[3]{0:T(128)} %pad_add_fusion.group_ref, bf16[384,768]{1,0:T(8,128)(2,1)} %get-tuple-element.48.refs_0_, bf16[384,768]{1,0:T(8,128)(2,1)} %copy-done.1, bf16[384,768]{1,0:T(8,128)(2,1)} %copy-done.2, bf16[384,768]{1,0:T(8,128)(2,1)} %copy-done.3, ...), custom_call_target="tpu_custom_call" | custom-call | bytes 1048576 | tf_op jit(solution)/shard_map/pallas_call | solution.py:369
  51.4 4.3 %shard_map.69 = (bf16[256,384]{1,0:T(8,128)(2,1)}, bf16[256,384]{1,0:T(8,128)(2,1)}) custom-call(s32[5]{0:T(128)} %stack.75.owner_ref.pos_ref, s32[3]{0:T(128)} %pad_add_fusion.group_ref, bf16[384,768]{1,0:T(8,128)(2,1)} %get-tuple-element.48.refs_0_, bf16[384,768]{1,0:T(8,128)(2,1)} %copy-done.1, bf16[384,768]{1,0:T(8,128)(2,1)} %copy-done.2, ...), custom_call_target="tpu_custom_call" | custom-call | bytes 1048576 | tf_op jit(solution)/shard_map/pallas_call | solution.py:369
  55.8 3.2 %collective-permute-start.9 = (bf16[256,1536]{1,0:T(8,128)(2,1)}, bf16[256,1536]{1,0:T(8,128)(2,1)S(1)}, u32[]{:S(2)}, u32[]{:S(2)}) collective-permute-start(bf16[256,1536]{1,0:T(8,128)(2,1)} %collective-permute-done.1.refs_7_.refs_5_), channel_id=1, source_target_pairs={{0,3},{1,0},{2,1},{3,2},{4,7},{5,4},{6,5},{7,6},{8,11},{9,8},{10,9... | collective-permute-start | bytes 2359304 | tf_op jit(solution)/shard_map/ppermute | solution.py:311
  59.1 2.0 %collective-permute-start.10 = (bf16[256,384]{1,0:T(8,128)(2,1)}, bf16[256,384]{1,0:T(8,128)(2,1)}, u32[]{:S(2)}, u32[]{:S(2)}) collective-permute-start(bf16[256,384]{1,0:T(8,128)(2,1)} %get-tuple-element.60), channel_id=1, source_target_pairs={{0,4},{1,5},{2,6},{3,7},{4,0},{5,1},{6,2},{7,3},{8,12},{9,13},{10,... | collective-permute-start | bytes 589832 | tf_op jit(solution)/shard_map/ppermute | solution.py:311
  61.1 5.4 %shard_map.70.kept_ref = bf16[1024,384]{1,0:T(8,128)(2,1)} custom-call(s32[5]{0:T(128)} %stack.75.owner_ref.pos_ref, s32[2]{0:T(128)} %pad_add_fusion.1.group_ref, bf16[384,768]{1,0:T(8,128)(2,1)} %get-tuple-element.48.refs_0_, bf16[384,768]{1,0:T(8,128)(2,1)} %copy-done.1, bf16[384,768]{1,0:T(8,128)(2,1)} %copy-done.2, bf16[384,768]{1,0:T(8,128)(2,1)} %copy-done.3, ...), custom_call_target="tpu_custom_call" | custom-call | bytes 1048576 | tf_op jit(solution)/shard_map/pallas_call | solution.py:369
  67.1 1.8 %collective-permute-start.12 = (bf16[128,1536]{1,0:T(8,128)(2,1)S(1)}, bf16[128,1536]{1,0:T(8,128)(2,1)S(1)}, u32[]{:S(2)}, u32[]{:S(2)}) collective-permute-start(bf16[128,1536]{1,0:T(8,128)(2,1)S(1)} %copy-done.15), channel_id=1, source_target_pairs={{0,4},{1,5},{2,6},{3,7},{4,0},{5,1},{6,2},{7,3},{8,12},{9,13},{10,... | collective-permute-start | bytes 1179656 | tf_op jit(solution)/shard_map/ppermute | solution.py:311
  69.5 15.9 %shard_map.71.first_ref = bf16[2048,256]{1,0:T(8,128)(2,1)} custom-call(s32[9]{0:T(128)} %stack.69.pos_ref, s32[1]{0:T(128)S(6)} %copy.11.len_ref, bf16[1024,384]{1,0:T(8,128)(2,1)} %shard_map.70.kept_ref, bf16[256,384]{1,0:T(8,128)(2,1)} %get-tuple-element.68.far_ref, bf16[512,384]{1,0:T(8,128)(2,1)} %copy-done.18, ...), custom_call_target="tpu_custom_call" | custom-call | flops 1000000000 | bytes 1048576 | tf_op jit(solution)/shard_map/pallas_call | solution.py:393
  87.3 3.6 %all-to-all-start.1 = ((bf16[8,256,256]{2,1,0:T(8,128)(2,1)}), bf16[8,256,256]{2,1,0:T(8,128)(2,1)S(1)}, u32[]{:S(2)}, u32[]{:S(2)}) async-start(bf16[8,256,256]{2,1,0:T(8,128)(2,1)} %bitcast.33), calls=%async_computation.1 | async-start | bytes 2097152 | tf_op jit(solution)/shard_map/all_to_all | solution.py:413
  90.8 1.8 %collective-permute-start.17 = (bf16[384,1536]{1,0:T(8,128)(2,1)}, bf16[384,1536]{1,0:T(8,128)(2,1)}, u32[]{:S(2)}, u32[]{:S(2)}) collective-permute-start(bf16[384,1536]{1,0:T(8,128)(2,1)} %copy-done.7), channel_id=1, source_target_pairs={{0,32},{32,0},{64,96},{96,64},{1,33},{33,1},{65,97},{97,65},{2,34}... | collective-permute-start | bytes 3538952 | tf_op jit(solution)/shard_map/ppermute | solution.py:419
  92.6 16.0 %shard_map.72.second_ref = bf16[2048,256]{1,0:T(8,128)(2,1)} custom-call(s32[9]{0:T(128)} %stack.69.pos_ref, s32[1]{0:T(128)S(6)} %copy.11.len_ref, bf16[1024,384]{1,0:T(8,128)(2,1)} %shard_map.70.kept_ref, bf16[256,384]{1,0:T(8,128)(2,1)} %get-tuple-element.68.far_ref, bf16[512,384]{1,0:T(8,128)(2,1)} %copy-done.18, ...), custom_call_target="tpu_custom_call" | custom-call | flops 10000000000 | bytes 1048576 | tf_op jit(solution)/shard_map/pallas_call | solution.py:393
  108.6 5.3 %all-to-all-start.2 = ((bf16[8,256,256]{2,1,0:T(8,128)(2,1)}), bf16[8,256,256]{2,1,0:T(8,128)(2,1)S(1)}, u32[]{:S(2)}, u32[]{:S(2)}) async-start(bf16[8,256,256]{2,1,0:T(8,128)(2,1)} %bitcast.34), calls=%async_computation.2 | async-start | bytes 2097152 | tf_op jit(solution)/shard_map/all_to_all | solution.py:413
  114.0 8.5 %shard_map.73 = (f32[768,384]{1,0:T(8,128)}, bf16[768,384]{1,0:T(8,128)(2,1)}) custom-call(s32[9]{0:T(128)} %stack.69.pos_ref, bf16[2048,256]{1,0:T(8,128)(2,1)} %shard_map.71.first_ref, bf16[2048,256]{1,0:T(8,128)(2,1)} %shard_map.72.second_ref, bf16[256,1536]{1,0:T(8,128)(2,1)} %get-tuple-element.49.refs_4_.refs_0_, ...), custom_call_target="tpu_custom_call" | custom-call | flops 2415919104 | bytes 1048576 | tf_op jit(solution)/shard_map/pallas_call | solution.py:426
  122.6 2.2 %collective-permute-done.16.got_ref = bf16[768,384]{1,0:T(8,128)(2,1)S(1)} collective-permute-done((bf16[768,384]{1,0:T(8,128)(2,1)}, bf16[768,384]{1,0:T(8,128)(2,1)S(1)}, u32[]{:S(2)}, u32[]{:S(2)}) %collective-permute-start.16) | collective-permute-done | bytes 589856 | tf_op jit(solution)/shard_map/ppermute | solution.py:315
  124.8 0.9 copy-done.10
  125.6 2.5 %shard_map.74 = bf16[64,36,128]{2,1,0:T(8,128)(2,1)} custom-call(f32[768,384]{1,0:T(8,128)} %get-tuple-element.79.keep_ref, bf16[768,384]{1,0:T(8,128)(2,1)} %copy-done.10), custom_call_target="tpu_custom_call" | custom-call | bytes 1048576 | tf_op jit(solution)/shard_map/pallas_call | solution.py:439
  128.8 10.0 %all-to-all-start.3 = ((bf16[64,36,128]{2,1,0:T(8,128)(2,1)}), bf16[64,36,128]{2,1,0:T(8,128)(2,1)S(1)}, u32[]{:S(2)}, u32[]{:S(2)}) async-start(bf16[64,36,128]{2,1,0:T(8,128)(2,1)} %shard_map.74), calls=%async_computation.3 | async-start | bytes 1310720 | tf_op jit(solution)/shard_map/all_to_all | solution.py:443
  138.8 9.6 %shard_map.75 = (bf16[256,1024]{1,0:T(8,128)(2,1)}, f32[256,1536]{1,0:T(8,128)}) custom-call(s32[5]{0:T(128)} %stack.75.owner_ref.pos_ref, bf16[8,256,256]{2,1,0:T(8,128)(2,1)} %copy-done.4, bf16[8,256,256]{2,1,0:T(8,128)(2,1)} %copy-done.5, bf16[384,3072]{1,0:T(8,128)(2,1)} %w0.1, bf16[384,3072]{1,0:T(8,128)(2,1)} %collective-permute-done.15.w1, ...), custom_call_target="tpu_custom_call" | custom-call | flops 2415919104 | bytes 1048576 | tf_op jit(solution)/shard_map/pallas_call | solution.py:444
  148.4 4.9 %all-to-all-done.3.parts_ref = bf16[64,36,128]{2,1,0:T(8,128)(2,1)S(1)} async-done(((bf16[64,36,128]{2,1,0:T(8,128)(2,1)}), bf16[64,36,128]{2,1,0:T(8,128)(2,1)S(1)}, u32[]{:S(2)}, u32[]{:S(2)}) %all-to-all-start.3) | async-done | bytes 589856 | tf_op jit(solution)/shard_map/all_to_all | solution.py:443
  153.4 0.9 copy-done.6
  154.2 1.9 %shard_map.76 = f32[12,3072]{1,0:T(8,128)} custom-call(bf16[64,36,128]{2,1,0:T(8,128)(2,1)} %copy-done.6), custom_call_target="tpu_custom_call" | custom-call | bytes 1048576 | tf_op jit(solution)/shard_map/pallas_call | solution.py:456
  (77 shorter events, 8.3 us)
Async XLA Ops:
  0.6 11.1 %copy-start.11 = (bf16[1,256,1024]{2,1,0:T(8,128)(2,1)S(1)}, bf16[1,256,1024]{2,1,0:T(8,128)(2,1)}, u32[]{:S(2)}) copy-start(bf16[1,256,1024]{2,1,0:T(8,128)(2,1)} %param.7) | copy-start | bytes 1572868
  4.1 30.8 %collective-permute-start.1 = (bf16[256,1536]{1,0:T(8,128)(2,1)}, bf16[256,1536]{1,0:T(8,128)(2,1)}, u32[]{:S(2)}, u32[]{:S(2)}) collective-permute-start(bf16[256,1536]{1,0:T(8,128)(2,1)} %get-tuple-element.49.refs_4_.refs_0_), channel_id=1, source_target_pairs={{0,4},{1,5},{2,6},{3,7},{4,0},{5,1},{6,2},{7,3},{8,12},{9,13},{10,... | collective-permute-start | bytes 2359304 | tf_op jit(solution)/shard_map/ppermute | solution.py:311
  6.2 28.7 %collective-permute-start.2 = (bf16[256,1536]{1,0:T(8,128)(2,1)}, bf16[256,1536]{1,0:T(8,128)(2,1)}, u32[]{:S(2)}, u32[]{:S(2)}) collective-permute-start(bf16[256,1536]{1,0:T(8,128)(2,1)} %get-tuple-element.49.refs_4_.refs_0_), channel_id=1, source_target_pairs={{0,3},{1,0},{2,1},{3,2},{4,7},{5,4},{6,5},{7,6},{8,11},{9,8},{10,9... | collective-permute-start | bytes 2359304 | tf_op jit(solution)/shard_map/ppermute | solution.py:311
  9.2 25.7 %collective-permute-start.3 = (bf16[256,1536]{1,0:T(8,128)(2,1)}, bf16[256,1536]{1,0:T(8,128)(2,1)}, u32[]{:S(2)}, u32[]{:S(2)}) collective-permute-start(bf16[256,1536]{1,0:T(8,128)(2,1)} %get-tuple-element.49.refs_4_.refs_0_), channel_id=1, source_target_pairs={{0,1},{1,2},{2,3},{3,0},{4,5},{5,6},{6,7},{7,4},{8,9},{9,10},{10,1... | collective-permute-start | bytes 2359304 | tf_op jit(solution)/shard_map/ppermute | solution.py:311
  9.2 25.7 %collective-permute-start = (bf16[384,768]{1,0:T(8,128)(2,1)}, bf16[384,768]{1,0:T(8,128)(2,1)S(1)}, u32[]{:S(2)}, u32[]{:S(2)}) collective-permute-start(bf16[384,768]{1,0:T(8,128)(2,1)} %get-tuple-element.48.refs_0_), channel_id=1, source_target_pairs={{0,8},{8,0},{1,9},{9,1},{2,10},{10,2},{3,11},{11,3},{4,12},{12,4},... | collective-permute-start | bytes 1769480 | tf_op jit(solution)/shard_map/ppermute | solution.py:315
  9.2 25.7 %collective-permute-start.4 = (bf16[384,768]{1,0:T(8,128)(2,1)}, bf16[384,768]{1,0:T(8,128)(2,1)S(1)}, u32[]{:S(2)}, u32[]{:S(2)}) collective-permute-start(bf16[384,768]{1,0:T(8,128)(2,1)} %get-tuple-element.48.refs_0_), channel_id=1, source_target_pairs={{0,20},{1,21},{2,22},{3,23},{4,16},{5,17},{6,18},{7,19},{16,4},{17... | collective-permute-start | bytes 1769480 | tf_op jit(solution)/shard_map/ppermute | solution.py:319
  11.8 8.5 %copy-start = (bf16[384,3072]{1,0:T(8,128)(2,1)S(1)}, bf16[384,3072]{1,0:T(8,128)(2,1)}, u32[]{:S(2)}) copy-start(bf16[384,3072]{1,0:T(8,128)(2,1)} %w0.1) | copy-start | bytes 7077892
  12.7 22.1 %all-to-all-start = ((bf16[8,256,128]{2,1,0:T(8,128)(2,1)}), bf16[8,256,128]{2,1,0:T(8,128)(2,1)}, u32[]{:S(2)}, u32[]{:S(2)}) async-start(bf16[8,256,128]{2,1,0:T(8,128)(2,1)} %bitcast.31), calls=%async_computation | async-start | bytes 1048576 | tf_op jit(solution)/shard_map/all_to_all | solution.py:356
  34.9 9.9 %copy-start.1 = (bf16[384,768]{1,0:T(8,128)(2,1)}, bf16[384,768]{1,0:T(8,128)(2,1)S(1)}, u32[]{:S(2)}) copy-start(bf16[384,768]{1,0:T(8,128)(2,1)S(1)} %collective-permute-done.refs_1_) | copy-start | bytes 1769476
  34.9 9.9 %copy-start.2 = (bf16[384,768]{1,0:T(8,128)(2,1)}, bf16[384,768]{1,0:T(8,128)(2,1)S(1)}, u32[]{:S(2)}) copy-start(bf16[384,768]{1,0:T(8,128)(2,1)S(1)} %collective-permute-done.4.refs_2_) | copy-start | bytes 1769476
  34.9 9.8 %collective-permute-start.5 = (bf16[384,768]{1,0:T(8,128)(2,1)S(1)}, bf16[384,768]{1,0:T(8,128)(2,1)S(1)}, u32[]{:S(2)}, u32[]{:S(2)}) collective-permute-start(bf16[384,768]{1,0:T(8,128)(2,1)S(1)} %collective-permute-done.4.refs_2_), channel_id=1, source_target_pairs={{0,8},{8,0},{1,9},{9,1},{2,10},{10,2},{3,11},{11,3},{4,12},{12,4},... | collective-permute-start | bytes 1769480 | tf_op jit(solution)/shard_map/ppermute | solution.py:315
  36.6 13.3 %collective-permute-start.6 = (bf16[128,1536]{1,0:T(8,128)(2,1)S(1)}, bf16[128,1536]{1,0:T(8,128)(2,1)S(1)}, u32[]{:S(2)}, u32[]{:S(2)}) collective-permute-start(bf16[128,1536]{1,0:T(8,128)(2,1)S(1)} %slice.8), channel_id=1, source_target_pairs={{0,1},{1,2},{2,3},{3,0},{4,5},{5,6},{6,7},{7,4},{8,9},{9,10},{10,1... | collective-permute-start | bytes 1179656 | tf_op jit(solution)/shard_map/ppermute | solution.py:311
  37.7 12.2 %collective-permute-start.7 = (bf16[128,1536]{1,0:T(8,128)(2,1)S(1)}, bf16[128,1536]{1,0:T(8,128)(2,1)S(1)}, u32[]{:S(2)}, u32[]{:S(2)}) collective-permute-start(bf16[128,1536]{1,0:T(8,128)(2,1)S(1)} %slice.9), channel_id=1, source_target_pairs={{0,3},{1,0},{2,1},{3,2},{4,7},{5,4},{6,5},{7,6},{8,11},{9,8},{10,9... | collective-permute-start | bytes 1179656 | tf_op jit(solution)/shard_map/ppermute | solution.py:311
  41.0 44.5 %collective-permute-start.14 = (bf16[384,1536]{1,0:T(8,128)(2,1)S(1)}, bf16[384,1536]{1,0:T(8,128)(2,1)S(1)}, u32[]{:S(2)}, u32[]{:S(2)}) collective-permute-start(bf16[384,1536]{1,0:T(8,128)(2,1)S(1)} %copy-done.9), channel_id=1, source_target_pairs={{0,20},{1,21},{2,22},{3,23},{4,16},{5,17},{6,18},{7,19},{16,4},{17... | collective-permute-start | bytes 3538952 | tf_op jit(solution)/shard_map/ppermute | solution.py:319
  49.8 17.3 %collective-permute-start.13 = (bf16[512,384]{1,0:T(8,128)(2,1)}, bf16[512,384]{1,0:T(8,128)(2,1)S(1)}, u32[]{:S(2)}, u32[]{:S(2)}) collective-permute-start(bf16[512,384]{1,0:T(8,128)(2,1)} %shard_map.68), channel_id=1, source_target_pairs={{0,4},{1,5},{2,6},{3,7},{4,0},{5,1},{6,2},{7,3},{8,12},{9,13},{10,... | collective-permute-start | bytes 1179656 | tf_op jit(solution)/shard_map/ppermute | solution.py:311
  55.7 10.8 %copy-start.13 = (bf16[128,1536]{1,0:T(8,128)(2,1)S(1)}, bf16[128,1536]{1,0:T(8,128)(2,1)}, u32[]{:S(2)}) copy-start(bf16[128,1536]{1,0:T(8,128)(2,1)} %copy-done.12) | copy-start | bytes 1179652
  55.7 11.3 %copy-start.15 = (bf16[128,1536]{1,0:T(8,128)(2,1)S(1)}, bf16[128,1536]{1,0:T(8,128)(2,1)}, u32[]{:S(2)}) copy-start(bf16[128,1536]{1,0:T(8,128)(2,1)} %copy-done.14) | copy-start | bytes 1179652
  55.7 29.8 %collective-permute-start.8 = (bf16[256,1536]{1,0:T(8,128)(2,1)}, bf16[256,1536]{1,0:T(8,128)(2,1)S(1)}, u32[]{:S(2)}, u32[]{:S(2)}) collective-permute-start(bf16[256,1536]{1,0:T(8,128)(2,1)} %collective-permute-done.1.refs_7_.refs_5_), channel_id=1, source_target_pairs={{0,1},{1,2},{2,3},{3,0},{4,5},{5,6},{6,7},{7,4},{8,9},{9,10},{10,1... | collective-permute-start | bytes 2359304 | tf_op jit(solution)/shard_map/ppermute | solution.py:311
  55.8 29.7 %collective-permute-start.9 = (bf16[256,1536]{1,0:T(8,128)(2,1)}, bf16[256,1536]{1,0:T(8,128)(2,1)S(1)}, u32[]{:S(2)}, u32[]{:S(2)}) collective-permute-start(bf16[256,1536]{1,0:T(8,128)(2,1)} %collective-permute-done.1.refs_7_.refs_5_), channel_id=1, source_target_pairs={{0,3},{1,0},{2,1},{3,2},{4,7},{5,4},{6,5},{7,6},{8,11},{9,8},{10,9... | collective-permute-start | bytes 2359304 | tf_op jit(solution)/shard_map/ppermute | solution.py:311
  59.1 7.4 %collective-permute-start.10 = (bf16[256,384]{1,0:T(8,128)(2,1)}, bf16[256,384]{1,0:T(8,128)(2,1)}, u32[]{:S(2)}, u32[]{:S(2)}) collective-permute-start(bf16[256,384]{1,0:T(8,128)(2,1)} %get-tuple-element.60), channel_id=1, source_target_pairs={{0,4},{1,5},{2,6},{3,7},{4,0},{5,1},{6,2},{7,3},{8,12},{9,13},{10,... | collective-permute-start | bytes 589832 | tf_op jit(solution)/shard_map/ppermute | solution.py:311
  66.5 18.9 %collective-permute-start.11 = (bf16[128,1536]{1,0:T(8,128)(2,1)S(1)}, bf16[128,1536]{1,0:T(8,128)(2,1)S(1)}, u32[]{:S(2)}, u32[]{:S(2)}) collective-permute-start(bf16[128,1536]{1,0:T(8,128)(2,1)S(1)} %copy-done.13), channel_id=1, source_target_pairs={{0,4},{1,5},{2,6},{3,7},{4,0},{5,1},{6,2},{7,3},{8,12},{9,13},{10,... | collective-permute-start | bytes 1179656 | tf_op jit(solution)/shard_map/ppermute | solution.py:311
  67.1 18.4 %collective-permute-start.12 = (bf16[128,1536]{1,0:T(8,128)(2,1)S(1)}, bf16[128,1536]{1,0:T(8,128)(2,1)S(1)}, u32[]{:S(2)}, u32[]{:S(2)}) collective-permute-start(bf16[128,1536]{1,0:T(8,128)(2,1)S(1)} %copy-done.15), channel_id=1, source_target_pairs={{0,4},{1,5},{2,6},{3,7},{4,0},{5,1},{6,2},{7,3},{8,12},{9,13},{10,... | collective-permute-start | bytes 1179656 | tf_op jit(solution)/shard_map/ppermute | solution.py:311
  85.5 23.1 %collective-permute-start.15 = (bf16[384,3072]{1,0:T(8,128)(2,1)S(1)}, bf16[384,3072]{1,0:T(8,128)(2,1)}, u32[]{:S(2)}, u32[]{:S(2)}) collective-permute-start(bf16[384,3072]{1,0:T(8,128)(2,1)S(1)} %copy-done), channel_id=1, source_target_pairs={{0,8},{8,0},{1,9},{9,1},{2,10},{10,2},{3,11},{11,3},{4,12},{12,4},... | collective-permute-start | bytes 7077896 | tf_op jit(solution)/shard_map/ppermute | solution.py:315
  87.3 21.4 %all-to-all-start.1 = ((bf16[8,256,256]{2,1,0:T(8,128)(2,1)}), bf16[8,256,256]{2,1,0:T(8,128)(2,1)S(1)}, u32[]{:S(2)}, u32[]{:S(2)}) async-start(bf16[8,256,256]{2,1,0:T(8,128)(2,1)} %bitcast.33), calls=%async_computation.1 | async-start | bytes 2097152 | tf_op jit(solution)/shard_map/all_to_all | solution.py:413
  90.8 37.3 %collective-permute-start.17 = (bf16[384,1536]{1,0:T(8,128)(2,1)}, bf16[384,1536]{1,0:T(8,128)(2,1)}, u32[]{:S(2)}, u32[]{:S(2)}) collective-permute-start(bf16[384,1536]{1,0:T(8,128)(2,1)} %copy-done.7), channel_id=1, source_target_pairs={{0,32},{32,0},{64,96},{96,64},{1,33},{33,1},{65,97},{97,65},{2,34}... | collective-permute-start | bytes 3538952 | tf_op jit(solution)/shard_map/ppermute | solution.py:419
  108.6 13.8 %copy-start.4 = (bf16[8,256,256]{2,1,0:T(8,128)(2,1)}, bf16[8,256,256]{2,1,0:T(8,128)(2,1)S(1)}, u32[]{:S(2)}) copy-start(bf16[8,256,256]{2,1,0:T(8,128)(2,1)S(1)} %all-to-all-done.1.first_ref) | copy-start | bytes 3145732
  108.6 19.6 %all-to-all-start.2 = ((bf16[8,256,256]{2,1,0:T(8,128)(2,1)}), bf16[8,256,256]{2,1,0:T(8,128)(2,1)S(1)}, u32[]{:S(2)}, u32[]{:S(2)}) async-start(bf16[8,256,256]{2,1,0:T(8,128)(2,1)} %bitcast.34), calls=%async_computation.2 | async-start | bytes 2097152 | tf_op jit(solution)/shard_map/all_to_all | solution.py:413
  122.5 2.3 %collective-permute-start.16 = (bf16[768,384]{1,0:T(8,128)(2,1)}, bf16[768,384]{1,0:T(8,128)(2,1)S(1)}, u32[]{:S(2)}, u32[]{:S(2)}) collective-permute-start(bf16[768,384]{1,0:T(8,128)(2,1)} %get-tuple-element.80), channel_id=1, source_target_pairs={{0,8},{8,0},{1,9},{9,1},{2,10},{10,2},{3,11},{11,3},{4,12},{12,4},... | collective-permute-start | bytes 1769480 | tf_op jit(solution)/shard_map/ppermute | solution.py:315
  128.2 10.6 %copy-start.5 = (bf16[8,256,256]{2,1,0:T(8,128)(2,1)}, bf16[8,256,256]{2,1,0:T(8,128)(2,1)S(1)}, u32[]{:S(2)}) copy-start(bf16[8,256,256]{2,1,0:T(8,128)(2,1)S(1)} %all-to-all-done.2.second_ref) | copy-start | bytes 3145732
  128.2 10.6 %collective-permute-start.18 = (bf16[384,1536]{1,0:T(8,128)(2,1)S(1)}, bf16[384,1536]{1,0:T(8,128)(2,1)}, u32[]{:S(2)}, u32[]{:S(2)}) collective-permute-start(bf16[384,1536]{1,0:T(8,128)(2,1)S(1)} %copy-done.8), channel_id=1, source_target_pairs={{0,8},{8,0},{1,9},{9,1},{2,10},{10,2},{3,11},{11,3},{4,12},{12,4},... | collective-permute-start | bytes 3538952 | tf_op jit(solution)/shard_map/ppermute | solution.py:315
  128.4 10.4 %collective-permute-start.19 = (bf16[384,1536]{1,0:T(8,128)(2,1)}, bf16[384,1536]{1,0:T(8,128)(2,1)}, u32[]{:S(2)}, u32[]{:S(2)}) collective-permute-start(bf16[384,1536]{1,0:T(8,128)(2,1)} %collective-permute-done.17.w3), channel_id=1, source_target_pairs={{0,8},{8,0},{1,9},{9,1},{2,10},{10,2},{3,11},{11,3},{4,12},{12,4},... | collective-permute-start | bytes 3538952 | tf_op jit(solution)/shard_map/ppermute | solution.py:315
  128.8 24.6 %all-to-all-start.3 = ((bf16[64,36,128]{2,1,0:T(8,128)(2,1)}), bf16[64,36,128]{2,1,0:T(8,128)(2,1)S(1)}, u32[]{:S(2)}, u32[]{:S(2)}) async-start(bf16[64,36,128]{2,1,0:T(8,128)(2,1)} %shard_map.74), calls=%async_computation.3 | async-start | bytes 1310720 | tf_op jit(solution)/shard_map/all_to_all | solution.py:443
  (13 other events, 21.4 us)

commit v12 on v11

--- a/solution.py
+++ b/solution.py
@@ -72,14 +72,18 @@
             pairs.append((weights[f].at[:, cols], held_weight.at[j, rows, :]))
     at = [sum(b.shape[0] for b in blocks[:i]) for i in range(n)]
     spots = [pl.ds(a, b.shape[0]) for a, b in zip(at, blocks)]
-    pairs += [(b, held.at[spot]) for b, spot in zip(blocks, spots)]
+    direct = held.shape[0] == 8
+    if not direct:
+        pairs += [(b, held.at[spot]) for b, spot in zip(blocks, spots)]
     copies = fetch(pairs, sems)
-    for copy in copies[: -n]:
+    for copy in copies[: 4 * len(outs)]:
         copy.wait()
     for i in range(n):
-        copies[i - n].wait()
-        for j, out_ref in enumerate(outs[:2]):
-            out_ref[spots[i], :] = dot(held[spots[i], :], held_weight[j]).astype(BF)
+        if not direct:
+            copies[i - n].wait()
+        rows = blocks[i][...] if direct else held[spots[i], :]
+        for j, out_ref in enumerate(outs):
+            out_ref[spots[i], :] = dot(rows, held_weight[j]).astype(BF)
 
 
 def attention_kernel(
@@ -369,10 +373,10 @@
         return call(
             functools.partial(project_kernel, len(rows)),
             (shape((height, 384)),) * count,
-            [SM, SM] + [ANY] * (4 + len(rows)),
+            [SM, SM] + [ANY] * 4 + [ANY if count == 1 else VM] * len(rows),
             scratch=[
                 pltpu.VMEM((count, D, 384), BF),
-                pltpu.VMEM((height, D), BF),
+                pltpu.VMEM((height if count == 1 else 8, D), BF),
                 pltpu.SemaphoreType.DMA((4 * count + len(rows),)),
             ],
         )(owners, groups, *columns, *rows)

time: 157 us -> 157 us (level)
  no operation moved by 1% of the time
where the time goes in v12:
time: 157 us; the launch traced here: 156 us
  Pallas kernels  71.9 us (46%)
  starting transfers between devices  49 us (31%)
  waiting for transfers between devices  20.9 us (13%)
  local copies, waits for them, and re-layouts  11.6 us (7%)
  between operations  1.67 us (1%)
    pallas_call x2, Pallas kernels, attend(): call(functools.partial(attention_kernel, head), shape((T, 256)), [SM, SM]...  31.9 us
    ppermute x11, starting transfers between devices, send(): return lax.ppermute(v, 'seq', way)  16.2 us
    pallas_call x3, Pallas kernels, project(): call(functools.partial(project_kernel, len(rows)), (shape((height, 384)),...  14.1 us
    all_to_all x1, waiting for transfers between devices, body(): lax.all_to_all(tie((upstream, normed))[0], 'seq', 0, 0, tiled=True)  13.6 us
    all_to_all x1, starting transfers between devices, body(): partial = lax.all_to_all(partial, ('dp', 'zh', 'seq'), 0, 0, tiled=True)  10 us
    pallas_call x1, Pallas kernels, body(): call(input_gradient_kernel, (shape((ROWS, 1024)), shape((ROWS, D), F32)),...  9.59 us
    all_to_all x2, starting transfers between devices, send_back(): lax.all_to_all(grads.reshape(SEQ, ROWS, 256), 'seq', 0, 0, tiled=True)  8.9 us
    pallas_call x1, Pallas kernels, body(): call(weight_gradient_kernel, (shape((768, 384), F32), shape((768, 384))),...  8.46 us
  transfers between devices with their start and end apart: 24, of which 4 were waited for; matrix products, arithmetic and copies ran while one was open for 5% of the time, Pallas kernels for 43%

profile of v12, /device:TPU:0, one launch (start us, length us, event | category | flops | bytes accessed | tf_op | source)
XLA Modules:
  0.0 156.3 jit_solution(14293254875361595819)
XLA Ops:
  0.7 3.5 %shard_map.67 = (bf16[256,1536]{1,0:T(8,128)(2,1)}, bf16[384,768]{1,0:T(8,128)(2,1)}) custom-call(s32[1]{0:T(128)} %bitcast.y_ref, bf16[256,1536]{1,0:T(8,128)(2,1)} %bitcast.29, bf16[384,3072]{1,0:T(8,128)(2,1)} %w0.1), custom_call_target="tpu_custom_call" | custom-call | bytes 1048576 | tf_op jit(solution)/shard_map/pallas_call | solution.py:346
  4.1 2.1 %collective-permute-start.1 = (bf16[256,1536]{1,0:T(8,128)(2,1)}, bf16[256,1536]{1,0:T(8,128)(2,1)}, u32[]{:S(2)}, u32[]{:S(2)}) collective-permute-start(bf16[256,1536]{1,0:T(8,128)(2,1)} %get-tuple-element.49.refs_4_.refs_0_), channel_id=1, source_target_pairs={{0,4},{1,5},{2,6},{3,7},{4,0},{5,1},{6,2},{7,3},{8,12},{9,13},{10,... | collective-permute-start | bytes 2359304 | tf_op jit(solution)/shard_map/ppermute | solution.py:315
  6.2 3.0 %collective-permute-start.2 = (bf16[256,1536]{1,0:T(8,128)(2,1)}, bf16[256,1536]{1,0:T(8,128)(2,1)}, u32[]{:S(2)}, u32[]{:S(2)}) collective-permute-start(bf16[256,1536]{1,0:T(8,128)(2,1)} %get-tuple-element.49.refs_4_.refs_0_), channel_id=1, source_target_pairs={{0,3},{1,0},{2,1},{3,2},{4,7},{5,4},{6,5},{7,6},{8,11},{9,8},{10,9... | collective-permute-start | bytes 2359304 | tf_op jit(solution)/shard_map/ppermute | solution.py:315
  9.2 2.5 %collective-permute-start.4 = (bf16[384,768]{1,0:T(8,128)(2,1)}, bf16[384,768]{1,0:T(8,128)(2,1)S(1)}, u32[]{:S(2)}, u32[]{:S(2)}) collective-permute-start(bf16[384,768]{1,0:T(8,128)(2,1)} %get-tuple-element.48.refs_0_), channel_id=1, source_target_pairs={{0,20},{1,21},{2,22},{3,23},{4,16},{5,17},{6,18},{7,19},{16,4},{17... | collective-permute-start | bytes 1769480 | tf_op jit(solution)/shard_map/ppermute | solution.py:323
  11.9 0.9 copy.10
  12.7 5.0 %all-to-all-start = ((bf16[8,256,128]{2,1,0:T(8,128)(2,1)}), bf16[8,256,128]{2,1,0:T(8,128)(2,1)}, u32[]{:S(2)}, u32[]{:S(2)}) async-start(bf16[8,256,128]{2,1,0:T(8,128)(2,1)} %bitcast.31), calls=%async_computation | async-start | bytes 1048576 | tf_op jit(solution)/shard_map/all_to_all | solution.py:360
  20.2 1.1 constant_dynamic-slice_fusion
  21.3 13.6 %all-to-all-done = bf16[8,256,128]{2,1,0:T(8,128)(2,1)} async-done(((bf16[8,256,128]{2,1,0:T(8,128)(2,1)}), bf16[8,256,128]{2,1,0:T(8,128)(2,1)}, u32[]{:S(2)}, u32[]{:S(2)}) %all-to-all-start) | async-done | bytes 524320 | tf_op jit(solution)/shard_map/all_to_all | solution.py:360
  35.0 1.5 slice.8
  36.6 1.0 slice.9
  37.7 3.3 %collective-permute-start.7 = (bf16[128,1536]{1,0:T(8,128)(2,1)S(1)}, bf16[128,1536]{1,0:T(8,128)(2,1)S(1)}, u32[]{:S(2)}, u32[]{:S(2)}) collective-permute-start(bf16[128,1536]{1,0:T(8,128)(2,1)S(1)} %slice.9), channel_id=1, source_target_pairs={{0,3},{1,0},{2,1},{3,2},{4,7},{5,4},{6,5},{7,6},{8,11},{9,8},{10,9... | collective-permute-start | bytes 1179656 | tf_op jit(solution)/shard_map/ppermute | solution.py:315
  41.0 3.8 %collective-permute-start.14 = (bf16[384,1536]{1,0:T(8,128)(2,1)S(1)}, bf16[384,1536]{1,0:T(8,128)(2,1)S(1)}, u32[]{:S(2)}, u32[]{:S(2)}) collective-permute-start(bf16[384,1536]{1,0:T(8,128)(2,1)S(1)} %copy-done.9), channel_id=1, source_target_pairs={{0,20},{1,21},{2,22},{3,23},{4,16},{5,17},{6,18},{7,19},{16,4},{17... | collective-permute-start | bytes 3538952 | tf_op jit(solution)/shard_map/ppermute | solution.py:323
  45.6 4.2 %shard_map.68 = bf16[512,384]{1,0:T(8,128)(2,1)} custom-call(s32[5]{0:T(128)} %stack.75.owner_ref.pos_ref, s32[3]{0:T(128)} %pad_add_fusion.group_ref, bf16[384,768]{1,0:T(8,128)(2,1)} %get-tuple-element.48.refs_0_, bf16[384,768]{1,0:T(8,128)(2,1)} %copy-done.1, bf16[384,768]{1,0:T(8,128)(2,1)} %copy-done.2, bf16[384,768]{1,0:T(8,128)(2,1)} %copy-done.3, ...), custom_call_target="tpu_custom_call" | custom-call | bytes 1048576 | tf_op jit(solution)/shard_map/pallas_call | solution.py:373
  51.4 4.5 %shard_map.69 = (bf16[256,384]{1,0:T(8,128)(2,1)}, bf16[256,384]{1,0:T(8,128)(2,1)}) custom-call(s32[5]{0:T(128)} %stack.75.owner_ref.pos_ref, s32[3]{0:T(128)} %pad_add_fusion.group_ref, bf16[384,768]{1,0:T(8,128)(2,1)} %get-tuple-element.48.refs_0_, bf16[384,768]{1,0:T(8,128)(2,1)} %copy-done.1, bf16[384,768]{1,0:T(8,128)(2,1)} %copy-done.2, ...), custom_call_target="tpu_custom_call" | custom-call | bytes 1048576 | tf_op jit(solution)/shard_map/pallas_call | solution.py:373
  56.0 3.2 %collective-permute-start.9 = (bf16[256,1536]{1,0:T(8,128)(2,1)}, bf16[256,1536]{1,0:T(8,128)(2,1)S(1)}, u32[]{:S(2)}, u32[]{:S(2)}) collective-permute-start(bf16[256,1536]{1,0:T(8,128)(2,1)} %collective-permute-done.1.refs_7_.refs_5_), channel_id=1, source_target_pairs={{0,3},{1,0},{2,1},{3,2},{4,7},{5,4},{6,5},{7,6},{8,11},{9,8},{10,9... | collective-permute-start | bytes 2359304 | tf_op jit(solution)/shard_map/ppermute | solution.py:315
  59.2 2.0 %collective-permute-start.10 = (bf16[256,384]{1,0:T(8,128)(2,1)}, bf16[256,384]{1,0:T(8,128)(2,1)}, u32[]{:S(2)}, u32[]{:S(2)}) collective-permute-start(bf16[256,384]{1,0:T(8,128)(2,1)} %get-tuple-element.60), channel_id=1, source_target_pairs={{0,4},{1,5},{2,6},{3,7},{4,0},{5,1},{6,2},{7,3},{8,12},{9,13},{10,... | collective-permute-start | bytes 589832 | tf_op jit(solution)/shard_map/ppermute | solution.py:315
  61.2 5.4 %shard_map.70.kept_ref = bf16[1024,384]{1,0:T(8,128)(2,1)} custom-call(s32[5]{0:T(128)} %stack.75.owner_ref.pos_ref, s32[2]{0:T(128)} %pad_add_fusion.1.group_ref, bf16[384,768]{1,0:T(8,128)(2,1)} %get-tuple-element.48.refs_0_, bf16[384,768]{1,0:T(8,128)(2,1)} %copy-done.1, bf16[384,768]{1,0:T(8,128)(2,1)} %copy-done.2, bf16[384,768]{1,0:T(8,128)(2,1)} %copy-done.3, ...), custom_call_target="tpu_custom_call" | custom-call | bytes 1048576 | tf_op jit(solution)/shard_map/pallas_call | solution.py:373
  67.2 1.8 %collective-permute-start.12 = (bf16[128,1536]{1,0:T(8,128)(2,1)S(1)}, bf16[128,1536]{1,0:T(8,128)(2,1)S(1)}, u32[]{:S(2)}, u32[]{:S(2)}) collective-permute-start(bf16[128,1536]{1,0:T(8,128)(2,1)S(1)} %copy-done.15), channel_id=1, source_target_pairs={{0,4},{1,5},{2,6},{3,7},{4,0},{5,1},{6,2},{7,3},{8,12},{9,13},{10,... | collective-permute-start | bytes 1179656 | tf_op jit(solution)/shard_map/ppermute | solution.py:315
  69.7 15.9 %shard_map.71.first_ref = bf16[2048,256]{1,0:T(8,128)(2,1)} custom-call(s32[9]{0:T(128)} %stack.69.pos_ref, s32[1]{0:T(128)S(6)} %copy.11.len_ref, bf16[1024,384]{1,0:T(8,128)(2,1)} %shard_map.70.kept_ref, bf16[256,384]{1,0:T(8,128)(2,1)} %get-tuple-element.68.far_ref, bf16[512,384]{1,0:T(8,128)(2,1)} %copy-done.18, ...), custom_call_target="tpu_custom_call" | custom-call | flops 1000000000 | bytes 1048576 | tf_op jit(solution)/shard_map/pallas_call | solution.py:397
  87.4 3.6 %all-to-all-start.1 = ((bf16[8,256,256]{2,1,0:T(8,128)(2,1)}), bf16[8,256,256]{2,1,0:T(8,128)(2,1)S(1)}, u32[]{:S(2)}, u32[]{:S(2)}) async-start(bf16[8,256,256]{2,1,0:T(8,128)(2,1)} %bitcast.33), calls=%async_computation.1 | async-start | bytes 2097152 | tf_op jit(solution)/shard_map/all_to_all | solution.py:417
  91.0 1.8 %collective-permute-start.17 = (bf16[384,1536]{1,0:T(8,128)(2,1)}, bf16[384,1536]{1,0:T(8,128)(2,1)}, u32[]{:S(2)}, u32[]{:S(2)}) collective-permute-start(bf16[384,1536]{1,0:T(8,128)(2,1)} %copy-done.7), channel_id=1, source_target_pairs={{0,32},{32,0},{64,96},{96,64},{1,33},{33,1},{65,97},{97,65},{2,34}... | collective-permute-start | bytes 3538952 | tf_op jit(solution)/shard_map/ppermute | solution.py:423
  92.8 16.0 %shard_map.72.second_ref = bf16[2048,256]{1,0:T(8,128)(2,1)} custom-call(s32[9]{0:T(128)} %stack.69.pos_ref, s32[1]{0:T(128)S(6)} %copy.11.len_ref, bf16[1024,384]{1,0:T(8,128)(2,1)} %shard_map.70.kept_ref, bf16[256,384]{1,0:T(8,128)(2,1)} %get-tuple-element.68.far_ref, bf16[512,384]{1,0:T(8,128)(2,1)} %copy-done.18, ...), custom_call_target="tpu_custom_call" | custom-call | flops 10000000000 | bytes 1048576 | tf_op jit(solution)/shard_map/pallas_call | solution.py:397
  108.8 5.3 %all-to-all-start.2 = ((bf16[8,256,256]{2,1,0:T(8,128)(2,1)}), bf16[8,256,256]{2,1,0:T(8,128)(2,1)S(1)}, u32[]{:S(2)}, u32[]{:S(2)}) async-start(bf16[8,256,256]{2,1,0:T(8,128)(2,1)} %bitcast.34), calls=%async_computation.2 | async-start | bytes 2097152 | tf_op jit(solution)/shard_map/all_to_all | solution.py:417
  114.1 8.5 %shard_map.73 = (f32[768,384]{1,0:T(8,128)}, bf16[768,384]{1,0:T(8,128)(2,1)}) custom-call(s32[9]{0:T(128)} %stack.69.pos_ref, bf16[2048,256]{1,0:T(8,128)(2,1)} %shard_map.71.first_ref, bf16[2048,256]{1,0:T(8,128)(2,1)} %shard_map.72.second_ref, bf16[256,1536]{1,0:T(8,128)(2,1)} %get-tuple-element.49.refs_4_.refs_0_, ...), custom_call_target="tpu_custom_call" | custom-call | flops 2415919104 | bytes 1048576 | tf_op jit(solution)/shard_map/pallas_call | solution.py:430
  122.7 2.2 %collective-permute-done.16.got_ref = bf16[768,384]{1,0:T(8,128)(2,1)S(1)} collective-permute-done((bf16[768,384]{1,0:T(8,128)(2,1)}, bf16[768,384]{1,0:T(8,128)(2,1)S(1)}, u32[]{:S(2)}, u32[]{:S(2)}) %collective-permute-start.16) | collective-permute-done | bytes 589856 | tf_op jit(solution)/shard_map/ppermute | solution.py:319
  124.9 0.9 copy-done.10
  125.8 2.5 %shard_map.74 = bf16[64,36,128]{2,1,0:T(8,128)(2,1)} custom-call(f32[768,384]{1,0:T(8,128)} %get-tuple-element.79.keep_ref, bf16[768,384]{1,0:T(8,128)(2,1)} %copy-done.10), custom_call_target="tpu_custom_call" | custom-call | bytes 1048576 | tf_op jit(solution)/shard_map/pallas_call | solution.py:443
  128.9 10.0 %all-to-all-start.3 = ((bf16[64,36,128]{2,1,0:T(8,128)(2,1)}), bf16[64,36,128]{2,1,0:T(8,128)(2,1)S(1)}, u32[]{:S(2)}, u32[]{:S(2)}) async-start(bf16[64,36,128]{2,1,0:T(8,128)(2,1)} %shard_map.74), calls=%async_computation.3 | async-start | bytes 1310720 | tf_op jit(solution)/shard_map/all_to_all | solution.py:447
  139.0 9.6 %shard_map.75 = (bf16[256,1024]{1,0:T(8,128)(2,1)}, f32[256,1536]{1,0:T(8,128)}) custom-call(s32[5]{0:T(128)} %stack.75.owner_ref.pos_ref, bf16[8,256,256]{2,1,0:T(8,128)(2,1)} %copy-done.4, bf16[8,256,256]{2,1,0:T(8,128)(2,1)} %copy-done.5, bf16[384,3072]{1,0:T(8,128)(2,1)} %w0.1, bf16[384,3072]{1,0:T(8,128)(2,1)} %collective-permute-done.15.w1, ...), custom_call_target="tpu_custom_call" | custom-call | flops 2415919104 | bytes 1048576 | tf_op jit(solution)/shard_map/pallas_call | solution.py:448
  148.6 4.9 %all-to-all-done.3.parts_ref = bf16[64,36,128]{2,1,0:T(8,128)(2,1)S(1)} async-done(((bf16[64,36,128]{2,1,0:T(8,128)(2,1)}), bf16[64,36,128]{2,1,0:T(8,128)(2,1)S(1)}, u32[]{:S(2)}, u32[]{:S(2)}) %all-to-all-start.3) | async-done | bytes 589856 | tf_op jit(solution)/shard_map/all_to_all | solution.py:447
  153.5 0.9 copy-done.6
  154.4 1.9 %shard_map.76 = f32[12,3072]{1,0:T(8,128)} custom-call(bf16[64,36,128]{2,1,0:T(8,128)(2,1)} %copy-done.6), custom_call_target="tpu_custom_call" | custom-call | bytes 1048576 | tf_op jit(solution)/shard_map/pallas_call | solution.py:460
  (77 shorter events, 8.3 us)
Async XLA Ops:
  0.6 11.1 %copy-start.11 = (bf16[1,256,1024]{2,1,0:T(8,128)(2,1)S(1)}, bf16[1,256,1024]{2,1,0:T(8,128)(2,1)}, u32[]{:S(2)}) copy-start(bf16[1,256,1024]{2,1,0:T(8,128)(2,1)} %param.7) | copy-start | bytes 1572868
  4.1 30.8 %collective-permute-start.1 = (bf16[256,1536]{1,0:T(8,128)(2,1)}, bf16[256,1536]{1,0:T(8,128)(2,1)}, u32[]{:S(2)}, u32[]{:S(2)}) collective-permute-start(bf16[256,1536]{1,0:T(8,128)(2,1)} %get-tuple-element.49.refs_4_.refs_0_), channel_id=1, source_target_pairs={{0,4},{1,5},{2,6},{3,7},{4,0},{5,1},{6,2},{7,3},{8,12},{9,13},{10,... | collective-permute-start | bytes 2359304 | tf_op jit(solution)/shard_map/ppermute | solution.py:315
  6.2 28.7 %collective-permute-start.2 = (bf16[256,1536]{1,0:T(8,128)(2,1)}, bf16[256,1536]{1,0:T(8,128)(2,1)}, u32[]{:S(2)}, u32[]{:S(2)}) collective-permute-start(bf16[256,1536]{1,0:T(8,128)(2,1)} %get-tuple-element.49.refs_4_.refs_0_), channel_id=1, source_target_pairs={{0,3},{1,0},{2,1},{3,2},{4,7},{5,4},{6,5},{7,6},{8,11},{9,8},{10,9... | collective-permute-start | bytes 2359304 | tf_op jit(solution)/shard_map/ppermute | solution.py:315
  9.2 25.7 %collective-permute-start.3 = (bf16[256,1536]{1,0:T(8,128)(2,1)}, bf16[256,1536]{1,0:T(8,128)(2,1)}, u32[]{:S(2)}, u32[]{:S(2)}) collective-permute-start(bf16[256,1536]{1,0:T(8,128)(2,1)} %get-tuple-element.49.refs_4_.refs_0_), channel_id=1, source_target_pairs={{0,1},{1,2},{2,3},{3,0},{4,5},{5,6},{6,7},{7,4},{8,9},{9,10},{10,1... | collective-permute-start | bytes 2359304 | tf_op jit(solution)/shard_map/ppermute | solution.py:315
  9.2 25.7 %collective-permute-start = (bf16[384,768]{1,0:T(8,128)(2,1)}, bf16[384,768]{1,0:T(8,128)(2,1)S(1)}, u32[]{:S(2)}, u32[]{:S(2)}) collective-permute-start(bf16[384,768]{1,0:T(8,128)(2,1)} %get-tuple-element.48.refs_0_), channel_id=1, source_target_pairs={{0,8},{8,0},{1,9},{9,1},{2,10},{10,2},{3,11},{11,3},{4,12},{12,4},... | collective-permute-start | bytes 1769480 | tf_op jit(solution)/shard_map/ppermute | solution.py:319
  9.2 25.7 %collective-permute-start.4 = (bf16[384,768]{1,0:T(8,128)(2,1)}, bf16[384,768]{1,0:T(8,128)(2,1)S(1)}, u32[]{:S(2)}, u32[]{:S(2)}) collective-permute-start(bf16[384,768]{1,0:T(8,128)(2,1)} %get-tuple-element.48.refs_0_), channel_id=1, source_target_pairs={{0,20},{1,21},{2,22},{3,23},{4,16},{5,17},{6,18},{7,19},{16,4},{17... | collective-permute-start | bytes 1769480 | tf_op jit(solution)/shard_map/ppermute | solution.py:323
  11.8 8.5 %copy-start = (bf16[384,3072]{1,0:T(8,128)(2,1)S(1)}, bf16[384,3072]{1,0:T(8,128)(2,1)}, u32[]{:S(2)}) copy-start(bf16[384,3072]{1,0:T(8,128)(2,1)} %w0.1) | copy-start | bytes 7077892
  12.7 22.1 %all-to-all-start = ((bf16[8,256,128]{2,1,0:T(8,128)(2,1)}), bf16[8,256,128]{2,1,0:T(8,128)(2,1)}, u32[]{:S(2)}, u32[]{:S(2)}) async-start(bf16[8,256,128]{2,1,0:T(8,128)(2,1)} %bitcast.31), calls=%async_computation | async-start | bytes 1048576 | tf_op jit(solution)/shard_map/all_to_all | solution.py:360
  34.9 9.9 %copy-start.1 = (bf16[384,768]{1,0:T(8,128)(2,1)}, bf16[384,768]{1,0:T(8,128)(2,1)S(1)}, u32[]{:S(2)}) copy-start(bf16[384,768]{1,0:T(8,128)(2,1)S(1)} %collective-permute-done.refs_1_) | copy-start | bytes 1769476
  34.9 9.9 %copy-start.2 = (bf16[384,768]{1,0:T(8,128)(2,1)}, bf16[384,768]{1,0:T(8,128)(2,1)S(1)}, u32[]{:S(2)}) copy-start(bf16[384,768]{1,0:T(8,128)(2,1)S(1)} %collective-permute-done.4.refs_2_) | copy-start | bytes 1769476
  34.9 9.8 %collective-permute-start.5 = (bf16[384,768]{1,0:T(8,128)(2,1)S(1)}, bf16[384,768]{1,0:T(8,128)(2,1)S(1)}, u32[]{:S(2)}, u32[]{:S(2)}) collective-permute-start(bf16[384,768]{1,0:T(8,128)(2,1)S(1)} %collective-permute-done.4.refs_2_), channel_id=1, source_target_pairs={{0,8},{8,0},{1,9},{9,1},{2,10},{10,2},{3,11},{11,3},{4,12},{12,4},... | collective-permute-start | bytes 1769480 | tf_op jit(solution)/shard_map/ppermute | solution.py:319
  36.6 13.3 %collective-permute-start.6 = (bf16[128,1536]{1,0:T(8,128)(2,1)S(1)}, bf16[128,1536]{1,0:T(8,128)(2,1)S(1)}, u32[]{:S(2)}, u32[]{:S(2)}) collective-permute-start(bf16[128,1536]{1,0:T(8,128)(2,1)S(1)} %slice.8), channel_id=1, source_target_pairs={{0,1},{1,2},{2,3},{3,0},{4,5},{5,6},{6,7},{7,4},{8,9},{9,10},{10,1... | collective-permute-start | bytes 1179656 | tf_op jit(solution)/shard_map/ppermute | solution.py:315
  37.7 12.2 %collective-permute-start.7 = (bf16[128,1536]{1,0:T(8,128)(2,1)S(1)}, bf16[128,1536]{1,0:T(8,128)(2,1)S(1)}, u32[]{:S(2)}, u32[]{:S(2)}) collective-permute-start(bf16[128,1536]{1,0:T(8,128)(2,1)S(1)} %slice.9), channel_id=1, source_target_pairs={{0,3},{1,0},{2,1},{3,2},{4,7},{5,4},{6,5},{7,6},{8,11},{9,8},{10,9... | collective-permute-start | bytes 1179656 | tf_op jit(solution)/shard_map/ppermute | solution.py:315
  41.0 44.7 %collective-permute-start.14 = (bf16[384,1536]{1,0:T(8,128)(2,1)S(1)}, bf16[384,1536]{1,0:T(8,128)(2,1)S(1)}, u32[]{:S(2)}, u32[]{:S(2)}) collective-permute-start(bf16[384,1536]{1,0:T(8,128)(2,1)S(1)} %copy-done.9), channel_id=1, source_target_pairs={{0,20},{1,21},{2,22},{3,23},{4,16},{5,17},{6,18},{7,19},{16,4},{17... | collective-permute-start | bytes 3538952 | tf_op jit(solution)/shard_map/ppermute | solution.py:323
  49.8 17.4 %collective-permute-start.13 = (bf16[512,384]{1,0:T(8,128)(2,1)}, bf16[512,384]{1,0:T(8,128)(2,1)S(1)}, u32[]{:S(2)}, u32[]{:S(2)}) collective-permute-start(bf16[512,384]{1,0:T(8,128)(2,1)} %shard_map.68), channel_id=1, source_target_pairs={{0,4},{1,5},{2,6},{3,7},{4,0},{5,1},{6,2},{7,3},{8,12},{9,13},{10,... | collective-permute-start | bytes 1179656 | tf_op jit(solution)/shard_map/ppermute | solution.py:315
  55.9 10.8 %copy-start.13 = (bf16[128,1536]{1,0:T(8,128)(2,1)S(1)}, bf16[128,1536]{1,0:T(8,128)(2,1)}, u32[]{:S(2)}) copy-start(bf16[128,1536]{1,0:T(8,128)(2,1)} %copy-done.12) | copy-start | bytes 1179652
  55.9 11.3 %copy-start.15 = (bf16[128,1536]{1,0:T(8,128)(2,1)S(1)}, bf16[128,1536]{1,0:T(8,128)(2,1)}, u32[]{:S(2)}) copy-start(bf16[128,1536]{1,0:T(8,128)(2,1)} %copy-done.14) | copy-start | bytes 1179652
  55.9 29.8 %collective-permute-start.8 = (bf16[256,1536]{1,0:T(8,128)(2,1)}, bf16[256,1536]{1,0:T(8,128)(2,1)S(1)}, u32[]{:S(2)}, u32[]{:S(2)}) collective-permute-start(bf16[256,1536]{1,0:T(8,128)(2,1)} %collective-permute-done.1.refs_7_.refs_5_), channel_id=1, source_target_pairs={{0,1},{1,2},{2,3},{3,0},{4,5},{5,6},{6,7},{7,4},{8,9},{9,10},{10,1... | collective-permute-start | bytes 2359304 | tf_op jit(solution)/shard_map/ppermute | solution.py:315
  56.0 29.7 %collective-permute-start.9 = (bf16[256,1536]{1,0:T(8,128)(2,1)}, bf16[256,1536]{1,0:T(8,128)(2,1)S(1)}, u32[]{:S(2)}, u32[]{:S(2)}) collective-permute-start(bf16[256,1536]{1,0:T(8,128)(2,1)} %collective-permute-done.1.refs_7_.refs_5_), channel_id=1, source_target_pairs={{0,3},{1,0},{2,1},{3,2},{4,7},{5,4},{6,5},{7,6},{8,11},{9,8},{10,9... | collective-permute-start | bytes 2359304 | tf_op jit(solution)/shard_map/ppermute | solution.py:315
  59.2 7.4 %collective-permute-start.10 = (bf16[256,384]{1,0:T(8,128)(2,1)}, bf16[256,384]{1,0:T(8,128)(2,1)}, u32[]{:S(2)}, u32[]{:S(2)}) collective-permute-start(bf16[256,384]{1,0:T(8,128)(2,1)} %get-tuple-element.60), channel_id=1, source_target_pairs={{0,4},{1,5},{2,6},{3,7},{4,0},{5,1},{6,2},{7,3},{8,12},{9,13},{10,... | collective-permute-start | bytes 589832 | tf_op jit(solution)/shard_map/ppermute | solution.py:315
  66.7 18.9 %collective-permute-start.11 = (bf16[128,1536]{1,0:T(8,128)(2,1)S(1)}, bf16[128,1536]{1,0:T(8,128)(2,1)S(1)}, u32[]{:S(2)}, u32[]{:S(2)}) collective-permute-start(bf16[128,1536]{1,0:T(8,128)(2,1)S(1)} %copy-done.13), channel_id=1, source_target_pairs={{0,4},{1,5},{2,6},{3,7},{4,0},{5,1},{6,2},{7,3},{8,12},{9,13},{10,... | collective-permute-start | bytes 1179656 | tf_op jit(solution)/shard_map/ppermute | solution.py:315
  67.2 18.4 %collective-permute-start.12 = (bf16[128,1536]{1,0:T(8,128)(2,1)S(1)}, bf16[128,1536]{1,0:T(8,128)(2,1)S(1)}, u32[]{:S(2)}, u32[]{:S(2)}) collective-permute-start(bf16[128,1536]{1,0:T(8,128)(2,1)S(1)} %copy-done.15), channel_id=1, source_target_pairs={{0,4},{1,5},{2,6},{3,7},{4,0},{5,1},{6,2},{7,3},{8,12},{9,13},{10,... | collective-permute-start | bytes 1179656 | tf_op jit(solution)/shard_map/ppermute | solution.py:315
  85.7 23.1 %collective-permute-start.15 = (bf16[384,3072]{1,0:T(8,128)(2,1)S(1)}, bf16[384,3072]{1,0:T(8,128)(2,1)}, u32[]{:S(2)}, u32[]{:S(2)}) collective-permute-start(bf16[384,3072]{1,0:T(8,128)(2,1)S(1)} %copy-done), channel_id=1, source_target_pairs={{0,8},{8,0},{1,9},{9,1},{2,10},{10,2},{3,11},{11,3},{4,12},{12,4},... | collective-permute-start | bytes 7077896 | tf_op jit(solution)/shard_map/ppermute | solution.py:319
  87.4 21.4 %all-to-all-start.1 = ((bf16[8,256,256]{2,1,0:T(8,128)(2,1)}), bf16[8,256,256]{2,1,0:T(8,128)(2,1)S(1)}, u32[]{:S(2)}, u32[]{:S(2)}) async-start(bf16[8,256,256]{2,1,0:T(8,128)(2,1)} %bitcast.33), calls=%async_computation.1 | async-start | bytes 2097152 | tf_op jit(solution)/shard_map/all_to_all | solution.py:417
  91.0 37.3 %collective-permute-start.17 = (bf16[384,1536]{1,0:T(8,128)(2,1)}, bf16[384,1536]{1,0:T(8,128)(2,1)}, u32[]{:S(2)}, u32[]{:S(2)}) collective-permute-start(bf16[384,1536]{1,0:T(8,128)(2,1)} %copy-done.7), channel_id=1, source_target_pairs={{0,32},{32,0},{64,96},{96,64},{1,33},{33,1},{65,97},{97,65},{2,34}... | collective-permute-start | bytes 3538952 | tf_op jit(solution)/shard_map/ppermute | solution.py:423
  108.8 13.8 %copy-start.4 = (bf16[8,256,256]{2,1,0:T(8,128)(2,1)}, bf16[8,256,256]{2,1,0:T(8,128)(2,1)S(1)}, u32[]{:S(2)}) copy-start(bf16[8,256,256]{2,1,0:T(8,128)(2,1)S(1)} %all-to-all-done.1.first_ref) | copy-start | bytes 3145732
  108.8 19.6 %all-to-all-start.2 = ((bf16[8,256,256]{2,1,0:T(8,128)(2,1)}), bf16[8,256,256]{2,1,0:T(8,128)(2,1)S(1)}, u32[]{:S(2)}, u32[]{:S(2)}) async-start(bf16[8,256,256]{2,1,0:T(8,128)(2,1)} %bitcast.34), calls=%async_computation.2 | async-start | bytes 2097152 | tf_op jit(solution)/shard_map/all_to_all | solution.py:417
  122.6 2.3 %collective-permute-start.16 = (bf16[768,384]{1,0:T(8,128)(2,1)}, bf16[768,384]{1,0:T(8,128)(2,1)S(1)}, u32[]{:S(2)}, u32[]{:S(2)}) collective-permute-start(bf16[768,384]{1,0:T(8,128)(2,1)} %get-tuple-element.80), channel_id=1, source_target_pairs={{0,8},{8,0},{1,9},{9,1},{2,10},{10,2},{3,11},{11,3},{4,12},{12,4},... | collective-permute-start | bytes 1769480 | tf_op jit(solution)/shard_map/ppermute | solution.py:319
  128.4 10.6 %copy-start.5 = (bf16[8,256,256]{2,1,0:T(8,128)(2,1)}, bf16[8,256,256]{2,1,0:T(8,128)(2,1)S(1)}, u32[]{:S(2)}) copy-start(bf16[8,256,256]{2,1,0:T(8,128)(2,1)S(1)} %all-to-all-done.2.second_ref) | copy-start | bytes 3145732
  128.4 10.6 %collective-permute-start.18 = (bf16[384,1536]{1,0:T(8,128)(2,1)S(1)}, bf16[384,1536]{1,0:T(8,128)(2,1)}, u32[]{:S(2)}, u32[]{:S(2)}) collective-permute-start(bf16[384,1536]{1,0:T(8,128)(2,1)S(1)} %copy-done.8), channel_id=1, source_target_pairs={{0,8},{8,0},{1,9},{9,1},{2,10},{10,2},{3,11},{11,3},{4,12},{12,4},... | collective-permute-start | bytes 3538952 | tf_op jit(solution)/shard_map/ppermute | solution.py:319
  128.5 10.4 %collective-permute-start.19 = (bf16[384,1536]{1,0:T(8,128)(2,1)}, bf16[384,1536]{1,0:T(8,128)(2,1)}, u32[]{:S(2)}, u32[]{:S(2)}) collective-permute-start(bf16[384,1536]{1,0:T(8,128)(2,1)} %collective-permute-done.17.w3), channel_id=1, source_target_pairs={{0,8},{8,0},{1,9},{9,1},{2,10},{10,2},{3,11},{11,3},{4,12},{12,4},... | collective-permute-start | bytes 3538952 | tf_op jit(solution)/shard_map/ppermute | solution.py:319
  128.9 24.6 %all-to-all-start.3 = ((bf16[64,36,128]{2,1,0:T(8,128)(2,1)}), bf16[64,36,128]{2,1,0:T(8,128)(2,1)S(1)}, u32[]{:S(2)}, u32[]{:S(2)}) async-start(bf16[64,36,128]{2,1,0:T(8,128)(2,1)} %shard_map.74), calls=%async_computation.3 | async-start | bytes 1310720 | tf_op jit(solution)/shard_map/all_to_all | solution.py:447
  (13 other events, 21.4 us)
